TPU v7x, 32 devices: a whole 2x2x4 slice. The times are simulated.
32 devices in a mesh: obs: 4 (over z), lat: 8 (over y, x, core).
Axes of the slice: x: 2, y: 2, z: 4, core: 2. Of those that a mesh axis runs over, the one named last changes fastest.
Arguments:
- footprints: bfloat16 [4, 8, 384, 128, 128], P('obs', 'lat'), may hold values from -0.078125 to 0.078125
- block_rows: int32 [4, 8, 384], P('obs', 'lat'), may hold values from 0 to 31
- block_cols: int32 [4, 8, 384], P('obs', 'lat'), may hold values from 0 to 639
- block_scale: int32 [4, 8, 384], P('obs', 'lat'), may hold values from 0 to 3
- lat_width: int32 [256], replicated, may hold values from 1 to 32, as said below
- lon_width: int32 [256], replicated, may hold values from 1 to 80
- obs_weight: float32 [16384], P('obs'), may hold values from 0.3 to 3
- solution: float32 [8, 4, 256, 640], P(None, None, 'lat'), may hold values from -6 to 6
- residual: float32 [8, 4, 256, 640], P(None, None, 'lat'), may hold values from -6 to 6
- direction: float32 [8, 4, 256, 640], P(None, None, 'lat'), may hold values from -6 to 6
Outputs:
- next_solution: float32 [8, 4, 256, 640], P(None, None, 'lat')
- next_residual: float32 [8, 4, 256, 640], P(None, None, 'lat')
- next_direction: float32 [8, 4, 256, 640], P(None, None, 'lat')
Inputs may be any that keep to these rules, and one draw needn't show every extreme that they name: `lat_width`: some latitude row has band width exactly 32.
All inputs are finite; a program needn't handle non-finite values.
Results may differ from a plain program's by a relative error of at most 0.00039.
Values may be sent and summed in bfloat16 or wider, within the bound.
No kernel may reach another device: no remote copies, remote signals or barrier semaphores. Data moves between devices by JAX's collectives and lax.ppermute only.
A program may use at most 128 MiB of HBM per device.

v0:
```python
import jax
import jax.numpy as jnp
from jax import lax
from jax.sharding import PartitionSpec as P


def lat_matrix(index_out, width_out, index_in, row_reach):
    decay_rows = row_reach / 2.0
    distance = jnp.abs(index_out[:, None] - index_in[None, :]).astype(jnp.float32)
    offsets = jnp.abs(jnp.arange(-row_reach, row_reach + 1)).astype(jnp.float32)
    limits = width_out.astype(jnp.float32)[:, None]
    weights = jnp.where(
        offsets[None, :] <= limits, jnp.exp(-2.0 * offsets / decay_rows)[None, :], 0.0
    )
    normal = jnp.sqrt(jnp.sum(weights, axis=1))
    return jnp.where(distance <= limits, jnp.exp(-distance / decay_rows), 0.0) / normal[:, None]


def lon_matrix(row_width, lon_points):
    lon_decay = lon_points / 32.0
    lon_reach = lon_points // 8
    lon_grid = jnp.arange(lon_points)
    apart_cells = jnp.abs(lon_grid[:, None] - lon_grid[None, :])
    apart_cells = jnp.minimum(apart_cells, lon_points - apart_cells).astype(jnp.float32)
    offsets = jnp.abs(jnp.arange(-lon_reach, lon_reach + 1)).astype(jnp.float32)
    limit_cells = row_width.astype(jnp.float32)
    normal = jnp.sqrt(
        jnp.sum(jnp.where(offsets <= limit_cells, jnp.exp(-2.0 * offsets / lon_decay), 0.0))
    )
    return jnp.where(apart_cells <= limit_cells, jnp.exp(-apart_cells / lon_decay), 0.0) / normal


def lon_apply(field_in, widths):
    lon_points = field_in.shape[3]

    def one_row(packed):
        slab_row, row_width = packed
        return jnp.einsum(
            "kwa,ab->kwb",
            slab_row,
            lon_matrix(row_width, lon_points),
            precision=lax.Precision.HIGHEST,
        )

    mixed_rows = lax.map(one_row, (jnp.moveaxis(field_in, 2, 0), widths))
    return jnp.moveaxis(mixed_rows, 0, 2)


def lat_apply(field_in, lat_width, adjoint_side):
    band_rows = field_in.shape[2]
    turned = lax.all_to_all(field_in, "lat", split_axis=3, concat_axis=2, tiled=True)
    lat_index = jnp.arange(turned.shape[2])
    weights = lat_matrix(lat_index, lat_width, lat_index, band_rows)
    if adjoint_side:
        weights = weights.T
    mixed_rows = jnp.einsum("ij,kwjl->kwil", weights, turned, precision=lax.Precision.HIGHEST)
    result = lax.all_to_all(mixed_rows, "lat", split_axis=2, concat_axis=3, tiled=True)
    return result


def inner_gram(left_field, right_field):
    left_rows = left_field.reshape(left_field.shape[0], -1)
    right_rows = right_field.reshape(right_field.shape[0], -1)
    return jnp.einsum("kx,jx->kj", left_rows, right_rows, precision=lax.Precision.HIGHEST)


def combine_columns(coeffs, field_in):
    return jnp.einsum("ba,bwix->awix", coeffs, field_in, precision=lax.Precision.HIGHEST)


def shards(
    footprints,
    block_rows,
    block_cols,
    block_scale,
    lat_width,
    lon_width,
    obs_weight,
    solution,
    residual,
    direction,
):
    highest = lax.Precision.HIGHEST
    rhs_count = direction.shape[0]
    band_rows = direction.shape[2]
    blocks = footprints[0, 0]
    row_list = block_rows[0, 0]
    col_list = block_cols[0, 0]
    scales = jnp.exp2(-block_scale[0, 0].astype(jnp.float32))
    block_edge = blocks.shape[1]
    row_blocks = obs_weight.shape[0] // block_edge
    lon_local = lax.dynamic_slice_in_dim(lon_width, lax.axis_index("lat") * band_rows, band_rows)
    rhs_share = rhs_count // lax.axis_size("obs")
    own_direction = lax.dynamic_slice_in_dim(
        direction, lax.axis_index("obs") * rhs_share, rhs_share, 0
    )
    own_spread = lat_apply(lon_apply(own_direction, lon_local), lat_width, False).astype(
        jnp.bfloat16
    )
    spread_cells = lax.all_gather(own_spread, "obs", axis=0, tiled=True)
    cell_values = spread_cells.reshape(rhs_count, -1, block_edge)
    col_blocks = cell_values.shape[1]
    picked = jnp.take(cell_values, col_list, axis=1)
    partial_value = (
        jnp.einsum("nrc,knc->knr", blocks, picked, preferred_element_type=jnp.float32)
        * scales[None, :, None]
    )
    row_hot = (row_list[:, None] == jnp.arange(row_blocks)[None, :]).astype(jnp.float32)
    forward = jnp.einsum("knr,nb->kbr", partial_value, row_hot, precision=highest).reshape(
        rhs_count, -1
    )
    summed = lax.psum(forward, "lat")
    obs_values = (summed * obs_weight[None, :]).astype(jnp.bfloat16)
    slab_values = obs_values.reshape(rhs_count, row_blocks, block_edge)
    pulled = jnp.take(slab_values, row_list, axis=1)
    adjoint_terms = (
        jnp.einsum("nrc,knr->knc", blocks, pulled, preferred_element_type=jnp.float32)
        * scales[None, :, None]
    )
    col_hot = (col_list[:, None] == jnp.arange(col_blocks)[None, :]).astype(jnp.float32)
    adjoint_local = jnp.einsum("knc,nb->kbc", adjoint_terms, col_hot, precision=highest).reshape(
        direction.shape
    )
    adjoint_share = lax.psum_scatter(adjoint_local, "obs", scatter_dimension=0, tiled=True)
    image_share = lon_apply(lat_apply(adjoint_share, lat_width, True), lon_local)
    image = direction + lax.all_gather(image_share, "obs", axis=0, tiled=True)
    gram_old, curvature = lax.psum(
        (inner_gram(residual, residual), inner_gram(direction, image)), "lat"
    )
    step_coef = jax.scipy.linalg.cho_solve((jnp.linalg.cholesky(curvature), True), gram_old)
    next_solution = solution + combine_columns(step_coef, direction)
    next_residual = residual - combine_columns(step_coef, image)
    gram_new = lax.psum(inner_gram(next_residual, next_residual), "lat")
    turn_coef = jax.scipy.linalg.cho_solve((jnp.linalg.cholesky(gram_old), True), gram_new)
    next_direction = next_residual + combine_columns(turn_coef, direction)
    return (next_solution, next_residual, next_direction)


def solution(mesh):
    return jax.shard_map(
        shards,
        mesh=mesh,
        in_specs=(
            P("obs", "lat", None, None, None),
            P("obs", "lat", None),
            P("obs", "lat", None),
            P("obs", "lat", None),
            P(),
            P(),
            P("obs"),
            P(None, None, "lat", None),
            P(None, None, "lat", None),
            P(None, None, "lat", None),
        ),
        out_specs=(
            P(None, None, "lat", None),
            P(None, None, "lat", None),
            P(None, None, "lat", None),
        ),
        check_vma=False,
    )
```

profile of v0, /device:TPU:0, one launch (start us, length us, event | category | flops | bytes accessed | tf_op | source)
XLA Modules:
  0.0 727.7 jit_solution(11207009930387597547)
XLA Ops:
  8.9 133.4 %while.24 = (s32[]{:T(128)}, f32[32,2,4,640]{3,2,1,0:T(4,128)S(1)}, f32[32,2,4,640]{3,2,1,0:T(4,128)S(1)}, s32[32]{0:T(128)S(1)}, s32[]{:T(128)}) while((s32[]{:T(128)}, f32[32,2,4,640]{3,2,1,0:T(4,128)S(1)}, f32[32,2,4,640]{3,2,1,0:T(4,128)S(1)}, s32[32]{0:T(128)S(1)}, s32[]{:T(128)}) %tuple.83), condition=%wide.region_2.3_spmd, body=%wide.region_0.2_spmd.sunk | while | flops 43418728 | bytes 42605 | solution.py:45
  146.0 3.9 reshape.172
  149.9 5.2 all-to-all-start
  155.3 10.9 %all-to-all-done = f32[8,1,20480]{2,1,0:T(1,128)S(1)} async-done(((f32[8,1,20480]{2,1,0:T(1,128)}), f32[8,1,20480]{2,1,0:T(1,128)S(1)}, u32[]{:S(2)}, u32[]{:S(2)}) %all-to-all-start) | async-done | bytes 655392 | tf_op jit(solution)/shard_map/all_to_all | solution.py:51
  172.3 3.1 convolution_bitcast_fusion.2
  175.8 12.2 %all_to_all.63 = bf16[2,4,256,80]{3,1,0,2:T(4,128)(2,1)S(1)} all-to-all(bf16[2,4,256,80]{3,1,0,2:T(4,128)(2,1)S(1)} %copy.258), channel_id=1, replica_groups=mesh['obs'=4,'lat'=8] {'lat'}, dimensions={2} | all-to-all | bytes 655360 | tf_op jit(solution)/shard_map/all_to_all | solution.py:57
  189.9 31.8 %all-gather.3.cloned.1.call-done = bf16[8,4,32,640]{3,2,1,0:T(8,128)(2,1)} async-done(((bf16[2,4,32,640]{3,2,1,0:T(8,128)(2,1)}), bf16[8,4,32,640]{3,2,1,0:T(8,128)(2,1)}) %all-gather.3.cloned.1.call-update) | async-done | bytes 1310736 | tf_op jit(solution)/shard_map/all_gather | solution.py:100
  226.9 9.9 %multiply_bitcast_fusion.1 = f32[8,384,128]{2,0,1:T(8,128)S(1)} fusion(bf16[1,1,384,128,128]{4,3,2,1,0:T(8,128)(2,1)} %param.17, bf16[384,8,128]{2,1,0:T(8,128)(2,1)S(1)} %gather_fusion, f32[384]{0:T(512)S(1)} %exponential_reduce_fusion, pred[384]{0:T(512)(128)(4,1)S(1)} %compare_and_fusion), kind=kOutput, calls=%fused_computation.73 | convolution fusion | flops 101449728 | bytes 14944128 | tf_op jit(solution)/shard_map/nrc,knc->knr/dot_general | solution.py:105
  238.4 52.0 %all-reduce.3.cloned.1.call-done = f32[8,4096]{1,0:T(8,128)} async-done(((f32[8,4096]{1,0:T(8,128)}), f32[8,4096]{1,0:T(8,128)}) %all-reduce.3.cloned.1.call-update) | async-done | bytes 131088 | tf_op jit(solution)/shard_map/psum | solution.py:112
  293.1 7.4 %multiply_bitcast_fusion = f32[8,384,128]{2,0,1:T(8,128)S(1)} fusion(bf16[1,1,384,128,128]{4,3,2,1,0:T(8,128)(2,1)} %param.17, bf16[384,8,128]{2,1,0:T(8,128)(2,1)S(1)} %gather_fusion.1, f32[384]{0:T(512)S(1)} %exponential_reduce_fusion, pred[384]{0:T(512)(128)(4,1)S(1)} %compare_and_fusion.1), kind=kOutput, calls=%fused_computation.72 | convolution fusion | flops 101449728 | bytes 14944128 | tf_op jit(solution)/shard_map/nrc,knr->knc/dot_general | solution.py:117
  304.7 51.6 %reduce-scatter.2.cloned.1.call-done = f32[2,4,32,640]{3,2,1,0:T(8,128)} async-done(((f32[8,4,32,640]{3,2,1,0:T(8,128)}), f32[2,4,32,640]{3,2,1,0:T(8,128)}) %reduce-scatter.2.cloned.1.call-update) | async-done | bytes 655376 | tf_op jit(solution)/shard_map/reduce_scatter | solution.py:124
  360.2 15.0 %all_to_all.64 = f32[8,1,20480]{2,1,0:T(1,128)S(1)} all-to-all(f32[8,1,20480]{2,1,0:T(1,128)S(1)} %reshape.174), channel_id=1, replica_groups=mesh['obs'=4,'lat'=8] {'lat'}, dimensions={0} | all-to-all | bytes 1310720 | tf_op jit(solution)/shard_map/all_to_all | solution.py:51
  385.3 3.6 all-to-all-start.3
  388.9 15.3 %all-to-all-done.3 = f32[2,4,256,80]{3,1,0,2:T(4,128)S(1)} async-done(((f32[2,4,256,80]{3,1,0,2:T(4,128)}), f32[2,4,256,80]{3,1,0,2:T(4,128)S(1)}, u32[]{:S(2)}, u32[]{:S(2)}) %all-to-all-start.3) | async-done | bytes 655392 | tf_op jit(solution)/shard_map/all_to_all | solution.py:57
  405.3 188.0 %while.25 = (s32[]{:T(128)}, f32[32,2,4,640]{3,0,2,1:T(8,128)}, f32[32,2,4,640]{3,0,2,1:T(8,128)S(1)}, s32[32]{0:T(128)S(1)}, s32[]{:T(128)}, /*index=5*/s32[]{:T(128)}) while((s32[]{:T(128)}, f32[32,2,4,640]{3,0,2,1:T(8,128)}, f32[32,2,4,640]{3,0,2,1:T(8,128)S(1)}, s32[32]{0:T(128)S(1)}, s32[]{:T(128)}, /*index=5*/s32[]{:T(128)}) %tuple.84), condition=%wide.region_8.9_spmd, body=%wide.region_6.8_spmd.sunk | while | flops 43418728 | bytes 163969 | solution.py:45
  593.3 10.0 %fusion.89 = f32[8,8]{0,1:T(8,128)S(1)} fusion(f32[8,4,32,640]{3,2,1,0:T(8,128)} %param.25), kind=kOutput, calls=%fused_computation.81 | convolution fusion | flops 62914560 | bytes 2621696 | tf_op jit(solution)/shard_map/kx,jx->kj/dot_general | solution.py:64
  603.3 42.9 %all-gather.5.cloned.1.call-done = f32[8,4,32,640]{3,2,1,0:T(8,128)} async-done(((f32[2,4,32,640]{3,2,1,0:T(8,128)}), f32[8,4,32,640]{3,2,1,0:T(8,128)}) %all-gather.5.cloned.1.call-update) | async-done | bytes 2621456 | tf_op jit(solution)/shard_map/all_gather | solution.py:126
  649.7 7.5 %fusion.84 = f32[8,8]{0,1:T(8,128)S(1)} fusion(f32[8,4,32,640]{3,2,1,0:T(8,128)S(1)} %copy-done, f32[8,4,32,640]{3,2,1,0:T(8,128)S(1)} %add.130), kind=kOutput, calls=%fused_computation.77 | convolution fusion | flops 62914560 | bytes 5243136 | tf_op jit(solution)/shard_map/kx,jx->kj/dot_general | solution.py:64
  657.3 13.8 %all-reduce = (f32[8,8]{0,1:T(8,128)S(1)}, f32[8,8]{0,1:T(8,128)S(1)}) all-reduce(f32[8,8]{0,1:T(8,128)S(1)} %fusion.89, f32[8,8]{0,1:T(8,128)S(1)} %fusion.84), channel_id=1, replica_groups=mesh['obs'=4,'lat'=8] {'lat'}, use_global_device_ids=true, to_apply=%region_12.14 | all-reduce | flops 128 | bytes 1024 | tf_op jit(solution)/shard_map/psum | solution.py:127
  674.3 7.4 %copy_subtract_fusion = f32[8,4,32,640]{3,0,2,1:T(8,128)S(1)} fusion(f32[8,4,32,640]{3,2,1,0:T(8,128)} %param.25, f32[8,8,1,1]{0,1,3,2:T(8,128)S(1)} %convolution_bitcast_fusion.5, f32[8,4,32,640]{3,2,1,0:T(8,128)} %copy-done.2), kind=kOutput, calls=%fused_computation.55 | convolution fusion | flops 63569920 | bytes 7864576 | tf_op jit(solution)/shard_map/ba,bwix->awix/dot_general | solution.py:68
  681.7 5.8 convolution_bitcast_fusion.4
  692.2 12.0 %psum.31 = f32[8,8]{1,0:T(8,128)S(1)} all-reduce(f32[8,8]{1,0:T(8,128)S(1)} %convolution_bitcast_fusion.4), channel_id=1, replica_groups=mesh['obs'=4,'lat'=8] {'lat'}, use_global_device_ids=true, to_apply=%region_13.16 | all-reduce | flops 64 | bytes 512 | tf_op jit(solution)/shard_map/psum | solution.py:133
  704.6 5.5 fusion.69
  713.7 5.1 copy_add_fusion
  (385 shorter events, 293.7 us)
Async XLA Ops:
  7.2 1.6 copy-start.9
  146.0 9.1 %copy-start.8 = (s32[256]{0:T(256)S(1)}, s32[256]{0:T(256)}, u32[]{:S(2)}) copy-start(s32[256]{0:T(256)} %param.21) | copy-start | bytes 3076
  149.9 16.3 %all-to-all-start = ((f32[8,1,20480]{2,1,0:T(1,128)}), f32[8,1,20480]{2,1,0:T(1,128)S(1)}, u32[]{:S(2)}, u32[]{:S(2)}) async-start(f32[8,1,20480]{2,1,0:T(1,128)} %reshape.172), calls=%async_computation | async-start | bytes 1310720 | tf_op jit(solution)/shard_map/all_to_all | solution.py:51
  155.1 66.6 %all-gather.3.cloned.1.call-start = ((), (), s32[]{:S(2)}) async-start(), calls=%async_computation.5 | async-start | bytes 1638400 | tf_op jit(solution)/shard_map/all_gather | solution.py:100
  175.5 14.2 %copy-start.6 = (s32[1,1,384]{2,1,0:T(1,128)S(1)}, s32[1,1,384]{2,1,0:T(1,128)}, u32[]{:S(2)}) copy-start(s32[1,1,384]{2,1,0:T(1,128)} %param.18) | copy-start | bytes 4612
  175.5 14.2 %copy-start.5 = (s32[1,1,384]{2,1,0:T(1,128)S(1)}, s32[1,1,384]{2,1,0:T(1,128)}, u32[]{:S(2)}) copy-start(s32[1,1,384]{2,1,0:T(1,128)} %param.19) | copy-start | bytes 4612
  175.5 14.3 %copy-start.7 = (s32[1,1,384]{2,1,0:T(1,128)S(1)}, s32[1,1,384]{2,1,0:T(1,128)}, u32[]{:S(2)}) copy-start(s32[1,1,384]{2,1,0:T(1,128)} %param.20) | copy-start | bytes 4612
  189.4 101.0 %all-reduce.3.cloned.1.call-start = ((), (), s32[]{:S(2)}) async-start(), calls=%async_computation.6 | async-start | bytes 262144 | tf_op jit(solution)/shard_map/psum | solution.py:112
  226.8 63.6 %copy-start.4 = (f32[4096]{0:T(1024)S(1)}, f32[4096]{0:T(1024)}, u32[]{:S(2)}) copy-start(f32[4096]{0:T(1024)} %param.23) | copy-start | bytes 49156
  238.4 118.0 %reduce-scatter.2.cloned.1.call-start = ((), (), s32[]{:S(2)}) async-start(), calls=%async_computation.7 | async-start | bytes 3276800 | tf_op jit(solution)/shard_map/reduce_scatter | solution.py:124
  385.3 18.9 %all-to-all-start.3 = ((f32[2,4,256,80]{3,1,0,2:T(4,128)}), f32[2,4,256,80]{3,1,0,2:T(4,128)S(1)}, u32[]{:S(2)}, u32[]{:S(2)}) async-start(f32[2,4,256,80]{3,1,0,2:T(4,128)} %copy.268), calls=%async_computation.4 | async-start | bytes 2097152 | tf_op jit(solution)/shard_map/all_to_all | solution.py:57
  388.8 257.4 %all-gather.5.cloned.1.call-start = ((), (), s32[]{:S(2)}) async-start(), calls=%async_computation.8 | async-start | bytes 3276800 | tf_op jit(solution)/shard_map/all_gather | solution.py:126
  593.3 52.9 %copy-start = (f32[8,4,32,640]{3,2,1,0:T(8,128)S(1)}, f32[8,4,32,640]{3,2,1,0:T(8,128)}, u32[]{:S(2)}) copy-start(f32[8,4,32,640]{3,2,1,0:T(8,128)} %param.26) | copy-start | bytes 7864324
  648.3 1.5 copy-start.2
  710.2 2.4 copy-start.1
  710.2 3.5 copy-start.3
Sparse Core Ops, SparseCore 0:
  189.5 32.0 all-gather.2
  238.5 51.9 all-reduce.2
  304.9 51.4 reduce-scatter.1
  593.5 52.6 all-gather.4
where the time goes:
time: 739 us; the launch traced here: 728 us
  waiting for transfers between devices  205 us (28%)
  matrix products  171 us (23%)
  local copies, waits for them, and re-layouts  135 us (18%)
  loops' own time  87.4 us (12%)
  blocking collectives  53 us (7%)
  other arithmetic  52.1 us (7%)
  between operations  14.7 us (2%)
  starting transfers between devices  9.1 us (1%)
    dot_general x64, matrix products, one_row(): jnp.einsum('kwa,ab->kwb', slab_row, lon_matrix(row_width, lon_points), pr...  103 us
    another operation x2, loops' own time, lon_apply(): mixed_rows = lax.map(one_row, (jnp.moveaxis(field_in, 2, 0), widths))  87.4 us
    dynamic_update_slice x64, local copies, waits for them, and re-layouts, lon_apply(): mixed_rows = lax.map(one_row, (jnp.moveaxis(field_in, 2, 0), widths))  54 us
    psum x1, waiting for transfers between devices, shards(): summed = lax.psum(forward, 'lat')  52 us
    reduce_scatter x1, waiting for transfers between devices, shards(): lax.psum_scatter(adjoint_local, 'obs', scatter_dimension=0, tiled=True)  51.6 us
    all_gather x1, waiting for transfers between devices, shards(): image = direction + lax.all_gather(image_share, 'obs', axis=0, tiled=True)  42.9 us
    reduce_sum x64, other arithmetic, lon_matrix(): jnp.sum(jnp.where(offsets <= limit_cells, jnp.exp(-2.0 * offsets / lon_de...  39.1 us
    dynamic_slice x96, local copies, waits for them, and re-layouts, lon_apply(): mixed_rows = lax.map(one_row, (jnp.moveaxis(field_in, 2, 0), widths))  38.2 us
  transfers between devices with their start and end apart: 6, of which 6 were waited for; matrix products, arithmetic and copies ran while one was open for 1% of the time, Pallas kernels for 0%

commit v1 on v0

v1 whole, which is shorter than its diff:
```python
import functools
import math

import jax
import jax.numpy as jnp
from jax import lax
from jax.experimental import pallas as pl
from jax.experimental.pallas import tpu as pltpu
from jax.sharding import PartitionSpec as P

LANES = 128
SUBLANES = 8
VMEM_BYTES = 40 * 1024 * 1024
HIGHEST = lax.Precision.HIGHEST


def params():
    return pltpu.CompilerParams(vmem_limit_bytes=VMEM_BYTES)


def cost(flops, nbytes):
    return pl.CostEstimate(flops=int(flops), bytes_accessed=int(nbytes), transcendentals=0)


def whole(shape):
    return pl.BlockSpec(shape, lambda *_: (0,) * len(shape))


def pow2(exponent):
    size = jnp.abs(exponent)
    up = jnp.ones(exponent.shape, jnp.float32)
    down = up
    for bit in range(7):
        on = ((size >> bit) & 1) == 1
        up = up * jnp.where(on, 2.0 ** (2**bit), 1.0)
        down = down * jnp.where(on, 2.0 ** -(2**bit), 1.0)
    return jnp.where(exponent < 0, down, up)


def exponent_of(peak):
    logs = jnp.log(jnp.maximum(peak, 1e-28)) * (1.0 / math.log(2.0))
    return jnp.ceil(logs + 1e-3).astype(jnp.int32)


def to_int(values, factor):
    return jnp.clip(jnp.round(values * factor), -32767.0, 32767.0).astype(jnp.int32)


def pack(high, low):
    return (high << 16) | (low & 0xFFFF)


def high_of(word):
    return word >> 16


def low_of(word):
    return (word << 16) >> 16


def pack_field(field_ref, word_ref, peak):
    weeks, rows, lon = field_ref.shape
    half = rows // 2
    exponent = exponent_of(jnp.max(peak, axis=0, keepdims=True))
    exponent = jnp.broadcast_to(exponent, (SUBLANES, lon))
    factor = pow2(15 - exponent)
    word_ref[weeks * half :, :] = exponent

    def one_week(week, carry):
        for start in range(0, half, SUBLANES):
            high = to_int(field_ref[week, start : start + SUBLANES, :], factor)
            low = to_int(field_ref[week, half + start : half + start + SUBLANES, :], factor)
            at = pl.multiple_of(week * half + start, SUBLANES)
            word_ref[pl.ds(at, SUBLANES), :] = pack(high, low)
        return carry

    lax.fori_loop(0, weeks, one_week, 0)


def word_scale(word_ref, half_rows):
    return pow2(word_ref[half_rows : half_rows + SUBLANES, :] - 15)


def lon_setup(lon):
    return lon / 32.0, (lon // 8 + 1).bit_length()


def lon_rows(rows, count, norm, lon):
    decay, bits = lon_setup(lon)
    total = -rows
    for side in (1, -1):
        window = rows
        taken = jnp.zeros_like(rows)
        for bit in range(bits):
            reach = 2**bit
            fade = math.exp(-reach / decay)
            shift = reach if side == 1 else lon - reach
            moved = window if bit == 0 else window + fade * pltpu.roll(taken, shift, 1)
            taken = jnp.where(((count >> bit) & 1) == 1, moved, taken)
            if bit + 1 < bits:
                window = window + fade * pltpu.roll(window, shift, 1)
        total = total + taken
    return total * norm


def lon_norm(count, lon):
    decay, _ = lon_setup(lon)
    ratio = math.exp(-2.0 / decay)
    ends = jnp.exp(count.astype(jnp.float32) * (-2.0 / decay))
    return 1.0 / jnp.sqrt(1.0 + (2.0 / (1.0 - ratio)) * (ratio - ends))


def lon_field(source_ref, count_ref, norm_ref, out_ref):
    weeks, rows, lon = source_ref.shape

    def one_group(group, peak):
        at = pl.multiple_of(group * SUBLANES, SUBLANES)
        count = count_ref[pl.ds(at, SUBLANES), :]
        norm = norm_ref[pl.ds(at, SUBLANES), :]

        def one_week(week, peak):
            rows_in = source_ref[week, pl.ds(at, SUBLANES), :]
            result = lon_rows(rows_in, count, norm, lon)
            out_ref[week, pl.ds(at, SUBLANES), :] = result
            return jnp.maximum(peak, jnp.abs(result))

        return lax.fori_loop(0, weeks, one_week, peak)

    return lax.fori_loop(0, rows // SUBLANES, one_group, jnp.zeros((SUBLANES, lon), jnp.float32))


def spread_lon_kernel(_, field_ref, count_ref, out_ref, word_ref, norm_ref):
    norm_ref[...] = lon_norm(count_ref[...], count_ref.shape[1])
    peak = lon_field(field_ref.at[0], count_ref, norm_ref, out_ref.at[0])
    pack_field(out_ref.at[0], word_ref.at[0], peak)


def spread_lon(direction, first, rhs, counts):
    _, weeks, rows, lon = direction.shape
    words = weeks * rows // 2 + SUBLANES
    return pl.pallas_call(
        spread_lon_kernel,
        grid_spec=pltpu.PrefetchScalarGridSpec(
            num_scalar_prefetch=1,
            grid=(rhs,),
            in_specs=[
                pl.BlockSpec((1, weeks, rows, lon), lambda k, first: (first[0] + k, 0, 0, 0)),
                whole((rows, lon)),
            ],
            out_specs=[
                pl.BlockSpec((1, weeks, rows, lon), lambda k, first: (k, 0, 0, 0)),
                pl.BlockSpec((1, words, lon), lambda k, first: (k, 0, 0)),
            ],
            scratch_shapes=[pltpu.VMEM((rows, lon), jnp.float32)],
        ),
        out_shape=[
            jax.ShapeDtypeStruct((rhs, weeks, rows, lon), jnp.float32),
            jax.ShapeDtypeStruct((rhs, words, lon), jnp.int32),
        ],
        compiler_params=params(),
        cost_estimate=cost(rhs * weeks * rows * lon * 100, rhs * weeks * rows * lon * 10),
        name="spread_lon",
    )(first, direction, counts)


def fill_window(window_ref, week, before_ref, own_ref, after_ref, scale_before, scale_after):
    _, rows, lon = own_ref.shape
    half = rows // 2
    for base, ref, scale in ((0, before_ref, scale_before), (2 * rows, after_ref, scale_after)):
        for start in range(0, half, SUBLANES):
            at = pl.multiple_of(week * half + start, SUBLANES)
            word = ref[pl.ds(at, SUBLANES), :]
            window_ref[base + start : base + start + SUBLANES, :] = (
                high_of(word).astype(jnp.float32) * scale
            )
            window_ref[base + half + start : base + half + start + SUBLANES, :] = (
                low_of(word).astype(jnp.float32) * scale
            )
    window_ref[rows : 2 * rows, :] = own_ref[week]


def spread_lat_kernel(slots, own_ref, before_ref, after_ref, weights_ref, hot_ref, *rest):
    picks, (window_ref, cells_ref) = rest[:slots], rest[slots:]
    _, weeks, rows, lon = own_ref.shape
    half_rows = weeks * rows // 2
    scale_before = word_scale(before_ref.at[0], half_rows)
    scale_after = word_scale(after_ref.at[0], half_rows)
    for week in range(weeks):
        fill_window(
            window_ref,
            week,
            before_ref.at[0],
            own_ref.at[0],
            after_ref.at[0],
            scale_before,
            scale_after,
        )
        mixed = jnp.dot(
            weights_ref[...],
            window_ref[...],
            precision=HIGHEST,
            preferred_element_type=jnp.float32,
        )
        for part in range(lon // LANES):
            at = (week * (lon // LANES) + part) * rows
            cells_ref[at : at + rows, :] = mixed[:, part * LANES : (part + 1) * LANES].astype(
                jnp.bfloat16
            )
    for slot in range(slots):
        picks[slot][0] = jnp.dot(
            hot_ref[slot], cells_ref[...], preferred_element_type=jnp.float32
        ).astype(jnp.bfloat16)


def spread_lat(own, before, after, weights, hot):
    rhs, weeks, rows, lon = own.shape
    slots, blocks, cols = hot.shape
    words = before.shape[1]
    word_spec = pl.BlockSpec((1, words, lon), lambda k: (k, 0, 0))
    return pl.pallas_call(
        functools.partial(spread_lat_kernel, slots),
        grid=(rhs,),
        in_specs=[
            pl.BlockSpec((1, weeks, rows, lon), lambda k: (k, 0, 0, 0)),
            word_spec,
            word_spec,
            whole(weights.shape),
            whole(hot.shape),
        ],
        out_specs=[pl.BlockSpec((1, blocks, LANES), lambda k: (k, 0, 0))] * slots,
        out_shape=[jax.ShapeDtypeStruct((rhs, blocks, LANES), jnp.bfloat16)] * slots,
        scratch_shapes=[
            pltpu.VMEM((3 * rows, lon), jnp.float32),
            pltpu.VMEM((cols, LANES), jnp.bfloat16),
        ],
        compiler_params=params(),
        cost_estimate=cost(rhs * slots * blocks * cols * LANES * 2, rhs * weeks * rows * lon * 10),
        name="spread_lat",
    )(own, before, after, weights, hot)


CHUNK = 32


def forward_kernel(slots, row_ref, scale_ref, blocks_ref, *rest):
    picks, (out_ref, cells_ref) = rest[:slots], rest[slots:]
    step = pl.program_id(0)
    chunk = blocks_ref.shape[0]
    rhs, count, _ = picks[0].shape
    lines = slots * rhs

    @pl.when(step == 0)
    def _():
        out_ref[...] = jnp.zeros_like(out_ref)
        for slot in range(slots):
            for k in range(rhs):
                cells_ref[pl.ds(slot * rhs + k, count, stride=lines), :] = picks[slot][k].astype(
                    jnp.float32
                )

    values = []
    for n in range(chunk):
        at = pl.multiple_of((step * chunk + n) * lines, lines)
        cells = cells_ref[pl.ds(at, lines), :].astype(jnp.bfloat16)
        values.append(
            lax.dot_general(
                cells,
                blocks_ref[n],
                (((1,), (1,)), ((), ())),
                preferred_element_type=jnp.float32,
            )
        )
    for n in range(chunk):
        index = step * chunk + n
        at = pl.multiple_of(row_ref[index] * lines, lines)
        out_ref[pl.ds(at, lines), :] += values[n] * scale_ref[index]


def forward(row_list, scales, blocks, picks, row_blocks):
    slots = len(picks)
    rhs, count, _ = picks[0].shape
    lines = slots * rhs
    edge = blocks.shape[1]
    return pl.pallas_call(
        functools.partial(forward_kernel, slots),
        grid_spec=pltpu.PrefetchScalarGridSpec(
            num_scalar_prefetch=2,
            grid=(count // CHUNK,),
            in_specs=[pl.BlockSpec((CHUNK, edge, edge), lambda n, *_: (n, 0, 0))]
            + [whole((rhs, count, edge))] * slots,
            out_specs=whole((row_blocks * lines, edge)),
            scratch_shapes=[pltpu.VMEM((count * lines, edge), jnp.float32)],
        ),
        out_shape=jax.ShapeDtypeStruct((row_blocks * lines, edge), jnp.float32),
        compiler_params=params(),
        cost_estimate=cost(blocks.size * 2 * lines, blocks.size * 2),
        name="forward",
    )(row_list, scales, blocks, *picks)


def adjoint_kernel(slots, rhs, row_ref, scale_ref, blocks_ref, values_ref, *rest):
    outs, (terms_ref,) = rest[:slots], rest[slots:]
    step = pl.program_id(0)
    chunk = blocks_ref.shape[0]
    lines = slots * rhs
    for n in range(chunk):
        index = step * chunk + n
        at = pl.multiple_of(row_ref[index] * lines, lines)
        pulled = values_ref[pl.ds(at, lines), :].astype(jnp.bfloat16)
        term = jnp.dot(pulled, blocks_ref[n], preferred_element_type=jnp.float32)
        to = pl.multiple_of(index * lines, lines)
        terms_ref[pl.ds(to, lines), :] = term * scale_ref[index]

    @pl.when(step == pl.num_programs(0) - 1)
    def _():
        count = terms_ref.shape[0] // lines
        half = count // 2
        for slot in range(slots):
            for k in range(rhs):
                terms = terms_ref[pl.ds(slot * rhs + k, count, stride=lines), :]
                peak = jnp.max(jnp.abs(terms), axis=0, keepdims=True)
                exponent = jnp.broadcast_to(exponent_of(peak), (SUBLANES, LANES))
                number = to_int(terms, pow2(15 - exponent)[:1])
                outs[slot][k, :half, :] = pack(number[:half], number[half:])
                outs[slot][k, half:, :] = exponent


def adjoint_terms(row_list, scales, blocks, values, slots, rhs):
    count, edge, _ = blocks.shape
    lines = slots * rhs
    words = count // 2 + SUBLANES
    return pl.pallas_call(
        functools.partial(adjoint_kernel, slots, rhs),
        grid_spec=pltpu.PrefetchScalarGridSpec(
            num_scalar_prefetch=2,
            grid=(count // CHUNK,),
            in_specs=[
                pl.BlockSpec((CHUNK, edge, edge), lambda n, *_: (n, 0, 0)),
                whole(values.shape),
            ],
            out_specs=[whole((rhs, words, edge))] * slots,
            scratch_shapes=[pltpu.VMEM((count * lines, edge), jnp.float32)],
        ),
        out_shape=[jax.ShapeDtypeStruct((rhs, words, edge), jnp.int32)] * slots,
        compiler_params=params(),
        cost_estimate=cost(blocks.size * 2 * lines, blocks.size * 2),
        name="adjoint",
    )(row_list, scales, blocks, values)


def gather_cells_kernel(slots, hot_ref, *rest):
    terms, (field_ref, word_ref, split_ref) = rest[:slots], rest[slots:]
    _, weeks, rows, lon = field_ref.shape
    count = hot_ref.shape[1] // slots
    half = count // 2
    for slot in range(slots):
        scale = word_scale(terms[slot].at[0], half)[:1]
        word = terms[slot][0, :half, :]
        for base, number in ((0, high_of(word)), (half, low_of(word))):
            coarse = (number + 128) >> 8
            fine = number - (coarse << 8)
            at = slot * count + base
            split_ref[at : at + half, :LANES] = (
                (coarse << 8).astype(jnp.float32) * scale
            ).astype(jnp.bfloat16)
            split_ref[at : at + half, LANES:] = (fine.astype(jnp.float32) * scale).astype(
                jnp.bfloat16
            )
    peak = jnp.zeros((SUBLANES, lon), jnp.float32)
    parts = lon // LANES
    for week in range(weeks):
        at = week * parts * rows
        both = jnp.dot(
            hot_ref[at : at + parts * rows, :],
            split_ref[...],
            preferred_element_type=jnp.float32,
        )
        cells = both[:, :LANES] + both[:, LANES:]
        for part in range(parts):
            field_ref[0, week, :, part * LANES : (part + 1) * LANES] = cells[
                part * rows : (part + 1) * rows
            ]
        for start in range(0, rows, SUBLANES):
            peak = jnp.maximum(peak, jnp.abs(field_ref[0, week, start : start + SUBLANES, :]))
    pack_field(field_ref.at[0], word_ref.at[0], peak)


def gather_cells(hot_turned, terms, weeks, rows, lon):
    slots = len(terms)
    rhs, words_in, edge = terms[0].shape
    words = weeks * rows // 2 + SUBLANES
    return pl.pallas_call(
        functools.partial(gather_cells_kernel, slots),
        grid=(rhs,),
        in_specs=[whole(hot_turned.shape)]
        + [pl.BlockSpec((1, words_in, edge), lambda k: (k, 0, 0))] * slots,
        out_specs=[
            pl.BlockSpec((1, weeks, rows, lon), lambda k: (k, 0, 0, 0)),
            pl.BlockSpec((1, words, lon), lambda k: (k, 0, 0)),
        ],
        out_shape=[
            jax.ShapeDtypeStruct((rhs, weeks, rows, lon), jnp.float32),
            jax.ShapeDtypeStruct((rhs, words, lon), jnp.int32),
        ],
        scratch_shapes=[pltpu.VMEM((hot_turned.shape[1], 2 * LANES), jnp.bfloat16)],
        compiler_params=params(),
        cost_estimate=cost(rhs * hot_turned.size * 4 * LANES, rhs * weeks * rows * lon * 10),
        name="gather_cells",
    )(hot_turned, *terms)


def pull_back_kernel(
    own_ref, before_ref, after_ref, weights_ref, count_ref, word_ref, window_ref, norm_ref, field_ref
):
    _, weeks, rows, lon = own_ref.shape
    half_rows = weeks * rows // 2
    norm_ref[...] = lon_norm(count_ref[...], lon)
    scale_before = word_scale(before_ref.at[0], half_rows)
    scale_after = word_scale(after_ref.at[0], half_rows)
    for week in range(weeks):
        fill_window(
            window_ref,
            week,
            before_ref.at[0],
            own_ref.at[0],
            after_ref.at[0],
            scale_before,
            scale_after,
        )
        field_ref[week] = jnp.dot(
            weights_ref[...],
            window_ref[...],
            precision=HIGHEST,
            preferred_element_type=jnp.float32,
        )
    peak = lon_field(field_ref, count_ref, norm_ref, field_ref)
    pack_field(field_ref, word_ref.at[0], peak)


def pull_back(own, before, after, weights, counts):
    rhs, weeks, rows, lon = own.shape
    words = before.shape[1]
    word_spec = pl.BlockSpec((1, words, lon), lambda k: (k, 0, 0))
    return pl.pallas_call(
        pull_back_kernel,
        grid=(rhs,),
        in_specs=[
            pl.BlockSpec((1, weeks, rows, lon), lambda k: (k, 0, 0, 0)),
            word_spec,
            word_spec,
            whole(weights.shape),
            whole(counts.shape),
        ],
        out_specs=word_spec,
        out_shape=jax.ShapeDtypeStruct((rhs, words, lon), jnp.int32),
        scratch_shapes=[
            pltpu.VMEM((3 * rows, lon), jnp.float32),
            pltpu.VMEM((rows, lon), jnp.float32),
            pltpu.VMEM((weeks, rows, lon), jnp.float32),
        ],
        compiler_params=params(),
        cost_estimate=cost(rhs * weeks * rows * lon * 300, rhs * weeks * rows * lon * 10),
        name="pull_back",
    )(own, before, after, weights, counts)


TILE = 4


def gram_kernel(slots, order_ref, residual_ref, direction_ref, *rest):
    words, (image_ref, gram_ref) = rest[:slots], rest[slots:]
    week = pl.program_id(0)
    rhs_count, _, rows, lon = direction_ref.shape
    rhs = words[0].shape[0]
    half = rows // 2
    half_rows = words[0].shape[1] - SUBLANES

    @pl.when(week == 0)
    def _():
        gram_ref[...] = jnp.zeros_like(gram_ref)

    for slot in range(slots):
        for k in range(rhs):
            index = order_ref[slot] + k
            scale = word_scale(words[slot].at[k], half_rows)
            for start in range(0, half, SUBLANES):
                at = pl.multiple_of(week * half + start, SUBLANES)
                word = words[slot][k, pl.ds(at, SUBLANES), :]
                for base, number in ((start, high_of(word)), (half + start, low_of(word))):
                    image_ref[index, 0, base : base + SUBLANES, :] = (
                        direction_ref[index, 0, base : base + SUBLANES, :]
                        + number.astype(jnp.float32) * scale
                    )

    pairs = (
        (residual_ref, residual_ref),
        (direction_ref, image_ref),
        (residual_ref, image_ref),
        (image_ref, image_ref),
    )
    for place, (left_ref, right_ref) in enumerate(pairs):
        for a0 in range(0, rhs_count, TILE):
            for b0 in range(0, rhs_count, TILE):
                if left_ref is right_ref and b0 < a0:
                    continue

                def one_group(group, sums):
                    at = pl.multiple_of(group * SUBLANES, SUBLANES)
                    sums = list(sums)
                    for lane in range(0, lon, LANES):
                        left = [
                            left_ref[a0 + a, 0, pl.ds(at, SUBLANES), lane : lane + LANES]
                            for a in range(TILE)
                        ]
                        right = [
                            right_ref[b0 + b, 0, pl.ds(at, SUBLANES), lane : lane + LANES]
                            for b in range(TILE)
                        ]
                        for a in range(TILE):
                            for b in range(TILE):
                                sums[a * TILE + b] = sums[a * TILE + b] + left[a] * right[b]
                    return tuple(sums)

                zero = jnp.zeros((SUBLANES, LANES), jnp.float32)
                sums = lax.fori_loop(0, rows // SUBLANES, one_group, (zero,) * TILE**2)
                for a in range(TILE):
                    for b in range(TILE):
                        at = (place * rhs_count + a0 + a) * rhs_count + b0 + b
                        gram_ref[at] += sums[a * TILE + b]


def grams(order, residual, direction, words):
    slots = len(words)
    rhs_count, weeks, rows, lon = direction.shape
    field = pl.BlockSpec((rhs_count, 1, rows, lon), lambda w, *_: (0, w, 0, 0))
    return pl.pallas_call(
        functools.partial(gram_kernel, slots),
        grid_spec=pltpu.PrefetchScalarGridSpec(
            num_scalar_prefetch=1,
            grid=(weeks,),
            in_specs=[field, field] + [whole(words[0].shape)] * slots,
            out_specs=[field, whole((4 * rhs_count**2, SUBLANES, LANES))],
        ),
        out_shape=[
            jax.ShapeDtypeStruct(direction.shape, jnp.float32),
            jax.ShapeDtypeStruct((4 * rhs_count**2, SUBLANES, LANES), jnp.float32),
        ],
        compiler_params=params(),
        cost_estimate=cost(8 * rhs_count * direction.size, 16 * direction.size),
        name="grams",
    )(order, residual, direction, *words)


def update_kernel(
    step_ref, turn_ref, solution_ref, residual_ref, direction_ref, image_ref, sol_out, res_out, dir_out
):
    rhs_count, _, rows, lon = direction_ref.shape

    def one_group(group, carry):
        at = pl.multiple_of(group * SUBLANES, SUBLANES)
        spot = pl.ds(at, SUBLANES)
        for a in range(rhs_count):
            moved = solution_ref[a, 0, spot, :]
            left = residual_ref[a, 0, spot, :]
            for b in range(rhs_count):
                coef = step_ref[b, a]
                moved = moved + coef * direction_ref[b, 0, spot, :]
                left = left - coef * image_ref[b, 0, spot, :]
            sol_out[a, 0, spot, :] = moved
            res_out[a, 0, spot, :] = left
            turned = left
            for b in range(rhs_count):
                turned = turned + turn_ref[b, a] * direction_ref[b, 0, spot, :]
            dir_out[a, 0, spot, :] = turned
        return carry

    lax.fori_loop(0, rows // SUBLANES, one_group, 0)


def update(step_coef, turn_coef, solution, residual, direction, image):
    rhs_count, weeks, rows, lon = direction.shape
    field = pl.BlockSpec((rhs_count, 1, rows, lon), lambda w, *_: (0, w, 0, 0))
    shape = jax.ShapeDtypeStruct(direction.shape, jnp.float32)
    return pl.pallas_call(
        update_kernel,
        grid_spec=pltpu.PrefetchScalarGridSpec(
            num_scalar_prefetch=2,
            grid=(weeks,),
            in_specs=[field] * 4,
            out_specs=[field] * 3,
        ),
        out_shape=[shape] * 3,
        compiler_params=params(),
        cost_estimate=cost(6 * rhs_count * direction.size, 28 * direction.size),
        name="update",
    )(step_coef, turn_coef, solution, residual, direction, image)


def shifted(value, axis, by):
    size = lax.axis_size(axis)
    return lax.ppermute(value, axis, [(i, (i + by) % size) for i in range(size)])


def neighbours(value, axis):
    size = lax.axis_size(axis)
    before = lax.ppermute(value, axis, [(i, i + 1) for i in range(size - 1)])
    after = lax.ppermute(value, axis, [(i + 1, i) for i in range(size - 1)])
    return before, after


def summed_over(value, axis):
    size = lax.axis_size(axis)
    if size & (size - 1):
        return lax.psum(value, axis)
    reach = 1
    while reach < size:
        value = value + lax.ppermute(value, axis, [(i, i ^ reach) for i in range(size)])
        reach *= 2
    return value


def lat_windows(lat_width, band, rows):
    decay = rows / 2.0
    total = lat_width.shape[0]
    offsets = jnp.abs(jnp.arange(-rows, rows + 1)).astype(jnp.float32)
    limits = lat_width.astype(jnp.float32)
    normal = jnp.sqrt(
        jnp.sum(
            jnp.where(
                offsets[None, :] <= limits[:, None], jnp.exp(-2.0 * offsets / decay)[None, :], 0.0
            ),
            axis=1,
        )
    )
    padded_limits = jnp.pad(limits, (rows, rows), constant_values=-1.0)
    padded_normal = jnp.pad(normal, (rows, rows), constant_values=1.0)
    near_limits = lax.dynamic_slice_in_dim(padded_limits, band * rows, 3 * rows)
    near_normal = lax.dynamic_slice_in_dim(padded_normal, band * rows, 3 * rows)
    distance = jnp.abs(
        jnp.arange(rows)[:, None] + rows - jnp.arange(3 * rows)[None, :]
    ).astype(jnp.float32)
    fade = jnp.exp(-distance / decay)
    own_limits, own_normal = near_limits[rows : 2 * rows, None], near_normal[rows : 2 * rows, None]
    spread = jnp.where(distance <= own_limits, fade, 0.0) / own_normal
    pulled = jnp.where(distance <= near_limits[None, :], fade, 0.0) / near_normal[None, :]
    return spread, pulled


def product(left, right):
    return jnp.dot(left, right, precision=HIGHEST)


def shards(
    footprints,
    block_rows,
    block_cols,
    block_scale,
    lat_width,
    lon_width,
    obs_weight,
    solution,
    residual,
    direction,
):
    rhs_count, weeks, rows, lon = direction.shape
    blocks = footprints[0, 0]
    count, edge, _ = blocks.shape
    row_list, col_list = block_rows[0, 0], block_cols[0, 0]
    scales = jnp.exp2(-block_scale[0, 0].astype(jnp.float32))
    row_blocks = obs_weight.shape[0] // edge
    slots = lax.axis_size("obs")
    rhs = rhs_count // slots
    slab, band = lax.axis_index("obs"), lax.axis_index("lat")
    parts = lon // edge
    cols = weeks * rows * parts

    own_width = lax.dynamic_slice_in_dim(lon_width, band * rows, rows)
    counts = jnp.broadcast_to(own_width[:, None] + 1, (rows, lon))
    lat_spread, lat_pulled = lat_windows(lat_width, band, rows)

    line, part = col_list // parts, col_list % parts
    place = ((line // rows) * parts + part) * rows + line % rows
    places = [place] + [shifted(place, "obs", -d) for d in range(1, slots)]
    places = jnp.stack(places)
    hot = (places[:, :, None] == jnp.arange(cols)[None, None, :]).astype(jnp.bfloat16)
    hot_turned = (jnp.arange(cols)[:, None] == places.reshape(1, -1)).astype(jnp.bfloat16)

    first = (slab * rhs).astype(jnp.int32).reshape(1)
    lon_own, lon_words = spread_lon(direction, first, rhs, counts)
    before, after = neighbours(lon_words, "lat")
    picks = spread_lat(lon_own, before, after, lat_spread, hot)
    cells = [picks[0]] + [shifted(picks[d], "obs", d) for d in range(1, slots)]
    sums = summed_over(forward(row_list, scales, blocks, cells, row_blocks), "lat")
    weighted = sums.reshape(row_blocks, slots * rhs, edge) * obs_weight.reshape(row_blocks, 1, edge)
    terms = adjoint_terms(
        row_list, scales, blocks, weighted.reshape(-1, edge), slots, rhs
    )
    terms = [terms[0]] + [shifted(terms[d], "obs", -d) for d in range(1, slots)]
    field, field_words = gather_cells(hot_turned, terms, weeks, rows, lon)
    before, after = neighbours(field_words, "lat")
    image_words = pull_back(field, before, after, lat_pulled, counts)
    image_words = [image_words] + [shifted(image_words, "obs", d) for d in range(1, slots)]
    order = (((slab - jnp.arange(slots)) % slots) * rhs).astype(jnp.int32)
    image, products = grams(order, residual, direction, image_words)

    sums = summed_over(jnp.sum(products, axis=(1, 2)), "lat")
    gram_old, curvature, mixed, gram_image = sums.reshape(4, rhs_count, rhs_count)
    upper = jnp.arange(rhs_count)[:, None] <= jnp.arange(rhs_count)[None, :]
    gram_old = jnp.where(upper, gram_old, gram_old.T)
    gram_image = jnp.where(upper, gram_image, gram_image.T)
    step_coef = jax.scipy.linalg.cho_solve((jnp.linalg.cholesky(curvature), True), gram_old)
    cross = product(mixed, step_coef)
    gram_new = gram_old - cross - cross.T + product(step_coef.T, product(gram_image, step_coef))
    turn_coef = jax.scipy.linalg.cho_solve((jnp.linalg.cholesky(gram_old), True), gram_new)
    return tuple(update(step_coef, turn_coef, solution, residual, direction, image))


def solution(mesh):
    return jax.shard_map(
        shards,
        mesh=mesh,
        in_specs=(
            P("obs", "lat", None, None, None),
            P("obs", "lat", None),
            P("obs", "lat", None),
            P("obs", "lat", None),
            P(),
            P(),
            P("obs"),
            P(None, None, "lat", None),
            P(None, None, "lat", None),
            P(None, None, "lat", None),
        ),
        out_specs=(
            P(None, None, "lat", None),
            P(None, None, "lat", None),
            P(None, None, "lat", None),
        ),
        check_vma=False,
    )
```

time: 739 us -> 223 us (0.30); the launches traced: 728 us -> 223 us
  matrix products: 171 us -> 1.21 us
  waiting for transfers between devices: 205 us -> 70.7 us
  local copies, waits for them, and re-layouts: 135 us -> 19.7 us
  loops' own time: 87.4 us -> 0 us
  Pallas kernels: 0 us -> 68.6 us
  blocking collectives: 53 us -> 0 us
  starting transfers between devices: 9.1 us -> 49.9 us
  other arithmetic: 52.1 us -> 11.9 us
  between operations: 14.7 us -> 0.97 us
    dot_general x76 -> x3, matrix products: 171 us -> 0.54 us  [product(): return jnp.dot(left, right, precision=HIGHEST)]
    another operation x2 -> x0, loops' own time: 87.4 us -> none  [lon_apply(): mixed_rows = lax.map(one_row, (jnp.moveaxis(field_in, 2, 0), widths))]
    all_gather x2 -> x0, waiting for transfers between devices: 74.7 us -> none  [the longest x1 42.9 us: shards(): image = direction + lax.all_gather(image_share, 'obs', axis=0, tiled=True)]
    ppermute x0 -> x22, waiting for transfers between devices: none -> 70.7 us  [the longest x12 57.3 us: shifted(): lax.ppermute(value, axis, [(i, (i + by) % size) for i in range(size)])]
    pallas_call x0 -> x8, Pallas kernels: none -> 68.6 us  [the longest x1 17 us: pull_back(): pl.pallas_call(pull_back_kernel, grid=(rhs,), in_specs=[pl.BlockSpec((1,...]
    dynamic_update_slice x64 -> x0, local copies, waits for them, and re-layouts: 54 us -> none  [lon_apply(): mixed_rows = lax.map(one_row, (jnp.moveaxis(field_in, 2, 0), widths))]
    psum x1 -> x0, waiting for transfers between devices: 52 us -> none  [shards(): summed = lax.psum(forward, 'lat')]
    reduce_scatter x1 -> x0, waiting for transfers between devices: 51.6 us -> none  [shards(): lax.psum_scatter(adjoint_local, 'obs', scatter_dimension=0, tiled=True)]
  transfers between devices with their start and end apart: 6 -> 22, of which waited for: 6 -> 14; matrix products, arithmetic and copies ran while one was open for 1% -> 1% of each run, Pallas kernels for 0% -> 7%
where the time goes in v1:
time: 223 us
  waiting for transfers between devices  70.7 us (32%)
  Pallas kernels  68.6 us (31%)
  starting transfers between devices  49.9 us (22%)
  local copies, waits for them, and re-layouts  19.7 us (9%)
  other arithmetic  11.9 us (5%)
    ppermute x12, waiting for transfers between devices, shifted(): lax.ppermute(value, axis, [(i, (i + by) % size) for i in range(size)])  57.3 us
    ppermute x6, starting transfers between devices, summed_over(): lax.ppermute(value, axis, [(i, i ^ reach) for i in range(size)])  21.8 us
    ppermute x12, starting transfers between devices, shifted(): lax.ppermute(value, axis, [(i, (i + by) % size) for i in range(size)])  19.4 us
    unnamed x28, local copies, waits for them, and re-layouts  18.6 us
    pallas_call x1, Pallas kernels, pull_back(): pl.pallas_call(pull_back_kernel, grid=(rhs,), in_specs=[pl.BlockSpec((1,...  17 us
    pallas_call x1, Pallas kernels, spread_lon(): pl.pallas_call(spread_lon_kernel, grid_spec=pltpu.PrefetchScalarGridSpec(...  15.6 us
    ppermute x6, waiting for transfers between devices, summed_over(): lax.ppermute(value, axis, [(i, i ^ reach) for i in range(size)])  11.8 us
    pallas_call x1, Pallas kernels, forward(): pl.pallas_call(functools.partial(forward_kernel, slots), grid_spec=pltpu....  8.96 us
  transfers between devices with their start and end apart: 22, of which 14 were waited for; matrix products, arithmetic and copies ran while one was open for 1% of the time, Pallas kernels for 7%

profile of v1, /device:TPU:0, one launch (start us, length us, event | category | flops | bytes accessed | tf_op | source)
XLA Modules:
  0.0 222.9 jit_solution(8458092325932440808)
XLA Ops:
  2.8 3.1 %collective-permute-start.2 = (s32[384]{0:T(512)S(1)}, s32[384]{0:T(512)S(1)}, u32[]{:S(2)}, u32[]{:S(2)}) collective-permute-start(s32[384]{0:T(512)S(1)} %fusion.19), channel_id=1, source_target_pairs={{0,8},{8,16},{16,24},{24,0},{1,9},{9,17},{17,25},{25,1},{2,10},{10... | collective-permute-start | bytes 4616 | tf_op jit(solution)/shard_map/ppermute | solution.py:601
  12.4 15.6 %spread_lon.1 = (f32[2,4,32,640]{3,2,1,0:T(8,128)S(1)}, s32[2,72,640]{2,1,0:T(8,128)S(1)}) custom-call(s32[1]{0:T(128)} %bitcast.4._, f32[8,4,32,640]{3,2,1,0:T(8,128)S(1)} %copy-done.2, s32[32,640]{1,0:T(8,128)S(1)} %broadcast_in_dim.18.count_ref), custom_call_target="tpu_custom_call" | custom-call | flops 16384000 | bytes 1638400 | tf_op jit(solution)/shard_map/spread_lon/pallas_call | solution.py:141
  29.3 3.1 %collective-permute-start.3 = (s32[2,72,640]{2,1,0:T(8,128)S(1)}, s32[2,72,640]{2,1,0:T(8,128)S(1)}, u32[]{:S(2)}, u32[]{:S(2)}) collective-permute-start(s32[2,72,640]{2,1,0:T(8,128)S(1)} %get-tuple-element.20), channel_id=1, source_target_pairs={{0,1},{1,2},{2,3},{3,4},{4,5},{5,6},{6,7},{8,9},{9,10},{10,11},{11... | collective-permute-start | bytes 1105928 | tf_op jit(solution)/shard_map/ppermute | solution.py:606
  37.4 2.8 %collective-permute-start.7 = (bf16[2,384,128]{2,1,0:T(8,128)(2,1)S(1)}, bf16[2,384,128]{2,1,0:T(8,128)(2,1)S(1)}, u32[]{:S(2)}, u32[]{:S(2)}) collective-permute-start(bf16[2,384,128]{2,1,0:T(8,128)(2,1)S(1)} %get-tuple-element.24), channel_id=1, source_target_pairs={{0,24},{8,0},{16,8},{24,16},{1,25},{9,1},{17,9},{25,17},{2,26},{10... | collective-permute-start | bytes 589832 | tf_op jit(solution)/shard_map/ppermute | solution.py:601
  40.3 3.8 %collective-permute-done.5.rest_1_ = bf16[2,384,128]{2,1,0:T(8,128)(2,1)S(1)} collective-permute-done((bf16[2,384,128]{2,1,0:T(8,128)(2,1)S(1)}, bf16[2,384,128]{2,1,0:T(8,128)(2,1)S(1)}, u32[]{:S(2)}, u32[]{:S(2)}) %collective-permute-start.5) | collective-permute-done | bytes 196640 | tf_op jit(solution)/shard_map/ppermute | solution.py:601
  44.1 9.8 %collective-permute-done.6.rest_2_ = bf16[2,384,128]{2,1,0:T(8,128)(2,1)S(1)} collective-permute-done((bf16[2,384,128]{2,1,0:T(8,128)(2,1)S(1)}, bf16[2,384,128]{2,1,0:T(8,128)(2,1)S(1)}, u32[]{:S(2)}, u32[]{:S(2)}) %collective-permute-start.6) | collective-permute-done | bytes 196640 | tf_op jit(solution)/shard_map/ppermute | solution.py:601
  53.9 4.6 %copy-done = bf16[1,1,384,128,128]{4,3,2,1,0:T(8,128)(2,1)S(1)} copy-done((bf16[1,1,384,128,128]{4,3,2,1,0:T(8,128)(2,1)S(1)}, bf16[1,1,384,128,128]{4,3,2,1,0:T(8,128)(2,1)}, u32[]{:S(2)}) %copy-start) | copy-done | bytes 12582936
  58.5 9.0 %forward.1 = f32[256,128]{1,0:T(8,128)S(1)} custom-call(s32[384]{0:T(512)S(1)} %reduce.7.row_ref, f32[384]{0:T(512)S(1)} %exponential_reduce_fusion.scale_ref, bf16[384,128,128]{2,1,0:T(8,128)(2,1)S(1)} %bitcast.66, bf16[2,384,128]{2,1,0:T(8,128)(2,1)S(1)} %get-tuple-element.21.rest_0_, bf16[2,384,128]{2,1,0:T(8,128)(2,1)S(1)} %collective-permute-done.5.rest_1_, ...), custom_call_target="tpu_custom_call" | custom-call | flops 100663296 | bytes 12582912 | tf_op jit(solution)/shard_map/forward/pallas_call | solution.py:284
  69.0 6.5 %collective-permute-start.9 = (f32[256,128]{1,0:T(8,128)S(1)}, f32[256,128]{1,0:T(8,128)S(1)}, u32[]{:S(2)}, u32[]{:S(2)}) collective-permute-start(f32[256,128]{1,0:T(8,128)S(1)} %add.173), channel_id=1, source_target_pairs={{0,2},{1,3},{2,0},{3,1},{4,6},{5,7},{6,4},{7,5},{8,10},{9,11},{10,... | collective-permute-start | bytes 393224 | tf_op jit(solution)/shard_map/ppermute | solution.py:617
  75.4 3.8 %collective-permute-done.9 = f32[256,128]{1,0:T(8,128)S(1)} collective-permute-done((f32[256,128]{1,0:T(8,128)S(1)}, f32[256,128]{1,0:T(8,128)S(1)}, u32[]{:S(2)}, u32[]{:S(2)}) %collective-permute-start.9) | collective-permute-done | bytes 131104 | tf_op jit(solution)/shard_map/ppermute | solution.py:617
  81.3 3.1 %collective-permute-done.10 = f32[256,128]{1,0:T(8,128)S(1)} collective-permute-done((f32[256,128]{1,0:T(8,128)S(1)}, f32[256,128]{1,0:T(8,128)S(1)}, u32[]{:S(2)}, u32[]{:S(2)}) %collective-permute-start.10) | collective-permute-done | bytes 131104 | tf_op jit(solution)/shard_map/ppermute | solution.py:617
  84.4 4.6 %copy-done.1 = bf16[1,1,384,128,128]{4,3,2,1,0:T(8,128)(2,1)S(1)} copy-done((bf16[1,1,384,128,128]{4,3,2,1,0:T(8,128)(2,1)S(1)}, bf16[1,1,384,128,128]{4,3,2,1,0:T(8,128)(2,1)}, u32[]{:S(2)}) %copy-start.1) | copy-done | bytes 12582936
  89.0 5.9 %adjoint.1 = (s32[2,200,128]{2,1,0:T(8,128)S(1)}, s32[2,200,128]{2,1,0:T(8,128)S(1)}, s32[2,200,128]{2,1,0:T(8,128)S(1)}, s32[2,200,128]{2,1,0:T(8,128)S(1)}) custom-call(s32[384]{0:T(512)S(1)} %reduce.7.row_ref, f32[384]{0:T(512)S(1)} %exponential_reduce_fusion.scale_ref, bf16[384,128,128]{2,1,0:T(8,128)(2,1)S(1)} %bitcast.67, ...), custom_call_target="tpu_custom_call" | custom-call | flops 100663296 | bytes 12582912 | tf_op jit(solution)/shard_map/adjoint/pallas_call | solution.py:332
  94.9 3.9 %collective-permute-start.11 = (s32[2,200,128]{2,1,0:T(8,128)S(1)}, s32[2,200,128]{2,1,0:T(8,128)S(1)}, u32[]{:S(2)}, u32[]{:S(2)}) collective-permute-start(s32[2,200,128]{2,1,0:T(8,128)S(1)} %get-tuple-element.26), channel_id=1, source_target_pairs={{0,24},{8,0},{16,8},{24,16},{1,25},{9,1},{17,9},{25,17},{2,26},{10... | collective-permute-start | bytes 614408 | tf_op jit(solution)/shard_map/ppermute | solution.py:601
  101.2 3.1 %collective-permute-done.11.rest_1_ = s32[2,200,128]{2,1,0:T(8,128)S(1)} collective-permute-done((s32[2,200,128]{2,1,0:T(8,128)S(1)}, s32[2,200,128]{2,1,0:T(8,128)S(1)}, u32[]{:S(2)}, u32[]{:S(2)}) %collective-permute-start.11) | collective-permute-done | bytes 204832 | tf_op jit(solution)/shard_map/ppermute | solution.py:601
  104.3 13.1 %collective-permute-done.12.rest_2_ = s32[2,200,128]{2,1,0:T(8,128)S(1)} collective-permute-done((s32[2,200,128]{2,1,0:T(8,128)S(1)}, s32[2,200,128]{2,1,0:T(8,128)S(1)}, u32[]{:S(2)}, u32[]{:S(2)}) %collective-permute-start.12) | collective-permute-done | bytes 204832 | tf_op jit(solution)/shard_map/ppermute | solution.py:601
  120.8 3.1 %collective-permute-start.14 = (s32[2,72,640]{2,1,0:T(8,128)S(1)}, s32[2,72,640]{2,1,0:T(8,128)S(1)}, u32[]{:S(2)}, u32[]{:S(2)}) collective-permute-start(s32[2,72,640]{2,1,0:T(8,128)S(1)} %get-tuple-element.30), channel_id=1, source_target_pairs={{0,1},{1,2},{2,3},{3,4},{4,5},{5,6},{6,7},{8,9},{9,10},{10,11},{11... | collective-permute-start | bytes 1105928 | tf_op jit(solution)/shard_map/ppermute | solution.py:606
  125.2 17.0 %pull_back.1.rest_0_ = s32[2,72,640]{2,1,0:T(8,128)S(1)} custom-call(f32[2,4,32,640]{3,2,1,0:T(8,128)S(1)} %get-tuple-element.29.own_ref, s32[2,72,640]{2,1,0:T(8,128)S(1)} %collective-permute-done.14.before_ref, s32[2,72,640]{2,1,0:T(8,128)S(1)} %collective-permute-done.15.after_ref, f32[32,96]{1,0:T(8,128)S(1)} %get-tuple-element.39.weights_ref, ...), custom_call_target="tpu_custom_call" | custom-call | flops 49152000 | bytes 1638400 | tf_op jit(solution)/shard_map/pull_back/pallas_call | solution.py:444
  145.0 7.0 %collective-permute-done.18.rest_3_ = s32[2,72,640]{2,1,0:T(8,128)S(1)} collective-permute-done((s32[2,72,640]{2,1,0:T(8,128)S(1)}, s32[2,72,640]{2,1,0:T(8,128)S(1)}, u32[]{:S(2)}, u32[]{:S(2)}) %collective-permute-start.18) | collective-permute-done | bytes 368672 | tf_op jit(solution)/shard_map/ppermute | solution.py:601
  152.0 20.4 %collective-permute-done.17.rest_2_ = s32[2,72,640]{2,1,0:T(8,128)S(1)} collective-permute-done((s32[2,72,640]{2,1,0:T(8,128)S(1)}, s32[2,72,640]{2,1,0:T(8,128)S(1)}, u32[]{:S(2)}, u32[]{:S(2)}) %collective-permute-start.17) | collective-permute-done | bytes 368672 | tf_op jit(solution)/shard_map/ppermute | solution.py:601
  172.4 8.9 %grams.1 = (f32[8,4,32,640]{3,2,1,0:T(8,128)S(1)}, f32[256,8,128]{2,1,0:T(8,128)S(1)}) custom-call(s32[4]{0:T(128)S(1)} %fusion.24.order_ref, f32[8,4,32,640]{3,2,1,0:T(8,128)S(1)} %copy-done.4, f32[8,4,32,640]{3,2,1,0:T(8,128)S(1)} %copy-done.3, s32[2,72,640]{2,1,0:T(8,128)S(1)} %pull_back.1.rest_0_, s32[2,72,640]{2,1,0:T(8,128)S(1)} %collective-permute-done.16.rest_1_, ...), custom_call_target="tpu_custom_call" | custom-call | flops 41943040 | bytes 10485760 | tf_op jit(solution)/shard_map/grams/pallas_call | solution.py:536
  186.0 3.6 %collective-permute-start.19 = (f32[256]{0:T(256)S(1)}, f32[256]{0:T(256)S(1)}, u32[]{:S(2)}, u32[]{:S(2)}) collective-permute-start(f32[256]{0:T(256)S(1)} %reduce_sum.19), channel_id=1, source_target_pairs={{0,1},{1,0},{2,3},{3,2},{4,5},{5,4},{6,7},{7,6},{8,9},{9,8},{10,11... | collective-permute-start | bytes 3080 | tf_op jit(solution)/shard_map/ppermute | solution.py:617
  190.4 7.0 %collective-permute-start.20 = (f32[256]{0:T(256)S(1)}, f32[256]{0:T(256)S(1)}, u32[]{:S(2)}, u32[]{:S(2)}) collective-permute-start(f32[256]{0:T(256)S(1)} %add.176), channel_id=1, source_target_pairs={{0,2},{1,3},{2,0},{3,1},{4,6},{5,7},{6,4},{7,5},{8,10},{9,11},{10,... | collective-permute-start | bytes 3080 | tf_op jit(solution)/shard_map/ppermute | solution.py:617
  215.4 7.5 %update.1 = (f32[8,4,32,640]{3,2,1,0:T(8,128)}, f32[8,4,32,640]{3,2,1,0:T(8,128)}, f32[8,4,32,640]{3,2,1,0:T(8,128)}) custom-call(f32[8,8]{1,0:T(8,128)S(1)} %fusion.11.step_ref, f32[8,8]{1,0:T(8,128)S(1)} %fusion.7.turn_ref, f32[8,4,32,640]{3,2,1,0:T(8,128)S(1)} %copy-done.6, f32[8,4,32,640]{3,2,1,0:T(8,128)S(1)} %copy-done.5, ...), custom_call_target="tpu_custom_call" | custom-call | flops 31457280 | bytes 18350080 | tf_op jit(solution)/shard_map/update/pallas_call | solution.py:584
  (120 shorter events, 51.7 us)
Async XLA Ops:
  2.8 30.1 %collective-permute-start.2 = (s32[384]{0:T(512)S(1)}, s32[384]{0:T(512)S(1)}, u32[]{:S(2)}, u32[]{:S(2)}) collective-permute-start(s32[384]{0:T(512)S(1)} %fusion.19), channel_id=1, source_target_pairs={{0,8},{8,16},{16,24},{24,0},{1,9},{9,17},{17,25},{25,1},{2,10},{10... | collective-permute-start | bytes 4616 | tf_op jit(solution)/shard_map/ppermute | solution.py:601
  5.9 27.0 %collective-permute-start.1 = (s32[384]{0:T(512)S(1)}, s32[384]{0:T(512)S(1)}, u32[]{:S(2)}, u32[]{:S(2)}) collective-permute-start(s32[384]{0:T(512)S(1)} %fusion.19), channel_id=1, source_target_pairs={{0,16},{8,24},{16,0},{24,8},{1,17},{9,25},{17,1},{25,9},{2,18},{10... | collective-permute-start | bytes 4616 | tf_op jit(solution)/shard_map/ppermute | solution.py:601
  8.5 24.5 %collective-permute-start = (s32[384]{0:T(512)S(1)}, s32[384]{0:T(512)S(1)}, u32[]{:S(2)}, u32[]{:S(2)}) collective-permute-start(s32[384]{0:T(512)S(1)} %fusion.19), channel_id=1, source_target_pairs={{0,24},{8,0},{16,8},{24,16},{1,25},{9,1},{17,9},{25,17},{2,26},{10... | collective-permute-start | bytes 4616 | tf_op jit(solution)/shard_map/ppermute | solution.py:601
  28.0 5.4 %collective-permute-start.4 = (s32[2,72,640]{2,1,0:T(8,128)S(1)}, s32[2,72,640]{2,1,0:T(8,128)S(1)}, u32[]{:S(2)}, u32[]{:S(2)}) collective-permute-start(s32[2,72,640]{2,1,0:T(8,128)S(1)} %get-tuple-element.20), channel_id=1, source_target_pairs={{1,0},{2,1},{3,2},{4,3},{5,4},{6,5},{7,6},{9,8},{10,9},{11,10},{12... | collective-permute-start | bytes 1105928 | tf_op jit(solution)/shard_map/ppermute | solution.py:607
  29.3 4.3 %collective-permute-start.3 = (s32[2,72,640]{2,1,0:T(8,128)S(1)}, s32[2,72,640]{2,1,0:T(8,128)S(1)}, u32[]{:S(2)}, u32[]{:S(2)}) collective-permute-start(s32[2,72,640]{2,1,0:T(8,128)S(1)} %get-tuple-element.20), channel_id=1, source_target_pairs={{0,1},{1,2},{2,3},{3,4},{4,5},{5,6},{6,7},{8,9},{9,10},{10,11},{11... | collective-permute-start | bytes 1105928 | tf_op jit(solution)/shard_map/ppermute | solution.py:606
  36.3 7.7 %collective-permute-start.5 = (bf16[2,384,128]{2,1,0:T(8,128)(2,1)S(1)}, bf16[2,384,128]{2,1,0:T(8,128)(2,1)S(1)}, u32[]{:S(2)}, u32[]{:S(2)}) collective-permute-start(bf16[2,384,128]{2,1,0:T(8,128)(2,1)S(1)} %get-tuple-element.22), channel_id=1, source_target_pairs={{0,8},{8,16},{16,24},{24,0},{1,9},{9,17},{17,25},{25,1},{2,10},{10... | collective-permute-start | bytes 589832 | tf_op jit(solution)/shard_map/ppermute | solution.py:601
  37.1 16.8 %collective-permute-start.6 = (bf16[2,384,128]{2,1,0:T(8,128)(2,1)S(1)}, bf16[2,384,128]{2,1,0:T(8,128)(2,1)S(1)}, u32[]{:S(2)}, u32[]{:S(2)}) collective-permute-start(bf16[2,384,128]{2,1,0:T(8,128)(2,1)S(1)} %get-tuple-element.23), channel_id=1, source_target_pairs={{0,16},{8,24},{16,0},{24,8},{1,17},{9,25},{17,1},{25,9},{2,18},{10... | collective-permute-start | bytes 589832 | tf_op jit(solution)/shard_map/ppermute | solution.py:601
  37.4 16.5 %collective-permute-start.7 = (bf16[2,384,128]{2,1,0:T(8,128)(2,1)S(1)}, bf16[2,384,128]{2,1,0:T(8,128)(2,1)S(1)}, u32[]{:S(2)}, u32[]{:S(2)}) collective-permute-start(bf16[2,384,128]{2,1,0:T(8,128)(2,1)S(1)} %get-tuple-element.24), channel_id=1, source_target_pairs={{0,24},{8,0},{16,8},{24,16},{1,25},{9,1},{17,9},{25,17},{2,26},{10... | collective-permute-start | bytes 589832 | tf_op jit(solution)/shard_map/ppermute | solution.py:601
  67.4 1.5 collective-permute-start.8
  69.0 10.3 %collective-permute-start.9 = (f32[256,128]{1,0:T(8,128)S(1)}, f32[256,128]{1,0:T(8,128)S(1)}, u32[]{:S(2)}, u32[]{:S(2)}) collective-permute-start(f32[256,128]{1,0:T(8,128)S(1)} %add.173), channel_id=1, source_target_pairs={{0,2},{1,3},{2,0},{3,1},{4,6},{5,7},{6,4},{7,5},{8,10},{9,11},{10,... | collective-permute-start | bytes 393224 | tf_op jit(solution)/shard_map/ppermute | solution.py:617
  79.3 5.1 %collective-permute-start.10 = (f32[256,128]{1,0:T(8,128)S(1)}, f32[256,128]{1,0:T(8,128)S(1)}, u32[]{:S(2)}, u32[]{:S(2)}) collective-permute-start(f32[256,128]{1,0:T(8,128)S(1)} %add.174), channel_id=1, source_target_pairs={{0,4},{1,5},{2,6},{3,7},{4,0},{5,1},{6,2},{7,3},{8,12},{9,13},{10,... | collective-permute-start | bytes 393224 | tf_op jit(solution)/shard_map/ppermute | solution.py:617
  94.9 9.4 %collective-permute-start.11 = (s32[2,200,128]{2,1,0:T(8,128)S(1)}, s32[2,200,128]{2,1,0:T(8,128)S(1)}, u32[]{:S(2)}, u32[]{:S(2)}) collective-permute-start(s32[2,200,128]{2,1,0:T(8,128)S(1)} %get-tuple-element.26), channel_id=1, source_target_pairs={{0,24},{8,0},{16,8},{24,16},{1,25},{9,1},{17,9},{25,17},{2,26},{10... | collective-permute-start | bytes 614408 | tf_op jit(solution)/shard_map/ppermute | solution.py:601
  98.8 18.6 %collective-permute-start.12 = (s32[2,200,128]{2,1,0:T(8,128)S(1)}, s32[2,200,128]{2,1,0:T(8,128)S(1)}, u32[]{:S(2)}, u32[]{:S(2)}) collective-permute-start(s32[2,200,128]{2,1,0:T(8,128)S(1)} %get-tuple-element.27), channel_id=1, source_target_pairs={{0,16},{8,24},{16,0},{24,8},{1,17},{9,25},{17,1},{25,9},{2,18},{10... | collective-permute-start | bytes 614408 | tf_op jit(solution)/shard_map/ppermute | solution.py:601
  100.6 16.9 %collective-permute-start.13 = (s32[2,200,128]{2,1,0:T(8,128)S(1)}, s32[2,200,128]{2,1,0:T(8,128)S(1)}, u32[]{:S(2)}, u32[]{:S(2)}) collective-permute-start(s32[2,200,128]{2,1,0:T(8,128)S(1)} %get-tuple-element.28), channel_id=1, source_target_pairs={{0,8},{8,16},{16,24},{24,0},{1,9},{9,17},{17,25},{25,1},{2,10},{10... | collective-permute-start | bytes 614408 | tf_op jit(solution)/shard_map/ppermute | solution.py:601
  117.4 55.0 %copy-start.3 = (f32[8,4,32,640]{3,2,1,0:T(8,128)S(1)}, f32[8,4,32,640]{3,2,1,0:T(8,128)}, u32[]{:S(2)}) copy-start(f32[8,4,32,640]{3,2,1,0:T(8,128)} %direction_ref.3) | copy-start | bytes 7864324
  117.4 55.0 %copy-start.4 = (f32[8,4,32,640]{3,2,1,0:T(8,128)S(1)}, f32[8,4,32,640]{3,2,1,0:T(8,128)}, u32[]{:S(2)}) copy-start(f32[8,4,32,640]{3,2,1,0:T(8,128)} %residual_ref.3) | copy-start | bytes 7864324
  119.5 4.4 %collective-permute-start.15 = (s32[2,72,640]{2,1,0:T(8,128)S(1)}, s32[2,72,640]{2,1,0:T(8,128)S(1)}, u32[]{:S(2)}, u32[]{:S(2)}) collective-permute-start(s32[2,72,640]{2,1,0:T(8,128)S(1)} %get-tuple-element.30), channel_id=1, source_target_pairs={{1,0},{2,1},{3,2},{4,3},{5,4},{6,5},{7,6},{9,8},{10,9},{11,10},{12... | collective-permute-start | bytes 1105928 | tf_op jit(solution)/shard_map/ppermute | solution.py:607
  120.8 4.3 %collective-permute-start.14 = (s32[2,72,640]{2,1,0:T(8,128)S(1)}, s32[2,72,640]{2,1,0:T(8,128)S(1)}, u32[]{:S(2)}, u32[]{:S(2)}) collective-permute-start(s32[2,72,640]{2,1,0:T(8,128)S(1)} %get-tuple-element.30), channel_id=1, source_target_pairs={{0,1},{1,2},{2,3},{3,4},{4,5},{5,6},{6,7},{8,9},{9,10},{10,11},{11... | collective-permute-start | bytes 1105928 | tf_op jit(solution)/shard_map/ppermute | solution.py:606
  142.2 9.8 %collective-permute-start.18 = (s32[2,72,640]{2,1,0:T(8,128)S(1)}, s32[2,72,640]{2,1,0:T(8,128)S(1)}, u32[]{:S(2)}, u32[]{:S(2)}) collective-permute-start(s32[2,72,640]{2,1,0:T(8,128)S(1)} %pull_back.1.rest_0_), channel_id=1, source_target_pairs={{0,24},{8,0},{16,8},{24,16},{1,25},{9,1},{17,9},{25,17},{2,26},{10... | collective-permute-start | bytes 1105928 | tf_op jit(solution)/shard_map/ppermute | solution.py:601
  142.3 30.2 %collective-permute-start.17 = (s32[2,72,640]{2,1,0:T(8,128)S(1)}, s32[2,72,640]{2,1,0:T(8,128)S(1)}, u32[]{:S(2)}, u32[]{:S(2)}) collective-permute-start(s32[2,72,640]{2,1,0:T(8,128)S(1)} %pull_back.1.rest_0_), channel_id=1, source_target_pairs={{0,16},{8,24},{16,0},{24,8},{1,17},{9,25},{17,1},{25,9},{2,18},{10... | collective-permute-start | bytes 1105928 | tf_op jit(solution)/shard_map/ppermute | solution.py:601
  143.1 29.4 %collective-permute-start.16 = (s32[2,72,640]{2,1,0:T(8,128)S(1)}, s32[2,72,640]{2,1,0:T(8,128)S(1)}, u32[]{:S(2)}, u32[]{:S(2)}) collective-permute-start(s32[2,72,640]{2,1,0:T(8,128)S(1)} %pull_back.1.rest_0_), channel_id=1, source_target_pairs={{0,8},{8,16},{16,24},{24,0},{1,9},{9,17},{17,25},{25,1},{2,10},{10... | collective-permute-start | bytes 1105928 | tf_op jit(solution)/shard_map/ppermute | solution.py:601
  186.0 4.4 %collective-permute-start.19 = (f32[256]{0:T(256)S(1)}, f32[256]{0:T(256)S(1)}, u32[]{:S(2)}, u32[]{:S(2)}) collective-permute-start(f32[256]{0:T(256)S(1)} %reduce_sum.19), channel_id=1, source_target_pairs={{0,1},{1,0},{2,3},{3,2},{4,5},{5,4},{6,7},{7,6},{8,9},{9,8},{10,11... | collective-permute-start | bytes 3080 | tf_op jit(solution)/shard_map/ppermute | solution.py:617
  190.4 8.6 %collective-permute-start.20 = (f32[256]{0:T(256)S(1)}, f32[256]{0:T(256)S(1)}, u32[]{:S(2)}, u32[]{:S(2)}) collective-permute-start(f32[256]{0:T(256)S(1)} %add.176), channel_id=1, source_target_pairs={{0,2},{1,3},{2,0},{3,1},{4,6},{5,7},{6,4},{7,5},{8,10},{9,11},{10,... | collective-permute-start | bytes 3080 | tf_op jit(solution)/shard_map/ppermute | solution.py:617
  199.0 3.8 %collective-permute-start.21 = (f32[256]{0:T(256)S(1)}, f32[256]{0:T(256)S(1)}, u32[]{:S(2)}, u32[]{:S(2)}) collective-permute-start(f32[256]{0:T(256)S(1)} %add.177), channel_id=1, source_target_pairs={{0,4},{1,5},{2,6},{3,7},{4,0},{5,1},{6,2},{7,3},{8,12},{9,13},{10,... | collective-permute-start | bytes 3080 | tf_op jit(solution)/shard_map/ppermute | solution.py:617
  (12 other events, 90.8 us)

commit v2 on v0

v2 whole, which is shorter than its diff:
```python
import functools
import math

import jax
import jax.numpy as jnp
from jax import lax
from jax.experimental import pallas as pl
from jax.experimental.pallas import tpu as pltpu
from jax.sharding import PartitionSpec as P

LANES = 128
CHUNK = 96
COPIES = 12
GROUP_RHS = 2
SUBLANES = 8
MIB = 1024 * 1024
HIGHEST = lax.Precision.HIGHEST


def params(mib):
    return pltpu.CompilerParams(vmem_limit_bytes=mib * MIB)


def cost(flops, nbytes):
    return pl.CostEstimate(flops=int(flops), bytes_accessed=int(nbytes), transcendentals=0)


def whole(shape):
    return pl.BlockSpec(shape, lambda *_: (0,) * len(shape), pipeline_mode=pl.Buffered(1))


def in_vmem(count):
    return [pl.BlockSpec(memory_space=pltpu.VMEM)] * count


def pow2(exponent):
    size = jnp.abs(exponent)
    up = jnp.ones(exponent.shape, jnp.float32)
    down = up
    for bit in range(7):
        on = ((size >> bit) & 1) == 1
        up = up * jnp.where(on, 2.0 ** (2**bit), 1.0)
        down = down * jnp.where(on, 2.0 ** -(2**bit), 1.0)
    return jnp.where(exponent < 0, down, up)


def exponent_of(peak):
    logs = jnp.log(jnp.maximum(peak, 1e-28)) * (1.0 / math.log(2.0))
    return jnp.ceil(logs + 1e-3).astype(jnp.int32)


def to_int(values, factor):
    return jnp.clip(jnp.round(values * factor), -32767.0, 32767.0).astype(jnp.int32)


def pack(high, low):
    return (high << 16) | (low & 0xFFFF)


def high_of(word):
    return word >> 16


def low_of(word):
    return (word << 16) >> 16


def words_of(rhs, weeks, rows):
    return rhs * weeks * rows // 2 + SUBLANES


def exponent_rows(peaks):
    line = lax.broadcasted_iota(jnp.int32, (SUBLANES, peaks[0].shape[1]), 0)
    found = jnp.zeros(line.shape, jnp.int32)
    for k, peak in enumerate(peaks):
        found = jnp.where(line == k, exponent_of(jnp.max(peak, axis=0, keepdims=True)), found)
    return found


def pack_field(field_ref, word_ref, peaks):
    rhs, weeks, rows, lon = field_ref.shape
    half = rows // 2
    exponents = exponent_rows(peaks)
    word_ref[rhs * weeks * half :, :] = exponents
    for k in range(rhs):
        factor = pow2(15 - jnp.broadcast_to(exponents[k : k + 1], (SUBLANES, lon)))

        def one_week(week, carry):
            for start in range(0, half, SUBLANES):
                high = to_int(field_ref[k, week, start : start + SUBLANES, :], factor)
                low = to_int(field_ref[k, week, half + start : half + start + SUBLANES, :], factor)
                at = pl.multiple_of((k * weeks + week) * half + start, SUBLANES)
                word_ref[pl.ds(at, SUBLANES), :] = pack(high, low)
            return carry

        lax.fori_loop(0, weeks, one_week, 0)


def word_scale(word_ref, body, k):
    row = word_ref[body + k : body + k + 1, :] - 15
    return pow2(jnp.broadcast_to(row, (SUBLANES, row.shape[1])))


def lon_setup(lon):
    return lon / 32.0, (lon // 8 + 1).bit_length()


def lon_rows(rows, count, norm, lon):
    decay, bits = lon_setup(lon)
    fields = rows.shape[0] // SUBLANES
    count = jnp.concatenate([count] * fields, axis=0)
    windows = [rows, rows]
    taken = [jnp.zeros_like(rows)] * 2
    for bit in range(bits):
        reach = 2**bit
        fade = math.exp(-reach / decay)
        chosen = ((count >> bit) & 1) == 1
        for side in range(2):
            shift = reach if side == 0 else lon - reach
            moved = windows[side]
            if bit:
                moved = moved + fade * pltpu.roll(taken[side], shift, 1)
            taken[side] = jnp.where(chosen, moved, taken[side])
            if bit + 1 < bits:
                windows[side] = windows[side] + fade * pltpu.roll(windows[side], shift, 1)
    return (taken[0] + taken[1] - rows) * jnp.concatenate([norm] * fields, axis=0)


def lon_norm(count, lon):
    decay, _ = lon_setup(lon)
    ratio = math.exp(-2.0 / decay)
    ends = jnp.exp(count.astype(jnp.float32) * (-2.0 / decay))
    return 1.0 / jnp.sqrt(1.0 + (2.0 / (1.0 - ratio)) * (ratio - ends))


def lon_field(source_ref, count_ref, out_ref):
    rhs, weeks, rows, lon = out_ref.shape

    def one_group(group, peaks):
        at = pl.multiple_of(group * SUBLANES, SUBLANES)
        count = count_ref[pl.ds(at, SUBLANES), :]
        norm = lon_norm(count, lon)
        fields = [source_ref[k, w, pl.ds(at, SUBLANES), :] for k in range(rhs) for w in range(weeks)]
        result = lon_rows(jnp.concatenate(fields, axis=0), count, norm, lon)
        peaks = list(peaks)
        for k in range(rhs):
            for w in range(weeks):
                start = (k * weeks + w) * SUBLANES
                part = result[start : start + SUBLANES]
                out_ref[k, w, pl.ds(at, SUBLANES), :] = part
                peaks[k] = jnp.maximum(peaks[k], jnp.abs(part))
        return tuple(peaks)

    zero = jnp.zeros((SUBLANES, lon), jnp.float32)
    return lax.fori_loop(0, rows // SUBLANES, one_group, (zero,) * rhs)


def spread_lon_kernel(_, field_ref, count_ref, out_ref, word_ref):
    pack_field(out_ref, word_ref, lon_field(field_ref, count_ref, out_ref))


def spread_lon(direction, first, rhs, counts):
    _, weeks, rows, lon = direction.shape
    words = words_of(rhs, weeks, rows)
    return pl.pallas_call(
        spread_lon_kernel,
        grid_spec=pltpu.PrefetchScalarGridSpec(
            num_scalar_prefetch=1,
            grid=(1,),
            in_specs=[
                pl.BlockSpec(
                    (rhs, weeks, rows, lon),
                    lambda _, first: (first[0], 0, 0, 0),
                    pipeline_mode=pl.Buffered(1),
                ),
                whole((rows, lon)),
            ],
            out_specs=[whole((rhs, weeks, rows, lon)), whole((words, lon))],
        ),
        out_shape=[
            jax.ShapeDtypeStruct((rhs, weeks, rows, lon), jnp.float32),
            jax.ShapeDtypeStruct((words, lon), jnp.int32),
        ],
        compiler_params=params(6),
        cost_estimate=cost(rhs * weeks * rows * lon * 100, rhs * weeks * rows * lon * 10),
        name="spread_lon",
    )(first, direction, counts)


def lat_mix(weights_ref, window_ref, k, week, before_ref, own_ref, after_ref, scales):
    rhs, weeks, rows, lon = own_ref.shape
    half = rows // 2
    for base, ref, scale in ((0, before_ref, scales[0]), (2 * rows, after_ref, scales[1])):
        for start in range(0, half, SUBLANES):
            at = (k * weeks + week) * half + start
            word = ref[at : at + SUBLANES, :]
            window_ref[base + start : base + start + SUBLANES, :] = (
                high_of(word).astype(jnp.float32) * scale
            )
            window_ref[base + half + start : base + half + start + SUBLANES, :] = (
                low_of(word).astype(jnp.float32) * scale
            )
    window_ref[rows : 2 * rows, :] = own_ref[k, week]
    return jnp.dot(
        weights_ref[...],
        window_ref[...],
        precision=HIGHEST,
        preferred_element_type=jnp.float32,
    )


def spread_lat_kernel(slots, own_ref, before_ref, after_ref, weights_ref, hot_ref, *rest):
    picks, (window_ref, cells_ref) = rest[:slots], rest[slots:]
    rhs, weeks, rows, lon = own_ref.shape
    body = before_ref.shape[0] - SUBLANES
    parts = lon // LANES
    for k in range(rhs):
        scales = word_scale(before_ref, body, k), word_scale(after_ref, body, k)
        for week in range(weeks):
            mixed = lat_mix(
                weights_ref, window_ref, k, week, before_ref, own_ref, after_ref, scales
            )
            for part in range(parts):
                at = (week * parts + part) * rows
                cells_ref[at : at + rows, k * LANES : (k + 1) * LANES] = mixed[
                    :, part * LANES : (part + 1) * LANES
                ].astype(jnp.bfloat16)
    for slot in range(slots):
        found = jnp.dot(
            hot_ref[slot], cells_ref[...], preferred_element_type=jnp.float32
        ).astype(jnp.bfloat16)
        for k in range(rhs):
            picks[slot][k] = found[:, k * LANES : (k + 1) * LANES]


def spread_lat(own, before, after, weights, hot):
    rhs, weeks, rows, lon = own.shape
    slots, blocks, cols = hot.shape
    return pl.pallas_call(
        functools.partial(spread_lat_kernel, slots),
        in_specs=in_vmem(5),
        out_specs=in_vmem(slots),
        out_shape=[jax.ShapeDtypeStruct((rhs, blocks, LANES), jnp.bfloat16)] * slots,
        scratch_shapes=[
            pltpu.VMEM((3 * rows, lon), jnp.float32),
            pltpu.VMEM((cols, rhs * LANES), jnp.bfloat16),
        ],
        compiler_params=params(10),
        cost_estimate=cost(rhs * slots * blocks * cols * LANES * 2, rhs * weeks * rows * lon * 10),
        name="spread_lat",
    )(own, before, after, weights, hot)


def chunk_of(count, most):
    return max(size for size in range(1, most + 1) if count % size == 0)


def preload_kernel(after_ref, blocks_ref, out_ref, done):
    del after_ref
    parts = done.shape[0]
    size = blocks_ref.shape[0] // parts
    copies = [
        pltpu.make_async_copy(
            blocks_ref.at[pl.ds(part * size, size)],
            out_ref.at[pl.ds(part * size, size)],
            done.at[part],
        )
        for part in range(parts)
    ]
    for copy in copies:
        copy.start()
    for copy in copies:
        copy.wait()


def preload(blocks, after):
    parts = chunk_of(blocks.shape[0], COPIES)
    return pl.pallas_call(
        preload_kernel,
        in_specs=[pl.BlockSpec(memory_space=pl.ANY)] * 2,
        out_specs=pl.BlockSpec(memory_space=pltpu.VMEM),
        out_shape=jax.ShapeDtypeStruct(blocks.shape, blocks.dtype),
        scratch_shapes=[pltpu.SemaphoreType.DMA((parts,))],
        compiler_params=params(13),
        cost_estimate=cost(0, blocks.size * 4),
        name="preload",
    )(after, blocks)


def forward_kernel(row_ref, scale_ref, blocks_ref, *rest):
    picks, (out_ref, cells_ref) = rest[:-2], rest[-2:]
    rhs, count, edge = picks[0].shape
    lines = len(picks) * rhs
    out_ref[...] = jnp.zeros_like(out_ref)
    for place, pick_ref in enumerate(picks):
        for k in range(rhs):
            cells_ref[pl.ds(place * rhs + k, count, stride=lines), :] = pick_ref[k].astype(
                jnp.float32
            )
    chunk = 2 * chunk_of(count // 2, CHUNK // 2)

    def one_chunk(step, carry):
        values = []
        for n in range(0, chunk, 2):
            index = step * chunk + n
            at = pl.multiple_of(index * lines, 2 * lines)
            both = lax.dot_general(
                cells_ref[pl.ds(at, 2 * lines), :].astype(jnp.bfloat16),
                blocks_ref[pl.ds(index, 2)].reshape(2 * edge, edge),
                (((1,), (1,)), ((), ())),
                preferred_element_type=jnp.float32,
            )
            values += [both[:lines, :edge], both[lines:, edge:]]
        for n in range(chunk):
            index = step * chunk + n
            at = pl.multiple_of(row_ref[index] * lines, lines)
            out_ref[pl.ds(at, lines), :] += values[n] * scale_ref[index]
        return carry

    lax.fori_loop(0, count // chunk, one_chunk, 0)


def forward(row_list, scales, blocks, picks, row_blocks):
    rhs, count, edge = picks[0].shape
    lines = len(picks) * rhs
    return pl.pallas_call(
        forward_kernel,
        in_specs=[pl.BlockSpec(memory_space=pltpu.SMEM)] * 2 + in_vmem(1 + len(picks)),
        out_specs=pl.BlockSpec(memory_space=pltpu.VMEM),
        out_shape=jax.ShapeDtypeStruct((row_blocks * lines, edge), jnp.float32),
        scratch_shapes=[pltpu.VMEM((count * lines, edge), jnp.float32)],
        compiler_params=params(15),
        cost_estimate=cost(blocks.size * 2 * lines, blocks.size * 2),
        name="forward",
    )(row_list, scales, blocks, *picks)


def adjoint_kernel(rhs, row_ref, scale_ref, blocks_ref, values_ref, *rest):
    outs, terms_ref = rest[:-1], rest[-1]
    lines = len(outs) * rhs
    count, edge, _ = blocks_ref.shape
    chunk = 2 * chunk_of(count // 2, CHUNK // 2)

    def one_chunk(step, carry):
        for n in range(0, chunk, 2):
            index = step * chunk + n
            pulled = [
                values_ref[pl.ds(pl.multiple_of(row_ref[index + q] * lines, lines), lines), :]
                for q in range(2)
            ]
            both = jnp.dot(
                jnp.concatenate(pulled, axis=0).astype(jnp.bfloat16),
                jnp.concatenate([blocks_ref[index + q] for q in range(2)], axis=1),
                preferred_element_type=jnp.float32,
            )
            for q in range(2):
                to = pl.multiple_of((index + q) * lines, lines)
                part = both[q * lines : (q + 1) * lines, q * edge : (q + 1) * edge]
                terms_ref[pl.ds(to, lines), :] = part * scale_ref[index + q]
        return carry

    lax.fori_loop(0, count // chunk, one_chunk, 0)
    half = count // 2
    for place, out_ref in enumerate(outs):
        terms = [terms_ref[pl.ds(place * rhs + k, count, stride=lines), :] for k in range(rhs)]
        exponents = exponent_rows([jnp.abs(term) for term in terms])
        out_ref[rhs * half :, :] = exponents
        for k in range(rhs):
            number = to_int(terms[k], pow2(15 - exponents[k : k + 1]))
            out_ref[k * half : (k + 1) * half, :] = pack(number[:half], number[half:])


def adjoint_terms(row_list, scales, blocks, values, outs, rhs):
    count, edge, _ = blocks.shape
    lines = outs * rhs
    words = rhs * count // 2 + SUBLANES
    return pl.pallas_call(
        functools.partial(adjoint_kernel, rhs),
        in_specs=[pl.BlockSpec(memory_space=pltpu.SMEM)] * 2 + in_vmem(2),
        out_specs=in_vmem(outs),
        out_shape=[jax.ShapeDtypeStruct((words, edge), jnp.int32)] * outs,
        scratch_shapes=[pltpu.VMEM((count * lines, edge), jnp.float32)],
        compiler_params=params(15),
        cost_estimate=cost(blocks.size * 2 * lines, blocks.size * 2),
        name="adjoint",
    )(row_list, scales, blocks, values)


def gather_cells_kernel(slots, hot_ref, *rest):
    terms, (field_ref, word_ref, split_ref) = rest[:slots], rest[slots:]
    rhs, weeks, rows, lon = field_ref.shape
    count = hot_ref.shape[1] // slots
    half = count // 2
    wide = rhs * LANES
    for slot in range(slots):
        for k in range(rhs):
            scale = word_scale(terms[slot], rhs * half, k)[:1]
            word = terms[slot][k * half : (k + 1) * half, :]
            for base, number in ((0, high_of(word)), (half, low_of(word))):
                coarse = (number + 128) >> 8
                fine = number - (coarse << 8)
                at = slot * count + base
                split_ref[at : at + half, k * LANES : (k + 1) * LANES] = (
                    (coarse << 8).astype(jnp.float32) * scale
                ).astype(jnp.bfloat16)
                split_ref[at : at + half, wide + k * LANES : wide + (k + 1) * LANES] = (
                    fine.astype(jnp.float32) * scale
                ).astype(jnp.bfloat16)
    peaks = [jnp.zeros((SUBLANES, lon), jnp.float32)] * rhs
    parts = lon // LANES
    for week in range(weeks):
        at = week * parts * rows
        both = jnp.dot(
            hot_ref[at : at + parts * rows, :],
            split_ref[...],
            preferred_element_type=jnp.float32,
        )
        cells = both[:, :wide] + both[:, wide:]
        for k in range(rhs):
            for part in range(parts):
                field_ref[k, week, :, part * LANES : (part + 1) * LANES] = cells[
                    part * rows : (part + 1) * rows, k * LANES : (k + 1) * LANES
                ]
            for start in range(0, rows, SUBLANES):
                peaks[k] = jnp.maximum(
                    peaks[k], jnp.abs(field_ref[k, week, start : start + SUBLANES, :])
                )
    pack_field(field_ref, word_ref, peaks)


def gather_cells(hot_turned, terms, rhs, weeks, rows, lon):
    slots = len(terms)
    return pl.pallas_call(
        functools.partial(gather_cells_kernel, slots),
        in_specs=in_vmem(1 + slots),
        out_specs=in_vmem(2),
        out_shape=[
            jax.ShapeDtypeStruct((rhs, weeks, rows, lon), jnp.float32),
            jax.ShapeDtypeStruct((words_of(rhs, weeks, rows), lon), jnp.int32),
        ],
        scratch_shapes=[pltpu.VMEM((hot_turned.shape[1], 2 * rhs * LANES), jnp.bfloat16)],
        compiler_params=params(12),
        cost_estimate=cost(rhs * hot_turned.size * 4 * LANES, rhs * weeks * rows * lon * 10),
        name="gather_cells",
    )(hot_turned, *terms)


def pull_back_kernel(
    own_ref, before_ref, after_ref, weights_ref, count_ref, word_ref, window_ref, field_ref
):
    rhs, weeks, rows, lon = own_ref.shape
    body = before_ref.shape[0] - SUBLANES
    for k in range(rhs):
        scales = word_scale(before_ref, body, k), word_scale(after_ref, body, k)
        for week in range(weeks):
            field_ref[k, week] = lat_mix(
                weights_ref, window_ref, k, week, before_ref, own_ref, after_ref, scales
            )
    pack_field(field_ref, word_ref, lon_field(field_ref, count_ref, field_ref))


def pull_back(own, before, after, weights, counts):
    rhs, weeks, rows, lon = own.shape
    return pl.pallas_call(
        pull_back_kernel,
        in_specs=in_vmem(5),
        out_specs=pl.BlockSpec(memory_space=pltpu.VMEM),
        out_shape=jax.ShapeDtypeStruct(before.shape, jnp.int32),
        scratch_shapes=[
            pltpu.VMEM((3 * rows, lon), jnp.float32),
            pltpu.VMEM((rhs, weeks, rows, lon), jnp.float32),
        ],
        compiler_params=params(8),
        cost_estimate=cost(rhs * weeks * rows * lon * 300, rhs * weeks * rows * lon * 10),
        name="pull_back",
    )(own, before, after, weights, counts)


PAIRS = 16


def gram_kernel(with_old, count, rhs, order_ref, sums_before, residual_ref, direction_ref, *rest):
    words, rest = rest[:count], rest[count:]
    news, gram_ref, sums_ref = rest[-count - 2 : -2], rest[-2], rest[-1]
    olds = rest[: -count - 2]
    rhs_count, weeks, rows, lon = direction_ref.shape
    half = rows // 2
    body = words[0].shape[0] - SUBLANES
    first = len(olds)

    def natural(place):
        return order_ref[place // rhs] + place % rhs

    for word_ref, new_ref, slot in zip(words, news, range(first, first + count)):
        for k in range(rhs):
            index = natural(slot * rhs + k)
            scale = word_scale(word_ref, body, k)

            def one_week(week, carry):
                for start in range(0, half, SUBLANES):
                    at = pl.multiple_of((k * weeks + week) * half + start, SUBLANES)
                    word = word_ref[pl.ds(at, SUBLANES), :]
                    for base, number in ((start, high_of(word)), (half + start, low_of(word))):
                        new_ref[k, week, base : base + SUBLANES, :] = (
                            direction_ref[index, week, base : base + SUBLANES, :]
                            + number.astype(jnp.float32) * scale
                        )
                return carry

            lax.fori_loop(0, weeks, one_week, 0)

    sums_ref[...] = jnp.zeros_like(sums_ref)
    row_groups = rows // SUBLANES

    def tile(index, lefts, rights, mirror):
        def one_group(step, sums):
            week = step // row_groups
            at = pl.multiple_of((step % row_groups) * SUBLANES, SUBLANES)
            sums = list(sums)
            for lane in range(0, lon, LANES):
                spot = (week, pl.ds(at, SUBLANES), slice(lane, lane + LANES))
                left = [ref[(k, *spot)] for ref, k, _ in lefts]
                right = [ref[(k, *spot)] for ref, k, _ in rights]
                for a in range(len(lefts)):
                    for b in range(len(rights)):
                        place = a * len(rights) + b
                        sums[place] = sums[place] + left[a] * right[b]
            return tuple(sums)

        zero = jnp.zeros((SUBLANES, LANES), jnp.float32)
        sums = lax.fori_loop(
            0, weeks * row_groups, one_group, (zero,) * (len(lefts) * len(rights))
        )
        for a, (_, _, row) in enumerate(lefts):
            for b, (_, _, column) in enumerate(rights):
                for row_at, column_at in ((row, column), (column, row))[: 1 + mirror]:
                    at = ((index * rhs_count + row_at) * rhs_count + column_at) * SUBLANES
                    at = pl.multiple_of(at, SUBLANES)
                    sums_ref[pl.ds(at, SUBLANES), :] = sums[a * len(rights) + b]

    def listed(refs, slot):
        return [
            (ref, k, natural((slot + place) * rhs + k))
            for place, ref in enumerate(refs)
            for k in range(rhs)
        ]

    def tiles(index, lefts, rights, mirror=False):
        wide = min(len(rights), 4)
        tall = PAIRS // wide
        for a in range(0, len(lefts), tall):
            for b in range(0, len(rights), wide):
                if lefts is rights and b + wide <= a:
                    continue
                tile(index, lefts[a : a + tall], rights[b : b + wide], mirror)

    residuals = [(residual_ref, k, k) for k in range(rhs_count)]
    directions = [(direction_ref, k, k) for k in range(rhs_count)]
    images = listed(news, first)
    if with_old:
        tiles(0, residuals, residuals, True)
    tiles(1, directions, images)
    tiles(2, residuals, images)
    tiles(3, images, images, True)
    if olds:
        tiles(3, listed(olds, 0), images, True)

    total = sums_ref.shape[0] // SUBLANES
    lanes = sums_ref[pl.ds(0, total, stride=SUBLANES), :]
    for line in range(1, SUBLANES):
        lanes = lanes + sums_ref[pl.ds(line, total, stride=SUBLANES), :]
    gram_ref[...] = sums_before[...] + lax.dot_general(
        jnp.ones((SUBLANES, LANES), jnp.float32),
        lanes,
        (((1,), (1,)), ((), ())),
        precision=HIGHEST,
        preferred_element_type=jnp.float32,
    )


def grams(order, sums, residual, direction, words, olds, with_old):
    rhs_count, weeks, rows, lon = direction.shape
    total = 4 * rhs_count**2
    rhs = (words[0].shape[0] - SUBLANES) * 2 // (weeks * rows)
    count = len(words)
    found = pl.pallas_call(
        functools.partial(gram_kernel, with_old, count, rhs),
        in_specs=[pl.BlockSpec(memory_space=pltpu.SMEM)] + in_vmem(3 + count + len(olds)),
        out_specs=in_vmem(count + 1),
        out_shape=[jax.ShapeDtypeStruct((rhs, weeks, rows, lon), jnp.float32)] * count
        + [jax.ShapeDtypeStruct((SUBLANES, total), jnp.float32)],
        scratch_shapes=[pltpu.VMEM((total * SUBLANES, LANES), jnp.float32)],
        compiler_params=params(14),
        cost_estimate=cost(8 * rhs_count * direction.size, 16 * direction.size),
        name="grams",
    )(order, sums, residual, direction, *words, *olds)
    return list(found[:-1]), found[-1]


def small_product(left, right):
    total = jnp.zeros((SUBLANES, LANES), jnp.float32)
    for j in range(SUBLANES):
        column = jnp.broadcast_to(left[:, j : j + 1], (SUBLANES, LANES))
        total = total + column * jnp.broadcast_to(right[j : j + 1, :], (SUBLANES, LANES))
    return total


def small_transpose(value):
    rest = jnp.zeros((LANES - SUBLANES, LANES), jnp.float32)
    return jnp.concatenate([value, rest], axis=0).T[:SUBLANES]


def small_solve(matrix, right):
    line = lax.broadcasted_iota(jnp.int32, (SUBLANES, LANES), 0)
    both = matrix + pltpu.roll(right, SUBLANES, 1)
    for j in range(SUBLANES):
        column = jnp.broadcast_to(both[:, j : j + 1], (SUBLANES, LANES))
        pivot = jnp.broadcast_to(both[j : j + 1, :], (SUBLANES, LANES))
        scaled = pivot / jnp.broadcast_to(both[j : j + 1, j : j + 1], (SUBLANES, LANES))
        both = jnp.where(line == j, scaled, both - column * scaled)
    lane = lax.broadcasted_iota(jnp.int32, (SUBLANES, LANES), 1)
    return jnp.where(lane < SUBLANES, pltpu.roll(both, LANES - SUBLANES, 1), 0.0)


def solve_steps(sums_ref, coef_ref):
    total = sums_ref.shape[1]
    size = SUBLANES
    place = lax.broadcasted_iota(jnp.int32, (size, total), 1)
    line = lax.broadcasted_iota(jnp.int32, (size, total), 0)
    spot = lax.broadcasted_iota(jnp.int32, (total, LANES), 0)
    lane = lax.broadcasted_iota(jnp.int32, (total, LANES), 1)
    to_column = jnp.where(spot % size == lane, 1.0, 0.0)
    sums = sums_ref[...]

    def matrix(index):
        rows = jnp.where(place // size == index * size + line, sums, 0.0)
        return jnp.dot(rows, to_column, precision=HIGHEST, preferred_element_type=jnp.float32)

    gram_old, curvature, mixed, gram_image = [matrix(index) for index in range(4)]
    curvature = 0.5 * (curvature + small_transpose(curvature))
    step = small_solve(curvature, gram_old)
    cross = small_product(mixed, step)
    both = small_product(small_transpose(step), small_product(gram_image, step))
    gram_new = gram_old - cross - small_transpose(cross) + both
    turn = small_solve(gram_old, gram_new)
    for index, matrix in enumerate((step, turn)):
        for b in range(size):
            for a in range(size):
                at = ((index * size + b) * size + a) * SUBLANES
                coef_ref[at : at + SUBLANES, :] = jnp.broadcast_to(
                    matrix[b : b + 1, a : a + 1], (SUBLANES, LANES)
                )


def summed_slots(terms, rhs):
    parts = [
        functools.reduce(lambda left, right: left + right, terms[at : at + rhs])
        for at in range(0, len(terms), rhs)
    ]
    while len(parts) > 1:
        parts = [left + right for left, right in zip(parts[::2], parts[1::2])]
    return parts[0]


def update_kernel(
    order_ref, sums_ref, solution_ref, residual_ref, direction_ref, *rest
):
    images, (sol_out, res_out, dir_out, coef_ref) = rest[:-4], rest[-4:]
    rhs_count, _, rows, lon = direction_ref.shape
    rhs = images[0].shape[0]

    @pl.when((pl.program_id(0) == 0) & (pl.program_id(1) == 0))
    def _():
        solve_steps(sums_ref, coef_ref)

    def coef(index, b, a):
        at = ((index * rhs_count + b) * rhs_count + a) * SUBLANES
        return coef_ref[pl.ds(pl.multiple_of(at, SUBLANES), SUBLANES), :]

    natural = [order_ref[slot] + k for slot in range(len(images)) for k in range(rhs)]

    def one_group(group, carry):
        at = pl.multiple_of(group * SUBLANES, SUBLANES)
        for lane in range(0, lon, LANES):
            spot = (0, pl.ds(at, SUBLANES), slice(lane, lane + LANES))
            directions = [direction_ref[(b, *spot)] for b in range(rhs_count)]
            image = [ref[(k, *spot)] for ref in images for k in range(rhs)]
            for a in range(rhs_count):
                moved = solution_ref[(a, *spot)]
                left = residual_ref[(a, *spot)]
                for b in range(rhs_count):
                    moved = moved + coef(0, b, a) * directions[b]
                left = left - summed_slots(
                    [coef(0, natural[b], a) * image[b] for b in range(rhs_count)], rhs
                )
                sol_out[(a, *spot)] = moved
                res_out[(a, *spot)] = left
                for b in range(rhs_count):
                    left = left + coef(1, b, a) * directions[b]
                dir_out[(a, *spot)] = left
        return carry

    lax.fori_loop(0, rows // SUBLANES, one_group, 0)


def update(order, sums, solution, residual, direction, images):
    rhs_count, weeks, rows, lon = direction.shape
    half = rows // 2

    def field(rhs):
        return pl.BlockSpec((rhs, 1, half, lon), lambda w, h, _: (0, w, h, 0))

    shape = jax.ShapeDtypeStruct(direction.shape, jnp.float32)
    return pl.pallas_call(
        update_kernel,
        grid_spec=pltpu.PrefetchScalarGridSpec(
            num_scalar_prefetch=1,
            grid=(weeks, 2),
            in_specs=[whole(sums.shape)]
            + [field(rhs_count)] * 3
            + [field(image.shape[0]) for image in images],
            out_specs=[field(rhs_count)] * 3,
            scratch_shapes=[pltpu.VMEM((2 * rhs_count**2 * SUBLANES, LANES), jnp.float32)],
        ),
        out_shape=[shape] * 3,
        compiler_params=params(10),
        cost_estimate=cost(6 * rhs_count * direction.size, 28 * direction.size),
        name="update",
    )(order, sums, solution, residual, direction, *images)


def crossed(value, axis, by):
    if by == 0:
        return value
    return lax.ppermute(value, axis, [(i, i ^ by) for i in range(lax.axis_size(axis))])


def neighbours(value, axis):
    size = lax.axis_size(axis)
    before = lax.ppermute(value, axis, [(i, i + 1) for i in range(size - 1)])
    after = lax.ppermute(value, axis, [(i + 1, i) for i in range(size - 1)])
    return before, after


def summed_over(value, axis):
    size = lax.axis_size(axis)
    reach = 1
    while reach < size:
        value = value + crossed(value, axis, reach)
        reach *= 2
    return value


def summed_in_halves(value, axis):
    size = lax.axis_size(axis)
    if size < 4:
        return summed_over(value, axis)
    half = value.shape[0] // 2
    low, high = value[:half], value[half:]
    even = lax.axis_index(axis) % 2 == 0
    mine = jnp.where(even, low, high) + crossed(jnp.where(even, high, low), axis, 1)
    reach = 2
    while reach < size:
        mine = mine + crossed(mine, axis, reach)
        reach *= 2
    other = crossed(mine, axis, 1)
    return jnp.concatenate([jnp.where(even, mine, other), jnp.where(even, other, mine)], axis=0)


def lat_windows(lat_width, band, rows):
    decay = rows / 2.0
    total = lat_width.shape[0]
    offsets = jnp.abs(jnp.arange(-rows, rows + 1)).astype(jnp.float32)
    limits = lat_width.astype(jnp.float32)
    normal = jnp.sqrt(
        jnp.sum(
            jnp.where(
                offsets[None, :] <= limits[:, None], jnp.exp(-2.0 * offsets / decay)[None, :], 0.0
            ),
            axis=1,
        )
    )
    padded_limits = jnp.pad(limits, (rows, rows), constant_values=-1.0)
    padded_normal = jnp.pad(normal, (rows, rows), constant_values=1.0)
    near_limits = lax.dynamic_slice_in_dim(padded_limits, band * rows, 3 * rows)
    near_normal = lax.dynamic_slice_in_dim(padded_normal, band * rows, 3 * rows)
    distance = jnp.abs(
        jnp.arange(rows)[:, None] + rows - jnp.arange(3 * rows)[None, :]
    ).astype(jnp.float32)
    fade = jnp.exp(-distance / decay)
    own_limits, own_normal = near_limits[rows : 2 * rows, None], near_normal[rows : 2 * rows, None]
    spread = jnp.where(distance <= own_limits, fade, 0.0) / own_normal
    pulled = jnp.where(distance <= near_limits[None, :], fade, 0.0) / near_normal[None, :]
    return spread, pulled


def shards(
    footprints,
    block_rows,
    block_cols,
    block_scale,
    lat_width,
    lon_width,
    obs_weight,
    solution,
    residual,
    direction,
):
    rhs_count, weeks, rows, lon = direction.shape
    blocks = footprints[0, 0]
    count, edge, _ = blocks.shape
    row_list, col_list = block_rows[0, 0], block_cols[0, 0]
    scales = jnp.exp2(-block_scale[0, 0].astype(jnp.float32))
    row_blocks = obs_weight.shape[0] // edge
    slots = lax.axis_size("obs")
    rhs = rhs_count // slots
    slab, band = lax.axis_index("obs"), lax.axis_index("lat")
    parts = lon // edge
    cols = weeks * rows * parts

    groups = rhs // GROUP_RHS if rhs % GROUP_RHS == 0 else 1
    each = rhs // groups
    first = (slab * groups).astype(jnp.int32)
    others = slab ^ jnp.arange(slots, dtype=jnp.int32)
    order = others * rhs
    own_width = lax.dynamic_slice_in_dim(lon_width, band * rows, rows)
    counts = jnp.broadcast_to(own_width[:, None] + 1, (rows, lon))

    line, part = col_list // parts, col_list % parts
    place = ((line // rows) * parts + part) * rows + line % rows
    places = place[None]
    reach = 1
    while reach < slots:
        places = jnp.concatenate([places, crossed(places, "obs", reach)], axis=0)
        reach *= 2

    lon_own, halos = [], []
    for group in range(groups):
        own, words = spread_lon(direction, (first + group).reshape(1), each, counts)
        lon_own.append(own)
        halos.append(neighbours(words, "lat"))

    hot = (places[:, :, None] == jnp.arange(cols)[None, None, :]).astype(jnp.bfloat16)
    hot_turned = (jnp.arange(cols)[:, None] == places.reshape(1, -1)).astype(jnp.bfloat16)
    lat_spread, lat_pulled = lat_windows(lat_width, band, rows)

    cells = [[None] * groups for _ in range(slots)]
    for group in range(groups):
        picks = spread_lat(lon_own[group], *halos[group], lat_spread, hot)
        for d in range(slots):
            cells[d][group] = crossed(picks[d], "obs", d)
    cells = [cell for slot_cells in cells for cell in slot_cells]
    near_blocks = preload(blocks, cells[0])
    sums = summed_in_halves(forward(row_list, scales, near_blocks, cells, row_blocks), "lat")
    weighted = sums.reshape(row_blocks, slots * rhs, edge) * obs_weight.reshape(row_blocks, 1, edge)
    terms = adjoint_terms(
        row_list, scales, near_blocks, weighted.reshape(-1, edge), slots * groups, each
    )
    images = [[None] * groups for _ in range(slots)]
    for group in range(groups):
        sent = [crossed(terms[d * groups + group], "obs", d) for d in range(slots)]
        field, words = gather_cells(hot_turned, sent, each, weeks, rows, lon)
        words = pull_back(field, *neighbours(words, "lat"), lat_pulled, counts)
        for d in range(slots):
            images[d][group] = crossed(words, "obs", d)

    starts = (order[:, None] + jnp.arange(groups, dtype=jnp.int32) * each).reshape(-1)
    products = jnp.zeros((SUBLANES, 4 * rhs_count**2), jnp.float32)
    found = []
    for d in range(slots):
        new, products = grams(starts, products, residual, direction, images[d], found, d == 0)
        found += new
    products = summed_over(products, "lat")
    return tuple(update(starts, products, solution, residual, direction, found))


def solution(mesh):
    return jax.shard_map(
        shards,
        mesh=mesh,
        in_specs=(
            P("obs", "lat", None, None, None),
            P("obs", "lat", None),
            P("obs", "lat", None),
            P("obs", "lat", None),
            P(),
            P(),
            P("obs"),
            P(None, None, "lat", None),
            P(None, None, "lat", None),
            P(None, None, "lat", None),
        ),
        out_specs=(
            P(None, None, "lat", None),
            P(None, None, "lat", None),
            P(None, None, "lat", None),
        ),
        check_vma=False,
    )
```

time: 739 us -> 165 us (0.22); the launches traced: 728 us -> 162 us
  matrix products: 171 us -> 0 us
  waiting for transfers between devices: 205 us -> 51.4 us
  local copies, waits for them, and re-layouts: 135 us -> 11.3 us
  loops' own time: 87.4 us -> 0 us
  blocking collectives: 53 us -> 0 us
  other arithmetic: 52.1 us -> 2.15 us
  Pallas kernels: 0 us -> 47 us
  starting transfers between devices: 9.1 us -> 49.1 us
  between operations: 14.7 us -> 0.97 us
    dot_general x76 -> x0, matrix products: 171 us -> none  [the longest x64 103 us: one_row(): jnp.einsum('kwa,ab->kwb', slab_row, lon_matrix(row_width, lon_points), pr...]
    another operation x2 -> x0, loops' own time: 87.4 us -> none  [lon_apply(): mixed_rows = lax.map(one_row, (jnp.moveaxis(field_in, 2, 0), widths))]
    all_gather x2 -> x0, waiting for transfers between devices: 74.7 us -> none  [the longest x1 42.9 us: shards(): image = direction + lax.all_gather(image_share, 'obs', axis=0, tiled=True)]
    dynamic_update_slice x64 -> x0, local copies, waits for them, and re-layouts: 54 us -> none  [lon_apply(): mixed_rows = lax.map(one_row, (jnp.moveaxis(field_in, 2, 0), widths))]
    psum x1 -> x0, waiting for transfers between devices: 52 us -> none  [shards(): summed = lax.psum(forward, 'lat')]
    reduce_scatter x1 -> x0, waiting for transfers between devices: 51.6 us -> none  [shards(): lax.psum_scatter(adjoint_local, 'obs', scatter_dimension=0, tiled=True)]
    ppermute x0 -> x22, waiting for transfers between devices: none -> 51.4 us  [the longest x18 47.5 us: crossed(): lax.ppermute(value, axis, [(i, i ^ by) for i in range(lax.axis_size(axis))])]
    ppermute x0 -> x22, starting transfers between devices: none -> 49.1 us  [the longest x18 42.6 us: crossed(): lax.ppermute(value, axis, [(i, i ^ by) for i in range(lax.axis_size(axis))])]
  transfers between devices with their start and end apart: 6 -> 22, of which waited for: 6 -> 16; matrix products, arithmetic and copies ran while one was open for 1% -> 1% of each run, Pallas kernels for 0% -> 7%
where the time goes in v2:
time: 165 us; the launch traced here: 162 us
  waiting for transfers between devices  51.4 us (31%)
  starting transfers between devices  49.1 us (30%)
  Pallas kernels  47 us (28%)
  local copies, waits for them, and re-layouts  11.3 us (7%)
  other arithmetic  2.15 us (1%)
    ppermute x18, waiting for transfers between devices, crossed(): lax.ppermute(value, axis, [(i, i ^ by) for i in range(lax.axis_size(axis))])  47.5 us
    ppermute x18, starting transfers between devices, crossed(): lax.ppermute(value, axis, [(i, i ^ by) for i in range(lax.axis_size(axis))])  42.6 us
    pallas_call x4, Pallas kernels, grams(): pl.pallas_call(functools.partial(gram_kernel, with_old, count, rhs), in_s...  12.8 us
    unnamed x24, local copies, waits for them, and re-layouts  10.9 us
    pallas_call x1, Pallas kernels, update(): pl.pallas_call(update_kernel, grid_spec=pltpu.PrefetchScalarGridSpec(num_...  10.7 us
    pallas_call x1, Pallas kernels, pull_back(): pl.pallas_call(pull_back_kernel, in_specs=in_vmem(5), out_specs=pl.BlockS...  5.93 us
    pallas_call x1, Pallas kernels, forward(): pl.pallas_call(forward_kernel, in_specs=[pl.BlockSpec(memory_space=pltpu....  4.78 us
    pallas_call x1, Pallas kernels, spread_lon(): pl.pallas_call(spread_lon_kernel, grid_spec=pltpu.PrefetchScalarGridSpec(...  4.71 us
  transfers between devices with their start and end apart: 22, of which 16 were waited for; matrix products, arithmetic and copies ran while one was open for 1% of the time, Pallas kernels for 7%

profile of v2, /device:TPU:0, one launch (start us, length us, event | category | flops | bytes accessed | tf_op | source)
XLA Modules:
  0.0 161.9 jit_solution(10720235129115999100)
XLA Ops:
  3.2 4.7 %spread_lon.1 = (f32[2,4,32,640]{3,2,1,0:T(8,128)S(1)}, s32[136,640]{1,0:T(8,128)S(1)}) custom-call(s32[1]{0:T(128)} %bitcast.3._, f32[8,4,32,640]{3,2,1,0:T(8,128)S(1)} %copy-done.2, s32[32,640]{1,0:T(8,128)S(1)} %broadcast_in_dim.21.count_ref), custom_call_target="tpu_custom_call" | custom-call | flops 16384000 | bytes 1638400 | tf_op jit(solution)/shard_map/spread_lon/pallas_call | solution.py:165
  15.7 3.1 %collective-permute-start.1 = (s32[2,384]{1,0:T(2,128)S(1)}, s32[2,384]{1,0:T(2,128)S(1)}, u32[]{:S(2)}, u32[]{:S(2)}) collective-permute-start(s32[2,384]{1,0:T(2,128)S(1)} %pad_add_fusion.1), channel_id=1, source_target_pairs={{0,16},{8,24},{16,0},{24,8},{1,17},{9,25},{17,1},{25,9},{2,18},{10... | collective-permute-start | bytes 9224 | tf_op jit(solution)/shard_map/ppermute | solution.py:735
  24.7 2.6 %collective-permute-start.5 = (bf16[2,384,128]{2,1,0:T(8,128)(2,1)S(1)}, bf16[2,384,128]{2,1,0:T(8,128)(2,1)S(1)}, u32[]{:S(2)}, u32[]{:S(2)}) collective-permute-start(bf16[2,384,128]{2,1,0:T(8,128)(2,1)S(1)} %get-tuple-element.27), channel_id=1, source_target_pairs={{0,16},{8,24},{16,0},{24,8},{1,17},{9,25},{17,1},{25,9},{2,18},{10... | collective-permute-start | bytes 589832 | tf_op jit(solution)/shard_map/ppermute | solution.py:735
  27.4 4.6 %copy-done.5 = bf16[1,1,384,128,128]{4,3,2,1,0:T(8,128)(2,1)S(1)} copy-done((bf16[1,1,384,128,128]{4,3,2,1,0:T(8,128)(2,1)S(1)}, bf16[1,1,384,128,128]{4,3,2,1,0:T(8,128)(2,1)}, u32[]{:S(2)}) %copy-start.5) | copy-done | bytes 12582936
  33.8 8.0 %collective-permute-done.5.rest_2_ = bf16[2,384,128]{2,1,0:T(8,128)(2,1)S(1)} collective-permute-done((bf16[2,384,128]{2,1,0:T(8,128)(2,1)S(1)}, bf16[2,384,128]{2,1,0:T(8,128)(2,1)S(1)}, u32[]{:S(2)}, u32[]{:S(2)}) %collective-permute-start.5) | collective-permute-done | bytes 196640 | tf_op jit(solution)/shard_map/ppermute | solution.py:735
  41.8 4.8 %forward.1 = f32[256,128]{1,0:T(8,128)S(1)} custom-call(s32[384]{0:T(512)S(1)} %reduce.row_ref, f32[384]{0:T(512)S(1)} %exponential_reduce_fusion.scale_ref, bf16[384,128,128]{2,1,0:T(8,128)(2,1)S(1)} %preload.1.blocks_ref, bf16[2,384,128]{2,1,0:T(8,128)(2,1)S(1)} %get-tuple-element.25.after_ref.rest_0_, ...), custom_call_target="tpu_custom_call" | custom-call | flops 100663296 | bytes 12582912 | tf_op jit(solution)/shard_map/forward/pallas_call | solution.py:326
  48.0 3.8 %collective-permute-start.8 = (f32[128,128]{1,0:T(8,128)S(1)}, f32[128,128]{1,0:T(8,128)S(1)}, u32[]{:S(2)}, u32[]{:S(2)}) collective-permute-start(f32[128,128]{1,0:T(8,128)S(1)} %select_add_fusion), channel_id=1, source_target_pairs={{0,2},{1,3},{2,0},{3,1},{4,6},{5,7},{6,4},{7,5},{8,10},{9,11},{10,... | collective-permute-start | bytes 196616 | tf_op jit(solution)/shard_map/ppermute | solution.py:735
  55.2 3.4 %collective-permute-done.9 = f32[128,128]{1,0:T(8,128)S(1)} collective-permute-done((f32[128,128]{1,0:T(8,128)S(1)}, f32[128,128]{1,0:T(8,128)S(1)}, u32[]{:S(2)}, u32[]{:S(2)}) %collective-permute-start.9) | collective-permute-done | bytes 65568 | tf_op jit(solution)/shard_map/ppermute | solution.py:735
  59.9 4.6 %copy-done.1 = bf16[384,128,128]{2,1,0:T(8,128)(2,1)S(1)} copy-done((bf16[384,128,128]{2,1,0:T(8,128)(2,1)S(1)}, bf16[384,128,128]{2,1,0:T(8,128)(2,1)}, u32[]{:S(2)}) %copy-start.1) | copy-done | bytes 12582936
  64.5 3.3 %adjoint.1 = (s32[392,128]{1,0:T(8,128)S(1)}, s32[392,128]{1,0:T(8,128)S(1)}, s32[392,128]{1,0:T(8,128)S(1)}, s32[392,128]{1,0:T(8,128)S(1)}) custom-call(s32[384]{0:T(512)S(1)} %reduce.row_ref, f32[384]{0:T(512)S(1)} %exponential_reduce_fusion.scale_ref, bf16[384,128,128]{2,1,0:T(8,128)(2,1)S(1)} %copy-done.1, f32[256,128]{1,0:T(8,128)S(1)} %maximum_multiply_fusion.values_ref), custom_call_target="tpu_custom_call" | custom-call | flops 100663296 | bytes 12582912 | tf_op jit(solution)/shard_map/adjoint/pallas_call | solution.py:377
  67.8 2.9 %collective-permute-start.11 = (s32[392,128]{1,0:T(8,128)S(1)}, s32[392,128]{1,0:T(8,128)S(1)}, u32[]{:S(2)}, u32[]{:S(2)}) collective-permute-start(s32[392,128]{1,0:T(8,128)S(1)} %get-tuple-element.30), channel_id=1, source_target_pairs={{0,8},{8,0},{16,24},{24,16},{1,9},{9,1},{17,25},{25,17},{2,10},{10... | collective-permute-start | bytes 602120 | tf_op jit(solution)/shard_map/ppermute | solution.py:735
  73.8 5.9 %collective-permute-done.11.rest_1_ = s32[392,128]{1,0:T(8,128)S(1)} collective-permute-done((s32[392,128]{1,0:T(8,128)S(1)}, s32[392,128]{1,0:T(8,128)S(1)}, u32[]{:S(2)}, u32[]{:S(2)}) %collective-permute-start.11) | collective-permute-done | bytes 200736 | tf_op jit(solution)/shard_map/ppermute | solution.py:735
  79.7 8.4 %collective-permute-done.12.rest_2_ = s32[392,128]{1,0:T(8,128)S(1)} collective-permute-done((s32[392,128]{1,0:T(8,128)S(1)}, s32[392,128]{1,0:T(8,128)S(1)}, u32[]{:S(2)}, u32[]{:S(2)}) %collective-permute-start.12) | collective-permute-done | bytes 200736 | tf_op jit(solution)/shard_map/ppermute | solution.py:735
  92.9 3.9 %collective-permute-done.15.after_ref = s32[136,640]{1,0:T(8,128)S(1)} collective-permute-done((s32[136,640]{1,0:T(8,128)S(1)}, s32[136,640]{1,0:T(8,128)S(1)}, u32[]{:S(2)}, u32[]{:S(2)}) %collective-permute-start.15) | collective-permute-done | bytes 348192 | tf_op jit(solution)/shard_map/ppermute | solution.py:741
  96.8 5.9 %pull_back.1.rest_0_ = s32[136,640]{1,0:T(8,128)S(1)} custom-call(f32[2,4,32,640]{3,2,1,0:T(8,128)S(1)} %get-tuple-element.33.own_ref, s32[136,640]{1,0:T(8,128)S(1)} %collective-permute-done.14.before_ref, s32[136,640]{1,0:T(8,128)S(1)} %collective-permute-done.15.after_ref, f32[32,96]{1,0:T(8,128)S(1)} %get-tuple-element.45.weights_ref, ...), custom_call_target="tpu_custom_call" | custom-call | flops 49152000 | bytes 1638400 | tf_op jit(solution)/shard_map/pull_back/pallas_call | solution.py:464
  102.8 3.9 %collective-permute-start.16 = (s32[136,640]{1,0:T(8,128)S(1)}, s32[136,640]{1,0:T(8,128)S(1)}, u32[]{:S(2)}, u32[]{:S(2)}) collective-permute-start(s32[136,640]{1,0:T(8,128)S(1)} %pull_back.1.rest_0_), channel_id=1, source_target_pairs={{0,8},{8,0},{16,24},{24,16},{1,9},{9,1},{17,25},{25,17},{2,10},{10... | collective-permute-start | bytes 1044488 | tf_op jit(solution)/shard_map/ppermute | solution.py:735
  109.1 3.9 %grams.4 = (f32[2,4,32,640]{3,2,1,0:T(8,128)S(1)}, f32[8,256]{1,0:T(8,128)S(1)}) custom-call(s32[4]{0:T(128)S(1)} %xor_multiply_fusion.order_ref, f32[8,256]{1,0:T(8,128)S(1)} %broadcast_in_dim.20.sums_before, f32[8,4,32,640]{3,2,1,0:T(8,128)S(1)} %copy-done.4, f32[8,4,32,640]{3,2,1,0:T(8,128)S(1)} %copy-done.3, s32[136,640]{1,0:T(8,128)S(1)} %pull_back.1.rest_0_), custom_call_target="tpu_custom_call" | custom-call | flops 41943040 | bytes 10485760 | tf_op jit(solution)/shard_map/grams/pallas_call | solution.py:586
  113.1 3.2 %collective-permute-done.16.rest_0_ = s32[136,640]{1,0:T(8,128)S(1)} collective-permute-done((s32[136,640]{1,0:T(8,128)S(1)}, s32[136,640]{1,0:T(8,128)S(1)}, u32[]{:S(2)}, u32[]{:S(2)}) %collective-permute-start.16) | collective-permute-done | bytes 348192 | tf_op jit(solution)/shard_map/ppermute | solution.py:735
  116.2 2.9 %grams.5 = (f32[2,4,32,640]{3,2,1,0:T(8,128)S(1)}, f32[8,256]{1,0:T(8,128)S(1)}) custom-call(s32[4]{0:T(128)S(1)} %xor_multiply_fusion.order_ref, f32[8,256]{1,0:T(8,128)S(1)} %get-tuple-element.35.sums_before, f32[8,4,32,640]{3,2,1,0:T(8,128)S(1)} %copy-done.4, f32[8,4,32,640]{3,2,1,0:T(8,128)S(1)} %copy-done.3, ...), custom_call_target="tpu_custom_call" | custom-call | flops 41943040 | bytes 10485760 | tf_op jit(solution)/shard_map/grams/pallas_call | solution.py:586
  119.1 3.0 %grams.6 = (f32[2,4,32,640]{3,2,1,0:T(8,128)S(1)}, f32[8,256]{1,0:T(8,128)S(1)}) custom-call(s32[4]{0:T(128)S(1)} %xor_multiply_fusion.order_ref, f32[8,256]{1,0:T(8,128)S(1)} %get-tuple-element.37.sums_before, f32[8,4,32,640]{3,2,1,0:T(8,128)S(1)} %copy-done.4, f32[8,4,32,640]{3,2,1,0:T(8,128)S(1)} %copy-done.3, ...), custom_call_target="tpu_custom_call" | custom-call | flops 41943040 | bytes 10485760 | tf_op jit(solution)/shard_map/grams/pallas_call | solution.py:586
  122.1 6.3 %collective-permute-done.18.rest_0_ = s32[136,640]{1,0:T(8,128)S(1)} collective-permute-done((s32[136,640]{1,0:T(8,128)S(1)}, s32[136,640]{1,0:T(8,128)S(1)}, u32[]{:S(2)}, u32[]{:S(2)}) %collective-permute-start.18) | collective-permute-done | bytes 348192 | tf_op jit(solution)/shard_map/ppermute | solution.py:735
  128.4 3.0 %grams.7 = (f32[2,4,32,640]{3,2,1,0:T(8,128)S(1)}, f32[8,256]{1,0:T(8,128)S(1)}) custom-call(s32[4]{0:T(128)S(1)} %xor_multiply_fusion.order_ref, f32[8,256]{1,0:T(8,128)S(1)} %get-tuple-element.39.sums_before, f32[8,4,32,640]{3,2,1,0:T(8,128)S(1)} %copy-done.4, f32[8,4,32,640]{3,2,1,0:T(8,128)S(1)} %copy-done.3, ...), custom_call_target="tpu_custom_call" | custom-call | flops 41943040 | bytes 10485760 | tf_op jit(solution)/shard_map/grams/pallas_call | solution.py:586
  131.4 11.4 %collective-permute-start.19 = (f32[8,256]{1,0:T(8,128)S(1)}, f32[8,256]{1,0:T(8,128)S(1)}, u32[]{:S(2)}, u32[]{:S(2)}) collective-permute-start(f32[8,256]{1,0:T(8,128)S(1)} %get-tuple-element.41), channel_id=1, source_target_pairs={{0,1},{1,0},{2,3},{3,2},{4,5},{5,4},{6,7},{7,6},{8,9},{9,8},{10,11... | collective-permute-start | bytes 24584 | tf_op jit(solution)/shard_map/ppermute | solution.py:735
  151.2 10.7 %update.1 = (f32[8,4,32,640]{3,2,1,0:T(8,128)}, f32[8,4,32,640]{3,2,1,0:T(8,128)}, f32[8,4,32,640]{3,2,1,0:T(8,128)}) custom-call(s32[4]{0:T(128)S(1)} %xor_multiply_fusion.order_ref, f32[8,256]{1,0:T(8,128)S(1)} %add.150.sums_ref, f32[8,4,32,640]{3,2,1,0:T(8,128)S(1)} %copy-done.6, f32[8,4,32,640]{3,2,1,0:T(8,128)S(1)} %copy-done.4, ...), custom_call_target="tpu_custom_call" | custom-call | flops 31457280 | bytes 18350080 | tf_op jit(solution)/shard_map/update/pallas_call | solution.py:714
  (87 shorter events, 42.9 us)
Async XLA Ops:
  8.0 12.9 %collective-permute-start.2 = (s32[136,640]{1,0:T(8,128)S(1)}, s32[136,640]{1,0:T(8,128)S(1)}, u32[]{:S(2)}, u32[]{:S(2)}) collective-permute-start(s32[136,640]{1,0:T(8,128)S(1)} %get-tuple-element.24), channel_id=1, source_target_pairs={{0,1},{1,2},{2,3},{3,4},{4,5},{5,6},{6,7},{8,9},{9,10},{10,11},{11... | collective-permute-start | bytes 1044488 | tf_op jit(solution)/shard_map/ppermute | solution.py:740
  10.3 10.5 %collective-permute-start.3 = (s32[136,640]{1,0:T(8,128)S(1)}, s32[136,640]{1,0:T(8,128)S(1)}, u32[]{:S(2)}, u32[]{:S(2)}) collective-permute-start(s32[136,640]{1,0:T(8,128)S(1)} %get-tuple-element.24), channel_id=1, source_target_pairs={{1,0},{2,1},{3,2},{4,3},{5,4},{6,5},{7,6},{9,8},{10,9},{11,10},{12... | collective-permute-start | bytes 1044488 | tf_op jit(solution)/shard_map/ppermute | solution.py:741
  11.7 4.0 %collective-permute-start = (s32[1,384]{1,0:T(1,128)S(1)}, s32[1,384]{1,0:T(1,128)S(1)}, u32[]{:S(2)}, u32[]{:S(2)}) collective-permute-start(s32[1,384]{1,0:T(1,128)S(1)} %fusion.4), channel_id=1, source_target_pairs={{0,8},{8,0},{16,24},{24,16},{1,9},{9,1},{17,25},{25,17},{2,10},{10... | collective-permute-start | bytes 4616 | tf_op jit(solution)/shard_map/ppermute | solution.py:735
  15.7 4.7 %collective-permute-start.1 = (s32[2,384]{1,0:T(2,128)S(1)}, s32[2,384]{1,0:T(2,128)S(1)}, u32[]{:S(2)}, u32[]{:S(2)}) collective-permute-start(s32[2,384]{1,0:T(2,128)S(1)} %pad_add_fusion.1), channel_id=1, source_target_pairs={{0,16},{8,24},{16,0},{24,8},{1,17},{9,25},{17,1},{25,9},{2,18},{10... | collective-permute-start | bytes 9224 | tf_op jit(solution)/shard_map/ppermute | solution.py:735
  22.8 11.0 %collective-permute-start.4 = (bf16[2,384,128]{2,1,0:T(8,128)(2,1)S(1)}, bf16[2,384,128]{2,1,0:T(8,128)(2,1)S(1)}, u32[]{:S(2)}, u32[]{:S(2)}) collective-permute-start(bf16[2,384,128]{2,1,0:T(8,128)(2,1)S(1)} %get-tuple-element.26), channel_id=1, source_target_pairs={{0,8},{8,0},{16,24},{24,16},{1,9},{9,1},{17,25},{25,17},{2,10},{10... | collective-permute-start | bytes 589832 | tf_op jit(solution)/shard_map/ppermute | solution.py:735
  24.7 17.1 %collective-permute-start.5 = (bf16[2,384,128]{2,1,0:T(8,128)(2,1)S(1)}, bf16[2,384,128]{2,1,0:T(8,128)(2,1)S(1)}, u32[]{:S(2)}, u32[]{:S(2)}) collective-permute-start(bf16[2,384,128]{2,1,0:T(8,128)(2,1)S(1)} %get-tuple-element.27), channel_id=1, source_target_pairs={{0,16},{8,24},{16,0},{24,8},{1,17},{9,25},{17,1},{25,9},{2,18},{10... | collective-permute-start | bytes 589832 | tf_op jit(solution)/shard_map/ppermute | solution.py:735
  27.3 14.5 %collective-permute-start.6 = (bf16[2,384,128]{2,1,0:T(8,128)(2,1)S(1)}, bf16[2,384,128]{2,1,0:T(8,128)(2,1)S(1)}, u32[]{:S(2)}, u32[]{:S(2)}) collective-permute-start(bf16[2,384,128]{2,1,0:T(8,128)(2,1)S(1)} %get-tuple-element.28), channel_id=1, source_target_pairs={{0,24},{8,16},{16,8},{24,0},{1,25},{9,17},{17,9},{25,1},{2,26},{10... | collective-permute-start | bytes 589832 | tf_op jit(solution)/shard_map/ppermute | solution.py:735
  33.0 26.9 %copy-start.7 = (f32[4096]{0:T(1024)S(1)}, f32[4096]{0:T(1024)}, u32[]{:S(2)}) copy-start(f32[4096]{0:T(1024)} %param.16) | copy-start | bytes 49156
  46.6 1.3 collective-permute-start.7
  48.0 6.2 %collective-permute-start.8 = (f32[128,128]{1,0:T(8,128)S(1)}, f32[128,128]{1,0:T(8,128)S(1)}, u32[]{:S(2)}, u32[]{:S(2)}) collective-permute-start(f32[128,128]{1,0:T(8,128)S(1)} %select_add_fusion), channel_id=1, source_target_pairs={{0,2},{1,3},{2,0},{3,1},{4,6},{5,7},{6,4},{7,5},{8,10},{9,11},{10,... | collective-permute-start | bytes 196616 | tf_op jit(solution)/shard_map/ppermute | solution.py:735
  54.2 4.3 %collective-permute-start.9 = (f32[128,128]{1,0:T(8,128)S(1)}, f32[128,128]{1,0:T(8,128)S(1)}, u32[]{:S(2)}, u32[]{:S(2)}) collective-permute-start(f32[128,128]{1,0:T(8,128)S(1)} %add.146), channel_id=1, source_target_pairs={{0,4},{1,5},{2,6},{3,7},{4,0},{5,1},{6,2},{7,3},{8,12},{9,13},{10,... | collective-permute-start | bytes 196616 | tf_op jit(solution)/shard_map/ppermute | solution.py:735
  58.6 1.3 collective-permute-start.10
  67.8 11.9 %collective-permute-start.11 = (s32[392,128]{1,0:T(8,128)S(1)}, s32[392,128]{1,0:T(8,128)S(1)}, u32[]{:S(2)}, u32[]{:S(2)}) collective-permute-start(s32[392,128]{1,0:T(8,128)S(1)} %get-tuple-element.30), channel_id=1, source_target_pairs={{0,8},{8,0},{16,24},{24,16},{1,9},{9,1},{17,25},{25,17},{2,10},{10... | collective-permute-start | bytes 602120 | tf_op jit(solution)/shard_map/ppermute | solution.py:735
  70.7 17.4 %collective-permute-start.12 = (s32[392,128]{1,0:T(8,128)S(1)}, s32[392,128]{1,0:T(8,128)S(1)}, u32[]{:S(2)}, u32[]{:S(2)}) collective-permute-start(s32[392,128]{1,0:T(8,128)S(1)} %get-tuple-element.31), channel_id=1, source_target_pairs={{0,16},{8,24},{16,0},{24,8},{1,17},{9,25},{17,1},{25,9},{2,18},{10... | collective-permute-start | bytes 602120 | tf_op jit(solution)/shard_map/ppermute | solution.py:735
  71.8 16.3 %collective-permute-start.13 = (s32[392,128]{1,0:T(8,128)S(1)}, s32[392,128]{1,0:T(8,128)S(1)}, u32[]{:S(2)}, u32[]{:S(2)}) collective-permute-start(s32[392,128]{1,0:T(8,128)S(1)} %get-tuple-element.32), channel_id=1, source_target_pairs={{0,24},{8,16},{16,8},{24,0},{1,25},{9,17},{17,9},{25,1},{2,26},{10... | collective-permute-start | bytes 602120 | tf_op jit(solution)/shard_map/ppermute | solution.py:735
  90.1 2.8 %collective-permute-start.14 = (s32[136,640]{1,0:T(8,128)S(1)}, s32[136,640]{1,0:T(8,128)S(1)}, u32[]{:S(2)}, u32[]{:S(2)}) collective-permute-start(s32[136,640]{1,0:T(8,128)S(1)} %get-tuple-element.34), channel_id=1, source_target_pairs={{0,1},{1,2},{2,3},{3,4},{4,5},{5,6},{6,7},{8,9},{9,10},{10,11},{11... | collective-permute-start | bytes 1044488 | tf_op jit(solution)/shard_map/ppermute | solution.py:740
  91.4 5.4 %collective-permute-start.15 = (s32[136,640]{1,0:T(8,128)S(1)}, s32[136,640]{1,0:T(8,128)S(1)}, u32[]{:S(2)}, u32[]{:S(2)}) collective-permute-start(s32[136,640]{1,0:T(8,128)S(1)} %get-tuple-element.34), channel_id=1, source_target_pairs={{1,0},{2,1},{3,2},{4,3},{5,4},{6,5},{7,6},{9,8},{10,9},{11,10},{12... | collective-permute-start | bytes 1044488 | tf_op jit(solution)/shard_map/ppermute | solution.py:741
  102.8 13.5 %collective-permute-start.16 = (s32[136,640]{1,0:T(8,128)S(1)}, s32[136,640]{1,0:T(8,128)S(1)}, u32[]{:S(2)}, u32[]{:S(2)}) collective-permute-start(s32[136,640]{1,0:T(8,128)S(1)} %pull_back.1.rest_0_), channel_id=1, source_target_pairs={{0,8},{8,0},{16,24},{24,16},{1,9},{9,1},{17,25},{25,17},{2,10},{10... | collective-permute-start | bytes 1044488 | tf_op jit(solution)/shard_map/ppermute | solution.py:735
  106.7 12.4 %collective-permute-start.17 = (s32[136,640]{1,0:T(8,128)S(1)}, s32[136,640]{1,0:T(8,128)S(1)}, u32[]{:S(2)}, u32[]{:S(2)}) collective-permute-start(s32[136,640]{1,0:T(8,128)S(1)} %pull_back.1.rest_0_), channel_id=1, source_target_pairs={{0,16},{8,24},{16,0},{24,8},{1,17},{9,25},{17,1},{25,9},{2,18},{10... | collective-permute-start | bytes 1044488 | tf_op jit(solution)/shard_map/ppermute | solution.py:735
  107.7 20.6 %collective-permute-start.18 = (s32[136,640]{1,0:T(8,128)S(1)}, s32[136,640]{1,0:T(8,128)S(1)}, u32[]{:S(2)}, u32[]{:S(2)}) collective-permute-start(s32[136,640]{1,0:T(8,128)S(1)} %pull_back.1.rest_0_), channel_id=1, source_target_pairs={{0,24},{8,16},{16,8},{24,0},{1,25},{9,17},{17,9},{25,1},{2,26},{10... | collective-permute-start | bytes 1044488 | tf_op jit(solution)/shard_map/ppermute | solution.py:735
  128.4 22.9 %copy-start.6 = (f32[8,4,32,640]{3,2,1,0:T(8,128)S(1)}, f32[8,4,32,640]{3,2,1,0:T(8,128)}, u32[]{:S(2)}) copy-start(f32[8,4,32,640]{3,2,1,0:T(8,128)} %solution_ref.1) | copy-start | bytes 7864324
  131.4 12.2 %collective-permute-start.19 = (f32[8,256]{1,0:T(8,128)S(1)}, f32[8,256]{1,0:T(8,128)S(1)}, u32[]{:S(2)}, u32[]{:S(2)}) collective-permute-start(f32[8,256]{1,0:T(8,128)S(1)} %get-tuple-element.41), channel_id=1, source_target_pairs={{0,1},{1,0},{2,3},{3,2},{4,5},{5,4},{6,7},{7,6},{8,9},{9,8},{10,11... | collective-permute-start | bytes 24584 | tf_op jit(solution)/shard_map/ppermute | solution.py:735
  143.6 3.9 %collective-permute-start.20 = (f32[8,256]{1,0:T(8,128)S(1)}, f32[8,256]{1,0:T(8,128)S(1)}, u32[]{:S(2)}, u32[]{:S(2)}) collective-permute-start(f32[8,256]{1,0:T(8,128)S(1)} %add.148), channel_id=1, source_target_pairs={{0,2},{1,3},{2,0},{3,1},{4,6},{5,7},{6,4},{7,5},{8,10},{9,11},{10,... | collective-permute-start | bytes 24584 | tf_op jit(solution)/shard_map/ppermute | solution.py:735
  147.5 3.8 %collective-permute-start.21 = (f32[8,256]{1,0:T(8,128)S(1)}, f32[8,256]{1,0:T(8,128)S(1)}, u32[]{:S(2)}, u32[]{:S(2)}) collective-permute-start(f32[8,256]{1,0:T(8,128)S(1)} %add.149), channel_id=1, source_target_pairs={{0,4},{1,5},{2,6},{3,7},{4,0},{5,1},{6,2},{7,3},{8,12},{9,13},{10,... | collective-permute-start | bytes 24584 | tf_op jit(solution)/shard_map/ppermute | solution.py:735
  (10 other events, 105.0 us)

commit v3 on v2

--- a/solution.py
+++ b/solution.py
@@ -11,7 +11,8 @@
 LANES = 128
 CHUNK = 96
 COPIES = 12
-GROUP_RHS = 2
+STREAM_MIB = 40
+BACK_GROUPS = 1
 SUBLANES = 8
 MIB = 1024 * 1024
 HIGHEST = lax.Precision.HIGHEST
@@ -155,36 +156,24 @@
     return lax.fori_loop(0, rows // SUBLANES, one_group, (zero,) * rhs)
 
 
-def spread_lon_kernel(_, field_ref, count_ref, out_ref, word_ref):
+def spread_lon_kernel(field_ref, count_ref, out_ref, word_ref):
     pack_field(out_ref, word_ref, lon_field(field_ref, count_ref, out_ref))
 
 
-def spread_lon(direction, first, rhs, counts):
-    _, weeks, rows, lon = direction.shape
-    words = words_of(rhs, weeks, rows)
+def spread_lon(field, counts):
+    rhs, weeks, rows, lon = field.shape
     return pl.pallas_call(
         spread_lon_kernel,
-        grid_spec=pltpu.PrefetchScalarGridSpec(
-            num_scalar_prefetch=1,
-            grid=(1,),
-            in_specs=[
-                pl.BlockSpec(
-                    (rhs, weeks, rows, lon),
-                    lambda _, first: (first[0], 0, 0, 0),
-                    pipeline_mode=pl.Buffered(1),
-                ),
-                whole((rows, lon)),
-            ],
-            out_specs=[whole((rhs, weeks, rows, lon)), whole((words, lon))],
-        ),
+        in_specs=in_vmem(2),
+        out_specs=in_vmem(2),
         out_shape=[
-            jax.ShapeDtypeStruct((rhs, weeks, rows, lon), jnp.float32),
-            jax.ShapeDtypeStruct((words, lon), jnp.int32),
+            jax.ShapeDtypeStruct(field.shape, jnp.float32),
+            jax.ShapeDtypeStruct((words_of(rhs, weeks, rows), lon), jnp.int32),
         ],
         compiler_params=params(6),
-        cost_estimate=cost(rhs * weeks * rows * lon * 100, rhs * weeks * rows * lon * 10),
+        cost_estimate=cost(field.size * 100, field.size * 10),
         name="spread_lon",
-    )(first, direction, counts)
+    )(field, counts)
 
 
 def lat_mix(weights_ref, window_ref, k, week, before_ref, own_ref, after_ref, scales):
@@ -281,7 +270,7 @@
         out_specs=pl.BlockSpec(memory_space=pltpu.VMEM),
         out_shape=jax.ShapeDtypeStruct(blocks.shape, blocks.dtype),
         scratch_shapes=[pltpu.SemaphoreType.DMA((parts,))],
-        compiler_params=params(13),
+        compiler_params=params(STREAM_MIB),
         cost_estimate=cost(0, blocks.size * 4),
         name="preload",
     )(after, blocks)
@@ -476,24 +465,17 @@
     )(own, before, after, weights, counts)
 
 
-PAIRS = 16
-
-
-def gram_kernel(with_old, count, rhs, order_ref, sums_before, residual_ref, direction_ref, *rest):
+def gram_kernel(with_old, places, count, rhs, order_ref, sums_before, residual_ref, direction_ref, *rest):
     words, rest = rest[:count], rest[count:]
     news, gram_ref, sums_ref = rest[-count - 2 : -2], rest[-2], rest[-1]
     olds = rest[: -count - 2]
     rhs_count, weeks, rows, lon = direction_ref.shape
     half = rows // 2
     body = words[0].shape[0] - SUBLANES
-    first = len(olds)
-
-    def natural(place):
-        return order_ref[place // rhs] + place % rhs
-
-    for word_ref, new_ref, slot in zip(words, news, range(first, first + count)):
+    old_places, new_places = places[: len(olds)], places[len(olds) :]
+    for word_ref, new_ref, place in zip(words, news, new_places):
         for k in range(rhs):
-            index = natural(slot * rhs + k)
+            index = order_ref[place] + k
             scale = word_scale(word_ref, body, k)
 
             def one_week(week, carry):
@@ -512,84 +494,70 @@
     sums_ref[...] = jnp.zeros_like(sums_ref)
     row_groups = rows // SUBLANES
 
-    def tile(index, lefts, rights, mirror):
-        def one_group(step, sums):
-            week = step // row_groups
-            at = pl.multiple_of((step % row_groups) * SUBLANES, SUBLANES)
+    def tile(blocks):
+        def one_week(week, sums):
             sums = list(sums)
-            for lane in range(0, lon, LANES):
-                spot = (week, pl.ds(at, SUBLANES), slice(lane, lane + LANES))
-                left = [ref[(k, *spot)] for ref, k, _ in lefts]
-                right = [ref[(k, *spot)] for ref, k, _ in rights]
-                for a in range(len(lefts)):
-                    for b in range(len(rights)):
-                        place = a * len(rights) + b
-                        sums[place] = sums[place] + left[a] * right[b]
+            for row in range(0, rows, SUBLANES):
+                for lane in range(0, lon, LANES):
+                    spot = (week, slice(row, row + SUBLANES), slice(lane, lane + LANES))
+                    place = 0
+                    for _, lefts, rights, _ in blocks:
+                        right = [ref[(k, *spot)] for ref, k, _ in rights]
+                        for ref, k, _ in lefts:
+                            left = ref[(k, *spot)]
+                            for b in range(len(rights)):
+                                sums[place] = sums[place] + left * right[b]
+                                place += 1
             return tuple(sums)
 
         zero = jnp.zeros((SUBLANES, LANES), jnp.float32)
-        sums = lax.fori_loop(
-            0, weeks * row_groups, one_group, (zero,) * (len(lefts) * len(rights))
-        )
-        for a, (_, _, row) in enumerate(lefts):
-            for b, (_, _, column) in enumerate(rights):
-                for row_at, column_at in ((row, column), (column, row))[: 1 + mirror]:
-                    at = ((index * rhs_count + row_at) * rhs_count + column_at) * SUBLANES
-                    at = pl.multiple_of(at, SUBLANES)
-                    sums_ref[pl.ds(at, SUBLANES), :] = sums[a * len(rights) + b]
-
-    def listed(refs, slot):
+        total = sum(len(lefts) * len(rights) for _, lefts, rights, _ in blocks)
+        sums = list(lax.fori_loop(0, weeks, one_week, (zero,) * total))
+        for index, lefts, rights, mirror in blocks:
+            for _, _, row in lefts:
+                for _, _, column in rights:
+                    lanes = jnp.sum(sums.pop(0), axis=0, keepdims=True)
+                    for row_at, column_at in ((row, column), (column, row))[: 1 + mirror]:
+                        at = (index * rhs_count + row_at) * rhs_count + column_at
+                        sums_ref[pl.ds(at, 1), :] = lanes
+
+    def listed(refs, places):
         return [
-            (ref, k, natural((slot + place) * rhs + k))
-            for place, ref in enumerate(refs)
-            for k in range(rhs)
+            (ref, k, order_ref[place] + k) for ref, place in zip(refs, places) for k in range(rhs)
         ]
-
-    def tiles(index, lefts, rights, mirror=False):
-        wide = min(len(rights), 4)
-        tall = PAIRS // wide
-        for a in range(0, len(lefts), tall):
-            for b in range(0, len(rights), wide):
-                if lefts is rights and b + wide <= a:
-                    continue
-                tile(index, lefts[a : a + tall], rights[b : b + wide], mirror)
 
     residuals = [(residual_ref, k, k) for k in range(rhs_count)]
     directions = [(direction_ref, k, k) for k in range(rhs_count)]
-    images = listed(news, first)
+    images = listed(news, new_places)
     if with_old:
-        tiles(0, residuals, residuals, True)
-    tiles(1, directions, images)
-    tiles(2, residuals, images)
-    tiles(3, images, images, True)
-    if olds:
-        tiles(3, listed(olds, 0), images, True)
-
-    total = sums_ref.shape[0] // SUBLANES
-    lanes = sums_ref[pl.ds(0, total, stride=SUBLANES), :]
-    for line in range(1, SUBLANES):
-        lanes = lanes + sums_ref[pl.ds(line, total, stride=SUBLANES), :]
+        for a in range(rhs_count):
+            tile([(0, residuals[a : a + 1], residuals[a:], True)])
+    for b in range(0, len(images), 2):
+        right = images[b : b + 2]
+        left = images[: b + len(right)] + listed(olds, old_places)
+        tile([(1, directions, right, False), (2, residuals, right, False), (3, left, right, True)])
+
     gram_ref[...] = sums_before[...] + lax.dot_general(
         jnp.ones((SUBLANES, LANES), jnp.float32),
-        lanes,
+        sums_ref[...],
         (((1,), (1,)), ((), ())),
         precision=HIGHEST,
         preferred_element_type=jnp.float32,
     )
 
 
-def grams(order, sums, residual, direction, words, olds, with_old):
+def grams(order, places, sums, residual, direction, words, olds, with_old):
     rhs_count, weeks, rows, lon = direction.shape
     total = 4 * rhs_count**2
     rhs = (words[0].shape[0] - SUBLANES) * 2 // (weeks * rows)
     count = len(words)
     found = pl.pallas_call(
-        functools.partial(gram_kernel, with_old, count, rhs),
+        functools.partial(gram_kernel, with_old, places, count, rhs),
         in_specs=[pl.BlockSpec(memory_space=pltpu.SMEM)] + in_vmem(3 + count + len(olds)),
         out_specs=in_vmem(count + 1),
         out_shape=[jax.ShapeDtypeStruct((rhs, weeks, rows, lon), jnp.float32)] * count
         + [jax.ShapeDtypeStruct((SUBLANES, total), jnp.float32)],
-        scratch_shapes=[pltpu.VMEM((total * SUBLANES, LANES), jnp.float32)],
+        scratch_shapes=[pltpu.VMEM((total, LANES), jnp.float32)],
         compiler_params=params(14),
         cost_estimate=cost(8 * rhs_count * direction.size, 16 * direction.size),
         name="grams",
@@ -610,16 +578,19 @@
     return jnp.concatenate([value, rest], axis=0).T[:SUBLANES]
 
 
-def small_solve(matrix, right):
+def small_solves(systems):
     line = lax.broadcasted_iota(jnp.int32, (SUBLANES, LANES), 0)
-    both = matrix + pltpu.roll(right, SUBLANES, 1)
+    lane = lax.broadcasted_iota(jnp.int32, (SUBLANES, LANES), 1)
+    states = [matrix + pltpu.roll(right, SUBLANES, 1) for matrix, right in systems]
     for j in range(SUBLANES):
-        column = jnp.broadcast_to(both[:, j : j + 1], (SUBLANES, LANES))
-        pivot = jnp.broadcast_to(both[j : j + 1, :], (SUBLANES, LANES))
-        scaled = pivot / jnp.broadcast_to(both[j : j + 1, j : j + 1], (SUBLANES, LANES))
-        both = jnp.where(line == j, scaled, both - column * scaled)
-    lane = lax.broadcasted_iota(jnp.int32, (SUBLANES, LANES), 1)
-    return jnp.where(lane < SUBLANES, pltpu.roll(both, LANES - SUBLANES, 1), 0.0)
+        for index, both in enumerate(states):
+            column = jnp.broadcast_to(both[:, j : j + 1], (SUBLANES, LANES))
+            pivot = jnp.broadcast_to(both[j : j + 1, :], (SUBLANES, LANES))
+            scaled = pivot / jnp.broadcast_to(both[j : j + 1, j : j + 1], (SUBLANES, LANES))
+            states[index] = jnp.where(line == j, scaled, both - column * scaled)
+    return [
+        jnp.where(lane < SUBLANES, pltpu.roll(both, LANES - SUBLANES, 1), 0.0) for both in states
+    ]
 
 
 def solve_steps(sums_ref, coef_ref):
@@ -638,11 +609,13 @@
 
     gram_old, curvature, mixed, gram_image = [matrix(index) for index in range(4)]
     curvature = 0.5 * (curvature + small_transpose(curvature))
-    step = small_solve(curvature, gram_old)
+    diagonal = lax.broadcasted_iota(jnp.int32, (size, LANES), 0)
+    identity = jnp.where(diagonal == lax.broadcasted_iota(jnp.int32, (size, LANES), 1), 1.0, 0.0)
+    step, old_inverse = small_solves([(curvature, gram_old), (gram_old, identity)])
     cross = small_product(mixed, step)
     both = small_product(small_transpose(step), small_product(gram_image, step))
     gram_new = gram_old - cross - small_transpose(cross) + both
-    turn = small_solve(gram_old, gram_new)
+    turn = small_product(old_inverse, gram_new)
     for index, matrix in enumerate((step, turn)):
         for b in range(size):
             for a in range(size):
@@ -735,6 +708,10 @@
     return lax.ppermute(value, axis, [(i, i ^ by) for i in range(lax.axis_size(axis))])
 
 
+def far_first(size):
+    return [1 << bit for bit in reversed(range(size.bit_length() - 1))]
+
+
 def neighbours(value, axis):
     size = lax.axis_size(axis)
     before = lax.ppermute(value, axis, [(i, i + 1) for i in range(size - 1)])
@@ -745,26 +722,12 @@
 def summed_over(value, axis):
     size = lax.axis_size(axis)
     reach = 1
+    before = value
     while reach < size:
+        before = value
         value = value + crossed(value, axis, reach)
         reach *= 2
-    return value
-
-
-def summed_in_halves(value, axis):
-    size = lax.axis_size(axis)
-    if size < 4:
-        return summed_over(value, axis)
-    half = value.shape[0] // 2
-    low, high = value[:half], value[half:]
-    even = lax.axis_index(axis) % 2 == 0
-    mine = jnp.where(even, low, high) + crossed(jnp.where(even, high, low), axis, 1)
-    reach = 2
-    while reach < size:
-        mine = mine + crossed(mine, axis, reach)
-        reach *= 2
-    other = crossed(mine, axis, 1)
-    return jnp.concatenate([jnp.where(even, mine, other), jnp.where(even, other, mine)], axis=0)
+    return value, before
 
 
 def lat_windows(lat_width, band, rows):
@@ -818,60 +781,72 @@
     parts = lon // edge
     cols = weeks * rows * parts
 
-    groups = rhs // GROUP_RHS if rhs % GROUP_RHS == 0 else 1
+    groups = chunk_of(rhs, BACK_GROUPS)
     each = rhs // groups
-    first = (slab * groups).astype(jnp.int32)
-    others = slab ^ jnp.arange(slots, dtype=jnp.int32)
-    order = others * rhs
+    order = (slab ^ jnp.arange(slots, dtype=jnp.int32)) * rhs
     own_width = lax.dynamic_slice_in_dim(lon_width, band * rows, rows)
     counts = jnp.broadcast_to(own_width[:, None] + 1, (rows, lon))
 
     line, part = col_list // parts, col_list % parts
     place = ((line // rows) * parts + part) * rows + line % rows
-    places = place[None]
-    reach = 1
-    while reach < slots:
-        places = jnp.concatenate([places, crossed(places, "obs", reach)], axis=0)
-        reach *= 2
-
-    lon_own, halos = [], []
-    for group in range(groups):
-        own, words = spread_lon(direction, (first + group).reshape(1), each, counts)
-        lon_own.append(own)
-        halos.append(neighbours(words, "lat"))
-
+    places = jnp.stack([crossed(place, "obs", d) for d in range(slots)])
+
+    lon_own, words = spread_lon(
+        lax.dynamic_slice_in_dim(direction, slab * rhs, rhs, 0), counts
+    )
+    halo = neighbours(words, "lat")
     hot = (places[:, :, None] == jnp.arange(cols)[None, None, :]).astype(jnp.bfloat16)
     hot_turned = (jnp.arange(cols)[:, None] == places.reshape(1, -1)).astype(jnp.bfloat16)
     lat_spread, lat_pulled = lat_windows(lat_width, band, rows)
 
-    cells = [[None] * groups for _ in range(slots)]
-    for group in range(groups):
-        picks = spread_lat(lon_own[group], *halos[group], lat_spread, hot)
-        for d in range(slots):
-            cells[d][group] = crossed(picks[d], "obs", d)
-    cells = [cell for slot_cells in cells for cell in slot_cells]
-    near_blocks = preload(blocks, cells[0])
-    sums = summed_in_halves(forward(row_list, scales, near_blocks, cells, row_blocks), "lat")
+    picks = spread_lat(lon_own, *halo, lat_spread, hot)
+    cells = [crossed(picks[d], "obs", d) for d in range(slots)]
+    near_blocks = preload(blocks, picks[0])
+    sums, partial = summed_over(forward(row_list, scales, near_blocks, cells, row_blocks), "lat")
+    near_blocks = preload(blocks, partial)
     weighted = sums.reshape(row_blocks, slots * rhs, edge) * obs_weight.reshape(row_blocks, 1, edge)
     terms = adjoint_terms(
         row_list, scales, near_blocks, weighted.reshape(-1, edge), slots * groups, each
     )
-    images = [[None] * groups for _ in range(slots)]
+    sent = [[crossed(terms[d * groups + g], "obs", d) for d in range(slots)] for g in range(groups)]
+    own = []
     for group in range(groups):
-        sent = [crossed(terms[d * groups + group], "obs", d) for d in range(slots)]
-        field, words = gather_cells(hot_turned, sent, each, weeks, rows, lon)
-        words = pull_back(field, *neighbours(words, "lat"), lat_pulled, counts)
-        for d in range(slots):
-            images[d][group] = crossed(words, "obs", d)
+        field, words = gather_cells(hot_turned, sent[group], each, weeks, rows, lon)
+        own.append(pull_back(field, *neighbours(words, "lat"), lat_pulled, counts))
 
     starts = (order[:, None] + jnp.arange(groups, dtype=jnp.int32) * each).reshape(-1)
     products = jnp.zeros((SUBLANES, 4 * rhs_count**2), jnp.float32)
-    found = []
-    for d in range(slots):
-        new, products = grams(starts, products, residual, direction, images[d], found, d == 0)
-        found += new
-    products = summed_over(products, "lat")
-    return tuple(update(starts, products, solution, residual, direction, found))
+    done, places, found = {}, (), []
+
+    def add_products(words, slot, group):
+        nonlocal products, places
+        places += (slot * groups + group,)
+        new, products = grams(
+            starts, places, products, residual, direction, [words], found, slot == group == 0
+        )
+        found.extend(new)
+        done[slot, group] = new[0]
+
+    arrived = [{0: words} for words in own]
+    for group in range(groups):
+        for reach in far_first(slots):
+            arrived[group][reach] = crossed(own[group], "obs", reach)
+        add_products(own[group], 0, group)
+    for group in range(groups):
+        near = [bits for bits in arrived[group] if bits == 1]
+        for bits in near:
+            add_products(arrived[group][bits], bits, group)
+    for reach in far_first(slots)[1:]:
+        for group in range(groups):
+            for bits in [bits for bits in arrived[group] if bits > reach and not bits % (2 * reach)]:
+                words, _ = lax.optimization_barrier((arrived[group][bits], done[1, group]))
+                arrived[group][bits | reach] = crossed(words, "obs", reach)
+    for bits in range(2, slots):
+        for group in range(groups):
+            add_products(arrived[group][bits], bits, group)
+    products, _ = summed_over(products, "lat")
+    images = [done[slot, group] for slot in range(slots) for group in range(groups)]
+    return tuple(update(starts, products, solution, residual, direction, images))
 
 
 def solution(mesh):

time: 165 us -> 157 us (0.952); the launches traced: 162 us -> 157 us
  local copies, waits for them, and re-layouts: 11.3 us -> 1.49 us
  starting transfers between devices: 49.1 us -> 45.5 us
  Pallas kernels: 47 us -> 50.5 us
  other arithmetic: 2.15 us -> 4.94 us
  waiting for transfers between devices: 51.4 us -> 53.5 us
    unnamed x24 -> x12, local copies, waits for them, and re-layouts: 10.9 us -> 0.03 us
    pallas_call x1 -> x2, Pallas kernels: 0.97 us -> 9.41 us  [preload(): pl.pallas_call(preload_kernel, in_specs=[pl.BlockSpec(memory_space=pl.ANY...]
    pallas_call x5, Pallas kernels: 17.5 us -> 13.5 us  [the longest x4 8.74 us: grams(): pl.pallas_call(functools.partial(gram_kernel, with_old, places, count, rh...]
    ppermute x18, starting transfers between devices: 42.6 us -> 39 us  [crossed(): lax.ppermute(value, axis, [(i, i ^ by) for i in range(lax.axis_size(axis))])]
    ppermute x18, waiting for transfers between devices: 47.5 us -> 50.9 us  [crossed(): lax.ppermute(value, axis, [(i, i ^ by) for i in range(lax.axis_size(axis))])]
  transfers between devices with their start and end apart: 22 -> 22, of which waited for: 16 -> 15; matrix products, arithmetic and copies ran while one was open for 1% -> 3% of each run, Pallas kernels for 7% -> 10%
where the time goes in v3:
time: 157 us
  waiting for transfers between devices  53.5 us (34%)
  Pallas kernels  50.5 us (32%)
  starting transfers between devices  45.5 us (29%)
  other arithmetic  4.94 us (3%)
    ppermute x18, waiting for transfers between devices, crossed(): lax.ppermute(value, axis, [(i, i ^ by) for i in range(lax.axis_size(axis))])  50.9 us
    ppermute x18, starting transfers between devices, crossed(): lax.ppermute(value, axis, [(i, i ^ by) for i in range(lax.axis_size(axis))])  39 us
    pallas_call x1, Pallas kernels, update(): pl.pallas_call(update_kernel, grid_spec=pltpu.PrefetchScalarGridSpec(num_...  9.76 us
    pallas_call x2, Pallas kernels, preload(): pl.pallas_call(preload_kernel, in_specs=[pl.BlockSpec(memory_space=pl.ANY...  9.41 us
    pallas_call x4, Pallas kernels, grams(): pl.pallas_call(functools.partial(gram_kernel, with_old, places, count, rh...  8.74 us
    pallas_call x1, Pallas kernels, pull_back(): pl.pallas_call(pull_back_kernel, in_specs=in_vmem(5), out_specs=pl.BlockS...  5.93 us
    pallas_call x1, Pallas kernels, forward(): pl.pallas_call(forward_kernel, in_specs=[pl.BlockSpec(memory_space=pltpu....  4.76 us
    pallas_call x1, Pallas kernels, spread_lon(): pl.pallas_call(spread_lon_kernel, in_specs=in_vmem(2), out_specs=in_vmem(...  4.72 us
  transfers between devices with their start and end apart: 22, of which 15 were waited for; matrix products, arithmetic and copies ran while one was open for 3% of the time, Pallas kernels for 10%

profile of v3, /device:TPU:0, one launch (start us, length us, event | category | flops | bytes accessed | tf_op | source)
XLA Modules:
  0.0 156.9 jit_solution(11651890112915493783)
XLA Ops:
  2.6 4.7 %spread_lon.1 = (f32[2,4,32,640]{3,2,1,0:T(8,128)S(1)}, s32[136,640]{1,0:T(8,128)S(1)}) custom-call(f32[2,4,32,640]{3,2,1,0:T(8,128)S(1)} %constant_dynamic-slice_fusion.field_ref, s32[32,640]{1,0:T(8,128)S(1)} %broadcast_in_dim.21.count_ref), custom_call_target="tpu_custom_call" | custom-call | flops 16384000 | bytes 1638400 | tf_op jit(solution)/shard_map/spread_lon/pallas_call | solution.py:165
  15.6 2.6 %collective-permute-start.1 = (s32[384]{0:T(512)S(1)}, s32[384]{0:T(512)S(1)}, u32[]{:S(2)}, u32[]{:S(2)}) collective-permute-start(s32[384]{0:T(512)S(1)} %fusion.6), channel_id=1, source_target_pairs={{0,16},{8,24},{16,0},{24,8},{1,17},{9,25},{17,1},{25,9},{2,18},{10... | collective-permute-start | bytes 4616 | tf_op jit(solution)/shard_map/ppermute | solution.py:708
  20.1 3.5 %collective-permute-done.2 = s32[384]{0:T(512)S(1)} collective-permute-done((s32[384]{0:T(512)S(1)}, s32[384]{0:T(512)S(1)}, u32[]{:S(2)}, u32[]{:S(2)}) %collective-permute-start.2) | collective-permute-done | bytes 1568 | tf_op jit(solution)/shard_map/ppermute | solution.py:708
  26.6 3.8 %collective-permute-start.7 = (bf16[2,384,128]{2,1,0:T(8,128)(2,1)S(1)}, bf16[2,384,128]{2,1,0:T(8,128)(2,1)S(1)}, u32[]{:S(2)}, u32[]{:S(2)}) collective-permute-start(bf16[2,384,128]{2,1,0:T(8,128)(2,1)S(1)} %get-tuple-element.29), channel_id=1, source_target_pairs={{0,24},{8,16},{16,8},{24,0},{1,25},{9,17},{17,9},{25,1},{2,26},{10... | collective-permute-start | bytes 589832 | tf_op jit(solution)/shard_map/ppermute | solution.py:708
  30.5 4.7 %preload.2.blocks_ref = bf16[384,128,128]{2,1,0:T(8,128)(2,1)S(1)} custom-call(bf16[2,384,128]{2,1,0:T(8,128)(2,1)S(1)} %get-tuple-element.26.after_ref.rest_0_, bf16[384,128,128]{2,1,0:T(8,128)(2,1)} %bitcast.21), custom_call_target="tpu_custom_call" | custom-call | bytes 25165824 | tf_op jit(solution)/shard_map/preload/pallas_call | solution.py:267
  35.7 7.6 %collective-permute-done.6.rest_2_ = bf16[2,384,128]{2,1,0:T(8,128)(2,1)S(1)} collective-permute-done((bf16[2,384,128]{2,1,0:T(8,128)(2,1)S(1)}, bf16[2,384,128]{2,1,0:T(8,128)(2,1)S(1)}, u32[]{:S(2)}, u32[]{:S(2)}) %collective-permute-start.6) | collective-permute-done | bytes 196640 | tf_op jit(solution)/shard_map/ppermute | solution.py:708
  43.3 4.8 %forward.1 = f32[256,128]{1,0:T(8,128)S(1)} custom-call(s32[384]{0:T(512)S(1)} %reduce.3.row_ref, f32[384]{0:T(512)S(1)} %exponential_reduce_fusion.scale_ref, bf16[384,128,128]{2,1,0:T(8,128)(2,1)S(1)} %preload.2.blocks_ref, bf16[2,384,128]{2,1,0:T(8,128)(2,1)S(1)} %get-tuple-element.26.after_ref.rest_0_, ...), custom_call_target="tpu_custom_call" | custom-call | flops 100663296 | bytes 12582912 | tf_op jit(solution)/shard_map/forward/pallas_call | solution.py:315
  49.5 3.2 %collective-permute-start.9 = (f32[256,128]{1,0:T(8,128)S(1)}, f32[256,128]{1,0:T(8,128)S(1)}, u32[]{:S(2)}, u32[]{:S(2)}) collective-permute-start(f32[256,128]{1,0:T(8,128)S(1)} %add.156), channel_id=1, source_target_pairs={{0,2},{1,3},{2,0},{3,1},{4,6},{5,7},{6,4},{7,5},{8,10},{9,11},{10,... | collective-permute-start | bytes 393224 | tf_op jit(solution)/shard_map/ppermute | solution.py:708
  52.7 3.8 %collective-permute-done.9 = f32[256,128]{1,0:T(8,128)S(1)} collective-permute-done((f32[256,128]{1,0:T(8,128)S(1)}, f32[256,128]{1,0:T(8,128)S(1)}, u32[]{:S(2)}, u32[]{:S(2)}) %collective-permute-start.9) | collective-permute-done | bytes 131104 | tf_op jit(solution)/shard_map/ppermute | solution.py:708
  58.5 4.7 %preload.3.blocks_ref = bf16[384,128,128]{2,1,0:T(8,128)(2,1)S(1)} custom-call(f32[256,128]{1,0:T(8,128)S(1)} %add.157.after_ref, bf16[384,128,128]{2,1,0:T(8,128)(2,1)} %bitcast.22), custom_call_target="tpu_custom_call" | custom-call | bytes 25165824 | tf_op jit(solution)/shard_map/preload/pallas_call | solution.py:267
  63.3 3.3 %adjoint.1 = (s32[392,128]{1,0:T(8,128)S(1)}, s32[392,128]{1,0:T(8,128)S(1)}, s32[392,128]{1,0:T(8,128)S(1)}, s32[392,128]{1,0:T(8,128)S(1)}) custom-call(s32[384]{0:T(512)S(1)} %reduce.3.row_ref, f32[384]{0:T(512)S(1)} %exponential_reduce_fusion.scale_ref, bf16[384,128,128]{2,1,0:T(8,128)(2,1)S(1)} %preload.3.blocks_ref, ...), custom_call_target="tpu_custom_call" | custom-call | flops 100663296 | bytes 12582912 | tf_op jit(solution)/shard_map/adjoint/pallas_call | solution.py:366
  66.6 2.7 %collective-permute-start.11 = (s32[392,128]{1,0:T(8,128)S(1)}, s32[392,128]{1,0:T(8,128)S(1)}, u32[]{:S(2)}, u32[]{:S(2)}) collective-permute-start(s32[392,128]{1,0:T(8,128)S(1)} %get-tuple-element.31), channel_id=1, source_target_pairs={{0,8},{8,0},{16,24},{24,16},{1,9},{9,1},{17,25},{25,17},{2,10},{10... | collective-permute-start | bytes 602120 | tf_op jit(solution)/shard_map/ppermute | solution.py:708
  72.4 3.9 %collective-permute-done.11.rest_1_ = s32[392,128]{1,0:T(8,128)S(1)} collective-permute-done((s32[392,128]{1,0:T(8,128)S(1)}, s32[392,128]{1,0:T(8,128)S(1)}, u32[]{:S(2)}, u32[]{:S(2)}) %collective-permute-start.11) | collective-permute-done | bytes 200736 | tf_op jit(solution)/shard_map/ppermute | solution.py:708
  76.2 9.9 %collective-permute-done.12.rest_2_ = s32[392,128]{1,0:T(8,128)S(1)} collective-permute-done((s32[392,128]{1,0:T(8,128)S(1)}, s32[392,128]{1,0:T(8,128)S(1)}, u32[]{:S(2)}, u32[]{:S(2)}) %collective-permute-start.12) | collective-permute-done | bytes 200736 | tf_op jit(solution)/shard_map/ppermute | solution.py:708
  91.0 2.7 %collective-permute-done.15.after_ref = s32[136,640]{1,0:T(8,128)S(1)} collective-permute-done((s32[136,640]{1,0:T(8,128)S(1)}, s32[136,640]{1,0:T(8,128)S(1)}, u32[]{:S(2)}, u32[]{:S(2)}) %collective-permute-start.15) | collective-permute-done | bytes 348192 | tf_op jit(solution)/shard_map/ppermute | solution.py:718
  93.7 5.9 %pull_back.1.rest_0_ = s32[136,640]{1,0:T(8,128)S(1)} custom-call(f32[2,4,32,640]{3,2,1,0:T(8,128)S(1)} %get-tuple-element.34.own_ref, s32[136,640]{1,0:T(8,128)S(1)} %collective-permute-done.14.before_ref, s32[136,640]{1,0:T(8,128)S(1)} %collective-permute-done.15.after_ref, f32[32,96]{1,0:T(8,128)S(1)} %get-tuple-element.47.weights_ref, ...), custom_call_target="tpu_custom_call" | custom-call | flops 49152000 | bytes 1638400 | tf_op jit(solution)/shard_map/pull_back/pallas_call | solution.py:453
  99.6 3.3 %collective-permute-start.16 = (s32[136,640]{1,0:T(8,128)S(1)}, s32[136,640]{1,0:T(8,128)S(1)}, u32[]{:S(2)}, u32[]{:S(2)}) collective-permute-start(s32[136,640]{1,0:T(8,128)S(1)} %pull_back.1.rest_0_), channel_id=1, source_target_pairs={{0,8},{8,0},{16,24},{24,16},{1,9},{9,1},{17,25},{25,17},{2,10},{10... | collective-permute-start | bytes 1044488 | tf_op jit(solution)/shard_map/ppermute | solution.py:708
  102.9 2.9 %grams.4 = (f32[2,4,32,640]{3,2,1,0:T(8,128)S(1)}, f32[8,256]{1,0:T(8,128)S(1)}) custom-call(s32[4]{0:T(128)S(1)} %xor_multiply_fusion.order_ref, f32[8,256]{1,0:T(8,128)S(1)} %broadcast_in_dim.20.sums_before, f32[8,4,32,640]{3,2,1,0:T(8,128)S(1)} %copy-done.1, f32[8,4,32,640]{3,2,1,0:T(8,128)S(1)} %copy-done, s32[136,640]{1,0:T(8,128)S(1)} %pull_back.1.rest_0_), custom_call_target="tpu_custom_call" | custom-call | flops 41943040 | bytes 10485760 | tf_op jit(solution)/shard_map/grams/pallas_call | solution.py:554
  105.8 4.6 %collective-permute-done.16.rest_0_ = s32[136,640]{1,0:T(8,128)S(1)} collective-permute-done((s32[136,640]{1,0:T(8,128)S(1)}, s32[136,640]{1,0:T(8,128)S(1)}, u32[]{:S(2)}, u32[]{:S(2)}) %collective-permute-start.16) | collective-permute-done | bytes 348192 | tf_op jit(solution)/shard_map/ppermute | solution.py:708
  112.3 3.6 %collective-permute-done.17.rest_0_ = s32[136,640]{1,0:T(8,128)S(1)} collective-permute-done((s32[136,640]{1,0:T(8,128)S(1)}, s32[136,640]{1,0:T(8,128)S(1)}, u32[]{:S(2)}, u32[]{:S(2)}) %collective-permute-start.17) | collective-permute-done | bytes 348192 | tf_op jit(solution)/shard_map/ppermute | solution.py:708
  117.8 6.8 %collective-permute-done.18.rest_0_ = s32[136,640]{1,0:T(8,128)S(1)} collective-permute-done((s32[136,640]{1,0:T(8,128)S(1)}, s32[136,640]{1,0:T(8,128)S(1)}, u32[]{:S(2)}, u32[]{:S(2)}) %collective-permute-start.18) | collective-permute-done | bytes 348192 | tf_op jit(solution)/shard_map/ppermute | solution.py:708
  126.7 3.9 %collective-permute-start.19 = (f32[8,256]{1,0:T(8,128)S(1)}, f32[8,256]{1,0:T(8,128)S(1)}, u32[]{:S(2)}, u32[]{:S(2)}) collective-permute-start(f32[8,256]{1,0:T(8,128)S(1)} %get-tuple-element.43), channel_id=1, source_target_pairs={{0,1},{1,0},{2,3},{3,2},{4,5},{5,4},{6,7},{7,6},{8,9},{9,8},{10,11... | collective-permute-start | bytes 24584 | tf_op jit(solution)/shard_map/ppermute | solution.py:708
  131.4 10.4 %collective-permute-start.20 = (f32[8,256]{1,0:T(8,128)S(1)}, f32[8,256]{1,0:T(8,128)S(1)}, u32[]{:S(2)}, u32[]{:S(2)}) collective-permute-start(f32[8,256]{1,0:T(8,128)S(1)} %add.159), channel_id=1, source_target_pairs={{0,2},{1,3},{2,0},{3,1},{4,6},{5,7},{6,4},{7,5},{8,10},{9,11},{10,... | collective-permute-start | bytes 24584 | tf_op jit(solution)/shard_map/ppermute | solution.py:708
  147.1 9.8 %update.1 = (f32[8,4,32,640]{3,2,1,0:T(8,128)}, f32[8,4,32,640]{3,2,1,0:T(8,128)}, f32[8,4,32,640]{3,2,1,0:T(8,128)}) custom-call(s32[4]{0:T(128)S(1)} %xor_multiply_fusion.order_ref, f32[8,256]{1,0:T(8,128)S(1)} %add.161.sums_ref, f32[8,4,32,640]{3,2,1,0:T(8,128)S(1)} %copy-done.2, f32[8,4,32,640]{3,2,1,0:T(8,128)S(1)} %copy-done.1, ...), custom_call_target="tpu_custom_call" | custom-call | flops 31457280 | bytes 18350080 | tf_op jit(solution)/shard_map/update/pallas_call | solution.py:687
  (80 shorter events, 38.9 us)
Async XLA Ops:
  7.3 16.7 %collective-permute-start.3 = (s32[136,640]{1,0:T(8,128)S(1)}, s32[136,640]{1,0:T(8,128)S(1)}, u32[]{:S(2)}, u32[]{:S(2)}) collective-permute-start(s32[136,640]{1,0:T(8,128)S(1)} %get-tuple-element.25), channel_id=1, source_target_pairs={{0,1},{1,2},{2,3},{3,4},{4,5},{5,6},{6,7},{8,9},{9,10},{10,11},{11... | collective-permute-start | bytes 1044488 | tf_op jit(solution)/shard_map/ppermute | solution.py:717
  9.7 14.4 %collective-permute-start.4 = (s32[136,640]{1,0:T(8,128)S(1)}, s32[136,640]{1,0:T(8,128)S(1)}, u32[]{:S(2)}, u32[]{:S(2)}) collective-permute-start(s32[136,640]{1,0:T(8,128)S(1)} %get-tuple-element.25), channel_id=1, source_target_pairs={{1,0},{2,1},{3,2},{4,3},{5,4},{6,5},{7,6},{9,8},{10,9},{11,10},{12... | collective-permute-start | bytes 1044488 | tf_op jit(solution)/shard_map/ppermute | solution.py:718
  13.2 6.2 %collective-permute-start = (s32[384]{0:T(512)S(1)}, s32[384]{0:T(512)S(1)}, u32[]{:S(2)}, u32[]{:S(2)}) collective-permute-start(s32[384]{0:T(512)S(1)} %fusion.6), channel_id=1, source_target_pairs={{0,8},{8,0},{16,24},{24,16},{1,9},{9,1},{17,25},{25,17},{2,10},{10... | collective-permute-start | bytes 4616 | tf_op jit(solution)/shard_map/ppermute | solution.py:708
  15.6 4.5 %collective-permute-start.1 = (s32[384]{0:T(512)S(1)}, s32[384]{0:T(512)S(1)}, u32[]{:S(2)}, u32[]{:S(2)}) collective-permute-start(s32[384]{0:T(512)S(1)} %fusion.6), channel_id=1, source_target_pairs={{0,16},{8,24},{16,0},{24,8},{1,17},{9,25},{17,1},{25,9},{2,18},{10... | collective-permute-start | bytes 4616 | tf_op jit(solution)/shard_map/ppermute | solution.py:708
  18.2 5.4 %collective-permute-start.2 = (s32[384]{0:T(512)S(1)}, s32[384]{0:T(512)S(1)}, u32[]{:S(2)}, u32[]{:S(2)}) collective-permute-start(s32[384]{0:T(512)S(1)} %fusion.6), channel_id=1, source_target_pairs={{0,24},{8,16},{16,8},{24,0},{1,25},{9,17},{17,9},{25,1},{2,26},{10... | collective-permute-start | bytes 4616 | tf_op jit(solution)/shard_map/ppermute | solution.py:708
  26.0 9.7 %collective-permute-start.5 = (bf16[2,384,128]{2,1,0:T(8,128)(2,1)S(1)}, bf16[2,384,128]{2,1,0:T(8,128)(2,1)S(1)}, u32[]{:S(2)}, u32[]{:S(2)}) collective-permute-start(bf16[2,384,128]{2,1,0:T(8,128)(2,1)S(1)} %get-tuple-element.27), channel_id=1, source_target_pairs={{0,8},{8,0},{16,24},{24,16},{1,9},{9,1},{17,25},{25,17},{2,10},{10... | collective-permute-start | bytes 589832 | tf_op jit(solution)/shard_map/ppermute | solution.py:708
  26.1 17.2 %collective-permute-start.6 = (bf16[2,384,128]{2,1,0:T(8,128)(2,1)S(1)}, bf16[2,384,128]{2,1,0:T(8,128)(2,1)S(1)}, u32[]{:S(2)}, u32[]{:S(2)}) collective-permute-start(bf16[2,384,128]{2,1,0:T(8,128)(2,1)S(1)} %get-tuple-element.28), channel_id=1, source_target_pairs={{0,16},{8,24},{16,0},{24,8},{1,17},{9,25},{17,1},{25,9},{2,18},{10... | collective-permute-start | bytes 589832 | tf_op jit(solution)/shard_map/ppermute | solution.py:708
  26.6 16.6 %collective-permute-start.7 = (bf16[2,384,128]{2,1,0:T(8,128)(2,1)S(1)}, bf16[2,384,128]{2,1,0:T(8,128)(2,1)S(1)}, u32[]{:S(2)}, u32[]{:S(2)}) collective-permute-start(bf16[2,384,128]{2,1,0:T(8,128)(2,1)S(1)} %get-tuple-element.29), channel_id=1, source_target_pairs={{0,24},{8,16},{16,8},{24,0},{1,25},{9,17},{17,9},{25,1},{2,26},{10... | collective-permute-start | bytes 589832 | tf_op jit(solution)/shard_map/ppermute | solution.py:708
  48.0 1.4 collective-permute-start.8
  49.5 7.0 %collective-permute-start.9 = (f32[256,128]{1,0:T(8,128)S(1)}, f32[256,128]{1,0:T(8,128)S(1)}, u32[]{:S(2)}, u32[]{:S(2)}) collective-permute-start(f32[256,128]{1,0:T(8,128)S(1)} %add.156), channel_id=1, source_target_pairs={{0,2},{1,3},{2,0},{3,1},{4,6},{5,7},{6,4},{7,5},{8,10},{9,11},{10,... | collective-permute-start | bytes 393224 | tf_op jit(solution)/shard_map/ppermute | solution.py:708
  56.5 6.7 %collective-permute-start.10 = (f32[256,128]{1,0:T(8,128)S(1)}, f32[256,128]{1,0:T(8,128)S(1)}, u32[]{:S(2)}, u32[]{:S(2)}) collective-permute-start(f32[256,128]{1,0:T(8,128)S(1)} %add.157.after_ref), channel_id=1, source_target_pairs={{0,4},{1,5},{2,6},{3,7},{4,0},{5,1},{6,2},{7,3},{8,12},{9,13},{10,... | collective-permute-start | bytes 393224 | tf_op jit(solution)/shard_map/ppermute | solution.py:708
  66.6 9.7 %collective-permute-start.11 = (s32[392,128]{1,0:T(8,128)S(1)}, s32[392,128]{1,0:T(8,128)S(1)}, u32[]{:S(2)}, u32[]{:S(2)}) collective-permute-start(s32[392,128]{1,0:T(8,128)S(1)} %get-tuple-element.31), channel_id=1, source_target_pairs={{0,8},{8,0},{16,24},{24,16},{1,9},{9,1},{17,25},{25,17},{2,10},{10... | collective-permute-start | bytes 602120 | tf_op jit(solution)/shard_map/ppermute | solution.py:708
  69.3 16.8 %collective-permute-start.12 = (s32[392,128]{1,0:T(8,128)S(1)}, s32[392,128]{1,0:T(8,128)S(1)}, u32[]{:S(2)}, u32[]{:S(2)}) collective-permute-start(s32[392,128]{1,0:T(8,128)S(1)} %get-tuple-element.32), channel_id=1, source_target_pairs={{0,16},{8,24},{16,0},{24,8},{1,17},{9,25},{17,1},{25,9},{2,18},{10... | collective-permute-start | bytes 602120 | tf_op jit(solution)/shard_map/ppermute | solution.py:708
  69.3 16.8 %collective-permute-start.13 = (s32[392,128]{1,0:T(8,128)S(1)}, s32[392,128]{1,0:T(8,128)S(1)}, u32[]{:S(2)}, u32[]{:S(2)}) collective-permute-start(s32[392,128]{1,0:T(8,128)S(1)} %get-tuple-element.33), channel_id=1, source_target_pairs={{0,24},{8,16},{16,8},{24,0},{1,25},{9,17},{17,9},{25,1},{2,26},{10... | collective-permute-start | bytes 602120 | tf_op jit(solution)/shard_map/ppermute | solution.py:708
  86.2 16.7 %copy-start.1 = (f32[8,4,32,640]{3,2,1,0:T(8,128)S(1)}, f32[8,4,32,640]{3,2,1,0:T(8,128)}, u32[]{:S(2)}) copy-start(f32[8,4,32,640]{3,2,1,0:T(8,128)} %residual_ref.9) | copy-start | bytes 7864324
  88.2 2.8 %collective-permute-start.14 = (s32[136,640]{1,0:T(8,128)S(1)}, s32[136,640]{1,0:T(8,128)S(1)}, u32[]{:S(2)}, u32[]{:S(2)}) collective-permute-start(s32[136,640]{1,0:T(8,128)S(1)} %get-tuple-element.35), channel_id=1, source_target_pairs={{0,1},{1,2},{2,3},{3,4},{4,5},{5,6},{6,7},{8,9},{9,10},{10,11},{11... | collective-permute-start | bytes 1044488 | tf_op jit(solution)/shard_map/ppermute | solution.py:717
  89.5 4.2 %collective-permute-start.15 = (s32[136,640]{1,0:T(8,128)S(1)}, s32[136,640]{1,0:T(8,128)S(1)}, u32[]{:S(2)}, u32[]{:S(2)}) collective-permute-start(s32[136,640]{1,0:T(8,128)S(1)} %get-tuple-element.35), channel_id=1, source_target_pairs={{1,0},{2,1},{3,2},{4,3},{5,4},{6,5},{7,6},{9,8},{10,9},{11,10},{12... | collective-permute-start | bytes 1044488 | tf_op jit(solution)/shard_map/ppermute | solution.py:718
  99.6 10.8 %collective-permute-start.16 = (s32[136,640]{1,0:T(8,128)S(1)}, s32[136,640]{1,0:T(8,128)S(1)}, u32[]{:S(2)}, u32[]{:S(2)}) collective-permute-start(s32[136,640]{1,0:T(8,128)S(1)} %pull_back.1.rest_0_), channel_id=1, source_target_pairs={{0,8},{8,0},{16,24},{24,16},{1,9},{9,1},{17,25},{25,17},{2,10},{10... | collective-permute-start | bytes 1044488 | tf_op jit(solution)/shard_map/ppermute | solution.py:708
  102.9 12.9 %collective-permute-start.17 = (s32[136,640]{1,0:T(8,128)S(1)}, s32[136,640]{1,0:T(8,128)S(1)}, u32[]{:S(2)}, u32[]{:S(2)}) collective-permute-start(s32[136,640]{1,0:T(8,128)S(1)} %pull_back.1.rest_0_), channel_id=1, source_target_pairs={{0,16},{8,24},{16,0},{24,8},{1,17},{9,25},{17,1},{25,9},{2,18},{10... | collective-permute-start | bytes 1044488 | tf_op jit(solution)/shard_map/ppermute | solution.py:708
  115.8 8.8 %collective-permute-start.18 = (s32[136,640]{1,0:T(8,128)S(1)}, s32[136,640]{1,0:T(8,128)S(1)}, u32[]{:S(2)}, u32[]{:S(2)}) collective-permute-start(s32[136,640]{1,0:T(8,128)S(1)} %collective-permute-done.17.rest_0_), channel_id=1, source_target_pairs={{0,8},{8,0},{16,24},{24,16},{1,9},{9,1},{17,25},{25,17},{2,10},{10... | collective-permute-start | bytes 1044488 | tf_op jit(solution)/shard_map/ppermute | solution.py:708
  124.6 22.5 %copy-start.2 = (f32[8,4,32,640]{3,2,1,0:T(8,128)S(1)}, f32[8,4,32,640]{3,2,1,0:T(8,128)}, u32[]{:S(2)}) copy-start(f32[8,4,32,640]{3,2,1,0:T(8,128)} %solution_ref.1) | copy-start | bytes 7864324
  126.7 4.7 %collective-permute-start.19 = (f32[8,256]{1,0:T(8,128)S(1)}, f32[8,256]{1,0:T(8,128)S(1)}, u32[]{:S(2)}, u32[]{:S(2)}) collective-permute-start(f32[8,256]{1,0:T(8,128)S(1)} %get-tuple-element.43), channel_id=1, source_target_pairs={{0,1},{1,0},{2,3},{3,2},{4,5},{5,4},{6,7},{7,6},{8,9},{9,8},{10,11... | collective-permute-start | bytes 24584 | tf_op jit(solution)/shard_map/ppermute | solution.py:708
  131.4 12.1 %collective-permute-start.20 = (f32[8,256]{1,0:T(8,128)S(1)}, f32[8,256]{1,0:T(8,128)S(1)}, u32[]{:S(2)}, u32[]{:S(2)}) collective-permute-start(f32[8,256]{1,0:T(8,128)S(1)} %add.159), channel_id=1, source_target_pairs={{0,2},{1,3},{2,0},{3,1},{4,6},{5,7},{6,4},{7,5},{8,10},{9,11},{10,... | collective-permute-start | bytes 24584 | tf_op jit(solution)/shard_map/ppermute | solution.py:708
  143.4 3.7 %collective-permute-start.21 = (f32[8,256]{1,0:T(8,128)S(1)}, f32[8,256]{1,0:T(8,128)S(1)}, u32[]{:S(2)}, u32[]{:S(2)}) collective-permute-start(f32[8,256]{1,0:T(8,128)S(1)} %add.160), channel_id=1, source_target_pairs={{0,4},{1,5},{2,6},{3,7},{4,0},{5,1},{6,2},{7,3},{8,12},{9,13},{10,... | collective-permute-start | bytes 24584 | tf_op jit(solution)/shard_map/ppermute | solution.py:708
  (4 other events, 35.1 us)

commit v4 on v3

--- a/solution.py
+++ b/solution.py
@@ -12,7 +12,8 @@
 CHUNK = 96
 COPIES = 12
 STREAM_MIB = 40
-BACK_GROUPS = 1
+KEPT, KEPT_OF = 1, 2
+BACK_GROUPS = 2
 SUBLANES = 8
 MIB = 1024 * 1024
 HIGHEST = lax.Precision.HIGHEST
@@ -244,13 +245,13 @@
     return max(size for size in range(1, most + 1) if count % size == 0)
 
 
-def preload_kernel(after_ref, blocks_ref, out_ref, done):
+def preload_kernel(first, after_ref, blocks_ref, out_ref, done):
     del after_ref
     parts = done.shape[0]
-    size = blocks_ref.shape[0] // parts
+    size = out_ref.shape[0] // parts
     copies = [
         pltpu.make_async_copy(
-            blocks_ref.at[pl.ds(part * size, size)],
+            blocks_ref.at[pl.ds(first + part * size, size)],
             out_ref.at[pl.ds(part * size, size)],
             done.at[part],
         )
@@ -262,22 +263,23 @@
         copy.wait()
 
 
-def preload(blocks, after):
-    parts = chunk_of(blocks.shape[0], COPIES)
+def preload(blocks, first, count, after):
+    parts = chunk_of(count, COPIES)
+    shape = (count, *blocks.shape[1:])
     return pl.pallas_call(
-        preload_kernel,
+        functools.partial(preload_kernel, first),
         in_specs=[pl.BlockSpec(memory_space=pl.ANY)] * 2,
         out_specs=pl.BlockSpec(memory_space=pltpu.VMEM),
-        out_shape=jax.ShapeDtypeStruct(blocks.shape, blocks.dtype),
+        out_shape=jax.ShapeDtypeStruct(shape, blocks.dtype),
         scratch_shapes=[pltpu.SemaphoreType.DMA((parts,))],
         compiler_params=params(STREAM_MIB),
-        cost_estimate=cost(0, blocks.size * 4),
+        cost_estimate=cost(0, count * blocks[0].size * 4),
         name="preload",
     )(after, blocks)
 
 
-def forward_kernel(row_ref, scale_ref, blocks_ref, *rest):
-    picks, (out_ref, cells_ref) = rest[:-2], rest[-2:]
+def forward_kernel(pieces, row_ref, scale_ref, *rest):
+    pieces, picks, (out_ref, cells_ref) = rest[:pieces], rest[pieces:-2], rest[-2:]
     rhs, count, edge = picks[0].shape
     lines = len(picks) * rhs
     out_ref[...] = jnp.zeros_like(out_ref)
@@ -286,60 +288,69 @@
             cells_ref[pl.ds(place * rhs + k, count, stride=lines), :] = pick_ref[k].astype(
                 jnp.float32
             )
-    chunk = 2 * chunk_of(count // 2, CHUNK // 2)
-
-    def one_chunk(step, carry):
+
+    def one_chunk(piece_ref, first, chunk, step, carry):
         values = []
         for n in range(0, chunk, 2):
             index = step * chunk + n
-            at = pl.multiple_of(index * lines, 2 * lines)
+            at = pl.multiple_of((first + index) * lines, 2 * lines)
             both = lax.dot_general(
                 cells_ref[pl.ds(at, 2 * lines), :].astype(jnp.bfloat16),
-                blocks_ref[pl.ds(index, 2)].reshape(2 * edge, edge),
+                piece_ref[pl.ds(index, 2)].reshape(2 * edge, edge),
                 (((1,), (1,)), ((), ())),
                 preferred_element_type=jnp.float32,
             )
             values += [both[:lines, :edge], both[lines:, edge:]]
         for n in range(chunk):
-            index = step * chunk + n
+            index = first + step * chunk + n
             at = pl.multiple_of(row_ref[index] * lines, lines)
             out_ref[pl.ds(at, lines), :] += values[n] * scale_ref[index]
         return carry
 
-    lax.fori_loop(0, count // chunk, one_chunk, 0)
-
-
-def forward(row_list, scales, blocks, picks, row_blocks):
+    over_chunks(pieces, one_chunk)
+
+
+def over_chunks(pieces, one_chunk):
+    first = 0
+    for piece_ref in pieces:
+        count = piece_ref.shape[0]
+        chunk = 2 * chunk_of(count // 2, CHUNK // 2)
+        lax.fori_loop(0, count // chunk, functools.partial(one_chunk, piece_ref, first, chunk), 0)
+        first += count
+
+
+def forward(row_list, scales, pieces, picks, row_blocks):
     rhs, count, edge = picks[0].shape
     lines = len(picks) * rhs
     return pl.pallas_call(
-        forward_kernel,
-        in_specs=[pl.BlockSpec(memory_space=pltpu.SMEM)] * 2 + in_vmem(1 + len(picks)),
+        functools.partial(forward_kernel, len(pieces)),
+        in_specs=[pl.BlockSpec(memory_space=pltpu.SMEM)] * 2 + in_vmem(len(pieces) + len(picks)),
         out_specs=pl.BlockSpec(memory_space=pltpu.VMEM),
         out_shape=jax.ShapeDtypeStruct((row_blocks * lines, edge), jnp.float32),
         scratch_shapes=[pltpu.VMEM((count * lines, edge), jnp.float32)],
         compiler_params=params(15),
-        cost_estimate=cost(blocks.size * 2 * lines, blocks.size * 2),
+        cost_estimate=cost(count * edge**2 * 2 * lines, count * edge**2 * 2),
         name="forward",
-    )(row_list, scales, blocks, *picks)
-
-
-def adjoint_kernel(rhs, row_ref, scale_ref, blocks_ref, values_ref, *rest):
-    outs, terms_ref = rest[:-1], rest[-1]
+    )(row_list, scales, *pieces, *picks)
+
+
+def adjoint_kernel(pieces, rhs, row_ref, scale_ref, *rest):
+    pieces, values_ref, outs, terms_ref = rest[:pieces], rest[pieces], rest[pieces + 1 : -1], rest[-1]
     lines = len(outs) * rhs
-    count, edge, _ = blocks_ref.shape
-    chunk = 2 * chunk_of(count // 2, CHUNK // 2)
-
-    def one_chunk(step, carry):
+    edge = values_ref.shape[1]
+    count = terms_ref.shape[0] // lines
+
+    def one_chunk(piece_ref, first, chunk, step, carry):
         for n in range(0, chunk, 2):
-            index = step * chunk + n
+            here = step * chunk + n
+            index = first + here
             pulled = [
                 values_ref[pl.ds(pl.multiple_of(row_ref[index + q] * lines, lines), lines), :]
                 for q in range(2)
             ]
             both = jnp.dot(
                 jnp.concatenate(pulled, axis=0).astype(jnp.bfloat16),
-                jnp.concatenate([blocks_ref[index + q] for q in range(2)], axis=1),
+                jnp.concatenate([piece_ref[here + q] for q in range(2)], axis=1),
                 preferred_element_type=jnp.float32,
             )
             for q in range(2):
@@ -348,7 +359,7 @@
                 terms_ref[pl.ds(to, lines), :] = part * scale_ref[index + q]
         return carry
 
-    lax.fori_loop(0, count // chunk, one_chunk, 0)
+    over_chunks(pieces, one_chunk)
     half = count // 2
     for place, out_ref in enumerate(outs):
         terms = [terms_ref[pl.ds(place * rhs + k, count, stride=lines), :] for k in range(rhs)]
@@ -359,20 +370,21 @@
             out_ref[k * half : (k + 1) * half, :] = pack(number[:half], number[half:])
 
 
-def adjoint_terms(row_list, scales, blocks, values, outs, rhs):
-    count, edge, _ = blocks.shape
+def adjoint_terms(row_list, scales, pieces, values, outs, rhs):
+    count = sum(piece.shape[0] for piece in pieces)
+    edge = values.shape[1]
     lines = outs * rhs
     words = rhs * count // 2 + SUBLANES
     return pl.pallas_call(
-        functools.partial(adjoint_kernel, rhs),
-        in_specs=[pl.BlockSpec(memory_space=pltpu.SMEM)] * 2 + in_vmem(2),
+        functools.partial(adjoint_kernel, len(pieces), rhs),
+        in_specs=[pl.BlockSpec(memory_space=pltpu.SMEM)] * 2 + in_vmem(len(pieces) + 1),
         out_specs=in_vmem(outs),
         out_shape=[jax.ShapeDtypeStruct((words, edge), jnp.int32)] * outs,
         scratch_shapes=[pltpu.VMEM((count * lines, edge), jnp.float32)],
         compiler_params=params(15),
-        cost_estimate=cost(blocks.size * 2 * lines, blocks.size * 2),
+        cost_estimate=cost(count * edge**2 * 2 * lines, count * edge**2 * 2),
         name="adjoint",
-    )(row_list, scales, blocks, values)
+    )(row_list, scales, *pieces, values)
 
 
 def gather_cells_kernel(slots, hot_ref, *rest):
@@ -772,7 +784,7 @@
     rhs_count, weeks, rows, lon = direction.shape
     blocks = footprints[0, 0]
     count, edge, _ = blocks.shape
-    row_list, col_list = block_rows[0, 0], block_cols[0, 0]
+    row_list = block_rows[0, 0]
     scales = jnp.exp2(-block_scale[0, 0].astype(jnp.float32))
     row_blocks = obs_weight.shape[0] // edge
     slots = lax.axis_size("obs")
@@ -787,9 +799,9 @@
     own_width = lax.dynamic_slice_in_dim(lon_width, band * rows, rows)
     counts = jnp.broadcast_to(own_width[:, None] + 1, (rows, lon))
 
-    line, part = col_list // parts, col_list % parts
-    place = ((line // rows) * parts + part) * rows + line % rows
-    places = jnp.stack([crossed(place, "obs", d) for d in range(slots)])
+    lists = jnp.concatenate([crossed(block_cols, "obs", d) for d in range(slots)], axis=0)[:, 0]
+    line, part = lists // parts, lists % parts
+    places = ((line // rows) * parts + part) * rows + line % rows
 
     lon_own, words = spread_lon(
         lax.dynamic_slice_in_dim(direction, slab * rhs, rhs, 0), counts
@@ -801,12 +813,16 @@
 
     picks = spread_lat(lon_own, *halo, lat_spread, hot)
     cells = [crossed(picks[d], "obs", d) for d in range(slots)]
-    near_blocks = preload(blocks, picks[0])
-    sums, partial = summed_over(forward(row_list, scales, near_blocks, cells, row_blocks), "lat")
-    near_blocks = preload(blocks, partial)
+    kept = count // KEPT_OF * KEPT if count % KEPT_OF == 0 else 0
+    stays = [preload(blocks, 0, kept, picks[0])] if kept else []
+    near = preload(blocks, kept, count - kept, picks[0])
+    sums, partial = summed_over(
+        forward(row_list, scales, [*stays, near], cells, row_blocks), "lat"
+    )
+    near = preload(blocks, kept, count - kept, partial)
     weighted = sums.reshape(row_blocks, slots * rhs, edge) * obs_weight.reshape(row_blocks, 1, edge)
     terms = adjoint_terms(
-        row_list, scales, near_blocks, weighted.reshape(-1, edge), slots * groups, each
+        row_list, scales, [*stays, near], weighted.reshape(-1, edge), slots * groups, each
     )
     sent = [[crossed(terms[d * groups + g], "obs", d) for d in range(slots)] for g in range(groups)]
     own = []
@@ -816,36 +832,33 @@
 
     starts = (order[:, None] + jnp.arange(groups, dtype=jnp.int32) * each).reshape(-1)
     products = jnp.zeros((SUBLANES, 4 * rhs_count**2), jnp.float32)
-    done, places, found = {}, (), []
-
-    def add_products(words, slot, group):
+    done, places = {}, ()
+
+    def add_products(slot):
         nonlocal products, places
-        places += (slot * groups + group,)
-        new, products = grams(
-            starts, places, products, residual, direction, [words], found, slot == group == 0
+        words = [arrived[group][slot] for group in range(groups)]
+        places += tuple(slot * groups + group for group in range(groups))
+        olds = [image for images in done.values() for image in images]
+        done[slot], products = grams(
+            starts, places, products, residual, direction, words, olds, slot == 0
         )
-        found.extend(new)
-        done[slot, group] = new[0]
 
     arrived = [{0: words} for words in own]
     for group in range(groups):
         for reach in far_first(slots):
             arrived[group][reach] = crossed(own[group], "obs", reach)
-        add_products(own[group], 0, group)
-    for group in range(groups):
-        near = [bits for bits in arrived[group] if bits == 1]
-        for bits in near:
-            add_products(arrived[group][bits], bits, group)
+    add_products(0)
     for reach in far_first(slots)[1:]:
         for group in range(groups):
             for bits in [bits for bits in arrived[group] if bits > reach and not bits % (2 * reach)]:
-                words, _ = lax.optimization_barrier((arrived[group][bits], done[1, group]))
+                words = arrived[group][bits]
+                if group == groups - 1:
+                    words, _ = lax.optimization_barrier((words, done[0][0]))
                 arrived[group][bits | reach] = crossed(words, "obs", reach)
-    for bits in range(2, slots):
-        for group in range(groups):
-            add_products(arrived[group][bits], bits, group)
+    for slot in range(1, slots):
+        add_products(slot)
     products, _ = summed_over(products, "lat")
-    images = [done[slot, group] for slot in range(slots) for group in range(groups)]
+    images = [image for slot in range(slots) for image in done[slot]]
     return tuple(update(starts, products, solution, residual, direction, images))
 
 

time: 157 us -> 148 us (0.943)
  waiting for transfers between devices: 53.5 us -> 29.8 us
  starting transfers between devices: 45.5 us -> 54.9 us
  local copies, waits for them, and re-layouts: 1.49 us -> 5.23 us
  Pallas kernels: 50.5 us -> 53.6 us
  other arithmetic: 4.94 us -> 2.95 us
    ppermute x18 -> x24, waiting for transfers between devices: 50.9 us -> 29.8 us  [crossed(): lax.ppermute(value, axis, [(i, i ^ by) for i in range(lax.axis_size(axis))])]
    ppermute x18 -> x24, starting transfers between devices: 39 us -> 45.7 us  [crossed(): lax.ppermute(value, axis, [(i, i ^ by) for i in range(lax.axis_size(axis))])]
    unnamed x12 -> x23, local copies, waits for them, and re-layouts: 0.03 us -> 3.66 us
    ppermute x2 -> x3, waiting for transfers between devices: 2.67 us -> 0.01 us  [neighbours(): after = lax.ppermute(value, axis, [(i + 1, i) for i in range(size - 1)])]
    pallas_call x4 -> x5, Pallas kernels: 17.4 us -> 19.1 us  [the longest x3 11.1 us: preload(): pl.pallas_call(functools.partial(preload_kernel, first), in_specs=[pl.Blo...]
    ppermute x2 -> x3, starting transfers between devices: 3.69 us -> 5.11 us  [neighbours(): before = lax.ppermute(value, axis, [(i, i + 1) for i in range(size - 1)])]
    ppermute x2 -> x3, starting transfers between devices: 2.76 us -> 4.06 us  [neighbours(): after = lax.ppermute(value, axis, [(i + 1, i) for i in range(size - 1)])]
    pallas_call x1 -> x2, Pallas kernels: 5.93 us -> 6.84 us  [pull_back(): pl.pallas_call(pull_back_kernel, in_specs=in_vmem(5), out_specs=pl.BlockS...]
  transfers between devices with their start and end apart: 22 -> 30, of which waited for: 15 -> 13; matrix products, arithmetic and copies ran while one was open for 3% -> 2% of each run, Pallas kernels for 10% -> 18%
where the time goes in v4:
time: 148 us; the launch traced here: 147 us
  starting transfers between devices  54.9 us (37%)
  Pallas kernels  53.6 us (36%)
  waiting for transfers between devices  29.8 us (20%)
  local copies, waits for them, and re-layouts  5.23 us (4%)
  other arithmetic  2.95 us (2%)
    ppermute x24, starting transfers between devices, crossed(): lax.ppermute(value, axis, [(i, i ^ by) for i in range(lax.axis_size(axis))])  45.7 us
    ppermute x24, waiting for transfers between devices, crossed(): lax.ppermute(value, axis, [(i, i ^ by) for i in range(lax.axis_size(axis))])  29.8 us
    pallas_call x3, Pallas kernels, preload(): pl.pallas_call(functools.partial(preload_kernel, first), in_specs=[pl.Blo...  11.1 us
    pallas_call x1, Pallas kernels, update(): pl.pallas_call(update_kernel, grid_spec=pltpu.PrefetchScalarGridSpec(num_...  9.65 us
    pallas_call x4, Pallas kernels, grams(): pl.pallas_call(functools.partial(gram_kernel, with_old, places, count, rh...  9.29 us
    pallas_call x2, Pallas kernels, pull_back(): pl.pallas_call(pull_back_kernel, in_specs=in_vmem(5), out_specs=pl.BlockS...  6.84 us
    ppermute x3, starting transfers between devices, neighbours(): before = lax.ppermute(value, axis, [(i, i + 1) for i in range(size - 1)])  5.11 us
    pallas_call x1, Pallas kernels, forward(): pl.pallas_call(functools.partial(forward_kernel, len(pieces)), in_specs=[...  4.77 us
  transfers between devices with their start and end apart: 30, of which 13 were waited for; matrix products, arithmetic and copies ran while one was open for 2% of the time, Pallas kernels for 18%

profile of v4, /device:TPU:0, one launch (start us, length us, event | category | flops | bytes accessed | tf_op | source)
XLA Modules:
  0.0 147.5 jit_solution(11524141705712528746)
XLA Ops:
  2.6 4.7 %spread_lon.1 = (f32[2,4,32,640]{3,2,1,0:T(8,128)S(1)}, s32[136,640]{1,0:T(8,128)S(1)}) custom-call(f32[2,4,32,640]{3,2,1,0:T(8,128)S(1)} %constant_dynamic-slice_fusion.field_ref, s32[32,640]{1,0:T(8,128)S(1)} %broadcast_in_dim.21.count_ref), custom_call_target="tpu_custom_call" | custom-call | flops 16384000 | bytes 1638400 | tf_op jit(solution)/shard_map/spread_lon/pallas_call | solution.py:166
  13.5 2.6 %collective-permute-start.1 = (s32[1,1,384]{2,1,0:T(1,128)}, s32[1,1,384]{2,1,0:T(1,128)S(1)}, u32[]{:S(2)}, u32[]{:S(2)}) collective-permute-start(s32[1,1,384]{2,1,0:T(1,128)} %param.12), channel_id=1, source_target_pairs={{0,16},{8,24},{16,0},{24,8},{1,17},{9,25},{17,1},{25,9},{2,18},{10... | collective-permute-start | bytes 4616 | tf_op jit(solution)/shard_map/ppermute | solution.py:720
  18.2 3.5 %collective-permute-done.2 = s32[1,1,384]{2,1,0:T(1,128)S(1)} collective-permute-done((s32[1,1,384]{2,1,0:T(1,128)}, s32[1,1,384]{2,1,0:T(1,128)S(1)}, u32[]{:S(2)}, u32[]{:S(2)}) %collective-permute-start.2) | collective-permute-done | bytes 1568 | tf_op jit(solution)/shard_map/ppermute | solution.py:720
  24.8 3.7 %collective-permute-start.7 = (bf16[2,384,128]{2,1,0:T(8,128)(2,1)S(1)}, bf16[2,384,128]{2,1,0:T(8,128)(2,1)S(1)}, u32[]{:S(2)}, u32[]{:S(2)}) collective-permute-start(bf16[2,384,128]{2,1,0:T(8,128)(2,1)S(1)} %get-tuple-element.39), channel_id=1, source_target_pairs={{0,24},{8,16},{16,8},{24,0},{1,25},{9,17},{17,9},{25,1},{2,26},{10... | collective-permute-start | bytes 589832 | tf_op jit(solution)/shard_map/ppermute | solution.py:720
  28.6 2.9 %preload.3.rest_0_ = bf16[192,128,128]{2,1,0:T(8,128)(2,1)S(1)} custom-call(bf16[2,384,128]{2,1,0:T(8,128)(2,1)S(1)} %get-tuple-element.36.after_ref.rest_2_, bf16[384,128,128]{2,1,0:T(8,128)(2,1)} %bitcast.30), custom_call_target="tpu_custom_call" | custom-call | bytes 12582912 | tf_op jit(solution)/shard_map/preload/pallas_call | solution.py:269
  31.5 5.1 %preload.4.rest_1_ = bf16[192,128,128]{2,1,0:T(8,128)(2,1)S(1)} custom-call(bf16[2,384,128]{2,1,0:T(8,128)(2,1)S(1)} %get-tuple-element.36.after_ref.rest_2_, bf16[384,128,128]{2,1,0:T(8,128)(2,1)} %bitcast.31), custom_call_target="tpu_custom_call" | custom-call | bytes 12582912 | tf_op jit(solution)/shard_map/preload/pallas_call | solution.py:269
  36.7 4.7 %collective-permute-done.6.rest_4_ = bf16[2,384,128]{2,1,0:T(8,128)(2,1)S(1)} collective-permute-done((bf16[2,384,128]{2,1,0:T(8,128)(2,1)S(1)}, bf16[2,384,128]{2,1,0:T(8,128)(2,1)S(1)}, u32[]{:S(2)}, u32[]{:S(2)}) %collective-permute-start.6) | collective-permute-done | bytes 196640 | tf_op jit(solution)/shard_map/ppermute | solution.py:720
  41.4 4.8 %forward.1 = f32[256,128]{1,0:T(8,128)S(1)} custom-call(s32[384]{0:T(512)S(1)} %reduce.1.row_ref, f32[384]{0:T(512)S(1)} %exponential_reduce_fusion.scale_ref, bf16[192,128,128]{2,1,0:T(8,128)(2,1)S(1)} %preload.3.rest_0_, bf16[192,128,128]{2,1,0:T(8,128)(2,1)S(1)} %preload.4.rest_1_, bf16[2,384,128]{2,1,0:T(8,128)(2,1)S(1)} %get-tuple-element.36.after_ref.rest_2_, ...), custom_call_target="tpu_custom_call" | custom-call | flops 100663296 | bytes 12582912 | tf_op jit(solution)/shard_map/forward/pallas_call | solution.py:325
  47.6 3.6 %collective-permute-start.9 = (f32[256,128]{1,0:T(8,128)S(1)}, f32[256,128]{1,0:T(8,128)S(1)}, u32[]{:S(2)}, u32[]{:S(2)}) collective-permute-start(f32[256,128]{1,0:T(8,128)S(1)} %add.183), channel_id=1, source_target_pairs={{0,2},{1,3},{2,0},{3,1},{4,6},{5,7},{6,4},{7,5},{8,10},{9,11},{10,... | collective-permute-start | bytes 393224 | tf_op jit(solution)/shard_map/ppermute | solution.py:720
  51.2 3.8 %collective-permute-done.9 = f32[256,128]{1,0:T(8,128)S(1)} collective-permute-done((f32[256,128]{1,0:T(8,128)S(1)}, f32[256,128]{1,0:T(8,128)S(1)}, u32[]{:S(2)}, u32[]{:S(2)}) %collective-permute-start.9) | collective-permute-done | bytes 131104 | tf_op jit(solution)/shard_map/ppermute | solution.py:720
  56.7 3.0 %preload.5.rest_1_ = bf16[192,128,128]{2,1,0:T(8,128)(2,1)S(1)} custom-call(f32[256,128]{1,0:T(8,128)S(1)} %add.184.after_ref, bf16[384,128,128]{2,1,0:T(8,128)(2,1)} %bitcast.32), custom_call_target="tpu_custom_call" | custom-call | bytes 12582912 | tf_op jit(solution)/shard_map/preload/pallas_call | solution.py:269
  61.4 3.3 %adjoint.1 = (s32[200,128]{1,0:T(8,128)S(1)}, s32[200,128]{1,0:T(8,128)S(1)}, s32[200,128]{1,0:T(8,128)S(1)}, s32[200,128]{1,0:T(8,128)S(1)}, s32[200,128]{1,0:T...) custom-call(s32[384]{0:T(512)S(1)} %reduce.1.row_ref, ...), custom_call_target="tpu_custom_call" | custom-call | flops 100663296 | bytes 12582912 | tf_op jit(solution)/shard_map/adjoint/pallas_call | solution.py:378
  64.7 2.7 %collective-permute-start.16 = (s32[200,128]{1,0:T(8,128)S(1)}, s32[200,128]{1,0:T(8,128)S(1)}, u32[]{:S(2)}, u32[]{:S(2)}) collective-permute-start(s32[200,128]{1,0:T(8,128)S(1)} %get-tuple-element.47), channel_id=1, source_target_pairs={{0,8},{8,0},{16,24},{24,16},{1,9},{9,1},{17,25},{25,17},{2,10},{10... | collective-permute-start | bytes 307208 | tf_op jit(solution)/shard_map/ppermute | solution.py:720
  74.9 3.9 %collective-permute-done.17.rest_2_ = s32[200,128]{1,0:T(8,128)S(1)} collective-permute-done((s32[200,128]{1,0:T(8,128)S(1)}, s32[200,128]{1,0:T(8,128)S(1)}, u32[]{:S(2)}, u32[]{:S(2)}) %collective-permute-start.17) | collective-permute-done | bytes 102432 | tf_op jit(solution)/shard_map/ppermute | solution.py:720
  82.5 3.5 %collective-permute-done.12.rest_2_ = s32[200,128]{1,0:T(8,128)S(1)} collective-permute-done((s32[200,128]{1,0:T(8,128)S(1)}, s32[200,128]{1,0:T(8,128)S(1)}, u32[]{:S(2)}, u32[]{:S(2)}) %collective-permute-start.12) | collective-permute-done | bytes 102432 | tf_op jit(solution)/shard_map/ppermute | solution.py:720
  89.9 3.4 %pull_back.3.rest_1_ = s32[72,640]{1,0:T(8,128)S(1)} custom-call(f32[1,4,32,640]{3,2,1,0:T(8,128)S(1)} %get-tuple-element.50.own_ref, s32[72,640]{1,0:T(8,128)S(1)} %collective-permute-done.19.before_ref, s32[72,640]{1,0:T(8,128)S(1)} %collective-permute-done.20.after_ref, f32[32,96]{1,0:T(8,128)S(1)} %get-tuple-element.69.weights_ref, ...), custom_call_target="tpu_custom_call" | custom-call | flops 24576000 | bytes 819200 | tf_op jit(solution)/shard_map/pull_back/pallas_call | solution.py:465
  93.4 5.6 %collective-permute-start.24 = (s32[72,640]{1,0:T(8,128)S(1)}, s32[72,640]{1,0:T(8,128)}, u32[]{:S(2)}, u32[]{:S(2)}) collective-permute-start(s32[72,640]{1,0:T(8,128)S(1)} %pull_back.3.rest_1_), channel_id=1, source_target_pairs={{0,16},{8,24},{16,0},{24,8},{1,17},{9,25},{17,1},{25,9},{2,18},{10... | collective-permute-start | bytes 552968 | tf_op jit(solution)/shard_map/ppermute | solution.py:720
  98.9 3.4 %pull_back.2.rest_0_ = s32[72,640]{1,0:T(8,128)S(1)} custom-call(f32[1,4,32,640]{3,2,1,0:T(8,128)S(1)} %get-tuple-element.44.own_ref, s32[72,640]{1,0:T(8,128)S(1)} %collective-permute-done.14.before_ref, s32[72,640]{1,0:T(8,128)S(1)} %collective-permute-done.15.after_ref, f32[32,96]{1,0:T(8,128)S(1)} %get-tuple-element.69.weights_ref, ...), custom_call_target="tpu_custom_call" | custom-call | flops 24576000 | bytes 819200 | tf_op jit(solution)/shard_map/pull_back/pallas_call | solution.py:465
  106.8 2.9 %grams.4 = (f32[1,4,32,640]{3,2,1,0:T(8,128)S(1)}, f32[1,4,32,640]{3,2,1,0:T(8,128)S(1)}, f32[8,256]{1,0:T(8,128)S(1)}) custom-call(s32[8]{0:T(128)S(1)} %add.165.order_ref, f32[8,256]{1,0:T(8,128)S(1)} %broadcast_in_dim.20.sums_before, f32[8,4,32,640]{3,2,1,0:T(8,128)S(1)} %copy-done.1, f32[8,4,32,640]{3,2,1,0:T(8,128)S(1)} %copy-done, ...), custom_call_target="tpu_custom_call" | custom-call | flops 41943040 | bytes 10485760 | tf_op jit(solution)/shard_map/grams/pallas_call | solution.py:566
  111.7 2.8 %collective-permute-done.23.rest_0_ = s32[72,640]{1,0:T(8,128)} collective-permute-done((s32[72,640]{1,0:T(8,128)S(1)}, s32[72,640]{1,0:T(8,128)}, u32[]{:S(2)}, u32[]{:S(2)}) %collective-permute-start.23) | collective-permute-done | bytes 184352 | tf_op jit(solution)/shard_map/ppermute | solution.py:720
  114.5 3.0 %collective-permute-start.25 = (s32[72,640]{1,0:T(8,128)}, s32[72,640]{1,0:T(8,128)S(1)}, u32[]{:S(2)}, u32[]{:S(2)}) collective-permute-start(s32[72,640]{1,0:T(8,128)} %collective-permute-done.23.rest_0_), channel_id=1, source_target_pairs={{0,8},{8,0},{16,24},{24,16},{1,9},{9,1},{17,25},{25,17},{2,10},{10... | collective-permute-start | bytes 552968 | tf_op jit(solution)/shard_map/ppermute | solution.py:720
  127.1 4.3 %collective-permute-start.28 = (f32[8,256]{1,0:T(8,128)S(1)}, f32[8,256]{1,0:T(8,128)S(1)}, u32[]{:S(2)}, u32[]{:S(2)}) collective-permute-start(f32[8,256]{1,0:T(8,128)S(1)} %add.186), channel_id=1, source_target_pairs={{0,2},{1,3},{2,0},{3,1},{4,6},{5,7},{6,4},{7,5},{8,10},{9,11},{10,... | collective-permute-start | bytes 24584 | tf_op jit(solution)/shard_map/ppermute | solution.py:720
  133.1 3.1 %collective-permute-start.29 = (f32[8,256]{1,0:T(8,128)S(1)}, f32[8,256]{1,0:T(8,128)S(1)}, u32[]{:S(2)}, u32[]{:S(2)}) collective-permute-start(f32[8,256]{1,0:T(8,128)S(1)} %add.187), channel_id=1, source_target_pairs={{0,4},{1,5},{2,6},{3,7},{4,0},{5,1},{6,2},{7,3},{8,12},{9,13},{10,... | collective-permute-start | bytes 24584 | tf_op jit(solution)/shard_map/ppermute | solution.py:720
  137.8 9.7 %update.1 = (f32[8,4,32,640]{3,2,1,0:T(8,128)}, f32[8,4,32,640]{3,2,1,0:T(8,128)}, f32[8,4,32,640]{3,2,1,0:T(8,128)}) custom-call(s32[8]{0:T(128)S(1)} %add.165.order_ref, f32[8,256]{1,0:T(8,128)S(1)} %add.188.sums_ref, f32[8,4,32,640]{3,2,1,0:T(8,128)S(1)} %copy-done.4, f32[8,4,32,640]{3,2,1,0:T(8,128)S(1)} %copy-done.2, f32[8,4,32,640]{3,2,1,0:T(8,128)S(1)} %copy-done, ...), custom_call_target="tpu_custom_call" | custom-call | flops 31457280 | bytes 18350080 | tf_op jit(solution)/shard_map/update/pallas_call | solution.py:699
  (111 shorter events, 52.5 us)
Async XLA Ops:
  7.3 14.9 %collective-permute-start.3 = (s32[136,640]{1,0:T(8,128)S(1)}, s32[136,640]{1,0:T(8,128)S(1)}, u32[]{:S(2)}, u32[]{:S(2)}) collective-permute-start(s32[136,640]{1,0:T(8,128)S(1)} %get-tuple-element.35), channel_id=1, source_target_pairs={{0,1},{1,2},{2,3},{3,4},{4,5},{5,6},{6,7},{8,9},{9,10},{10,11},{11... | collective-permute-start | bytes 1044488 | tf_op jit(solution)/shard_map/ppermute | solution.py:729
  9.7 12.5 %collective-permute-start.4 = (s32[136,640]{1,0:T(8,128)S(1)}, s32[136,640]{1,0:T(8,128)S(1)}, u32[]{:S(2)}, u32[]{:S(2)}) collective-permute-start(s32[136,640]{1,0:T(8,128)S(1)} %get-tuple-element.35), channel_id=1, source_target_pairs={{1,0},{2,1},{3,2},{4,3},{5,4},{6,5},{7,6},{9,8},{10,9},{11,10},{12... | collective-permute-start | bytes 1044488 | tf_op jit(solution)/shard_map/ppermute | solution.py:730
  11.0 6.9 %collective-permute-start = (s32[1,1,384]{2,1,0:T(1,128)}, s32[1,1,384]{2,1,0:T(1,128)S(1)}, u32[]{:S(2)}, u32[]{:S(2)}) collective-permute-start(s32[1,1,384]{2,1,0:T(1,128)} %param.12), channel_id=1, source_target_pairs={{0,8},{8,0},{16,24},{24,16},{1,9},{9,1},{17,25},{25,17},{2,10},{10... | collective-permute-start | bytes 4616 | tf_op jit(solution)/shard_map/ppermute | solution.py:720
  24.1 12.6 %collective-permute-start.5 = (bf16[2,384,128]{2,1,0:T(8,128)(2,1)S(1)}, bf16[2,384,128]{2,1,0:T(8,128)(2,1)S(1)}, u32[]{:S(2)}, u32[]{:S(2)}) collective-permute-start(bf16[2,384,128]{2,1,0:T(8,128)(2,1)S(1)} %get-tuple-element.37), channel_id=1, source_target_pairs={{0,8},{8,0},{16,24},{24,16},{1,9},{9,1},{17,25},{25,17},{2,10},{10... | collective-permute-start | bytes 589832 | tf_op jit(solution)/shard_map/ppermute | solution.py:720
  24.2 17.2 %collective-permute-start.6 = (bf16[2,384,128]{2,1,0:T(8,128)(2,1)S(1)}, bf16[2,384,128]{2,1,0:T(8,128)(2,1)S(1)}, u32[]{:S(2)}, u32[]{:S(2)}) collective-permute-start(bf16[2,384,128]{2,1,0:T(8,128)(2,1)S(1)} %get-tuple-element.38), channel_id=1, source_target_pairs={{0,16},{8,24},{16,0},{24,8},{1,17},{9,25},{17,1},{25,9},{2,18},{10... | collective-permute-start | bytes 589832 | tf_op jit(solution)/shard_map/ppermute | solution.py:720
  24.8 16.6 %collective-permute-start.7 = (bf16[2,384,128]{2,1,0:T(8,128)(2,1)S(1)}, bf16[2,384,128]{2,1,0:T(8,128)(2,1)S(1)}, u32[]{:S(2)}, u32[]{:S(2)}) collective-permute-start(bf16[2,384,128]{2,1,0:T(8,128)(2,1)S(1)} %get-tuple-element.39), channel_id=1, source_target_pairs={{0,24},{8,16},{16,8},{24,0},{1,25},{9,17},{17,9},{25,1},{2,26},{10... | collective-permute-start | bytes 589832 | tf_op jit(solution)/shard_map/ppermute | solution.py:720
  47.6 7.4 %collective-permute-start.9 = (f32[256,128]{1,0:T(8,128)S(1)}, f32[256,128]{1,0:T(8,128)S(1)}, u32[]{:S(2)}, u32[]{:S(2)}) collective-permute-start(f32[256,128]{1,0:T(8,128)S(1)} %add.183), channel_id=1, source_target_pairs={{0,2},{1,3},{2,0},{3,1},{4,6},{5,7},{6,4},{7,5},{8,10},{9,11},{10,... | collective-permute-start | bytes 393224 | tf_op jit(solution)/shard_map/ppermute | solution.py:720
  64.7 7.8 %collective-permute-start.16 = (s32[200,128]{1,0:T(8,128)S(1)}, s32[200,128]{1,0:T(8,128)S(1)}, u32[]{:S(2)}, u32[]{:S(2)}) collective-permute-start(s32[200,128]{1,0:T(8,128)S(1)} %get-tuple-element.47), channel_id=1, source_target_pairs={{0,8},{8,0},{16,24},{24,16},{1,9},{9,1},{17,25},{25,17},{2,10},{10... | collective-permute-start | bytes 307208 | tf_op jit(solution)/shard_map/ppermute | solution.py:720
  67.4 11.3 %collective-permute-start.17 = (s32[200,128]{1,0:T(8,128)S(1)}, s32[200,128]{1,0:T(8,128)S(1)}, u32[]{:S(2)}, u32[]{:S(2)}) collective-permute-start(s32[200,128]{1,0:T(8,128)S(1)} %get-tuple-element.48), channel_id=1, source_target_pairs={{0,16},{8,24},{16,0},{24,8},{1,17},{9,25},{17,1},{25,9},{2,18},{10... | collective-permute-start | bytes 307208 | tf_op jit(solution)/shard_map/ppermute | solution.py:720
  68.0 10.7 %collective-permute-start.18 = (s32[200,128]{1,0:T(8,128)S(1)}, s32[200,128]{1,0:T(8,128)S(1)}, u32[]{:S(2)}, u32[]{:S(2)}) collective-permute-start(s32[200,128]{1,0:T(8,128)S(1)} %get-tuple-element.49), channel_id=1, source_target_pairs={{0,24},{8,16},{16,8},{24,0},{1,25},{9,17},{17,9},{25,1},{2,26},{10... | collective-permute-start | bytes 307208 | tf_op jit(solution)/shard_map/ppermute | solution.py:720
  69.9 12.7 %collective-permute-start.11 = (s32[200,128]{1,0:T(8,128)S(1)}, s32[200,128]{1,0:T(8,128)S(1)}, u32[]{:S(2)}, u32[]{:S(2)}) collective-permute-start(s32[200,128]{1,0:T(8,128)S(1)} %get-tuple-element.41), channel_id=1, source_target_pairs={{0,8},{8,0},{16,24},{24,16},{1,9},{9,1},{17,25},{25,17},{2,10},{10... | collective-permute-start | bytes 307208 | tf_op jit(solution)/shard_map/ppermute | solution.py:720
  71.0 15.1 %collective-permute-start.12 = (s32[200,128]{1,0:T(8,128)S(1)}, s32[200,128]{1,0:T(8,128)S(1)}, u32[]{:S(2)}, u32[]{:S(2)}) collective-permute-start(s32[200,128]{1,0:T(8,128)S(1)} %get-tuple-element.42), channel_id=1, source_target_pairs={{0,16},{8,24},{16,0},{24,8},{1,17},{9,25},{17,1},{25,9},{2,18},{10... | collective-permute-start | bytes 307208 | tf_op jit(solution)/shard_map/ppermute | solution.py:720
  72.4 13.6 %collective-permute-start.13 = (s32[200,128]{1,0:T(8,128)S(1)}, s32[200,128]{1,0:T(8,128)S(1)}, u32[]{:S(2)}, u32[]{:S(2)}) collective-permute-start(s32[200,128]{1,0:T(8,128)S(1)} %get-tuple-element.43), channel_id=1, source_target_pairs={{0,24},{8,16},{16,8},{24,0},{1,25},{9,17},{17,9},{25,1},{2,26},{10... | collective-permute-start | bytes 307208 | tf_op jit(solution)/shard_map/ppermute | solution.py:720
  79.8 10.1 %collective-permute-start.19 = (s32[72,640]{1,0:T(8,128)S(1)}, s32[72,640]{1,0:T(8,128)S(1)}, u32[]{:S(2)}, u32[]{:S(2)}) collective-permute-start(s32[72,640]{1,0:T(8,128)S(1)} %get-tuple-element.51), channel_id=1, source_target_pairs={{0,1},{1,2},{2,3},{3,4},{4,5},{5,6},{6,7},{8,9},{9,10},{10,11},{11... | collective-permute-start | bytes 552968 | tf_op jit(solution)/shard_map/ppermute | solution.py:729
  81.2 8.7 %collective-permute-start.20 = (s32[72,640]{1,0:T(8,128)S(1)}, s32[72,640]{1,0:T(8,128)S(1)}, u32[]{:S(2)}, u32[]{:S(2)}) collective-permute-start(s32[72,640]{1,0:T(8,128)S(1)} %get-tuple-element.51), channel_id=1, source_target_pairs={{1,0},{2,1},{3,2},{4,3},{5,4},{6,5},{7,6},{9,8},{10,9},{11,10},{12... | collective-permute-start | bytes 552968 | tf_op jit(solution)/shard_map/ppermute | solution.py:730
  87.1 11.8 %collective-permute-start.14 = (s32[72,640]{1,0:T(8,128)S(1)}, s32[72,640]{1,0:T(8,128)S(1)}, u32[]{:S(2)}, u32[]{:S(2)}) collective-permute-start(s32[72,640]{1,0:T(8,128)S(1)} %get-tuple-element.45), channel_id=1, source_target_pairs={{0,1},{1,2},{2,3},{3,4},{4,5},{5,6},{6,7},{8,9},{9,10},{10,11},{11... | collective-permute-start | bytes 552968 | tf_op jit(solution)/shard_map/ppermute | solution.py:729
  88.4 10.5 %collective-permute-start.15 = (s32[72,640]{1,0:T(8,128)S(1)}, s32[72,640]{1,0:T(8,128)S(1)}, u32[]{:S(2)}, u32[]{:S(2)}) collective-permute-start(s32[72,640]{1,0:T(8,128)S(1)} %get-tuple-element.45), channel_id=1, source_target_pairs={{1,0},{2,1},{3,2},{4,3},{5,4},{6,5},{7,6},{9,8},{10,9},{11,10},{12... | collective-permute-start | bytes 552968 | tf_op jit(solution)/shard_map/ppermute | solution.py:730
  93.4 16.4 %collective-permute-start.24 = (s32[72,640]{1,0:T(8,128)S(1)}, s32[72,640]{1,0:T(8,128)}, u32[]{:S(2)}, u32[]{:S(2)}) collective-permute-start(s32[72,640]{1,0:T(8,128)S(1)} %pull_back.3.rest_1_), channel_id=1, source_target_pairs={{0,16},{8,24},{16,0},{24,8},{1,17},{9,25},{17,1},{25,9},{2,18},{10... | collective-permute-start | bytes 552968 | tf_op jit(solution)/shard_map/ppermute | solution.py:720
  98.9 18.5 %collective-permute-start.22 = (s32[72,640]{1,0:T(8,128)S(1)}, s32[72,640]{1,0:T(8,128)S(1)}, u32[]{:S(2)}, u32[]{:S(2)}) collective-permute-start(s32[72,640]{1,0:T(8,128)S(1)} %pull_back.3.rest_1_), channel_id=1, source_target_pairs={{0,8},{8,0},{16,24},{24,16},{1,9},{9,1},{17,25},{25,17},{2,10},{10... | collective-permute-start | bytes 552968 | tf_op jit(solution)/shard_map/ppermute | solution.py:720
  102.4 15.1 %collective-permute-start.21 = (s32[72,640]{1,0:T(8,128)S(1)}, s32[72,640]{1,0:T(8,128)S(1)}, u32[]{:S(2)}, u32[]{:S(2)}) collective-permute-start(s32[72,640]{1,0:T(8,128)S(1)} %pull_back.2.rest_0_), channel_id=1, source_target_pairs={{0,8},{8,0},{16,24},{24,16},{1,9},{9,1},{17,25},{25,17},{2,10},{10... | collective-permute-start | bytes 552968 | tf_op jit(solution)/shard_map/ppermute | solution.py:720
  104.5 10.0 %collective-permute-start.23 = (s32[72,640]{1,0:T(8,128)S(1)}, s32[72,640]{1,0:T(8,128)}, u32[]{:S(2)}, u32[]{:S(2)}) collective-permute-start(s32[72,640]{1,0:T(8,128)S(1)} %pull_back.2.rest_0_), channel_id=1, source_target_pairs={{0,16},{8,24},{16,0},{24,8},{1,17},{9,25},{17,1},{25,9},{2,18},{10... | collective-permute-start | bytes 552968 | tf_op jit(solution)/shard_map/ppermute | solution.py:720
  109.7 12.1 %collective-permute-start.26 = (s32[72,640]{1,0:T(8,128)}, s32[72,640]{1,0:T(8,128)S(1)}, u32[]{:S(2)}, u32[]{:S(2)}) collective-permute-start(s32[72,640]{1,0:T(8,128)} %collective-permute-done.24.rest_1_), channel_id=1, source_target_pairs={{0,8},{8,0},{16,24},{24,16},{1,9},{9,1},{17,25},{25,17},{2,10},{10... | collective-permute-start | bytes 552968 | tf_op jit(solution)/shard_map/ppermute | solution.py:720
  114.5 8.9 %collective-permute-start.25 = (s32[72,640]{1,0:T(8,128)}, s32[72,640]{1,0:T(8,128)S(1)}, u32[]{:S(2)}, u32[]{:S(2)}) collective-permute-start(s32[72,640]{1,0:T(8,128)} %collective-permute-done.23.rest_0_), channel_id=1, source_target_pairs={{0,8},{8,0},{16,24},{24,16},{1,9},{9,1},{17,25},{25,17},{2,10},{10... | collective-permute-start | bytes 552968 | tf_op jit(solution)/shard_map/ppermute | solution.py:720
  127.1 6.0 %collective-permute-start.28 = (f32[8,256]{1,0:T(8,128)S(1)}, f32[8,256]{1,0:T(8,128)S(1)}, u32[]{:S(2)}, u32[]{:S(2)}) collective-permute-start(f32[8,256]{1,0:T(8,128)S(1)} %add.186), channel_id=1, source_target_pairs={{0,2},{1,3},{2,0},{3,1},{4,6},{5,7},{6,4},{7,5},{8,10},{9,11},{10,... | collective-permute-start | bytes 24584 | tf_op jit(solution)/shard_map/ppermute | solution.py:720
  (16 other events, 114.3 us)

commit v5 on v4

--- a/solution.py
+++ b/solution.py
@@ -177,19 +177,20 @@
     )(field, counts)
 
 
-def lat_mix(weights_ref, window_ref, k, week, before_ref, own_ref, after_ref, scales):
+def lat_mix(side_ref, weights_ref, window_ref, k, week, pair_ref, own_ref, cross_ref, scales):
     rhs, weeks, rows, lon = own_ref.shape
     half = rows // 2
-    for base, ref, scale in ((0, before_ref, scales[0]), (2 * rows, after_ref, scales[1])):
+    before = 2 * rows * (1 - side_ref[0])
+    for base, ref, scale in (
+        (before, pair_ref, scales[0]),
+        (2 * rows - before, cross_ref, scales[1]),
+    ):
         for start in range(0, half, SUBLANES):
             at = (k * weeks + week) * half + start
             word = ref[at : at + SUBLANES, :]
-            window_ref[base + start : base + start + SUBLANES, :] = (
-                high_of(word).astype(jnp.float32) * scale
-            )
-            window_ref[base + half + start : base + half + start + SUBLANES, :] = (
-                low_of(word).astype(jnp.float32) * scale
-            )
+            for to, number in ((start, high_of(word)), (half + start, low_of(word))):
+                to = pl.multiple_of(base + to, SUBLANES)
+                window_ref[pl.ds(to, SUBLANES), :] = number.astype(jnp.float32) * scale
     window_ref[rows : 2 * rows, :] = own_ref[k, week]
     return jnp.dot(
         weights_ref[...],
@@ -199,16 +200,16 @@
     )
 
 
-def spread_lat_kernel(slots, own_ref, before_ref, after_ref, weights_ref, hot_ref, *rest):
+def spread_lat_kernel(slots, side_ref, own_ref, pair_ref, cross_ref, weights_ref, hot_ref, *rest):
     picks, (window_ref, cells_ref) = rest[:slots], rest[slots:]
     rhs, weeks, rows, lon = own_ref.shape
-    body = before_ref.shape[0] - SUBLANES
+    body = pair_ref.shape[0] - SUBLANES
     parts = lon // LANES
     for k in range(rhs):
-        scales = word_scale(before_ref, body, k), word_scale(after_ref, body, k)
+        scales = word_scale(pair_ref, body, k), word_scale(cross_ref, body, k)
         for week in range(weeks):
             mixed = lat_mix(
-                weights_ref, window_ref, k, week, before_ref, own_ref, after_ref, scales
+                side_ref, weights_ref, window_ref, k, week, pair_ref, own_ref, cross_ref, scales
             )
             for part in range(parts):
                 at = (week * parts + part) * rows
@@ -223,12 +224,12 @@
             picks[slot][k] = found[:, k * LANES : (k + 1) * LANES]
 
 
-def spread_lat(own, before, after, weights, hot):
+def spread_lat(side, own, pair, cross, weights, hot):
     rhs, weeks, rows, lon = own.shape
     slots, blocks, cols = hot.shape
     return pl.pallas_call(
         functools.partial(spread_lat_kernel, slots),
-        in_specs=in_vmem(5),
+        in_specs=[pl.BlockSpec(memory_space=pltpu.SMEM)] + in_vmem(5),
         out_specs=in_vmem(slots),
         out_shape=[jax.ShapeDtypeStruct((rhs, blocks, LANES), jnp.bfloat16)] * slots,
         scratch_shapes=[
@@ -238,7 +239,7 @@
         compiler_params=params(10),
         cost_estimate=cost(rhs * slots * blocks * cols * LANES * 2, rhs * weeks * rows * lon * 10),
         name="spread_lat",
-    )(own, before, after, weights, hot)
+    )(side, own, pair, cross, weights, hot)
 
 
 def chunk_of(count, most):
@@ -447,26 +448,26 @@
 
 
 def pull_back_kernel(
-    own_ref, before_ref, after_ref, weights_ref, count_ref, word_ref, window_ref, field_ref
+    side_ref, own_ref, pair_ref, cross_ref, weights_ref, count_ref, word_ref, window_ref, field_ref
 ):
     rhs, weeks, rows, lon = own_ref.shape
-    body = before_ref.shape[0] - SUBLANES
+    body = pair_ref.shape[0] - SUBLANES
     for k in range(rhs):
-        scales = word_scale(before_ref, body, k), word_scale(after_ref, body, k)
+        scales = word_scale(pair_ref, body, k), word_scale(cross_ref, body, k)
         for week in range(weeks):
             field_ref[k, week] = lat_mix(
-                weights_ref, window_ref, k, week, before_ref, own_ref, after_ref, scales
+                side_ref, weights_ref, window_ref, k, week, pair_ref, own_ref, cross_ref, scales
             )
     pack_field(field_ref, word_ref, lon_field(field_ref, count_ref, field_ref))
 
 
-def pull_back(own, before, after, weights, counts):
+def pull_back(side, own, pair, cross, weights, counts):
     rhs, weeks, rows, lon = own.shape
     return pl.pallas_call(
         pull_back_kernel,
-        in_specs=in_vmem(5),
+        in_specs=[pl.BlockSpec(memory_space=pltpu.SMEM)] + in_vmem(5),
         out_specs=pl.BlockSpec(memory_space=pltpu.VMEM),
-        out_shape=jax.ShapeDtypeStruct(before.shape, jnp.int32),
+        out_shape=jax.ShapeDtypeStruct(pair.shape, jnp.int32),
         scratch_shapes=[
             pltpu.VMEM((3 * rows, lon), jnp.float32),
             pltpu.VMEM((rhs, weeks, rows, lon), jnp.float32),
@@ -474,18 +475,16 @@
         compiler_params=params(8),
         cost_estimate=cost(rhs * weeks * rows * lon * 300, rhs * weeks * rows * lon * 10),
         name="pull_back",
-    )(own, before, after, weights, counts)
-
-
-def gram_kernel(with_old, places, count, rhs, order_ref, sums_before, residual_ref, direction_ref, *rest):
-    words, rest = rest[:count], rest[count:]
-    news, gram_ref, sums_ref = rest[-count - 2 : -2], rest[-2], rest[-1]
-    olds = rest[: -count - 2]
+    )(side, own, pair, cross, weights, counts)
+
+
+def gram_kernel(places, count, rhs, order_ref, sums_before, residual_ref, direction_ref, *rest):
+    words, (image_ref, gram_ref, sums_ref) = rest[:count], rest[-3:]
     rhs_count, weeks, rows, lon = direction_ref.shape
     half = rows // 2
     body = words[0].shape[0] - SUBLANES
-    old_places, new_places = places[: len(olds)], places[len(olds) :]
-    for word_ref, new_ref, place in zip(words, news, new_places):
+    old_places, new_places = places[:-count], places[-count:]
+    for word_ref, place in zip(words, new_places):
         for k in range(rhs):
             index = order_ref[place] + k
             scale = word_scale(word_ref, body, k)
@@ -495,7 +494,7 @@
                     at = pl.multiple_of((k * weeks + week) * half + start, SUBLANES)
                     word = word_ref[pl.ds(at, SUBLANES), :]
                     for base, number in ((start, high_of(word)), (half + start, low_of(word))):
-                        new_ref[k, week, base : base + SUBLANES, :] = (
+                        image_ref[index, week, base : base + SUBLANES, :] = (
                             direction_ref[index, week, base : base + SUBLANES, :]
                             + number.astype(jnp.float32) * scale
                         )
@@ -533,20 +532,19 @@
                         at = (index * rhs_count + row_at) * rhs_count + column_at
                         sums_ref[pl.ds(at, 1), :] = lanes
 
-    def listed(refs, places):
-        return [
-            (ref, k, order_ref[place] + k) for ref, place in zip(refs, places) for k in range(rhs)
-        ]
+    def listed(places):
+        found = [order_ref[place] + k for place in places for k in range(rhs)]
+        return [(image_ref, index, index) for index in found]
 
     residuals = [(residual_ref, k, k) for k in range(rhs_count)]
     directions = [(direction_ref, k, k) for k in range(rhs_count)]
-    images = listed(news, new_places)
-    if with_old:
+    images = listed(new_places)
+    if not old_places:
         for a in range(rhs_count):
             tile([(0, residuals[a : a + 1], residuals[a:], True)])
     for b in range(0, len(images), 2):
         right = images[b : b + 2]
-        left = images[: b + len(right)] + listed(olds, old_places)
+        left = images[: b + len(right)] + listed(old_places)
         tile([(1, directions, right, False), (2, residuals, right, False), (3, left, right, True)])
 
     gram_ref[...] = sums_before[...] + lax.dot_general(
@@ -558,23 +556,25 @@
     )
 
 
-def grams(order, places, sums, residual, direction, words, olds, with_old):
+def grams(order, places, sums, residual, direction, words, images):
     rhs_count, weeks, rows, lon = direction.shape
     total = 4 * rhs_count**2
     rhs = (words[0].shape[0] - SUBLANES) * 2 // (weeks * rows)
     count = len(words)
-    found = pl.pallas_call(
-        functools.partial(gram_kernel, with_old, places, count, rhs),
-        in_specs=[pl.BlockSpec(memory_space=pltpu.SMEM)] + in_vmem(3 + count + len(olds)),
-        out_specs=in_vmem(count + 1),
-        out_shape=[jax.ShapeDtypeStruct((rhs, weeks, rows, lon), jnp.float32)] * count
-        + [jax.ShapeDtypeStruct((SUBLANES, total), jnp.float32)],
+    return pl.pallas_call(
+        functools.partial(gram_kernel, places, count, rhs),
+        in_specs=[pl.BlockSpec(memory_space=pltpu.SMEM)] + in_vmem(3 + count + len(images)),
+        out_specs=in_vmem(2),
+        out_shape=[
+            jax.ShapeDtypeStruct(direction.shape, jnp.float32),
+            jax.ShapeDtypeStruct((SUBLANES, total), jnp.float32),
+        ],
         scratch_shapes=[pltpu.VMEM((total, LANES), jnp.float32)],
+        input_output_aliases={4 + count: 0} if images else {},
         compiler_params=params(14),
         cost_estimate=cost(8 * rhs_count * direction.size, 16 * direction.size),
         name="grams",
-    )(order, sums, residual, direction, *words, *olds)
-    return list(found[:-1]), found[-1]
+    )(order, sums, residual, direction, *words, *images)
 
 
 def small_product(left, right):
@@ -605,113 +605,104 @@
     ]
 
 
-def solve_steps(sums_ref, coef_ref):
+def solve_steps(sums_ref):
     total = sums_ref.shape[1]
     size = SUBLANES
     place = lax.broadcasted_iota(jnp.int32, (size, total), 1)
     line = lax.broadcasted_iota(jnp.int32, (size, total), 0)
     spot = lax.broadcasted_iota(jnp.int32, (total, LANES), 0)
     lane = lax.broadcasted_iota(jnp.int32, (total, LANES), 1)
-    to_column = jnp.where(spot % size == lane, 1.0, 0.0)
     sums = sums_ref[...]
 
-    def matrix(index):
-        rows = jnp.where(place // size == index * size + line, sums, 0.0)
-        return jnp.dot(rows, to_column, precision=HIGHEST, preferred_element_type=jnp.float32)
-
-    gram_old, curvature, mixed, gram_image = [matrix(index) for index in range(4)]
-    curvature = 0.5 * (curvature + small_transpose(curvature))
+    def matrix(index, turned=False):
+        row, column = place % size, spot // size % size
+        if not turned:
+            row, column = place // size % size, spot % size
+        here = (place // size**2 == index) & (row == line)
+        return jnp.dot(
+            jnp.where(here, sums, 0.0),
+            jnp.where(column == lane, 1.0, 0.0),
+            precision=HIGHEST,
+            preferred_element_type=jnp.float32,
+        )
+
+    gram_old, gram_image = matrix(0), matrix(3)
+    curvature = 0.5 * (matrix(1) + matrix(1, True))
+    mixed, mixed_turned = matrix(2), matrix(2, True)
     diagonal = lax.broadcasted_iota(jnp.int32, (size, LANES), 0)
     identity = jnp.where(diagonal == lax.broadcasted_iota(jnp.int32, (size, LANES), 1), 1.0, 0.0)
     step, old_inverse = small_solves([(curvature, gram_old), (gram_old, identity)])
-    cross = small_product(mixed, step)
-    both = small_product(small_transpose(step), small_product(gram_image, step))
-    gram_new = gram_old - cross - small_transpose(cross) + both
-    turn = small_product(old_inverse, gram_new)
-    for index, matrix in enumerate((step, turn)):
-        for b in range(size):
-            for a in range(size):
-                at = ((index * size + b) * size + a) * SUBLANES
-                coef_ref[at : at + SUBLANES, :] = jnp.broadcast_to(
-                    matrix[b : b + 1, a : a + 1], (SUBLANES, LANES)
-                )
-
-
-def summed_slots(terms, rhs):
-    parts = [
-        functools.reduce(lambda left, right: left + right, terms[at : at + rhs])
-        for at in range(0, len(terms), rhs)
+    step_turned = small_transpose(step)
+    rest = small_product(gram_image, step) - mixed_turned
+    gram_new = gram_old - small_product(mixed, step) + small_product(step_turned, rest)
+    return step_turned, small_product(gram_new, old_inverse)
+
+
+def spread_coefficients(turned):
+    size = SUBLANES
+    wide = 4 * size**2
+    lane = lax.broadcasted_iota(jnp.int32, (size, wide), 1)
+    line = lax.broadcasted_iota(jnp.int32, (size, wide), 0)
+    spread = jnp.zeros((size, wide), jnp.float32)
+    for b in range(size):
+        column = jnp.broadcast_to(turned[:, b : b + 1], (size, wide))
+        spread = spread + jnp.where(lane // size % size == b, column, 0.0)
+    high = spread.astype(jnp.bfloat16).astype(jnp.float32)
+    spread = jnp.where(lane < 2 * size**2, high, spread - high)
+    own = (lane % size == line) & (lane < 3 * size**2)
+    rows = [
+        jnp.where(own, jnp.broadcast_to(spread[a : a + 1], (size, wide)), 0.0) for a in range(size)
     ]
-    while len(parts) > 1:
-        parts = [left + right for left, right in zip(parts[::2], parts[1::2])]
-    return parts[0]
+    return jnp.concatenate(rows, axis=0)
+
+
+def split_rows(ref, row):
+    value = jnp.concatenate([ref[b, 0, row : row + SUBLANES, :] for b in range(ref.shape[0])], axis=0)
+    high = value.astype(jnp.bfloat16)
+    low = (value - high.astype(jnp.float32)).astype(jnp.bfloat16)
+    return jnp.concatenate([high, low, high], axis=0)
 
 
 def update_kernel(
-    order_ref, sums_ref, solution_ref, residual_ref, direction_ref, *rest
+    sums_ref, solution_ref, residual_ref, direction_ref, image_ref, sol_out, res_out, dir_out, coef_ref
 ):
-    images, (sol_out, res_out, dir_out, coef_ref) = rest[:-4], rest[-4:]
     rhs_count, _, rows, lon = direction_ref.shape
-    rhs = images[0].shape[0]
-
-    @pl.when((pl.program_id(0) == 0) & (pl.program_id(1) == 0))
+    size = rhs_count * SUBLANES
+
+    @pl.when(pl.program_id(0) == 0)
     def _():
-        solve_steps(sums_ref, coef_ref)
-
-    def coef(index, b, a):
-        at = ((index * rhs_count + b) * rhs_count + a) * SUBLANES
-        return coef_ref[pl.ds(pl.multiple_of(at, SUBLANES), SUBLANES), :]
-
-    natural = [order_ref[slot] + k for slot in range(len(images)) for k in range(rhs)]
-
-    def one_group(group, carry):
-        at = pl.multiple_of(group * SUBLANES, SUBLANES)
-        for lane in range(0, lon, LANES):
-            spot = (0, pl.ds(at, SUBLANES), slice(lane, lane + LANES))
-            directions = [direction_ref[(b, *spot)] for b in range(rhs_count)]
-            image = [ref[(k, *spot)] for ref in images for k in range(rhs)]
-            for a in range(rhs_count):
-                moved = solution_ref[(a, *spot)]
-                left = residual_ref[(a, *spot)]
-                for b in range(rhs_count):
-                    moved = moved + coef(0, b, a) * directions[b]
-                left = left - summed_slots(
-                    [coef(0, natural[b], a) * image[b] for b in range(rhs_count)], rhs
-                )
-                sol_out[(a, *spot)] = moved
-                res_out[(a, *spot)] = left
-                for b in range(rhs_count):
-                    left = left + coef(1, b, a) * directions[b]
-                dir_out[(a, *spot)] = left
-        return carry
-
-    lax.fori_loop(0, rows // SUBLANES, one_group, 0)
-
-
-def update(order, sums, solution, residual, direction, images):
+        step_turned, turn_turned = solve_steps(sums_ref)
+        coefs = [spread_coefficients(step_turned), spread_coefficients(turn_turned)]
+        coef_ref[...] = jnp.concatenate(coefs, axis=0).astype(jnp.bfloat16)
+
+    for row in range(0, rows, SUBLANES):
+        coefs = coef_ref[:, : 3 * size]
+        moves = jnp.dot(coefs, split_rows(direction_ref, row), preferred_element_type=jnp.float32)
+        drops = jnp.dot(coefs[:size], split_rows(image_ref, row), preferred_element_type=jnp.float32)
+        for a in range(rhs_count):
+            at = a * SUBLANES
+            spot = (a, 0, slice(row, row + SUBLANES), slice(None))
+            sol_out[spot] = solution_ref[spot] + moves[at : at + SUBLANES]
+            left = residual_ref[spot] - drops[at : at + SUBLANES]
+            res_out[spot] = left
+            dir_out[spot] = left + moves[size + at : size + at + SUBLANES]
+
+
+def update(sums, solution, residual, direction, image):
     rhs_count, weeks, rows, lon = direction.shape
-    half = rows // 2
-
-    def field(rhs):
-        return pl.BlockSpec((rhs, 1, half, lon), lambda w, h, _: (0, w, h, 0))
-
+    field = pl.BlockSpec((rhs_count, 1, rows, lon), lambda w: (0, w, 0, 0))
     shape = jax.ShapeDtypeStruct(direction.shape, jnp.float32)
     return pl.pallas_call(
         update_kernel,
-        grid_spec=pltpu.PrefetchScalarGridSpec(
-            num_scalar_prefetch=1,
-            grid=(weeks, 2),
-            in_specs=[whole(sums.shape)]
-            + [field(rhs_count)] * 3
-            + [field(image.shape[0]) for image in images],
-            out_specs=[field(rhs_count)] * 3,
-            scratch_shapes=[pltpu.VMEM((2 * rhs_count**2 * SUBLANES, LANES), jnp.float32)],
-        ),
+        grid=(weeks,),
+        in_specs=[whole(sums.shape)] + [field] * 4,
+        out_specs=[field] * 3,
+        scratch_shapes=[pltpu.VMEM((2 * rhs_count * SUBLANES, 4 * rhs_count * SUBLANES), jnp.bfloat16)],
         out_shape=[shape] * 3,
-        compiler_params=params(10),
+        compiler_params=params(16),
         cost_estimate=cost(6 * rhs_count * direction.size, 28 * direction.size),
         name="update",
-    )(order, sums, solution, residual, direction, *images)
+    )(sums, solution, residual, direction, image)
 
 
 def crossed(value, axis, by):
@@ -726,9 +717,9 @@
 
 def neighbours(value, axis):
     size = lax.axis_size(axis)
-    before = lax.ppermute(value, axis, [(i, i + 1) for i in range(size - 1)])
-    after = lax.ppermute(value, axis, [(i + 1, i) for i in range(size - 1)])
-    return before, after
+    outer = [(i, i + 1) for i in range(1, size - 1, 2)]
+    outer += [(after, before) for before, after in outer]
+    return crossed(value, axis, 1), lax.ppermute(value, axis, outer)
 
 
 def summed_over(value, axis):
@@ -810,8 +801,9 @@
     hot = (places[:, :, None] == jnp.arange(cols)[None, None, :]).astype(jnp.bfloat16)
     hot_turned = (jnp.arange(cols)[:, None] == places.reshape(1, -1)).astype(jnp.bfloat16)
     lat_spread, lat_pulled = lat_windows(lat_width, band, rows)
-
-    picks = spread_lat(lon_own, *halo, lat_spread, hot)
+    side = (band % 2).astype(jnp.int32).reshape(1)
+
+    picks = spread_lat(side, lon_own, *halo, lat_spread, hot)
     cells = [crossed(picks[d], "obs", d) for d in range(slots)]
     kept = count // KEPT_OF * KEPT if count % KEPT_OF == 0 else 0
     stays = [preload(blocks, 0, kept, picks[0])] if kept else []
@@ -828,38 +820,35 @@
     own = []
     for group in range(groups):
         field, words = gather_cells(hot_turned, sent[group], each, weeks, rows, lon)
-        own.append(pull_back(field, *neighbours(words, "lat"), lat_pulled, counts))
+        own.append(pull_back(side, field, *neighbours(words, "lat"), lat_pulled, counts))
 
     starts = (order[:, None] + jnp.arange(groups, dtype=jnp.int32) * each).reshape(-1)
     products = jnp.zeros((SUBLANES, 4 * rhs_count**2), jnp.float32)
-    done, places = {}, ()
+    images, places = [], ()
 
     def add_products(slot):
-        nonlocal products, places
+        nonlocal products, places, images
         words = [arrived[group][slot] for group in range(groups)]
         places += tuple(slot * groups + group for group in range(groups))
-        olds = [image for images in done.values() for image in images]
-        done[slot], products = grams(
-            starts, places, products, residual, direction, words, olds, slot == 0
-        )
+        *images, products = grams(starts, places, products, residual, direction, words, images)
 
     arrived = [{0: words} for words in own]
     for group in range(groups):
         for reach in far_first(slots):
             arrived[group][reach] = crossed(own[group], "obs", reach)
     add_products(0)
+    first_products = products
     for reach in far_first(slots)[1:]:
         for group in range(groups):
             for bits in [bits for bits in arrived[group] if bits > reach and not bits % (2 * reach)]:
                 words = arrived[group][bits]
                 if group == groups - 1:
-                    words, _ = lax.optimization_barrier((words, done[0][0]))
+                    words, _ = lax.optimization_barrier((words, first_products))
                 arrived[group][bits | reach] = crossed(words, "obs", reach)
     for slot in range(1, slots):
         add_products(slot)
     products, _ = summed_over(products, "lat")
-    images = [image for slot in range(slots) for image in done[slot]]
-    return tuple(update(starts, products, solution, residual, direction, images))
+    return tuple(update(products, solution, residual, direction, *images))
 
 
 def solution(mesh):

time: 148 us -> 139 us (0.939)
  starting transfers between devices: 54.9 us -> 51.4 us
  waiting for transfers between devices: 29.8 us -> 26.8 us
  Pallas kernels: 53.6 us -> 50.9 us
    ppermute x6 -> x3, starting transfers between devices: 9.17 us -> 2.33 us  [neighbours(): return (crossed(value, axis, 1), lax.ppermute(value, axis, outer))]
    ppermute x24 -> x27, starting transfers between devices: 45.7 us -> 49.1 us  [crossed(): lax.ppermute(value, axis, [(i, i ^ by) for i in range(lax.axis_size(axis))])]
    ppermute x24 -> x27, waiting for transfers between devices: 29.8 us -> 26.8 us  [crossed(): lax.ppermute(value, axis, [(i, i ^ by) for i in range(lax.axis_size(axis))])]
    pallas_call x8, Pallas kernels: 27.7 us -> 25 us  [the longest x4 9.61 us: grams(): pl.pallas_call(functools.partial(gram_kernel, places, count, rhs), in_spe...]
  transfers between devices with their start and end apart: 30 -> 30, of which waited for: 13 -> 12; matrix products, arithmetic and copies ran while one was open for 2% -> 2% of each run, Pallas kernels for 18% -> 20%
where the time goes in v5:
time: 139 us
  starting transfers between devices  51.4 us (37%)
  Pallas kernels  50.9 us (37%)
  waiting for transfers between devices  26.8 us (19%)
  local copies, waits for them, and re-layouts  5.64 us (4%)
  other arithmetic  2.95 us (2%)
    ppermute x27, starting transfers between devices, crossed(): lax.ppermute(value, axis, [(i, i ^ by) for i in range(lax.axis_size(axis))])  49.1 us
    ppermute x27, waiting for transfers between devices, crossed(): lax.ppermute(value, axis, [(i, i ^ by) for i in range(lax.axis_size(axis))])  26.8 us
    pallas_call x3, Pallas kernels, preload(): pl.pallas_call(functools.partial(preload_kernel, first), in_specs=[pl.Blo...  11.1 us
    pallas_call x4, Pallas kernels, grams(): pl.pallas_call(functools.partial(gram_kernel, places, count, rhs), in_spe...  9.61 us
    pallas_call x2, Pallas kernels, pull_back(): pl.pallas_call(pull_back_kernel, in_specs=[pl.BlockSpec(memory_space=pltp...  6.97 us
    pallas_call x1, Pallas kernels, update(): pl.pallas_call(update_kernel, grid=(weeks,), in_specs=[whole(sums.shape)]...  6.39 us
    pallas_call x1, Pallas kernels, forward(): pl.pallas_call(functools.partial(forward_kernel, len(pieces)), in_specs=[...  4.76 us
    pallas_call x1, Pallas kernels, spread_lon(): pl.pallas_call(spread_lon_kernel, in_specs=in_vmem(2), out_specs=in_vmem(...  4.72 us
  transfers between devices with their start and end apart: 30, of which 12 were waited for; matrix products, arithmetic and copies ran while one was open for 2% of the time, Pallas kernels for 20%

profile of v5, /device:TPU:0, one launch (start us, length us, event | category | flops | bytes accessed | tf_op | source)
XLA Modules:
  0.0 138.7 jit_solution(9561441464697042505)
XLA Ops:
  2.6 4.7 %spread_lon.1 = (f32[2,4,32,640]{3,2,1,0:T(8,128)S(1)}, s32[136,640]{1,0:T(8,128)S(1)}) custom-call(f32[2,4,32,640]{3,2,1,0:T(8,128)S(1)} %constant_dynamic-slice_fusion.field_ref, s32[32,640]{1,0:T(8,128)S(1)} %broadcast_in_dim.21.count_ref), custom_call_target="tpu_custom_call" | custom-call | flops 16384000 | bytes 1638400 | tf_op jit(solution)/shard_map/spread_lon/pallas_call | solution.py:166
  8.5 2.7 %collective-permute-start = (s32[1,1,384]{2,1,0:T(1,128)}, s32[1,1,384]{2,1,0:T(1,128)S(1)}, u32[]{:S(2)}, u32[]{:S(2)}) collective-permute-start(s32[1,1,384]{2,1,0:T(1,128)} %param.12), channel_id=1, source_target_pairs={{0,8},{8,0},{16,24},{24,16},{1,9},{9,1},{17,25},{25,17},{2,10},{10... | collective-permute-start | bytes 4616 | tf_op jit(solution)/shard_map/ppermute | solution.py:711
  11.2 2.6 %collective-permute-start.1 = (s32[1,1,384]{2,1,0:T(1,128)}, s32[1,1,384]{2,1,0:T(1,128)S(1)}, u32[]{:S(2)}, u32[]{:S(2)}) collective-permute-start(s32[1,1,384]{2,1,0:T(1,128)} %param.12), channel_id=1, source_target_pairs={{0,16},{8,24},{16,0},{24,8},{1,17},{9,25},{17,1},{25,9},{2,18},{10... | collective-permute-start | bytes 4616 | tf_op jit(solution)/shard_map/ppermute | solution.py:711
  15.9 3.5 %collective-permute-done.2 = s32[1,1,384]{2,1,0:T(1,128)S(1)} collective-permute-done((s32[1,1,384]{2,1,0:T(1,128)}, s32[1,1,384]{2,1,0:T(1,128)S(1)}, u32[]{:S(2)}, u32[]{:S(2)}) %collective-permute-start.2) | collective-permute-done | bytes 1568 | tf_op jit(solution)/shard_map/ppermute | solution.py:711
  22.7 3.7 %collective-permute-start.7 = (bf16[2,384,128]{2,1,0:T(8,128)(2,1)S(1)}, bf16[2,384,128]{2,1,0:T(8,128)(2,1)S(1)}, u32[]{:S(2)}, u32[]{:S(2)}) collective-permute-start(bf16[2,384,128]{2,1,0:T(8,128)(2,1)S(1)} %get-tuple-element.35), channel_id=1, source_target_pairs={{0,24},{8,16},{16,8},{24,0},{1,25},{9,17},{17,9},{25,1},{2,26},{10... | collective-permute-start | bytes 589832 | tf_op jit(solution)/shard_map/ppermute | solution.py:711
  26.5 2.9 %preload.3.rest_0_ = bf16[192,128,128]{2,1,0:T(8,128)(2,1)S(1)} custom-call(bf16[2,384,128]{2,1,0:T(8,128)(2,1)S(1)} %get-tuple-element.32.after_ref.rest_2_, bf16[384,128,128]{2,1,0:T(8,128)(2,1)} %bitcast.31), custom_call_target="tpu_custom_call" | custom-call | bytes 12582912 | tf_op jit(solution)/shard_map/preload/pallas_call | solution.py:270
  29.4 5.1 %preload.4.rest_1_ = bf16[192,128,128]{2,1,0:T(8,128)(2,1)S(1)} custom-call(bf16[2,384,128]{2,1,0:T(8,128)(2,1)S(1)} %get-tuple-element.32.after_ref.rest_2_, bf16[384,128,128]{2,1,0:T(8,128)(2,1)} %bitcast.32), custom_call_target="tpu_custom_call" | custom-call | bytes 12582912 | tf_op jit(solution)/shard_map/preload/pallas_call | solution.py:270
  36.2 4.8 %forward.1 = f32[256,128]{1,0:T(8,128)S(1)} custom-call(s32[384]{0:T(512)S(1)} %reduce.1.row_ref, f32[384]{0:T(512)S(1)} %exponential_reduce_fusion.scale_ref, bf16[192,128,128]{2,1,0:T(8,128)(2,1)S(1)} %preload.3.rest_0_, bf16[192,128,128]{2,1,0:T(8,128)(2,1)S(1)} %preload.4.rest_1_, bf16[2,384,128]{2,1,0:T(8,128)(2,1)S(1)} %get-tuple-element.32.after_ref.rest_2_, ...), custom_call_target="tpu_custom_call" | custom-call | flops 100663296 | bytes 12582912 | tf_op jit(solution)/shard_map/forward/pallas_call | solution.py:326
  41.0 4.4 %collective-permute-start.8 = (f32[256,128]{1,0:T(8,128)S(1)}, f32[256,128]{1,0:T(8,128)S(1)}, u32[]{:S(2)}, u32[]{:S(2)}) collective-permute-start(f32[256,128]{1,0:T(8,128)S(1)} %forward.1), channel_id=1, source_target_pairs={{0,1},{1,0},{2,3},{3,2},{4,5},{5,4},{6,7},{7,6},{8,9},{9,8},{10,11... | collective-permute-start | bytes 393224 | tf_op jit(solution)/shard_map/ppermute | solution.py:711
  48.7 4.0 %collective-permute-done.9 = f32[256,128]{1,0:T(8,128)S(1)} collective-permute-done((f32[256,128]{1,0:T(8,128)S(1)}, f32[256,128]{1,0:T(8,128)S(1)}, u32[]{:S(2)}, u32[]{:S(2)}) %collective-permute-start.9) | collective-permute-done | bytes 131104 | tf_op jit(solution)/shard_map/ppermute | solution.py:711
  55.0 3.0 %preload.5.rest_1_ = bf16[192,128,128]{2,1,0:T(8,128)(2,1)S(1)} custom-call(f32[256,128]{1,0:T(8,128)S(1)} %add.189.after_ref, bf16[384,128,128]{2,1,0:T(8,128)(2,1)} %bitcast.33), custom_call_target="tpu_custom_call" | custom-call | bytes 12582912 | tf_op jit(solution)/shard_map/preload/pallas_call | solution.py:270
  59.7 3.3 %adjoint.1 = (s32[200,128]{1,0:T(8,128)S(1)}, s32[200,128]{1,0:T(8,128)S(1)}, s32[200,128]{1,0:T(8,128)S(1)}, s32[200,128]{1,0:T(8,128)S(1)}, s32[200,128]{1,0:T...) custom-call(s32[384]{0:T(512)S(1)} %reduce.1.row_ref, ...), custom_call_target="tpu_custom_call" | custom-call | flops 100663296 | bytes 12582912 | tf_op jit(solution)/shard_map/adjoint/pallas_call | solution.py:379
  63.0 2.8 %collective-permute-start.16 = (s32[200,128]{1,0:T(8,128)S(1)}, s32[200,128]{1,0:T(8,128)S(1)}, u32[]{:S(2)}, u32[]{:S(2)}) collective-permute-start(s32[200,128]{1,0:T(8,128)S(1)} %get-tuple-element.43), channel_id=1, source_target_pairs={{0,8},{8,0},{16,24},{24,16},{1,9},{9,1},{17,25},{25,17},{2,10},{10... | collective-permute-start | bytes 307208 | tf_op jit(solution)/shard_map/ppermute | solution.py:711
  73.3 3.8 %collective-permute-done.17.rest_2_ = s32[200,128]{1,0:T(8,128)S(1)} collective-permute-done((s32[200,128]{1,0:T(8,128)S(1)}, s32[200,128]{1,0:T(8,128)S(1)}, u32[]{:S(2)}, u32[]{:S(2)}) %collective-permute-start.17) | collective-permute-done | bytes 102432 | tf_op jit(solution)/shard_map/ppermute | solution.py:711
  79.1 5.5 %collective-permute-done.12.rest_2_ = s32[200,128]{1,0:T(8,128)S(1)} collective-permute-done((s32[200,128]{1,0:T(8,128)S(1)}, s32[200,128]{1,0:T(8,128)S(1)}, u32[]{:S(2)}, u32[]{:S(2)}) %collective-permute-start.12) | collective-permute-done | bytes 102432 | tf_op jit(solution)/shard_map/ppermute | solution.py:711
  86.6 3.5 %pull_back.3.rest_1_ = s32[72,640]{1,0:T(8,128)S(1)} custom-call(s32[1]{0:T(128)} %bitcast.side_ref, f32[1,4,32,640]{3,2,1,0:T(8,128)S(1)} %get-tuple-element.46.own_ref, s32[72,640]{1,0:T(8,128)S(1)} %collective-permute-done.19.pair_ref, s32[72,640]{1,0:T(8,128)S(1)} %collective-permute-done.20.cross_ref, f32[32,96]{1,0:T(8,128)S(1)} %get-tuple-element.61.weights_ref, ...), custom_call_target="tpu_custom_call" | custom-call | flops 24576000 | bytes 819200 | tf_op jit(solution)/shard_map/pull_back/pallas_call | solution.py:466
  90.1 3.6 %collective-permute-start.24 = (s32[72,640]{1,0:T(8,128)S(1)}, s32[72,640]{1,0:T(8,128)S(1)}, u32[]{:S(2)}, u32[]{:S(2)}) collective-permute-start(s32[72,640]{1,0:T(8,128)S(1)} %pull_back.3.rest_1_), channel_id=1, source_target_pairs={{0,16},{8,24},{16,0},{24,8},{1,17},{9,25},{17,1},{25,9},{2,18},{10... | collective-permute-start | bytes 552968 | tf_op jit(solution)/shard_map/ppermute | solution.py:711
  93.7 3.5 %pull_back.2.rest_0_ = s32[72,640]{1,0:T(8,128)S(1)} custom-call(s32[1]{0:T(128)} %bitcast.side_ref, f32[1,4,32,640]{3,2,1,0:T(8,128)S(1)} %get-tuple-element.40.own_ref, s32[72,640]{1,0:T(8,128)S(1)} %collective-permute-done.14.pair_ref, s32[72,640]{1,0:T(8,128)S(1)} %collective-permute-done.15.cross_ref, f32[32,96]{1,0:T(8,128)S(1)} %get-tuple-element.61.weights_ref, ...), custom_call_target="tpu_custom_call" | custom-call | flops 24576000 | bytes 819200 | tf_op jit(solution)/shard_map/pull_back/pallas_call | solution.py:466
  101.8 2.9 %grams.4 = (f32[8,4,32,640]{3,2,1,0:T(8,128)S(1)}, f32[8,256]{1,0:T(8,128)S(1)}) custom-call(s32[8]{0:T(128)S(1)} %add.169.order_ref, f32[8,256]{1,0:T(8,128)S(1)} %broadcast_in_dim.20.sums_before, f32[8,4,32,640]{3,2,1,0:T(8,128)S(1)} %copy-done.1, f32[8,4,32,640]{3,2,1,0:T(8,128)S(1)} %copy-done, s32[72,640]{1,0:T(8,128)S(1)} %pull_back.2.rest_0_, ...), custom_call_target="tpu_custom_call" | custom-call | flops 41943040 | bytes 10485760 | tf_op jit(solution)/shard_map/grams/pallas_call | solution.py:564
  108.3 3.3 %collective-permute-start.25 = (s32[72,640]{1,0:T(8,128)}, s32[72,640]{1,0:T(8,128)S(1)}, u32[]{:S(2)}, u32[]{:S(2)}) collective-permute-start(s32[72,640]{1,0:T(8,128)} %collective-permute-done.23.rest_0_), channel_id=1, source_target_pairs={{0,8},{8,0},{16,24},{24,16},{1,9},{9,1},{17,25},{25,17},{2,10},{10... | collective-permute-start | bytes 552968 | tf_op jit(solution)/shard_map/ppermute | solution.py:711
  119.7 2.4 %collective-permute-start.27 = (f32[8,256]{1,0:T(8,128)S(1)}, f32[8,256]{1,0:T(8,128)S(1)}, u32[]{:S(2)}, u32[]{:S(2)}) collective-permute-start(f32[8,256]{1,0:T(8,128)S(1)} %get-tuple-element.55), channel_id=1, source_target_pairs={{0,1},{1,0},{2,3},{3,2},{4,5},{5,4},{6,7},{7,6},{8,9},{9,8},{10,11... | collective-permute-start | bytes 24584 | tf_op jit(solution)/shard_map/ppermute | solution.py:711
  122.9 3.0 %collective-permute-start.28 = (f32[8,256]{1,0:T(8,128)S(1)}, f32[8,256]{1,0:T(8,128)S(1)}, u32[]{:S(2)}, u32[]{:S(2)}) collective-permute-start(f32[8,256]{1,0:T(8,128)S(1)} %add.191), channel_id=1, source_target_pairs={{0,2},{1,3},{2,0},{3,1},{4,6},{5,7},{6,4},{7,5},{8,10},{9,11},{10,... | collective-permute-start | bytes 24584 | tf_op jit(solution)/shard_map/ppermute | solution.py:711
  127.5 3.2 %collective-permute-start.29 = (f32[8,256]{1,0:T(8,128)S(1)}, f32[8,256]{1,0:T(8,128)S(1)}, u32[]{:S(2)}, u32[]{:S(2)}) collective-permute-start(f32[8,256]{1,0:T(8,128)S(1)} %add.192), channel_id=1, source_target_pairs={{0,4},{1,5},{2,6},{3,7},{4,0},{5,1},{6,2},{7,3},{8,12},{9,13},{10,... | collective-permute-start | bytes 24584 | tf_op jit(solution)/shard_map/ppermute | solution.py:711
  132.3 6.4 %update.1 = (f32[8,4,32,640]{3,2,1,0:T(8,128)}, f32[8,4,32,640]{3,2,1,0:T(8,128)}, f32[8,4,32,640]{3,2,1,0:T(8,128)}) custom-call(f32[8,256]{1,0:T(8,128)S(1)} %add.193.sums_ref, f32[8,4,32,640]{3,2,1,0:T(8,128)S(1)} %copy-done.4, f32[8,4,32,640]{3,2,1,0:T(8,128)S(1)} %copy-done.2, f32[8,4,32,640]{3,2,1,0:T(8,128)S(1)} %copy-done, ...), custom_call_target="tpu_custom_call" | custom-call | flops 31457280 | bytes 18350080 | tf_op jit(solution)/shard_map/update/pallas_call | solution.py:695
  (111 shorter events, 49.3 us)
Async XLA Ops:
  7.3 12.6 %collective-permute-start.3 = (s32[136,640]{1,0:T(8,128)S(1)}, s32[136,640]{1,0:T(8,128)S(1)}, u32[]{:S(2)}, u32[]{:S(2)}) collective-permute-start(s32[136,640]{1,0:T(8,128)S(1)} %get-tuple-element.31), channel_id=1, source_target_pairs={{0,1},{1,0},{2,3},{3,2},{4,5},{5,4},{6,7},{7,6},{8,9},{9,8},{10,11... | collective-permute-start | bytes 1044488 | tf_op jit(solution)/shard_map/ppermute | solution.py:711
  7.8 12.0 %collective-permute-start.4 = (s32[136,640]{1,0:T(8,128)S(1)}, s32[136,640]{1,0:T(8,128)S(1)}, u32[]{:S(2)}, u32[]{:S(2)}) collective-permute-start(s32[136,640]{1,0:T(8,128)S(1)} %get-tuple-element.31), channel_id=1, source_target_pairs={{1,2},{3,4},{5,6},{2,1},{4,3},{6,5},{9,10},{11,12},{13,14},{10,9},... | collective-permute-start | bytes 1044488 | tf_op jit(solution)/shard_map/ppermute | solution.py:722
  8.5 7.1 %collective-permute-start = (s32[1,1,384]{2,1,0:T(1,128)}, s32[1,1,384]{2,1,0:T(1,128)S(1)}, u32[]{:S(2)}, u32[]{:S(2)}) collective-permute-start(s32[1,1,384]{2,1,0:T(1,128)} %param.12), channel_id=1, source_target_pairs={{0,8},{8,0},{16,24},{24,16},{1,9},{9,1},{17,25},{25,17},{2,10},{10... | collective-permute-start | bytes 4616 | tf_op jit(solution)/shard_map/ppermute | solution.py:711
  13.8 5.6 %collective-permute-start.2 = (s32[1,1,384]{2,1,0:T(1,128)}, s32[1,1,384]{2,1,0:T(1,128)S(1)}, u32[]{:S(2)}, u32[]{:S(2)}) collective-permute-start(s32[1,1,384]{2,1,0:T(1,128)} %param.12), channel_id=1, source_target_pairs={{0,24},{8,16},{16,8},{24,0},{1,25},{9,17},{17,9},{25,1},{2,26},{10... | collective-permute-start | bytes 4616 | tf_op jit(solution)/shard_map/ppermute | solution.py:711
  21.9 12.6 %collective-permute-start.5 = (bf16[2,384,128]{2,1,0:T(8,128)(2,1)S(1)}, bf16[2,384,128]{2,1,0:T(8,128)(2,1)S(1)}, u32[]{:S(2)}, u32[]{:S(2)}) collective-permute-start(bf16[2,384,128]{2,1,0:T(8,128)(2,1)S(1)} %get-tuple-element.33), channel_id=1, source_target_pairs={{0,8},{8,0},{16,24},{24,16},{1,9},{9,1},{17,25},{25,17},{2,10},{10... | collective-permute-start | bytes 589832 | tf_op jit(solution)/shard_map/ppermute | solution.py:711
  22.0 12.5 %collective-permute-start.6 = (bf16[2,384,128]{2,1,0:T(8,128)(2,1)S(1)}, bf16[2,384,128]{2,1,0:T(8,128)(2,1)S(1)}, u32[]{:S(2)}, u32[]{:S(2)}) collective-permute-start(bf16[2,384,128]{2,1,0:T(8,128)(2,1)S(1)} %get-tuple-element.34), channel_id=1, source_target_pairs={{0,16},{8,24},{16,0},{24,8},{1,17},{9,25},{17,1},{25,9},{2,18},{10... | collective-permute-start | bytes 589832 | tf_op jit(solution)/shard_map/ppermute | solution.py:711
  22.7 13.5 %collective-permute-start.7 = (bf16[2,384,128]{2,1,0:T(8,128)(2,1)S(1)}, bf16[2,384,128]{2,1,0:T(8,128)(2,1)S(1)}, u32[]{:S(2)}, u32[]{:S(2)}) collective-permute-start(bf16[2,384,128]{2,1,0:T(8,128)(2,1)S(1)} %get-tuple-element.35), channel_id=1, source_target_pairs={{0,24},{8,16},{16,8},{24,0},{1,25},{9,17},{17,9},{25,1},{2,26},{10... | collective-permute-start | bytes 589832 | tf_op jit(solution)/shard_map/ppermute | solution.py:711
  46.4 6.3 %collective-permute-start.9 = (f32[256,128]{1,0:T(8,128)S(1)}, f32[256,128]{1,0:T(8,128)S(1)}, u32[]{:S(2)}, u32[]{:S(2)}) collective-permute-start(f32[256,128]{1,0:T(8,128)S(1)} %add.188), channel_id=1, source_target_pairs={{0,2},{1,3},{2,0},{3,1},{4,6},{5,7},{6,4},{7,5},{8,10},{9,11},{10,... | collective-permute-start | bytes 393224 | tf_op jit(solution)/shard_map/ppermute | solution.py:711
  63.0 8.2 %collective-permute-start.16 = (s32[200,128]{1,0:T(8,128)S(1)}, s32[200,128]{1,0:T(8,128)S(1)}, u32[]{:S(2)}, u32[]{:S(2)}) collective-permute-start(s32[200,128]{1,0:T(8,128)S(1)} %get-tuple-element.43), channel_id=1, source_target_pairs={{0,8},{8,0},{16,24},{24,16},{1,9},{9,1},{17,25},{25,17},{2,10},{10... | collective-permute-start | bytes 307208 | tf_op jit(solution)/shard_map/ppermute | solution.py:711
  65.8 11.3 %collective-permute-start.17 = (s32[200,128]{1,0:T(8,128)S(1)}, s32[200,128]{1,0:T(8,128)S(1)}, u32[]{:S(2)}, u32[]{:S(2)}) collective-permute-start(s32[200,128]{1,0:T(8,128)S(1)} %get-tuple-element.44), channel_id=1, source_target_pairs={{0,16},{8,24},{16,0},{24,8},{1,17},{9,25},{17,1},{25,9},{2,18},{10... | collective-permute-start | bytes 307208 | tf_op jit(solution)/shard_map/ppermute | solution.py:711
  66.8 10.3 %collective-permute-start.18 = (s32[200,128]{1,0:T(8,128)S(1)}, s32[200,128]{1,0:T(8,128)S(1)}, u32[]{:S(2)}, u32[]{:S(2)}) collective-permute-start(s32[200,128]{1,0:T(8,128)S(1)} %get-tuple-element.45), channel_id=1, source_target_pairs={{0,24},{8,16},{16,8},{24,0},{1,25},{9,17},{17,9},{25,1},{2,26},{10... | collective-permute-start | bytes 307208 | tf_op jit(solution)/shard_map/ppermute | solution.py:711
  68.3 10.8 %collective-permute-start.11 = (s32[200,128]{1,0:T(8,128)S(1)}, s32[200,128]{1,0:T(8,128)S(1)}, u32[]{:S(2)}, u32[]{:S(2)}) collective-permute-start(s32[200,128]{1,0:T(8,128)S(1)} %get-tuple-element.37), channel_id=1, source_target_pairs={{0,8},{8,0},{16,24},{24,16},{1,9},{9,1},{17,25},{25,17},{2,10},{10... | collective-permute-start | bytes 307208 | tf_op jit(solution)/shard_map/ppermute | solution.py:711
  69.3 15.3 %collective-permute-start.12 = (s32[200,128]{1,0:T(8,128)S(1)}, s32[200,128]{1,0:T(8,128)S(1)}, u32[]{:S(2)}, u32[]{:S(2)}) collective-permute-start(s32[200,128]{1,0:T(8,128)S(1)} %get-tuple-element.38), channel_id=1, source_target_pairs={{0,16},{8,24},{16,0},{24,8},{1,17},{9,25},{17,1},{25,9},{2,18},{10... | collective-permute-start | bytes 307208 | tf_op jit(solution)/shard_map/ppermute | solution.py:711
  71.2 13.4 %collective-permute-start.13 = (s32[200,128]{1,0:T(8,128)S(1)}, s32[200,128]{1,0:T(8,128)S(1)}, u32[]{:S(2)}, u32[]{:S(2)}) collective-permute-start(s32[200,128]{1,0:T(8,128)S(1)} %get-tuple-element.39), channel_id=1, source_target_pairs={{0,24},{8,16},{16,8},{24,0},{1,25},{9,17},{17,9},{25,1},{2,26},{10... | collective-permute-start | bytes 307208 | tf_op jit(solution)/shard_map/ppermute | solution.py:711
  78.2 8.4 %collective-permute-start.19 = (s32[72,640]{1,0:T(8,128)S(1)}, s32[72,640]{1,0:T(8,128)S(1)}, u32[]{:S(2)}, u32[]{:S(2)}) collective-permute-start(s32[72,640]{1,0:T(8,128)S(1)} %get-tuple-element.47), channel_id=1, source_target_pairs={{0,1},{1,0},{2,3},{3,2},{4,5},{5,4},{6,7},{7,6},{8,9},{9,8},{10,11... | collective-permute-start | bytes 552968 | tf_op jit(solution)/shard_map/ppermute | solution.py:711
  78.2 8.4 %collective-permute-start.20 = (s32[72,640]{1,0:T(8,128)S(1)}, s32[72,640]{1,0:T(8,128)S(1)}, u32[]{:S(2)}, u32[]{:S(2)}) collective-permute-start(s32[72,640]{1,0:T(8,128)S(1)} %get-tuple-element.47), channel_id=1, source_target_pairs={{1,2},{3,4},{5,6},{2,1},{4,3},{6,5},{9,10},{11,12},{13,14},{10,9},... | collective-permute-start | bytes 552968 | tf_op jit(solution)/shard_map/ppermute | solution.py:722
  85.6 8.1 %collective-permute-start.14 = (s32[72,640]{1,0:T(8,128)S(1)}, s32[72,640]{1,0:T(8,128)S(1)}, u32[]{:S(2)}, u32[]{:S(2)}) collective-permute-start(s32[72,640]{1,0:T(8,128)S(1)} %get-tuple-element.41), channel_id=1, source_target_pairs={{0,1},{1,0},{2,3},{3,2},{4,5},{5,4},{6,7},{7,6},{8,9},{9,8},{10,11... | collective-permute-start | bytes 552968 | tf_op jit(solution)/shard_map/ppermute | solution.py:711
  85.7 8.0 %collective-permute-start.15 = (s32[72,640]{1,0:T(8,128)S(1)}, s32[72,640]{1,0:T(8,128)S(1)}, u32[]{:S(2)}, u32[]{:S(2)}) collective-permute-start(s32[72,640]{1,0:T(8,128)S(1)} %get-tuple-element.41), channel_id=1, source_target_pairs={{1,2},{3,4},{5,6},{2,1},{4,3},{6,5},{9,10},{11,12},{13,14},{10,9},... | collective-permute-start | bytes 552968 | tf_op jit(solution)/shard_map/ppermute | solution.py:722
  90.1 14.6 %collective-permute-start.24 = (s32[72,640]{1,0:T(8,128)S(1)}, s32[72,640]{1,0:T(8,128)S(1)}, u32[]{:S(2)}, u32[]{:S(2)}) collective-permute-start(s32[72,640]{1,0:T(8,128)S(1)} %pull_back.3.rest_1_), channel_id=1, source_target_pairs={{0,16},{8,24},{16,0},{24,8},{1,17},{9,25},{17,1},{25,9},{2,18},{10... | collective-permute-start | bytes 552968 | tf_op jit(solution)/shard_map/ppermute | solution.py:711
  93.7 17.9 %collective-permute-start.22 = (s32[72,640]{1,0:T(8,128)S(1)}, s32[72,640]{1,0:T(8,128)S(1)}, u32[]{:S(2)}, u32[]{:S(2)}) collective-permute-start(s32[72,640]{1,0:T(8,128)S(1)} %pull_back.3.rest_1_), channel_id=1, source_target_pairs={{0,8},{8,0},{16,24},{24,16},{1,9},{9,1},{17,25},{25,17},{2,10},{10... | collective-permute-start | bytes 552968 | tf_op jit(solution)/shard_map/ppermute | solution.py:711
  97.2 14.4 %collective-permute-start.21 = (s32[72,640]{1,0:T(8,128)S(1)}, s32[72,640]{1,0:T(8,128)}, u32[]{:S(2)}, u32[]{:S(2)}) collective-permute-start(s32[72,640]{1,0:T(8,128)S(1)} %pull_back.2.rest_0_), channel_id=1, source_target_pairs={{0,8},{8,0},{16,24},{24,16},{1,9},{9,1},{17,25},{25,17},{2,10},{10... | collective-permute-start | bytes 552968 | tf_op jit(solution)/shard_map/ppermute | solution.py:711
  99.3 9.0 %collective-permute-start.23 = (s32[72,640]{1,0:T(8,128)S(1)}, s32[72,640]{1,0:T(8,128)}, u32[]{:S(2)}, u32[]{:S(2)}) collective-permute-start(s32[72,640]{1,0:T(8,128)S(1)} %pull_back.2.rest_0_), channel_id=1, source_target_pairs={{0,16},{8,24},{16,0},{24,8},{1,17},{9,25},{17,1},{25,9},{2,18},{10... | collective-permute-start | bytes 552968 | tf_op jit(solution)/shard_map/ppermute | solution.py:711
  104.7 11.5 %collective-permute-start.26 = (s32[72,640]{1,0:T(8,128)S(1)}, s32[72,640]{1,0:T(8,128)S(1)}, u32[]{:S(2)}, u32[]{:S(2)}) collective-permute-start(s32[72,640]{1,0:T(8,128)S(1)} %collective-permute-done.24.rest_1_), channel_id=1, source_target_pairs={{0,8},{8,0},{16,24},{24,16},{1,9},{9,1},{17,25},{25,17},{2,10},{10... | collective-permute-start | bytes 552968 | tf_op jit(solution)/shard_map/ppermute | solution.py:711
  108.3 9.3 %collective-permute-start.25 = (s32[72,640]{1,0:T(8,128)}, s32[72,640]{1,0:T(8,128)S(1)}, u32[]{:S(2)}, u32[]{:S(2)}) collective-permute-start(s32[72,640]{1,0:T(8,128)} %collective-permute-done.23.rest_0_), channel_id=1, source_target_pairs={{0,8},{8,0},{16,24},{24,16},{1,9},{9,1},{17,25},{25,17},{2,10},{10... | collective-permute-start | bytes 552968 | tf_op jit(solution)/shard_map/ppermute | solution.py:711
  (16 other events, 113.2 us)

commit v6 on v5

--- a/solution.py
+++ b/solution.py
@@ -67,8 +67,28 @@
     return (word << 16) >> 16
 
 
-def words_of(rhs, weeks, rows):
-    return rhs * weeks * rows // 2 + SUBLANES
+def words_shape(rhs, weeks, rows, lon):
+    parts = lon // LANES
+    tail = -(-rhs * parts // SUBLANES) * SUBLANES
+    return parts * (rhs * weeks * rows // 2) + tail, LANES
+
+
+def words_at(word_ref, body, at, parts):
+    found = []
+    for part in range(parts):
+        start = part * body + at
+        if not isinstance(start, int):
+            start = pl.multiple_of(start, SUBLANES)
+        found.append(word_ref[pl.ds(start, SUBLANES), :])
+    return jnp.concatenate(found, axis=1)
+
+
+def field_scale(word_ref, body, k, parts):
+    first = parts * (body + k)
+    row = jnp.concatenate(
+        [word_ref[first + part : first + part + 1, :] for part in range(parts)], axis=1
+    )
+    return pow2(jnp.broadcast_to(row, (SUBLANES, row.shape[1])) - 15)
 
 
 def exponent_rows(peaks):
@@ -81,21 +101,31 @@
 
 def pack_field(field_ref, word_ref, peaks):
     rhs, weeks, rows, lon = field_ref.shape
-    half = rows // 2
-    exponents = exponent_rows(peaks)
-    word_ref[rhs * weeks * half :, :] = exponents
+    half, parts = rows // 2, lon // LANES
+    body = rhs * weeks * half
+    tail = word_ref.shape[0] - parts * body
+    line = lax.broadcasted_iota(jnp.int32, (tail, LANES), 0)
+    kept = jnp.zeros((tail, LANES), jnp.int32)
     for k in range(rhs):
-        factor = pow2(15 - jnp.broadcast_to(exponents[k : k + 1], (SUBLANES, lon)))
+        exponent = exponent_of(jnp.max(peaks[k], axis=0, keepdims=True))
+        for part in range(parts):
+            own = exponent[:, part * LANES : (part + 1) * LANES]
+            kept = jnp.where(line == k * parts + part, own, kept)
+        factor = pow2(15 - jnp.broadcast_to(exponent, (SUBLANES, lon)))
 
         def one_week(week, carry):
             for start in range(0, half, SUBLANES):
                 high = to_int(field_ref[k, week, start : start + SUBLANES, :], factor)
                 low = to_int(field_ref[k, week, half + start : half + start + SUBLANES, :], factor)
-                at = pl.multiple_of((k * weeks + week) * half + start, SUBLANES)
-                word_ref[pl.ds(at, SUBLANES), :] = pack(high, low)
+                word = pack(high, low)
+                for part in range(parts):
+                    at = part * body + (k * weeks + week) * half + start
+                    at = pl.multiple_of(at, SUBLANES)
+                    word_ref[pl.ds(at, SUBLANES), :] = word[:, part * LANES : (part + 1) * LANES]
             return carry
 
         lax.fori_loop(0, weeks, one_week, 0)
+    word_ref[parts * body :, :] = kept
 
 
 def word_scale(word_ref, body, k):
@@ -169,7 +199,7 @@
         out_specs=in_vmem(2),
         out_shape=[
             jax.ShapeDtypeStruct(field.shape, jnp.float32),
-            jax.ShapeDtypeStruct((words_of(rhs, weeks, rows), lon), jnp.int32),
+            jax.ShapeDtypeStruct(words_shape(rhs, weeks, rows, lon), jnp.int32),
         ],
         compiler_params=params(6),
         cost_estimate=cost(field.size * 100, field.size * 10),
@@ -180,6 +210,7 @@
 def lat_mix(side_ref, weights_ref, window_ref, k, week, pair_ref, own_ref, cross_ref, scales):
     rhs, weeks, rows, lon = own_ref.shape
     half = rows // 2
+    body, parts = rhs * weeks * half, lon // LANES
     before = 2 * rows * (1 - side_ref[0])
     for base, ref, scale in (
         (before, pair_ref, scales[0]),
@@ -187,7 +218,7 @@
     ):
         for start in range(0, half, SUBLANES):
             at = (k * weeks + week) * half + start
-            word = ref[at : at + SUBLANES, :]
+            word = words_at(ref, body, at, parts)
             for to, number in ((start, high_of(word)), (half + start, low_of(word))):
                 to = pl.multiple_of(base + to, SUBLANES)
                 window_ref[pl.ds(to, SUBLANES), :] = number.astype(jnp.float32) * scale
@@ -203,10 +234,10 @@
 def spread_lat_kernel(slots, side_ref, own_ref, pair_ref, cross_ref, weights_ref, hot_ref, *rest):
     picks, (window_ref, cells_ref) = rest[:slots], rest[slots:]
     rhs, weeks, rows, lon = own_ref.shape
-    body = pair_ref.shape[0] - SUBLANES
     parts = lon // LANES
+    body = rhs * weeks * rows // 2
     for k in range(rhs):
-        scales = word_scale(pair_ref, body, k), word_scale(cross_ref, body, k)
+        scales = [field_scale(ref, body, k, parts) for ref in (pair_ref, cross_ref)]
         for week in range(weeks):
             mixed = lat_mix(
                 side_ref, weights_ref, window_ref, k, week, pair_ref, own_ref, cross_ref, scales
@@ -438,7 +469,7 @@
         out_specs=in_vmem(2),
         out_shape=[
             jax.ShapeDtypeStruct((rhs, weeks, rows, lon), jnp.float32),
-            jax.ShapeDtypeStruct((words_of(rhs, weeks, rows), lon), jnp.int32),
+            jax.ShapeDtypeStruct(words_shape(rhs, weeks, rows, lon), jnp.int32),
         ],
         scratch_shapes=[pltpu.VMEM((hot_turned.shape[1], 2 * rhs * LANES), jnp.bfloat16)],
         compiler_params=params(12),
@@ -451,9 +482,10 @@
     side_ref, own_ref, pair_ref, cross_ref, weights_ref, count_ref, word_ref, window_ref, field_ref
 ):
     rhs, weeks, rows, lon = own_ref.shape
-    body = pair_ref.shape[0] - SUBLANES
+    parts = lon // LANES
+    body = rhs * weeks * rows // 2
     for k in range(rhs):
-        scales = word_scale(pair_ref, body, k), word_scale(cross_ref, body, k)
+        scales = [field_scale(ref, body, k, parts) for ref in (pair_ref, cross_ref)]
         for week in range(weeks):
             field_ref[k, week] = lat_mix(
                 side_ref, weights_ref, window_ref, k, week, pair_ref, own_ref, cross_ref, scales
@@ -482,17 +514,16 @@
     words, (image_ref, gram_ref, sums_ref) = rest[:count], rest[-3:]
     rhs_count, weeks, rows, lon = direction_ref.shape
     half = rows // 2
-    body = words[0].shape[0] - SUBLANES
+    body, parts = rhs * weeks * half, lon // LANES
     old_places, new_places = places[:-count], places[-count:]
     for word_ref, place in zip(words, new_places):
         for k in range(rhs):
             index = order_ref[place] + k
-            scale = word_scale(word_ref, body, k)
+            scale = field_scale(word_ref, body, k, parts)
 
             def one_week(week, carry):
                 for start in range(0, half, SUBLANES):
-                    at = pl.multiple_of((k * weeks + week) * half + start, SUBLANES)
-                    word = word_ref[pl.ds(at, SUBLANES), :]
+                    word = words_at(word_ref, body, (k * weeks + week) * half + start, parts)
                     for base, number in ((start, high_of(word)), (half + start, low_of(word))):
                         image_ref[index, week, base : base + SUBLANES, :] = (
                             direction_ref[index, week, base : base + SUBLANES, :]
@@ -556,10 +587,9 @@
     )
 
 
-def grams(order, places, sums, residual, direction, words, images):
+def grams(order, places, sums, residual, direction, words, rhs, images):
     rhs_count, weeks, rows, lon = direction.shape
     total = 4 * rhs_count**2
-    rhs = (words[0].shape[0] - SUBLANES) * 2 // (weeks * rows)
     count = len(words)
     return pl.pallas_call(
         functools.partial(gram_kernel, places, count, rhs),
@@ -830,7 +860,9 @@
         nonlocal products, places, images
         words = [arrived[group][slot] for group in range(groups)]
         places += tuple(slot * groups + group for group in range(groups))
-        *images, products = grams(starts, places, products, residual, direction, words, images)
+        *images, products = grams(
+            starts, places, products, residual, direction, words, each, images
+        )
 
     arrived = [{0: words} for words in own]
     for group in range(groups):

time: 139 us -> 136 us (0.978)
  no operation moved by 1% of the time
where the time goes in v6:
time: 136 us
  Pallas kernels  50.4 us (37%)
  starting transfers between devices  50.3 us (37%)
  waiting for transfers between devices  25.8 us (19%)
  local copies, waits for them, and re-layouts  5.64 us (4%)
  other arithmetic  2.95 us (2%)
    ppermute x27, starting transfers between devices, crossed(): lax.ppermute(value, axis, [(i, i ^ by) for i in range(lax.axis_size(axis))])  48 us
    ppermute x27, waiting for transfers between devices, crossed(): lax.ppermute(value, axis, [(i, i ^ by) for i in range(lax.axis_size(axis))])  25.8 us
    pallas_call x3, Pallas kernels, preload(): pl.pallas_call(functools.partial(preload_kernel, first), in_specs=[pl.Blo...  11.1 us
    pallas_call x4, Pallas kernels, grams(): pl.pallas_call(functools.partial(gram_kernel, places, count, rhs), in_spe...  9.14 us
    pallas_call x2, Pallas kernels, pull_back(): pl.pallas_call(pull_back_kernel, in_specs=[pl.BlockSpec(memory_space=pltp...  6.97 us
    pallas_call x1, Pallas kernels, update(): pl.pallas_call(update_kernel, grid=(weeks,), in_specs=[whole(sums.shape)]...  6.37 us
    pallas_call x1, Pallas kernels, forward(): pl.pallas_call(functools.partial(forward_kernel, len(pieces)), in_specs=[...  4.77 us
    pallas_call x1, Pallas kernels, spread_lon(): pl.pallas_call(spread_lon_kernel, in_specs=in_vmem(2), out_specs=in_vmem(...  4.72 us
  transfers between devices with their start and end apart: 30, of which 12 were waited for; matrix products, arithmetic and copies ran while one was open for 2% of the time, Pallas kernels for 20%

profile of v6, /device:TPU:0, one launch (start us, length us, event | category | flops | bytes accessed | tf_op | source)
XLA Modules:
  0.0 136.1 jit_solution(6513073150395291318)
XLA Ops:
  2.6 4.7 %spread_lon.1 = (f32[2,4,32,640]{3,2,1,0:T(8,128)S(1)}, s32[656,128]{1,0:T(8,128)S(1)}) custom-call(f32[2,4,32,640]{3,2,1,0:T(8,128)S(1)} %constant_dynamic-slice_fusion.field_ref, s32[32,640]{1,0:T(8,128)S(1)} %broadcast_in_dim.21.count_ref), custom_call_target="tpu_custom_call" | custom-call | flops 16384000 | bytes 1638400 | tf_op jit(solution)/shard_map/spread_lon/pallas_call | solution.py:196
  8.5 2.7 %collective-permute-start = (s32[1,1,384]{2,1,0:T(1,128)}, s32[1,1,384]{2,1,0:T(1,128)S(1)}, u32[]{:S(2)}, u32[]{:S(2)}) collective-permute-start(s32[1,1,384]{2,1,0:T(1,128)} %param.12), channel_id=1, source_target_pairs={{0,8},{8,0},{16,24},{24,16},{1,9},{9,1},{17,25},{25,17},{2,10},{10... | collective-permute-start | bytes 4616 | tf_op jit(solution)/shard_map/ppermute | solution.py:741
  11.2 2.6 %collective-permute-start.1 = (s32[1,1,384]{2,1,0:T(1,128)}, s32[1,1,384]{2,1,0:T(1,128)S(1)}, u32[]{:S(2)}, u32[]{:S(2)}) collective-permute-start(s32[1,1,384]{2,1,0:T(1,128)} %param.12), channel_id=1, source_target_pairs={{0,16},{8,24},{16,0},{24,8},{1,17},{9,25},{17,1},{25,9},{2,18},{10... | collective-permute-start | bytes 4616 | tf_op jit(solution)/shard_map/ppermute | solution.py:741
  15.9 3.5 %collective-permute-done.2 = s32[1,1,384]{2,1,0:T(1,128)S(1)} collective-permute-done((s32[1,1,384]{2,1,0:T(1,128)}, s32[1,1,384]{2,1,0:T(1,128)S(1)}, u32[]{:S(2)}, u32[]{:S(2)}) %collective-permute-start.2) | collective-permute-done | bytes 1568 | tf_op jit(solution)/shard_map/ppermute | solution.py:741
  22.7 3.7 %collective-permute-start.7 = (bf16[2,384,128]{2,1,0:T(8,128)(2,1)S(1)}, bf16[2,384,128]{2,1,0:T(8,128)(2,1)S(1)}, u32[]{:S(2)}, u32[]{:S(2)}) collective-permute-start(bf16[2,384,128]{2,1,0:T(8,128)(2,1)S(1)} %get-tuple-element.35), channel_id=1, source_target_pairs={{0,24},{8,16},{16,8},{24,0},{1,25},{9,17},{17,9},{25,1},{2,26},{10... | collective-permute-start | bytes 589832 | tf_op jit(solution)/shard_map/ppermute | solution.py:741
  26.5 2.9 %preload.3.rest_0_ = bf16[192,128,128]{2,1,0:T(8,128)(2,1)S(1)} custom-call(bf16[2,384,128]{2,1,0:T(8,128)(2,1)S(1)} %get-tuple-element.32.after_ref.rest_2_, bf16[384,128,128]{2,1,0:T(8,128)(2,1)} %bitcast.31), custom_call_target="tpu_custom_call" | custom-call | bytes 12582912 | tf_op jit(solution)/shard_map/preload/pallas_call | solution.py:301
  29.4 5.1 %preload.4.rest_1_ = bf16[192,128,128]{2,1,0:T(8,128)(2,1)S(1)} custom-call(bf16[2,384,128]{2,1,0:T(8,128)(2,1)S(1)} %get-tuple-element.32.after_ref.rest_2_, bf16[384,128,128]{2,1,0:T(8,128)(2,1)} %bitcast.32), custom_call_target="tpu_custom_call" | custom-call | bytes 12582912 | tf_op jit(solution)/shard_map/preload/pallas_call | solution.py:301
  36.5 4.8 %forward.1 = f32[256,128]{1,0:T(8,128)S(1)} custom-call(s32[384]{0:T(512)S(1)} %reduce.1.row_ref, f32[384]{0:T(512)S(1)} %exponential_reduce_fusion.scale_ref, bf16[192,128,128]{2,1,0:T(8,128)(2,1)S(1)} %preload.3.rest_0_, bf16[192,128,128]{2,1,0:T(8,128)(2,1)S(1)} %preload.4.rest_1_, bf16[2,384,128]{2,1,0:T(8,128)(2,1)S(1)} %get-tuple-element.32.after_ref.rest_2_, ...), custom_call_target="tpu_custom_call" | custom-call | flops 100663296 | bytes 12582912 | tf_op jit(solution)/shard_map/forward/pallas_call | solution.py:357
  41.2 4.1 %collective-permute-start.8 = (f32[256,128]{1,0:T(8,128)S(1)}, f32[256,128]{1,0:T(8,128)S(1)}, u32[]{:S(2)}, u32[]{:S(2)}) collective-permute-start(f32[256,128]{1,0:T(8,128)S(1)} %forward.1), channel_id=1, source_target_pairs={{0,1},{1,0},{2,3},{3,2},{4,5},{5,4},{6,7},{7,6},{8,9},{9,8},{10,11... | collective-permute-start | bytes 393224 | tf_op jit(solution)/shard_map/ppermute | solution.py:741
  46.4 2.3 %collective-permute-start.9 = (f32[256,128]{1,0:T(8,128)S(1)}, f32[256,128]{1,0:T(8,128)S(1)}, u32[]{:S(2)}, u32[]{:S(2)}) collective-permute-start(f32[256,128]{1,0:T(8,128)S(1)} %add.188), channel_id=1, source_target_pairs={{0,2},{1,3},{2,0},{3,1},{4,6},{5,7},{6,4},{7,5},{8,10},{9,11},{10,... | collective-permute-start | bytes 393224 | tf_op jit(solution)/shard_map/ppermute | solution.py:741
  48.7 3.9 %collective-permute-done.9 = f32[256,128]{1,0:T(8,128)S(1)} collective-permute-done((f32[256,128]{1,0:T(8,128)S(1)}, f32[256,128]{1,0:T(8,128)S(1)}, u32[]{:S(2)}, u32[]{:S(2)}) %collective-permute-start.9) | collective-permute-done | bytes 131104 | tf_op jit(solution)/shard_map/ppermute | solution.py:741
  54.8 3.0 %preload.5.rest_1_ = bf16[192,128,128]{2,1,0:T(8,128)(2,1)S(1)} custom-call(f32[256,128]{1,0:T(8,128)S(1)} %add.189.after_ref, bf16[384,128,128]{2,1,0:T(8,128)(2,1)} %bitcast.33), custom_call_target="tpu_custom_call" | custom-call | bytes 12582912 | tf_op jit(solution)/shard_map/preload/pallas_call | solution.py:301
  59.4 3.3 %adjoint.1 = (s32[200,128]{1,0:T(8,128)S(1)}, s32[200,128]{1,0:T(8,128)S(1)}, s32[200,128]{1,0:T(8,128)S(1)}, s32[200,128]{1,0:T(8,128)S(1)}, s32[200,128]{1,0:T...) custom-call(s32[384]{0:T(512)S(1)} %reduce.1.row_ref, ...), custom_call_target="tpu_custom_call" | custom-call | flops 100663296 | bytes 12582912 | tf_op jit(solution)/shard_map/adjoint/pallas_call | solution.py:410
  62.7 3.1 %collective-permute-start.16 = (s32[200,128]{1,0:T(8,128)S(1)}, s32[200,128]{1,0:T(8,128)S(1)}, u32[]{:S(2)}, u32[]{:S(2)}) collective-permute-start(s32[200,128]{1,0:T(8,128)S(1)} %get-tuple-element.43), channel_id=1, source_target_pairs={{0,8},{8,0},{16,24},{24,16},{1,9},{9,1},{17,25},{25,17},{2,10},{10... | collective-permute-start | bytes 307208 | tf_op jit(solution)/shard_map/ppermute | solution.py:741
  73.3 3.9 %collective-permute-done.17.rest_2_ = s32[200,128]{1,0:T(8,128)S(1)} collective-permute-done((s32[200,128]{1,0:T(8,128)S(1)}, s32[200,128]{1,0:T(8,128)S(1)}, u32[]{:S(2)}, u32[]{:S(2)}) %collective-permute-start.17) | collective-permute-done | bytes 102432 | tf_op jit(solution)/shard_map/ppermute | solution.py:741
  79.1 5.4 %collective-permute-done.12.rest_2_ = s32[200,128]{1,0:T(8,128)S(1)} collective-permute-done((s32[200,128]{1,0:T(8,128)S(1)}, s32[200,128]{1,0:T(8,128)S(1)}, u32[]{:S(2)}, u32[]{:S(2)}) %collective-permute-start.12) | collective-permute-done | bytes 102432 | tf_op jit(solution)/shard_map/ppermute | solution.py:741
  86.5 3.5 %pull_back.3.rest_1_ = s32[328,128]{1,0:T(8,128)S(1)} custom-call(s32[1]{0:T(128)} %bitcast.side_ref, f32[1,4,32,640]{3,2,1,0:T(8,128)S(1)} %get-tuple-element.46.own_ref, s32[328,128]{1,0:T(8,128)S(1)} %collective-permute-done.19.pair_ref, s32[328,128]{1,0:T(8,128)S(1)} %collective-permute-done.20.cross_ref, f32[32,96]{1,0:T(8,128)S(1)} %get-tuple-element.61.weights_ref, ...), custom_call_target="tpu_custom_call" | custom-call | flops 24576000 | bytes 819200 | tf_op jit(solution)/shard_map/pull_back/pallas_call | solution.py:498
  90.0 3.6 %collective-permute-start.24 = (s32[328,128]{1,0:T(8,128)S(1)}, s32[328,128]{1,0:T(8,128)S(1)}, u32[]{:S(2)}, u32[]{:S(2)}) collective-permute-start(s32[328,128]{1,0:T(8,128)S(1)} %pull_back.3.rest_1_), channel_id=1, source_target_pairs={{0,16},{8,24},{16,0},{24,8},{1,17},{9,25},{17,1},{25,9},{2,18},{10... | collective-permute-start | bytes 503816 | tf_op jit(solution)/shard_map/ppermute | solution.py:741
  93.6 3.5 %pull_back.2.rest_0_ = s32[328,128]{1,0:T(8,128)S(1)} custom-call(s32[1]{0:T(128)} %bitcast.side_ref, f32[1,4,32,640]{3,2,1,0:T(8,128)S(1)} %get-tuple-element.40.own_ref, s32[328,128]{1,0:T(8,128)S(1)} %collective-permute-done.14.pair_ref, s32[328,128]{1,0:T(8,128)S(1)} %collective-permute-done.15.cross_ref, f32[32,96]{1,0:T(8,128)S(1)} %get-tuple-element.61.weights_ref, ...), custom_call_target="tpu_custom_call" | custom-call | flops 24576000 | bytes 819200 | tf_op jit(solution)/shard_map/pull_back/pallas_call | solution.py:498
  101.8 2.9 %grams.4 = (f32[8,4,32,640]{3,2,1,0:T(8,128)S(1)}, f32[8,256]{1,0:T(8,128)S(1)}) custom-call(s32[8]{0:T(128)S(1)} %add.169.order_ref, f32[8,256]{1,0:T(8,128)S(1)} %broadcast_in_dim.20.sums_before, f32[8,4,32,640]{3,2,1,0:T(8,128)S(1)} %copy-done.1, f32[8,4,32,640]{3,2,1,0:T(8,128)S(1)} %copy-done, s32[328,128]{1,0:T(8,128)S(1)} %pull_back.2.rest_0_, ...), custom_call_target="tpu_custom_call" | custom-call | flops 41943040 | bytes 10485760 | tf_op jit(solution)/shard_map/grams/pallas_call | solution.py:594
  107.5 3.2 %collective-permute-start.25 = (s32[328,128]{1,0:T(8,128)S(1)}, s32[328,128]{1,0:T(8,128)S(1)}, u32[]{:S(2)}, u32[]{:S(2)}) collective-permute-start(s32[328,128]{1,0:T(8,128)S(1)} %collective-permute-done.23.rest_0_), channel_id=1, source_target_pairs={{0,8},{8,0},{16,24},{24,16},{1,9},{9,1},{17,25},{25,17},{2,10},{10... | collective-permute-start | bytes 503816 | tf_op jit(solution)/shard_map/ppermute | solution.py:741
  120.5 3.0 %collective-permute-start.28 = (f32[8,256]{1,0:T(8,128)S(1)}, f32[8,256]{1,0:T(8,128)S(1)}, u32[]{:S(2)}, u32[]{:S(2)}) collective-permute-start(f32[8,256]{1,0:T(8,128)S(1)} %add.191), channel_id=1, source_target_pairs={{0,2},{1,3},{2,0},{3,1},{4,6},{5,7},{6,4},{7,5},{8,10},{9,11},{10,... | collective-permute-start | bytes 24584 | tf_op jit(solution)/shard_map/ppermute | solution.py:741
  125.1 3.1 %collective-permute-start.29 = (f32[8,256]{1,0:T(8,128)S(1)}, f32[8,256]{1,0:T(8,128)S(1)}, u32[]{:S(2)}, u32[]{:S(2)}) collective-permute-start(f32[8,256]{1,0:T(8,128)S(1)} %add.192), channel_id=1, source_target_pairs={{0,4},{1,5},{2,6},{3,7},{4,0},{5,1},{6,2},{7,3},{8,12},{9,13},{10,... | collective-permute-start | bytes 24584 | tf_op jit(solution)/shard_map/ppermute | solution.py:741
  129.8 6.4 %update.1 = (f32[8,4,32,640]{3,2,1,0:T(8,128)}, f32[8,4,32,640]{3,2,1,0:T(8,128)}, f32[8,4,32,640]{3,2,1,0:T(8,128)}) custom-call(f32[8,256]{1,0:T(8,128)S(1)} %add.193.sums_ref, f32[8,4,32,640]{3,2,1,0:T(8,128)S(1)} %copy-done.4, f32[8,4,32,640]{3,2,1,0:T(8,128)S(1)} %copy-done.2, f32[8,4,32,640]{3,2,1,0:T(8,128)S(1)} %copy-done, ...), custom_call_target="tpu_custom_call" | custom-call | flops 31457280 | bytes 18350080 | tf_op jit(solution)/shard_map/update/pallas_call | solution.py:725
  (111 shorter events, 47.3 us)
Async XLA Ops:
  7.3 12.6 %collective-permute-start.3 = (s32[656,128]{1,0:T(8,128)S(1)}, s32[656,128]{1,0:T(8,128)S(1)}, u32[]{:S(2)}, u32[]{:S(2)}) collective-permute-start(s32[656,128]{1,0:T(8,128)S(1)} %get-tuple-element.31), channel_id=1, source_target_pairs={{0,1},{1,0},{2,3},{3,2},{4,5},{5,4},{6,7},{7,6},{8,9},{9,8},{10,11... | collective-permute-start | bytes 1007624 | tf_op jit(solution)/shard_map/ppermute | solution.py:741
  7.9 12.0 %collective-permute-start.4 = (s32[656,128]{1,0:T(8,128)S(1)}, s32[656,128]{1,0:T(8,128)S(1)}, u32[]{:S(2)}, u32[]{:S(2)}) collective-permute-start(s32[656,128]{1,0:T(8,128)S(1)} %get-tuple-element.31), channel_id=1, source_target_pairs={{1,2},{3,4},{5,6},{2,1},{4,3},{6,5},{9,10},{11,12},{13,14},{10,9},... | collective-permute-start | bytes 1007624 | tf_op jit(solution)/shard_map/ppermute | solution.py:752
  8.5 7.1 %collective-permute-start = (s32[1,1,384]{2,1,0:T(1,128)}, s32[1,1,384]{2,1,0:T(1,128)S(1)}, u32[]{:S(2)}, u32[]{:S(2)}) collective-permute-start(s32[1,1,384]{2,1,0:T(1,128)} %param.12), channel_id=1, source_target_pairs={{0,8},{8,0},{16,24},{24,16},{1,9},{9,1},{17,25},{25,17},{2,10},{10... | collective-permute-start | bytes 4616 | tf_op jit(solution)/shard_map/ppermute | solution.py:741
  13.8 5.6 %collective-permute-start.2 = (s32[1,1,384]{2,1,0:T(1,128)}, s32[1,1,384]{2,1,0:T(1,128)S(1)}, u32[]{:S(2)}, u32[]{:S(2)}) collective-permute-start(s32[1,1,384]{2,1,0:T(1,128)} %param.12), channel_id=1, source_target_pairs={{0,24},{8,16},{16,8},{24,0},{1,25},{9,17},{17,9},{25,1},{2,26},{10... | collective-permute-start | bytes 4616 | tf_op jit(solution)/shard_map/ppermute | solution.py:741
  22.0 12.6 %collective-permute-start.5 = (bf16[2,384,128]{2,1,0:T(8,128)(2,1)S(1)}, bf16[2,384,128]{2,1,0:T(8,128)(2,1)S(1)}, u32[]{:S(2)}, u32[]{:S(2)}) collective-permute-start(bf16[2,384,128]{2,1,0:T(8,128)(2,1)S(1)} %get-tuple-element.33), channel_id=1, source_target_pairs={{0,8},{8,0},{16,24},{24,16},{1,9},{9,1},{17,25},{25,17},{2,10},{10... | collective-permute-start | bytes 589832 | tf_op jit(solution)/shard_map/ppermute | solution.py:741
  22.0 12.5 %collective-permute-start.6 = (bf16[2,384,128]{2,1,0:T(8,128)(2,1)S(1)}, bf16[2,384,128]{2,1,0:T(8,128)(2,1)S(1)}, u32[]{:S(2)}, u32[]{:S(2)}) collective-permute-start(bf16[2,384,128]{2,1,0:T(8,128)(2,1)S(1)} %get-tuple-element.34), channel_id=1, source_target_pairs={{0,16},{8,24},{16,0},{24,8},{1,17},{9,25},{17,1},{25,9},{2,18},{10... | collective-permute-start | bytes 589832 | tf_op jit(solution)/shard_map/ppermute | solution.py:741
  22.7 13.8 %collective-permute-start.7 = (bf16[2,384,128]{2,1,0:T(8,128)(2,1)S(1)}, bf16[2,384,128]{2,1,0:T(8,128)(2,1)S(1)}, u32[]{:S(2)}, u32[]{:S(2)}) collective-permute-start(bf16[2,384,128]{2,1,0:T(8,128)(2,1)S(1)} %get-tuple-element.35), channel_id=1, source_target_pairs={{0,24},{8,16},{16,8},{24,0},{1,25},{9,17},{17,9},{25,1},{2,26},{10... | collective-permute-start | bytes 589832 | tf_op jit(solution)/shard_map/ppermute | solution.py:741
  46.4 6.2 %collective-permute-start.9 = (f32[256,128]{1,0:T(8,128)S(1)}, f32[256,128]{1,0:T(8,128)S(1)}, u32[]{:S(2)}, u32[]{:S(2)}) collective-permute-start(f32[256,128]{1,0:T(8,128)S(1)} %add.188), channel_id=1, source_target_pairs={{0,2},{1,3},{2,0},{3,1},{4,6},{5,7},{6,4},{7,5},{8,10},{9,11},{10,... | collective-permute-start | bytes 393224 | tf_op jit(solution)/shard_map/ppermute | solution.py:741
  62.7 8.2 %collective-permute-start.16 = (s32[200,128]{1,0:T(8,128)S(1)}, s32[200,128]{1,0:T(8,128)S(1)}, u32[]{:S(2)}, u32[]{:S(2)}) collective-permute-start(s32[200,128]{1,0:T(8,128)S(1)} %get-tuple-element.43), channel_id=1, source_target_pairs={{0,8},{8,0},{16,24},{24,16},{1,9},{9,1},{17,25},{25,17},{2,10},{10... | collective-permute-start | bytes 307208 | tf_op jit(solution)/shard_map/ppermute | solution.py:741
  65.8 11.3 %collective-permute-start.17 = (s32[200,128]{1,0:T(8,128)S(1)}, s32[200,128]{1,0:T(8,128)S(1)}, u32[]{:S(2)}, u32[]{:S(2)}) collective-permute-start(s32[200,128]{1,0:T(8,128)S(1)} %get-tuple-element.44), channel_id=1, source_target_pairs={{0,16},{8,24},{16,0},{24,8},{1,17},{9,25},{17,1},{25,9},{2,18},{10... | collective-permute-start | bytes 307208 | tf_op jit(solution)/shard_map/ppermute | solution.py:741
  66.5 10.6 %collective-permute-start.18 = (s32[200,128]{1,0:T(8,128)S(1)}, s32[200,128]{1,0:T(8,128)S(1)}, u32[]{:S(2)}, u32[]{:S(2)}) collective-permute-start(s32[200,128]{1,0:T(8,128)S(1)} %get-tuple-element.45), channel_id=1, source_target_pairs={{0,24},{8,16},{16,8},{24,0},{1,25},{9,17},{17,9},{25,1},{2,26},{10... | collective-permute-start | bytes 307208 | tf_op jit(solution)/shard_map/ppermute | solution.py:741
  68.3 10.8 %collective-permute-start.11 = (s32[200,128]{1,0:T(8,128)S(1)}, s32[200,128]{1,0:T(8,128)S(1)}, u32[]{:S(2)}, u32[]{:S(2)}) collective-permute-start(s32[200,128]{1,0:T(8,128)S(1)} %get-tuple-element.37), channel_id=1, source_target_pairs={{0,8},{8,0},{16,24},{24,16},{1,9},{9,1},{17,25},{25,17},{2,10},{10... | collective-permute-start | bytes 307208 | tf_op jit(solution)/shard_map/ppermute | solution.py:741
  69.4 15.1 %collective-permute-start.12 = (s32[200,128]{1,0:T(8,128)S(1)}, s32[200,128]{1,0:T(8,128)S(1)}, u32[]{:S(2)}, u32[]{:S(2)}) collective-permute-start(s32[200,128]{1,0:T(8,128)S(1)} %get-tuple-element.38), channel_id=1, source_target_pairs={{0,16},{8,24},{16,0},{24,8},{1,17},{9,25},{17,1},{25,9},{2,18},{10... | collective-permute-start | bytes 307208 | tf_op jit(solution)/shard_map/ppermute | solution.py:741
  70.9 13.6 %collective-permute-start.13 = (s32[200,128]{1,0:T(8,128)S(1)}, s32[200,128]{1,0:T(8,128)S(1)}, u32[]{:S(2)}, u32[]{:S(2)}) collective-permute-start(s32[200,128]{1,0:T(8,128)S(1)} %get-tuple-element.39), channel_id=1, source_target_pairs={{0,24},{8,16},{16,8},{24,0},{1,25},{9,17},{17,9},{25,1},{2,26},{10... | collective-permute-start | bytes 307208 | tf_op jit(solution)/shard_map/ppermute | solution.py:741
  78.2 8.3 %collective-permute-start.19 = (s32[328,128]{1,0:T(8,128)S(1)}, s32[328,128]{1,0:T(8,128)S(1)}, u32[]{:S(2)}, u32[]{:S(2)}) collective-permute-start(s32[328,128]{1,0:T(8,128)S(1)} %get-tuple-element.47), channel_id=1, source_target_pairs={{0,1},{1,0},{2,3},{3,2},{4,5},{5,4},{6,7},{7,6},{8,9},{9,8},{10,11... | collective-permute-start | bytes 503816 | tf_op jit(solution)/shard_map/ppermute | solution.py:741
  78.3 8.2 %collective-permute-start.20 = (s32[328,128]{1,0:T(8,128)S(1)}, s32[328,128]{1,0:T(8,128)S(1)}, u32[]{:S(2)}, u32[]{:S(2)}) collective-permute-start(s32[328,128]{1,0:T(8,128)S(1)} %get-tuple-element.47), channel_id=1, source_target_pairs={{1,2},{3,4},{5,6},{2,1},{4,3},{6,5},{9,10},{11,12},{13,14},{10,9},... | collective-permute-start | bytes 503816 | tf_op jit(solution)/shard_map/ppermute | solution.py:752
  85.5 8.0 %collective-permute-start.14 = (s32[328,128]{1,0:T(8,128)S(1)}, s32[328,128]{1,0:T(8,128)S(1)}, u32[]{:S(2)}, u32[]{:S(2)}) collective-permute-start(s32[328,128]{1,0:T(8,128)S(1)} %get-tuple-element.41), channel_id=1, source_target_pairs={{0,1},{1,0},{2,3},{3,2},{4,5},{5,4},{6,7},{7,6},{8,9},{9,8},{10,11... | collective-permute-start | bytes 503816 | tf_op jit(solution)/shard_map/ppermute | solution.py:741
  85.6 8.0 %collective-permute-start.15 = (s32[328,128]{1,0:T(8,128)S(1)}, s32[328,128]{1,0:T(8,128)S(1)}, u32[]{:S(2)}, u32[]{:S(2)}) collective-permute-start(s32[328,128]{1,0:T(8,128)S(1)} %get-tuple-element.41), channel_id=1, source_target_pairs={{1,2},{3,4},{5,6},{2,1},{4,3},{6,5},{9,10},{11,12},{13,14},{10,9},... | collective-permute-start | bytes 503816 | tf_op jit(solution)/shard_map/ppermute | solution.py:752
  90.0 14.7 %collective-permute-start.24 = (s32[328,128]{1,0:T(8,128)S(1)}, s32[328,128]{1,0:T(8,128)S(1)}, u32[]{:S(2)}, u32[]{:S(2)}) collective-permute-start(s32[328,128]{1,0:T(8,128)S(1)} %pull_back.3.rest_1_), channel_id=1, source_target_pairs={{0,16},{8,24},{16,0},{24,8},{1,17},{9,25},{17,1},{25,9},{2,18},{10... | collective-permute-start | bytes 503816 | tf_op jit(solution)/shard_map/ppermute | solution.py:741
  93.6 17.1 %collective-permute-start.22 = (s32[328,128]{1,0:T(8,128)S(1)}, s32[328,128]{1,0:T(8,128)S(1)}, u32[]{:S(2)}, u32[]{:S(2)}) collective-permute-start(s32[328,128]{1,0:T(8,128)S(1)} %pull_back.3.rest_1_), channel_id=1, source_target_pairs={{0,8},{8,0},{16,24},{24,16},{1,9},{9,1},{17,25},{25,17},{2,10},{10... | collective-permute-start | bytes 503816 | tf_op jit(solution)/shard_map/ppermute | solution.py:741
  97.1 13.6 %collective-permute-start.21 = (s32[328,128]{1,0:T(8,128)S(1)}, s32[328,128]{1,0:T(8,128)}, u32[]{:S(2)}, u32[]{:S(2)}) collective-permute-start(s32[328,128]{1,0:T(8,128)S(1)} %pull_back.2.rest_0_), channel_id=1, source_target_pairs={{0,8},{8,0},{16,24},{24,16},{1,9},{9,1},{17,25},{25,17},{2,10},{10... | collective-permute-start | bytes 503816 | tf_op jit(solution)/shard_map/ppermute | solution.py:741
  99.1 8.3 %collective-permute-start.23 = (s32[328,128]{1,0:T(8,128)S(1)}, s32[328,128]{1,0:T(8,128)S(1)}, u32[]{:S(2)}, u32[]{:S(2)}) collective-permute-start(s32[328,128]{1,0:T(8,128)S(1)} %pull_back.2.rest_0_), channel_id=1, source_target_pairs={{0,16},{8,24},{16,0},{24,8},{1,17},{9,25},{17,1},{25,9},{2,18},{10... | collective-permute-start | bytes 503816 | tf_op jit(solution)/shard_map/ppermute | solution.py:741
  104.7 10.2 %collective-permute-start.26 = (s32[328,128]{1,0:T(8,128)S(1)}, s32[328,128]{1,0:T(8,128)S(1)}, u32[]{:S(2)}, u32[]{:S(2)}) collective-permute-start(s32[328,128]{1,0:T(8,128)S(1)} %collective-permute-done.24.rest_1_), channel_id=1, source_target_pairs={{0,8},{8,0},{16,24},{24,16},{1,9},{9,1},{17,25},{25,17},{2,10},{10... | collective-permute-start | bytes 503816 | tf_op jit(solution)/shard_map/ppermute | solution.py:741
  107.5 8.5 %collective-permute-start.25 = (s32[328,128]{1,0:T(8,128)S(1)}, s32[328,128]{1,0:T(8,128)S(1)}, u32[]{:S(2)}, u32[]{:S(2)}) collective-permute-start(s32[328,128]{1,0:T(8,128)S(1)} %collective-permute-done.23.rest_0_), channel_id=1, source_target_pairs={{0,8},{8,0},{16,24},{24,16},{1,9},{9,1},{17,25},{25,17},{2,10},{10... | collective-permute-start | bytes 503816 | tf_op jit(solution)/shard_map/ppermute | solution.py:741
  (16 other events, 110.2 us)

commit v7 on v6

--- a/solution.py
+++ b/solution.py
@@ -753,13 +753,15 @@
 
 
 def summed_over(value, axis):
-    size = lax.axis_size(axis)
-    reach = 1
+    bits = far_first(lax.axis_size(axis))[::-1]
     before = value
-    while reach < size:
+    for step in [bits[:1]] + [bits[at : at + 2] for at in range(1, len(bits), 2)]:
         before = value
-        value = value + crossed(value, axis, reach)
-        reach *= 2
+        for reach in step[:1]:
+            value = value + crossed(before, axis, reach)
+        for reach in step[1:]:
+            far = crossed(before, axis, reach) + crossed(before, axis, reach | step[0])
+            value = value + far
     return value, before
 
 

time: 136 us -> 134 us (0.985)
  local copies, waits for them, and re-layouts: 5.64 us -> 4.06 us
    unnamed x23, local copies, waits for them, and re-layouts: 4.07 us -> 2.49 us
    ppermute x27 -> x29, waiting for transfers between devices: 25.8 us -> 24.8 us  [crossed(): lax.ppermute(value, axis, [(i, i ^ by) for i in range(lax.axis_size(axis))])]
    ppermute x27 -> x29, starting transfers between devices: 48 us -> 48 us  [crossed(): lax.ppermute(value, axis, [(i, i ^ by) for i in range(lax.axis_size(axis))])]
  transfers between devices with their start and end apart: 30 -> 32, of which waited for: 12 -> 14; matrix products, arithmetic and copies ran while one was open for 2% -> 2% of each run, Pallas kernels for 20% -> 20%
where the time goes in v7:
time: 134 us
  Pallas kernels  50.5 us (38%)
  starting transfers between devices  50.3 us (38%)
  waiting for transfers between devices  24.8 us (19%)
  local copies, waits for them, and re-layouts  4.06 us (3%)
  other arithmetic  2.94 us (2%)
    ppermute x29, starting transfers between devices, crossed(): lax.ppermute(value, axis, [(i, i ^ by) for i in range(lax.axis_size(axis))])  48 us
    ppermute x29, waiting for transfers between devices, crossed(): lax.ppermute(value, axis, [(i, i ^ by) for i in range(lax.axis_size(axis))])  24.8 us
    pallas_call x3, Pallas kernels, preload(): pl.pallas_call(functools.partial(preload_kernel, first), in_specs=[pl.Blo...  11.1 us
    pallas_call x4, Pallas kernels, grams(): pl.pallas_call(functools.partial(gram_kernel, places, count, rhs), in_spe...  9.14 us
    pallas_call x2, Pallas kernels, pull_back(): pl.pallas_call(pull_back_kernel, in_specs=[pl.BlockSpec(memory_space=pltp...  6.97 us
    pallas_call x1, Pallas kernels, update(): pl.pallas_call(update_kernel, grid=(weeks,), in_specs=[whole(sums.shape)]...  6.38 us
    pallas_call x1, Pallas kernels, forward(): pl.pallas_call(functools.partial(forward_kernel, len(pieces)), in_specs=[...  4.77 us
    pallas_call x1, Pallas kernels, spread_lon(): pl.pallas_call(spread_lon_kernel, in_specs=in_vmem(2), out_specs=in_vmem(...  4.72 us
  transfers between devices with their start and end apart: 32, of which 14 were waited for; matrix products, arithmetic and copies ran while one was open for 2% of the time, Pallas kernels for 20%

profile of v7, /device:TPU:0, one launch (start us, length us, event | category | flops | bytes accessed | tf_op | source)
XLA Modules:
  0.0 133.6 jit_solution(8200470652830621200)
XLA Ops:
  2.6 4.7 %spread_lon.1 = (f32[2,4,32,640]{3,2,1,0:T(8,128)S(1)}, s32[656,128]{1,0:T(8,128)S(1)}) custom-call(f32[2,4,32,640]{3,2,1,0:T(8,128)S(1)} %constant_dynamic-slice_fusion.field_ref, s32[32,640]{1,0:T(8,128)S(1)} %broadcast_in_dim.21.count_ref), custom_call_target="tpu_custom_call" | custom-call | flops 16384000 | bytes 1638400 | tf_op jit(solution)/shard_map/spread_lon/pallas_call | solution.py:196
  8.5 2.7 %collective-permute-start = (s32[1,1,384]{2,1,0:T(1,128)}, s32[1,1,384]{2,1,0:T(1,128)S(1)}, u32[]{:S(2)}, u32[]{:S(2)}) collective-permute-start(s32[1,1,384]{2,1,0:T(1,128)} %param.12), channel_id=1, source_target_pairs={{0,8},{8,0},{16,24},{24,16},{1,9},{9,1},{17,25},{25,17},{2,10},{10... | collective-permute-start | bytes 4616 | tf_op jit(solution)/shard_map/ppermute | solution.py:741
  11.2 2.6 %collective-permute-start.1 = (s32[1,1,384]{2,1,0:T(1,128)}, s32[1,1,384]{2,1,0:T(1,128)S(1)}, u32[]{:S(2)}, u32[]{:S(2)}) collective-permute-start(s32[1,1,384]{2,1,0:T(1,128)} %param.12), channel_id=1, source_target_pairs={{0,16},{8,24},{16,0},{24,8},{1,17},{9,25},{17,1},{25,9},{2,18},{10... | collective-permute-start | bytes 4616 | tf_op jit(solution)/shard_map/ppermute | solution.py:741
  15.9 3.5 %collective-permute-done.2 = s32[1,1,384]{2,1,0:T(1,128)S(1)} collective-permute-done((s32[1,1,384]{2,1,0:T(1,128)}, s32[1,1,384]{2,1,0:T(1,128)S(1)}, u32[]{:S(2)}, u32[]{:S(2)}) %collective-permute-start.2) | collective-permute-done | bytes 1568 | tf_op jit(solution)/shard_map/ppermute | solution.py:741
  22.7 3.7 %collective-permute-start.7 = (bf16[2,384,128]{2,1,0:T(8,128)(2,1)S(1)}, bf16[2,384,128]{2,1,0:T(8,128)(2,1)S(1)}, u32[]{:S(2)}, u32[]{:S(2)}) collective-permute-start(bf16[2,384,128]{2,1,0:T(8,128)(2,1)S(1)} %get-tuple-element.35), channel_id=1, source_target_pairs={{0,24},{8,16},{16,8},{24,0},{1,25},{9,17},{17,9},{25,1},{2,26},{10... | collective-permute-start | bytes 589832 | tf_op jit(solution)/shard_map/ppermute | solution.py:741
  26.5 2.9 %preload.3.rest_0_ = bf16[192,128,128]{2,1,0:T(8,128)(2,1)S(1)} custom-call(bf16[2,384,128]{2,1,0:T(8,128)(2,1)S(1)} %get-tuple-element.32.after_ref.rest_2_, bf16[384,128,128]{2,1,0:T(8,128)(2,1)} %bitcast.31), custom_call_target="tpu_custom_call" | custom-call | bytes 12582912 | tf_op jit(solution)/shard_map/preload/pallas_call | solution.py:301
  29.4 5.1 %preload.4.rest_1_ = bf16[192,128,128]{2,1,0:T(8,128)(2,1)S(1)} custom-call(bf16[2,384,128]{2,1,0:T(8,128)(2,1)S(1)} %get-tuple-element.32.after_ref.rest_2_, bf16[384,128,128]{2,1,0:T(8,128)(2,1)} %bitcast.32), custom_call_target="tpu_custom_call" | custom-call | bytes 12582912 | tf_op jit(solution)/shard_map/preload/pallas_call | solution.py:301
  36.5 4.8 %forward.1 = f32[256,128]{1,0:T(8,128)S(1)} custom-call(s32[384]{0:T(512)S(1)} %reduce.1.row_ref, f32[384]{0:T(512)S(1)} %exponential_reduce_fusion.scale_ref, bf16[192,128,128]{2,1,0:T(8,128)(2,1)S(1)} %preload.3.rest_0_, bf16[192,128,128]{2,1,0:T(8,128)(2,1)S(1)} %preload.4.rest_1_, bf16[2,384,128]{2,1,0:T(8,128)(2,1)S(1)} %get-tuple-element.32.after_ref.rest_2_, ...), custom_call_target="tpu_custom_call" | custom-call | flops 100663296 | bytes 12582912 | tf_op jit(solution)/shard_map/forward/pallas_call | solution.py:357
  41.2 4.1 %collective-permute-start.8 = (f32[256,128]{1,0:T(8,128)S(1)}, f32[256,128]{1,0:T(8,128)S(1)}, u32[]{:S(2)}, u32[]{:S(2)}) collective-permute-start(f32[256,128]{1,0:T(8,128)S(1)} %forward.1), channel_id=1, source_target_pairs={{0,1},{1,0},{2,3},{3,2},{4,5},{5,4},{6,7},{7,6},{8,9},{9,8},{10,11... | collective-permute-start | bytes 393224 | tf_op jit(solution)/shard_map/ppermute | solution.py:741
  46.4 2.7 %collective-permute-start.10 = (f32[256,128]{1,0:T(8,128)S(1)}, f32[256,128]{1,0:T(8,128)S(1)}, u32[]{:S(2)}, u32[]{:S(2)}) collective-permute-start(f32[256,128]{1,0:T(8,128)S(1)} %add.194.after_ref), channel_id=1, source_target_pairs={{0,4},{1,5},{2,6},{3,7},{4,0},{5,1},{6,2},{7,3},{8,12},{9,13},{10,... | collective-permute-start | bytes 393224 | tf_op jit(solution)/shard_map/ppermute | solution.py:741
  50.7 3.0 %preload.5.rest_1_ = bf16[192,128,128]{2,1,0:T(8,128)(2,1)S(1)} custom-call(f32[256,128]{1,0:T(8,128)S(1)} %add.194.after_ref, bf16[384,128,128]{2,1,0:T(8,128)(2,1)} %bitcast.33), custom_call_target="tpu_custom_call" | custom-call | bytes 12582912 | tf_op jit(solution)/shard_map/preload/pallas_call | solution.py:301
  57.1 3.3 %adjoint.1 = (s32[200,128]{1,0:T(8,128)S(1)}, s32[200,128]{1,0:T(8,128)S(1)}, s32[200,128]{1,0:T(8,128)S(1)}, s32[200,128]{1,0:T(8,128)S(1)}, s32[200,128]{1,0:T...) custom-call(s32[384]{0:T(512)S(1)} %reduce.1.row_ref, ...), custom_call_target="tpu_custom_call" | custom-call | flops 100663296 | bytes 12582912 | tf_op jit(solution)/shard_map/adjoint/pallas_call | solution.py:410
  60.4 3.6 %collective-permute-start.17 = (s32[200,128]{1,0:T(8,128)S(1)}, s32[200,128]{1,0:T(8,128)S(1)}, u32[]{:S(2)}, u32[]{:S(2)}) collective-permute-start(s32[200,128]{1,0:T(8,128)S(1)} %get-tuple-element.43), channel_id=1, source_target_pairs={{0,8},{8,0},{16,24},{24,16},{1,9},{9,1},{17,25},{25,17},{2,10},{10... | collective-permute-start | bytes 307208 | tf_op jit(solution)/shard_map/ppermute | solution.py:741
  64.1 2.3 %collective-permute-start.19 = (s32[200,128]{1,0:T(8,128)S(1)}, s32[200,128]{1,0:T(8,128)S(1)}, u32[]{:S(2)}, u32[]{:S(2)}) collective-permute-start(s32[200,128]{1,0:T(8,128)S(1)} %get-tuple-element.45), channel_id=1, source_target_pairs={{0,24},{8,16},{16,8},{24,0},{1,25},{9,17},{17,9},{25,1},{2,26},{10... | collective-permute-start | bytes 307208 | tf_op jit(solution)/shard_map/ppermute | solution.py:741
  68.5 2.3 %collective-permute-start.14 = (s32[200,128]{1,0:T(8,128)S(1)}, s32[200,128]{1,0:T(8,128)S(1)}, u32[]{:S(2)}, u32[]{:S(2)}) collective-permute-start(s32[200,128]{1,0:T(8,128)S(1)} %get-tuple-element.39), channel_id=1, source_target_pairs={{0,24},{8,16},{16,8},{24,0},{1,25},{9,17},{17,9},{25,1},{2,26},{10... | collective-permute-start | bytes 307208 | tf_op jit(solution)/shard_map/ppermute | solution.py:741
  71.4 3.8 %collective-permute-done.18.rest_2_ = s32[200,128]{1,0:T(8,128)S(1)} collective-permute-done((s32[200,128]{1,0:T(8,128)S(1)}, s32[200,128]{1,0:T(8,128)S(1)}, u32[]{:S(2)}, u32[]{:S(2)}) %collective-permute-start.18) | collective-permute-done | bytes 102432 | tf_op jit(solution)/shard_map/ppermute | solution.py:741
  77.2 5.5 %collective-permute-done.13.rest_2_ = s32[200,128]{1,0:T(8,128)S(1)} collective-permute-done((s32[200,128]{1,0:T(8,128)S(1)}, s32[200,128]{1,0:T(8,128)S(1)}, u32[]{:S(2)}, u32[]{:S(2)}) %collective-permute-start.13) | collective-permute-done | bytes 102432 | tf_op jit(solution)/shard_map/ppermute | solution.py:741
  84.8 3.5 %pull_back.3.rest_1_ = s32[328,128]{1,0:T(8,128)S(1)} custom-call(s32[1]{0:T(128)} %bitcast.side_ref, f32[1,4,32,640]{3,2,1,0:T(8,128)S(1)} %get-tuple-element.46.own_ref, s32[328,128]{1,0:T(8,128)S(1)} %collective-permute-done.20.pair_ref, s32[328,128]{1,0:T(8,128)S(1)} %collective-permute-done.21.cross_ref, f32[32,96]{1,0:T(8,128)S(1)} %get-tuple-element.61.weights_ref, ...), custom_call_target="tpu_custom_call" | custom-call | flops 24576000 | bytes 819200 | tf_op jit(solution)/shard_map/pull_back/pallas_call | solution.py:498
  88.2 4.3 %collective-permute-start.25 = (s32[328,128]{1,0:T(8,128)S(1)}, s32[328,128]{1,0:T(8,128)S(1)}, u32[]{:S(2)}, u32[]{:S(2)}) collective-permute-start(s32[328,128]{1,0:T(8,128)S(1)} %pull_back.3.rest_1_), channel_id=1, source_target_pairs={{0,16},{8,24},{16,0},{24,8},{1,17},{9,25},{17,1},{25,9},{2,18},{10... | collective-permute-start | bytes 503816 | tf_op jit(solution)/shard_map/ppermute | solution.py:741
  92.6 3.5 %pull_back.2.rest_0_ = s32[328,128]{1,0:T(8,128)S(1)} custom-call(s32[1]{0:T(128)} %bitcast.side_ref, f32[1,4,32,640]{3,2,1,0:T(8,128)S(1)} %get-tuple-element.40.own_ref, s32[328,128]{1,0:T(8,128)S(1)} %collective-permute-done.15.pair_ref, s32[328,128]{1,0:T(8,128)S(1)} %collective-permute-done.16.cross_ref, f32[32,96]{1,0:T(8,128)S(1)} %get-tuple-element.61.weights_ref, ...), custom_call_target="tpu_custom_call" | custom-call | flops 24576000 | bytes 819200 | tf_op jit(solution)/shard_map/pull_back/pallas_call | solution.py:498
  100.7 2.9 %grams.4 = (f32[8,4,32,640]{3,2,1,0:T(8,128)S(1)}, f32[8,256]{1,0:T(8,128)S(1)}) custom-call(s32[8]{0:T(128)S(1)} %add.175.order_ref, f32[8,256]{1,0:T(8,128)S(1)} %broadcast_in_dim.20.sums_before, f32[8,4,32,640]{3,2,1,0:T(8,128)S(1)} %copy-done.1, f32[8,4,32,640]{3,2,1,0:T(8,128)S(1)} %copy-done, s32[328,128]{1,0:T(8,128)S(1)} %pull_back.2.rest_0_, ...), custom_call_target="tpu_custom_call" | custom-call | flops 41943040 | bytes 10485760 | tf_op jit(solution)/shard_map/grams/pallas_call | solution.py:594
  106.5 3.1 %collective-permute-start.26 = (s32[328,128]{1,0:T(8,128)S(1)}, s32[328,128]{1,0:T(8,128)S(1)}, u32[]{:S(2)}, u32[]{:S(2)}) collective-permute-start(s32[328,128]{1,0:T(8,128)S(1)} %collective-permute-done.24.rest_0_), channel_id=1, source_target_pairs={{0,8},{8,0},{16,24},{24,16},{1,9},{9,1},{17,25},{25,17},{2,10},{10... | collective-permute-start | bytes 503816 | tf_op jit(solution)/shard_map/ppermute | solution.py:741
  119.5 2.5 %collective-permute-start.29 = (f32[8,256]{1,0:T(8,128)S(1)}, f32[8,256]{1,0:T(8,128)S(1)}, u32[]{:S(2)}, u32[]{:S(2)}) collective-permute-start(f32[8,256]{1,0:T(8,128)S(1)} %add.198), channel_id=1, source_target_pairs={{0,2},{1,3},{2,0},{3,1},{4,6},{5,7},{6,4},{7,5},{8,10},{9,11},{10,... | collective-permute-start | bytes 24584 | tf_op jit(solution)/shard_map/ppermute | solution.py:741
  127.2 6.4 %update.1 = (f32[8,4,32,640]{3,2,1,0:T(8,128)}, f32[8,4,32,640]{3,2,1,0:T(8,128)}, f32[8,4,32,640]{3,2,1,0:T(8,128)}) custom-call(f32[8,256]{1,0:T(8,128)S(1)} %add_add_fusion.sums_ref, f32[8,4,32,640]{3,2,1,0:T(8,128)S(1)} %copy-done.4, f32[8,4,32,640]{3,2,1,0:T(8,128)S(1)} %copy-done.2, f32[8,4,32,640]{3,2,1,0:T(8,128)S(1)} %copy-done, ...), custom_call_target="tpu_custom_call" | custom-call | flops 31457280 | bytes 18350080 | tf_op jit(solution)/shard_map/update/pallas_call | solution.py:725
  (113 shorter events, 45.9 us)
Async XLA Ops:
  7.3 12.6 %collective-permute-start.3 = (s32[656,128]{1,0:T(8,128)S(1)}, s32[656,128]{1,0:T(8,128)S(1)}, u32[]{:S(2)}, u32[]{:S(2)}) collective-permute-start(s32[656,128]{1,0:T(8,128)S(1)} %get-tuple-element.31), channel_id=1, source_target_pairs={{0,1},{1,0},{2,3},{3,2},{4,5},{5,4},{6,7},{7,6},{8,9},{9,8},{10,11... | collective-permute-start | bytes 1007624 | tf_op jit(solution)/shard_map/ppermute | solution.py:741
  7.9 12.0 %collective-permute-start.4 = (s32[656,128]{1,0:T(8,128)S(1)}, s32[656,128]{1,0:T(8,128)S(1)}, u32[]{:S(2)}, u32[]{:S(2)}) collective-permute-start(s32[656,128]{1,0:T(8,128)S(1)} %get-tuple-element.31), channel_id=1, source_target_pairs={{1,2},{3,4},{5,6},{2,1},{4,3},{6,5},{9,10},{11,12},{13,14},{10,9},... | collective-permute-start | bytes 1007624 | tf_op jit(solution)/shard_map/ppermute | solution.py:752
  8.5 7.1 %collective-permute-start = (s32[1,1,384]{2,1,0:T(1,128)}, s32[1,1,384]{2,1,0:T(1,128)S(1)}, u32[]{:S(2)}, u32[]{:S(2)}) collective-permute-start(s32[1,1,384]{2,1,0:T(1,128)} %param.12), channel_id=1, source_target_pairs={{0,8},{8,0},{16,24},{24,16},{1,9},{9,1},{17,25},{25,17},{2,10},{10... | collective-permute-start | bytes 4616 | tf_op jit(solution)/shard_map/ppermute | solution.py:741
  22.0 12.6 %collective-permute-start.5 = (bf16[2,384,128]{2,1,0:T(8,128)(2,1)S(1)}, bf16[2,384,128]{2,1,0:T(8,128)(2,1)S(1)}, u32[]{:S(2)}, u32[]{:S(2)}) collective-permute-start(bf16[2,384,128]{2,1,0:T(8,128)(2,1)S(1)} %get-tuple-element.33), channel_id=1, source_target_pairs={{0,8},{8,0},{16,24},{24,16},{1,9},{9,1},{17,25},{25,17},{2,10},{10... | collective-permute-start | bytes 589832 | tf_op jit(solution)/shard_map/ppermute | solution.py:741
  22.0 12.5 %collective-permute-start.6 = (bf16[2,384,128]{2,1,0:T(8,128)(2,1)S(1)}, bf16[2,384,128]{2,1,0:T(8,128)(2,1)S(1)}, u32[]{:S(2)}, u32[]{:S(2)}) collective-permute-start(bf16[2,384,128]{2,1,0:T(8,128)(2,1)S(1)} %get-tuple-element.34), channel_id=1, source_target_pairs={{0,16},{8,24},{16,0},{24,8},{1,17},{9,25},{17,1},{25,9},{2,18},{10... | collective-permute-start | bytes 589832 | tf_op jit(solution)/shard_map/ppermute | solution.py:741
  22.7 13.8 %collective-permute-start.7 = (bf16[2,384,128]{2,1,0:T(8,128)(2,1)S(1)}, bf16[2,384,128]{2,1,0:T(8,128)(2,1)S(1)}, u32[]{:S(2)}, u32[]{:S(2)}) collective-permute-start(bf16[2,384,128]{2,1,0:T(8,128)(2,1)S(1)} %get-tuple-element.35), channel_id=1, source_target_pairs={{0,24},{8,16},{16,8},{24,0},{1,25},{9,17},{17,9},{25,1},{2,26},{10... | collective-permute-start | bytes 589832 | tf_op jit(solution)/shard_map/ppermute | solution.py:741
  46.4 8.7 %collective-permute-start.10 = (f32[256,128]{1,0:T(8,128)S(1)}, f32[256,128]{1,0:T(8,128)S(1)}, u32[]{:S(2)}, u32[]{:S(2)}) collective-permute-start(f32[256,128]{1,0:T(8,128)S(1)} %add.194.after_ref), channel_id=1, source_target_pairs={{0,4},{1,5},{2,6},{3,7},{4,0},{5,1},{6,2},{7,3},{8,12},{9,13},{10,... | collective-permute-start | bytes 393224 | tf_op jit(solution)/shard_map/ppermute | solution.py:741
  49.1 7.3 %collective-permute-start.11 = (f32[256,128]{1,0:T(8,128)S(1)}, f32[256,128]{1,0:T(8,128)S(1)}, u32[]{:S(2)}, u32[]{:S(2)}) collective-permute-start(f32[256,128]{1,0:T(8,128)S(1)} %add.194.after_ref), channel_id=1, source_target_pairs={{0,6},{1,7},{2,4},{3,5},{4,2},{5,3},{6,0},{7,1},{8,14},{9,15},{10,... | collective-permute-start | bytes 393224 | tf_op jit(solution)/shard_map/ppermute | solution.py:741
  60.4 8.2 %collective-permute-start.17 = (s32[200,128]{1,0:T(8,128)S(1)}, s32[200,128]{1,0:T(8,128)S(1)}, u32[]{:S(2)}, u32[]{:S(2)}) collective-permute-start(s32[200,128]{1,0:T(8,128)S(1)} %get-tuple-element.43), channel_id=1, source_target_pairs={{0,8},{8,0},{16,24},{24,16},{1,9},{9,1},{17,25},{25,17},{2,10},{10... | collective-permute-start | bytes 307208 | tf_op jit(solution)/shard_map/ppermute | solution.py:741
  64.0 11.2 %collective-permute-start.18 = (s32[200,128]{1,0:T(8,128)S(1)}, s32[200,128]{1,0:T(8,128)S(1)}, u32[]{:S(2)}, u32[]{:S(2)}) collective-permute-start(s32[200,128]{1,0:T(8,128)S(1)} %get-tuple-element.44), channel_id=1, source_target_pairs={{0,16},{8,24},{16,0},{24,8},{1,17},{9,25},{17,1},{25,9},{2,18},{10... | collective-permute-start | bytes 307208 | tf_op jit(solution)/shard_map/ppermute | solution.py:741
  64.1 11.1 %collective-permute-start.19 = (s32[200,128]{1,0:T(8,128)S(1)}, s32[200,128]{1,0:T(8,128)S(1)}, u32[]{:S(2)}, u32[]{:S(2)}) collective-permute-start(s32[200,128]{1,0:T(8,128)S(1)} %get-tuple-element.45), channel_id=1, source_target_pairs={{0,24},{8,16},{16,8},{24,0},{1,25},{9,17},{17,9},{25,1},{2,26},{10... | collective-permute-start | bytes 307208 | tf_op jit(solution)/shard_map/ppermute | solution.py:741
  66.4 10.7 %collective-permute-start.12 = (s32[200,128]{1,0:T(8,128)S(1)}, s32[200,128]{1,0:T(8,128)S(1)}, u32[]{:S(2)}, u32[]{:S(2)}) collective-permute-start(s32[200,128]{1,0:T(8,128)S(1)} %get-tuple-element.37), channel_id=1, source_target_pairs={{0,8},{8,0},{16,24},{24,16},{1,9},{9,1},{17,25},{25,17},{2,10},{10... | collective-permute-start | bytes 307208 | tf_op jit(solution)/shard_map/ppermute | solution.py:741
  67.6 15.2 %collective-permute-start.13 = (s32[200,128]{1,0:T(8,128)S(1)}, s32[200,128]{1,0:T(8,128)S(1)}, u32[]{:S(2)}, u32[]{:S(2)}) collective-permute-start(s32[200,128]{1,0:T(8,128)S(1)} %get-tuple-element.38), channel_id=1, source_target_pairs={{0,16},{8,24},{16,0},{24,8},{1,17},{9,25},{17,1},{25,9},{2,18},{10... | collective-permute-start | bytes 307208 | tf_op jit(solution)/shard_map/ppermute | solution.py:741
  68.5 14.2 %collective-permute-start.14 = (s32[200,128]{1,0:T(8,128)S(1)}, s32[200,128]{1,0:T(8,128)S(1)}, u32[]{:S(2)}, u32[]{:S(2)}) collective-permute-start(s32[200,128]{1,0:T(8,128)S(1)} %get-tuple-element.39), channel_id=1, source_target_pairs={{0,24},{8,16},{16,8},{24,0},{1,25},{9,17},{17,9},{25,1},{2,26},{10... | collective-permute-start | bytes 307208 | tf_op jit(solution)/shard_map/ppermute | solution.py:741
  76.3 8.4 %collective-permute-start.20 = (s32[328,128]{1,0:T(8,128)S(1)}, s32[328,128]{1,0:T(8,128)S(1)}, u32[]{:S(2)}, u32[]{:S(2)}) collective-permute-start(s32[328,128]{1,0:T(8,128)S(1)} %get-tuple-element.47), channel_id=1, source_target_pairs={{0,1},{1,0},{2,3},{3,2},{4,5},{5,4},{6,7},{7,6},{8,9},{9,8},{10,11... | collective-permute-start | bytes 503816 | tf_op jit(solution)/shard_map/ppermute | solution.py:741
  76.4 8.4 %collective-permute-start.21 = (s32[328,128]{1,0:T(8,128)S(1)}, s32[328,128]{1,0:T(8,128)S(1)}, u32[]{:S(2)}, u32[]{:S(2)}) collective-permute-start(s32[328,128]{1,0:T(8,128)S(1)} %get-tuple-element.47), channel_id=1, source_target_pairs={{1,2},{3,4},{5,6},{2,1},{4,3},{6,5},{9,10},{11,12},{13,14},{10,9},... | collective-permute-start | bytes 503816 | tf_op jit(solution)/shard_map/ppermute | solution.py:752
  83.8 8.8 %collective-permute-start.15 = (s32[328,128]{1,0:T(8,128)S(1)}, s32[328,128]{1,0:T(8,128)S(1)}, u32[]{:S(2)}, u32[]{:S(2)}) collective-permute-start(s32[328,128]{1,0:T(8,128)S(1)} %get-tuple-element.41), channel_id=1, source_target_pairs={{0,1},{1,0},{2,3},{3,2},{4,5},{5,4},{6,7},{7,6},{8,9},{9,8},{10,11... | collective-permute-start | bytes 503816 | tf_op jit(solution)/shard_map/ppermute | solution.py:741
  83.9 8.7 %collective-permute-start.16 = (s32[328,128]{1,0:T(8,128)S(1)}, s32[328,128]{1,0:T(8,128)S(1)}, u32[]{:S(2)}, u32[]{:S(2)}) collective-permute-start(s32[328,128]{1,0:T(8,128)S(1)} %get-tuple-element.41), channel_id=1, source_target_pairs={{1,2},{3,4},{5,6},{2,1},{4,3},{6,5},{9,10},{11,12},{13,14},{10,9},... | collective-permute-start | bytes 503816 | tf_op jit(solution)/shard_map/ppermute | solution.py:752
  88.2 15.4 %collective-permute-start.25 = (s32[328,128]{1,0:T(8,128)S(1)}, s32[328,128]{1,0:T(8,128)S(1)}, u32[]{:S(2)}, u32[]{:S(2)}) collective-permute-start(s32[328,128]{1,0:T(8,128)S(1)} %pull_back.3.rest_1_), channel_id=1, source_target_pairs={{0,16},{8,24},{16,0},{24,8},{1,17},{9,25},{17,1},{25,9},{2,18},{10... | collective-permute-start | bytes 503816 | tf_op jit(solution)/shard_map/ppermute | solution.py:741
  92.5 17.0 %collective-permute-start.23 = (s32[328,128]{1,0:T(8,128)S(1)}, s32[328,128]{1,0:T(8,128)S(1)}, u32[]{:S(2)}, u32[]{:S(2)}) collective-permute-start(s32[328,128]{1,0:T(8,128)S(1)} %pull_back.3.rest_1_), channel_id=1, source_target_pairs={{0,8},{8,0},{16,24},{24,16},{1,9},{9,1},{17,25},{25,17},{2,10},{10... | collective-permute-start | bytes 503816 | tf_op jit(solution)/shard_map/ppermute | solution.py:741
  96.0 13.5 %collective-permute-start.22 = (s32[328,128]{1,0:T(8,128)S(1)}, s32[328,128]{1,0:T(8,128)}, u32[]{:S(2)}, u32[]{:S(2)}) collective-permute-start(s32[328,128]{1,0:T(8,128)S(1)} %pull_back.2.rest_0_), channel_id=1, source_target_pairs={{0,8},{8,0},{16,24},{24,16},{1,9},{9,1},{17,25},{25,17},{2,10},{10... | collective-permute-start | bytes 503816 | tf_op jit(solution)/shard_map/ppermute | solution.py:741
  98.1 8.3 %collective-permute-start.24 = (s32[328,128]{1,0:T(8,128)S(1)}, s32[328,128]{1,0:T(8,128)S(1)}, u32[]{:S(2)}, u32[]{:S(2)}) collective-permute-start(s32[328,128]{1,0:T(8,128)S(1)} %pull_back.2.rest_0_), channel_id=1, source_target_pairs={{0,16},{8,24},{16,0},{24,8},{1,17},{9,25},{17,1},{25,9},{2,18},{10... | collective-permute-start | bytes 503816 | tf_op jit(solution)/shard_map/ppermute | solution.py:741
  103.6 10.2 %collective-permute-start.27 = (s32[328,128]{1,0:T(8,128)S(1)}, s32[328,128]{1,0:T(8,128)S(1)}, u32[]{:S(2)}, u32[]{:S(2)}) collective-permute-start(s32[328,128]{1,0:T(8,128)S(1)} %collective-permute-done.25.rest_1_), channel_id=1, source_target_pairs={{0,8},{8,0},{16,24},{24,16},{1,9},{9,1},{17,25},{25,17},{2,10},{10... | collective-permute-start | bytes 503816 | tf_op jit(solution)/shard_map/ppermute | solution.py:741
  106.5 8.1 %collective-permute-start.26 = (s32[328,128]{1,0:T(8,128)S(1)}, s32[328,128]{1,0:T(8,128)S(1)}, u32[]{:S(2)}, u32[]{:S(2)}) collective-permute-start(s32[328,128]{1,0:T(8,128)S(1)} %collective-permute-done.24.rest_0_), channel_id=1, source_target_pairs={{0,8},{8,0},{16,24},{24,16},{1,9},{9,1},{17,25},{25,17},{2,10},{10... | collective-permute-start | bytes 503816 | tf_op jit(solution)/shard_map/ppermute | solution.py:741
  (18 other events, 127.8 us)

commit v8 on v7

--- a/solution.py
+++ b/solution.py
@@ -822,7 +822,10 @@
     own_width = lax.dynamic_slice_in_dim(lon_width, band * rows, rows)
     counts = jnp.broadcast_to(own_width[:, None] + 1, (rows, lon))
 
-    lists = jnp.concatenate([crossed(block_cols, "obs", d) for d in range(slots)], axis=0)[:, 0]
+    lists = block_cols
+    for reach in reversed(far_first(slots)):
+        lists = jnp.concatenate([lists, crossed(lists, "obs", reach)], axis=0)
+    lists = lists[:, 0]
     line, part = lists // parts, lists % parts
     places = ((line // rows) * parts + part) * rows + line % rows
 

time: 134 us -> 135 us (level)
  waiting for transfers between devices: 24.8 us -> 26.9 us
    ppermute x29 -> x28, waiting for transfers between devices: 24.8 us -> 26.9 us  [crossed(): lax.ppermute(value, axis, [(i, i ^ by) for i in range(lax.axis_size(axis))])]
    ppermute x29 -> x28, starting transfers between devices: 48 us -> 46.7 us  [crossed(): lax.ppermute(value, axis, [(i, i ^ by) for i in range(lax.axis_size(axis))])]
  transfers between devices with their start and end apart: 32 -> 31, of which waited for: 14 -> 11; matrix products, arithmetic and copies ran while one was open for 2% -> 3% of each run, Pallas kernels for 20% -> 20%
where the time goes in v8:
time: 135 us
  Pallas kernels  50.5 us (37%)
  starting transfers between devices  49 us (36%)
  waiting for transfers between devices  26.9 us (20%)
  local copies, waits for them, and re-layouts  4.05 us (3%)
  other arithmetic  3.62 us (3%)
    ppermute x28, starting transfers between devices, crossed(): lax.ppermute(value, axis, [(i, i ^ by) for i in range(lax.axis_size(axis))])  46.7 us
    ppermute x28, waiting for transfers between devices, crossed(): lax.ppermute(value, axis, [(i, i ^ by) for i in range(lax.axis_size(axis))])  26.9 us
    pallas_call x3, Pallas kernels, preload(): pl.pallas_call(functools.partial(preload_kernel, first), in_specs=[pl.Blo...  11.1 us
    pallas_call x4, Pallas kernels, grams(): pl.pallas_call(functools.partial(gram_kernel, places, count, rhs), in_spe...  9.14 us
    pallas_call x2, Pallas kernels, pull_back(): pl.pallas_call(pull_back_kernel, in_specs=[pl.BlockSpec(memory_space=pltp...  6.97 us
    pallas_call x1, Pallas kernels, update(): pl.pallas_call(update_kernel, grid=(weeks,), in_specs=[whole(sums.shape)]...  6.38 us
    pallas_call x1, Pallas kernels, forward(): pl.pallas_call(functools.partial(forward_kernel, len(pieces)), in_specs=[...  4.77 us
    pallas_call x1, Pallas kernels, spread_lon(): pl.pallas_call(spread_lon_kernel, in_specs=in_vmem(2), out_specs=in_vmem(...  4.72 us
  transfers between devices with their start and end apart: 31, of which 11 were waited for; matrix products, arithmetic and copies ran while one was open for 3% of the time, Pallas kernels for 20%

profile of v8, /device:TPU:0, one launch (start us, length us, event | category | flops | bytes accessed | tf_op | source)
XLA Modules:
  0.0 135.1 jit_solution(2234497403816207681)
XLA Ops:
  2.6 4.7 %spread_lon.1 = (f32[2,4,32,640]{3,2,1,0:T(8,128)S(1)}, s32[656,128]{1,0:T(8,128)S(1)}) custom-call(f32[2,4,32,640]{3,2,1,0:T(8,128)S(1)} %constant_dynamic-slice_fusion.field_ref, s32[32,640]{1,0:T(8,128)S(1)} %broadcast_in_dim.21.count_ref), custom_call_target="tpu_custom_call" | custom-call | flops 16384000 | bytes 1638400 | tf_op jit(solution)/shard_map/spread_lon/pallas_call | solution.py:196
  8.5 2.7 %collective-permute-start = (s32[1,1,384]{2,1,0:T(1,128)}, s32[1,1,384]{2,1,0:T(1,128)S(1)}, u32[]{:S(2)}, u32[]{:S(2)}) collective-permute-start(s32[1,1,384]{2,1,0:T(1,128)} %param.12), channel_id=1, source_target_pairs={{0,8},{8,0},{16,24},{24,16},{1,9},{9,1},{17,25},{25,17},{2,10},{10... | collective-permute-start | bytes 4616 | tf_op jit(solution)/shard_map/ppermute | solution.py:741
  13.7 3.0 %collective-permute-start.1 = (s32[2,1,384]{2,1,0:T(1,128)S(1)}, s32[2,1,384]{2,1,0:T(1,128)S(1)}, u32[]{:S(2)}, u32[]{:S(2)}) collective-permute-start(s32[2,1,384]{2,1,0:T(1,128)S(1)} %pad_add_fusion), channel_id=1, source_target_pairs={{0,16},{8,24},{16,0},{24,8},{1,17},{9,25},{17,1},{25,9},{2,18},{10... | collective-permute-start | bytes 9224 | tf_op jit(solution)/shard_map/ppermute | solution.py:741
  22.8 2.6 %collective-permute-start.5 = (bf16[2,384,128]{2,1,0:T(8,128)(2,1)S(1)}, bf16[2,384,128]{2,1,0:T(8,128)(2,1)S(1)}, u32[]{:S(2)}, u32[]{:S(2)}) collective-permute-start(bf16[2,384,128]{2,1,0:T(8,128)(2,1)S(1)} %get-tuple-element.34), channel_id=1, source_target_pairs={{0,16},{8,24},{16,0},{24,8},{1,17},{9,25},{17,1},{25,9},{2,18},{10... | collective-permute-start | bytes 589832 | tf_op jit(solution)/shard_map/ppermute | solution.py:741
  25.5 2.9 %preload.3.rest_0_ = bf16[192,128,128]{2,1,0:T(8,128)(2,1)S(1)} custom-call(bf16[2,384,128]{2,1,0:T(8,128)(2,1)S(1)} %get-tuple-element.32.after_ref.rest_2_, bf16[384,128,128]{2,1,0:T(8,128)(2,1)} %bitcast.31), custom_call_target="tpu_custom_call" | custom-call | bytes 12582912 | tf_op jit(solution)/shard_map/preload/pallas_call | solution.py:301
  28.4 5.1 %preload.4.rest_1_ = bf16[192,128,128]{2,1,0:T(8,128)(2,1)S(1)} custom-call(bf16[2,384,128]{2,1,0:T(8,128)(2,1)S(1)} %get-tuple-element.32.after_ref.rest_2_, bf16[384,128,128]{2,1,0:T(8,128)(2,1)} %bitcast.32), custom_call_target="tpu_custom_call" | custom-call | bytes 12582912 | tf_op jit(solution)/shard_map/preload/pallas_call | solution.py:301
  33.5 5.0 %collective-permute-done.6.rest_5_ = bf16[2,384,128]{2,1,0:T(8,128)(2,1)S(1)} collective-permute-done((bf16[2,384,128]{2,1,0:T(8,128)(2,1)S(1)}, bf16[2,384,128]{2,1,0:T(8,128)(2,1)S(1)}, u32[]{:S(2)}, u32[]{:S(2)}) %collective-permute-start.6) | collective-permute-done | bytes 196640 | tf_op jit(solution)/shard_map/ppermute | solution.py:741
  38.5 4.8 %forward.1 = f32[256,128]{1,0:T(8,128)S(1)} custom-call(s32[384]{0:T(512)S(1)} %reduce.1.row_ref, f32[384]{0:T(512)S(1)} %exponential_reduce_fusion.scale_ref, bf16[192,128,128]{2,1,0:T(8,128)(2,1)S(1)} %preload.3.rest_0_, bf16[192,128,128]{2,1,0:T(8,128)(2,1)S(1)} %preload.4.rest_1_, bf16[2,384,128]{2,1,0:T(8,128)(2,1)S(1)} %get-tuple-element.32.after_ref.rest_2_, ...), custom_call_target="tpu_custom_call" | custom-call | flops 100663296 | bytes 12582912 | tf_op jit(solution)/shard_map/forward/pallas_call | solution.py:357
  47.7 3.5 %collective-permute-start.8 = (f32[256,128]{1,0:T(8,128)S(1)}, f32[256,128]{1,0:T(8,128)S(1)}, u32[]{:S(2)}, u32[]{:S(2)}) collective-permute-start(f32[256,128]{1,0:T(8,128)S(1)} %add.194.after_ref), channel_id=1, source_target_pairs={{0,2},{1,3},{2,0},{3,1},{4,6},{5,7},{6,4},{7,5},{8,10},{9,11},{10,... | collective-permute-start | bytes 393224 | tf_op jit(solution)/shard_map/ppermute | solution.py:741
  51.3 3.0 %preload.5.rest_1_ = bf16[192,128,128]{2,1,0:T(8,128)(2,1)S(1)} custom-call(f32[256,128]{1,0:T(8,128)S(1)} %add.194.after_ref, bf16[384,128,128]{2,1,0:T(8,128)(2,1)} %bitcast.33), custom_call_target="tpu_custom_call" | custom-call | bytes 12582912 | tf_op jit(solution)/shard_map/preload/pallas_call | solution.py:301
  54.3 3.3 %collective-permute-done.8 = f32[256,128]{1,0:T(8,128)S(1)} collective-permute-done((f32[256,128]{1,0:T(8,128)S(1)}, f32[256,128]{1,0:T(8,128)S(1)}, u32[]{:S(2)}, u32[]{:S(2)}) %collective-permute-start.8) | collective-permute-done | bytes 131104 | tf_op jit(solution)/shard_map/ppermute | solution.py:741
  57.6 3.3 %adjoint.1 = (s32[200,128]{1,0:T(8,128)S(1)}, s32[200,128]{1,0:T(8,128)S(1)}, s32[200,128]{1,0:T(8,128)S(1)}, s32[200,128]{1,0:T(8,128)S(1)}, s32[200,128]{1,0:T...) custom-call(s32[384]{0:T(512)S(1)} %reduce.1.row_ref, ...), custom_call_target="tpu_custom_call" | custom-call | flops 100663296 | bytes 12582912 | tf_op jit(solution)/shard_map/adjoint/pallas_call | solution.py:410
  60.9 3.0 %collective-permute-start.16 = (s32[200,128]{1,0:T(8,128)S(1)}, s32[200,128]{1,0:T(8,128)S(1)}, u32[]{:S(2)}, u32[]{:S(2)}) collective-permute-start(s32[200,128]{1,0:T(8,128)S(1)} %get-tuple-element.43), channel_id=1, source_target_pairs={{0,8},{8,0},{16,24},{24,16},{1,9},{9,1},{17,25},{25,17},{2,10},{10... | collective-permute-start | bytes 307208 | tf_op jit(solution)/shard_map/ppermute | solution.py:741
  71.6 3.6 %collective-permute-done.17.rest_2_ = s32[200,128]{1,0:T(8,128)S(1)} collective-permute-done((s32[200,128]{1,0:T(8,128)S(1)}, s32[200,128]{1,0:T(8,128)S(1)}, u32[]{:S(2)}, u32[]{:S(2)}) %collective-permute-start.17) | collective-permute-done | bytes 102432 | tf_op jit(solution)/shard_map/ppermute | solution.py:741
  77.1 6.0 %collective-permute-done.12.rest_2_ = s32[200,128]{1,0:T(8,128)S(1)} collective-permute-done((s32[200,128]{1,0:T(8,128)S(1)}, s32[200,128]{1,0:T(8,128)S(1)}, u32[]{:S(2)}, u32[]{:S(2)}) %collective-permute-start.12) | collective-permute-done | bytes 102432 | tf_op jit(solution)/shard_map/ppermute | solution.py:741
  85.2 3.5 %pull_back.3.rest_1_ = s32[328,128]{1,0:T(8,128)S(1)} custom-call(s32[1]{0:T(128)} %bitcast.side_ref, f32[1,4,32,640]{3,2,1,0:T(8,128)S(1)} %get-tuple-element.46.own_ref, s32[328,128]{1,0:T(8,128)S(1)} %collective-permute-done.19.pair_ref, s32[328,128]{1,0:T(8,128)S(1)} %collective-permute-done.20.cross_ref, f32[32,96]{1,0:T(8,128)S(1)} %get-tuple-element.61.weights_ref, ...), custom_call_target="tpu_custom_call" | custom-call | flops 24576000 | bytes 819200 | tf_op jit(solution)/shard_map/pull_back/pallas_call | solution.py:498
  88.7 5.4 %collective-permute-start.24 = (s32[328,128]{1,0:T(8,128)S(1)}, s32[328,128]{1,0:T(8,128)S(1)}, u32[]{:S(2)}, u32[]{:S(2)}) collective-permute-start(s32[328,128]{1,0:T(8,128)S(1)} %pull_back.3.rest_1_), channel_id=1, source_target_pairs={{0,16},{8,24},{16,0},{24,8},{1,17},{9,25},{17,1},{25,9},{2,18},{10... | collective-permute-start | bytes 503816 | tf_op jit(solution)/shard_map/ppermute | solution.py:741
  94.1 3.5 %pull_back.2.rest_0_ = s32[328,128]{1,0:T(8,128)S(1)} custom-call(s32[1]{0:T(128)} %bitcast.side_ref, f32[1,4,32,640]{3,2,1,0:T(8,128)S(1)} %get-tuple-element.40.own_ref, s32[328,128]{1,0:T(8,128)S(1)} %collective-permute-done.14.pair_ref, s32[328,128]{1,0:T(8,128)S(1)} %collective-permute-done.15.cross_ref, f32[32,96]{1,0:T(8,128)S(1)} %get-tuple-element.61.weights_ref, ...), custom_call_target="tpu_custom_call" | custom-call | flops 24576000 | bytes 819200 | tf_op jit(solution)/shard_map/pull_back/pallas_call | solution.py:498
  97.6 2.1 %collective-permute-start.21 = (s32[328,128]{1,0:T(8,128)S(1)}, s32[328,128]{1,0:T(8,128)}, u32[]{:S(2)}, u32[]{:S(2)}) collective-permute-start(s32[328,128]{1,0:T(8,128)S(1)} %pull_back.2.rest_0_), channel_id=1, source_target_pairs={{0,8},{8,0},{16,24},{24,16},{1,9},{9,1},{17,25},{25,17},{2,10},{10... | collective-permute-start | bytes 503816 | tf_op jit(solution)/shard_map/ppermute | solution.py:741
  102.0 2.9 %grams.4 = (f32[8,4,32,640]{3,2,1,0:T(8,128)S(1)}, f32[8,256]{1,0:T(8,128)S(1)}) custom-call(s32[8]{0:T(128)S(1)} %add.175.order_ref, f32[8,256]{1,0:T(8,128)S(1)} %broadcast_in_dim.20.sums_before, f32[8,4,32,640]{3,2,1,0:T(8,128)S(1)} %copy-done.1, f32[8,4,32,640]{3,2,1,0:T(8,128)S(1)} %copy-done, s32[328,128]{1,0:T(8,128)S(1)} %pull_back.2.rest_0_, ...), custom_call_target="tpu_custom_call" | custom-call | flops 41943040 | bytes 10485760 | tf_op jit(solution)/shard_map/grams/pallas_call | solution.py:594
  108.0 2.9 %collective-permute-start.25 = (s32[328,128]{1,0:T(8,128)S(1)}, s32[328,128]{1,0:T(8,128)S(1)}, u32[]{:S(2)}, u32[]{:S(2)}) collective-permute-start(s32[328,128]{1,0:T(8,128)S(1)} %collective-permute-done.23.rest_0_), channel_id=1, source_target_pairs={{0,8},{8,0},{16,24},{24,16},{1,9},{9,1},{17,25},{25,17},{2,10},{10... | collective-permute-start | bytes 503816 | tf_op jit(solution)/shard_map/ppermute | solution.py:741
  111.0 2.2 %grams.5 = (f32[8,4,32,640]{3,2,1,0:T(8,128)S(1)}, f32[8,256]{1,0:T(8,128)S(1)}) custom-call(s32[8]{0:T(128)S(1)} %add.175.order_ref, f32[8,256]{1,0:T(8,128)S(1)} %get-tuple-element.48.sums_before, f32[8,4,32,640]{3,2,1,0:T(8,128)S(1)} %copy-done.1, f32[8,4,32,640]{3,2,1,0:T(8,128)S(1)} %copy-done, ...), custom_call_target="tpu_custom_call", output_to_operand_aliasing={{0}: (6, {})} | custom-call | flops 41943040 | bytes 10485760 | tf_op jit(solution)/shard_map/grams/pallas_call | solution.py:594
  120.7 2.7 %collective-permute-start.28 = (f32[8,256]{1,0:T(8,128)S(1)}, f32[8,256]{1,0:T(8,128)S(1)}, u32[]{:S(2)}, u32[]{:S(2)}) collective-permute-start(f32[8,256]{1,0:T(8,128)S(1)} %add.198), channel_id=1, source_target_pairs={{0,2},{1,3},{2,0},{3,1},{4,6},{5,7},{6,4},{7,5},{8,10},{9,11},{10,... | collective-permute-start | bytes 24584 | tf_op jit(solution)/shard_map/ppermute | solution.py:741
  128.7 6.4 %update.1 = (f32[8,4,32,640]{3,2,1,0:T(8,128)}, f32[8,4,32,640]{3,2,1,0:T(8,128)}, f32[8,4,32,640]{3,2,1,0:T(8,128)}) custom-call(f32[8,256]{1,0:T(8,128)S(1)} %add_add_fusion.sums_ref, f32[8,4,32,640]{3,2,1,0:T(8,128)S(1)} %copy-done.4, f32[8,4,32,640]{3,2,1,0:T(8,128)S(1)} %copy-done.2, f32[8,4,32,640]{3,2,1,0:T(8,128)S(1)} %copy-done, ...), custom_call_target="tpu_custom_call" | custom-call | flops 31457280 | bytes 18350080 | tf_op jit(solution)/shard_map/update/pallas_call | solution.py:725
  (111 shorter events, 46.2 us)
Async XLA Ops:
  7.3 11.4 %collective-permute-start.2 = (s32[656,128]{1,0:T(8,128)S(1)}, s32[656,128]{1,0:T(8,128)S(1)}, u32[]{:S(2)}, u32[]{:S(2)}) collective-permute-start(s32[656,128]{1,0:T(8,128)S(1)} %get-tuple-element.31), channel_id=1, source_target_pairs={{0,1},{1,0},{2,3},{3,2},{4,5},{5,4},{6,7},{7,6},{8,9},{9,8},{10,11... | collective-permute-start | bytes 1007624 | tf_op jit(solution)/shard_map/ppermute | solution.py:741
  7.9 10.9 %collective-permute-start.3 = (s32[656,128]{1,0:T(8,128)S(1)}, s32[656,128]{1,0:T(8,128)S(1)}, u32[]{:S(2)}, u32[]{:S(2)}) collective-permute-start(s32[656,128]{1,0:T(8,128)S(1)} %get-tuple-element.31), channel_id=1, source_target_pairs={{1,2},{3,4},{5,6},{2,1},{4,3},{6,5},{9,10},{11,12},{13,14},{10,9},... | collective-permute-start | bytes 1007624 | tf_op jit(solution)/shard_map/ppermute | solution.py:752
  20.8 12.7 %collective-permute-start.4 = (bf16[2,384,128]{2,1,0:T(8,128)(2,1)S(1)}, bf16[2,384,128]{2,1,0:T(8,128)(2,1)S(1)}, u32[]{:S(2)}, u32[]{:S(2)}) collective-permute-start(bf16[2,384,128]{2,1,0:T(8,128)(2,1)S(1)} %get-tuple-element.33), channel_id=1, source_target_pairs={{0,8},{8,0},{16,24},{24,16},{1,9},{9,1},{17,25},{25,17},{2,10},{10... | collective-permute-start | bytes 589832 | tf_op jit(solution)/shard_map/ppermute | solution.py:741
  22.8 10.7 %collective-permute-start.5 = (bf16[2,384,128]{2,1,0:T(8,128)(2,1)S(1)}, bf16[2,384,128]{2,1,0:T(8,128)(2,1)S(1)}, u32[]{:S(2)}, u32[]{:S(2)}) collective-permute-start(bf16[2,384,128]{2,1,0:T(8,128)(2,1)S(1)} %get-tuple-element.34), channel_id=1, source_target_pairs={{0,16},{8,24},{16,0},{24,8},{1,17},{9,25},{17,1},{25,9},{2,18},{10... | collective-permute-start | bytes 589832 | tf_op jit(solution)/shard_map/ppermute | solution.py:741
  25.4 13.1 %collective-permute-start.6 = (bf16[2,384,128]{2,1,0:T(8,128)(2,1)S(1)}, bf16[2,384,128]{2,1,0:T(8,128)(2,1)S(1)}, u32[]{:S(2)}, u32[]{:S(2)}) collective-permute-start(bf16[2,384,128]{2,1,0:T(8,128)(2,1)S(1)} %get-tuple-element.35), channel_id=1, source_target_pairs={{0,24},{8,16},{16,8},{24,0},{1,25},{9,17},{17,9},{25,1},{2,26},{10... | collective-permute-start | bytes 589832 | tf_op jit(solution)/shard_map/ppermute | solution.py:741
  46.3 8.0 %collective-permute-start.10 = (f32[256,128]{1,0:T(8,128)S(1)}, f32[256,128]{1,0:T(8,128)S(1)}, u32[]{:S(2)}, u32[]{:S(2)}) collective-permute-start(f32[256,128]{1,0:T(8,128)S(1)} %add.194.after_ref), channel_id=1, source_target_pairs={{0,6},{1,7},{2,4},{3,5},{4,2},{5,3},{6,0},{7,1},{8,14},{9,15},{10,... | collective-permute-start | bytes 393224 | tf_op jit(solution)/shard_map/ppermute | solution.py:741
  47.7 9.8 %collective-permute-start.8 = (f32[256,128]{1,0:T(8,128)S(1)}, f32[256,128]{1,0:T(8,128)S(1)}, u32[]{:S(2)}, u32[]{:S(2)}) collective-permute-start(f32[256,128]{1,0:T(8,128)S(1)} %add.194.after_ref), channel_id=1, source_target_pairs={{0,2},{1,3},{2,0},{3,1},{4,6},{5,7},{6,4},{7,5},{8,10},{9,11},{10,... | collective-permute-start | bytes 393224 | tf_op jit(solution)/shard_map/ppermute | solution.py:741
  51.2 6.4 %collective-permute-start.9 = (f32[256,128]{1,0:T(8,128)S(1)}, f32[256,128]{1,0:T(8,128)S(1)}, u32[]{:S(2)}, u32[]{:S(2)}) collective-permute-start(f32[256,128]{1,0:T(8,128)S(1)} %add.194.after_ref), channel_id=1, source_target_pairs={{0,4},{1,5},{2,6},{3,7},{4,0},{5,1},{6,2},{7,3},{8,12},{9,13},{10,... | collective-permute-start | bytes 393224 | tf_op jit(solution)/shard_map/ppermute | solution.py:741
  60.9 8.5 %collective-permute-start.16 = (s32[200,128]{1,0:T(8,128)S(1)}, s32[200,128]{1,0:T(8,128)S(1)}, u32[]{:S(2)}, u32[]{:S(2)}) collective-permute-start(s32[200,128]{1,0:T(8,128)S(1)} %get-tuple-element.43), channel_id=1, source_target_pairs={{0,8},{8,0},{16,24},{24,16},{1,9},{9,1},{17,25},{25,17},{2,10},{10... | collective-permute-start | bytes 307208 | tf_op jit(solution)/shard_map/ppermute | solution.py:741
  63.9 11.2 %collective-permute-start.17 = (s32[200,128]{1,0:T(8,128)S(1)}, s32[200,128]{1,0:T(8,128)S(1)}, u32[]{:S(2)}, u32[]{:S(2)}) collective-permute-start(s32[200,128]{1,0:T(8,128)S(1)} %get-tuple-element.44), channel_id=1, source_target_pairs={{0,16},{8,24},{16,0},{24,8},{1,17},{9,25},{17,1},{25,9},{2,18},{10... | collective-permute-start | bytes 307208 | tf_op jit(solution)/shard_map/ppermute | solution.py:741
  65.0 10.1 %collective-permute-start.18 = (s32[200,128]{1,0:T(8,128)S(1)}, s32[200,128]{1,0:T(8,128)S(1)}, u32[]{:S(2)}, u32[]{:S(2)}) collective-permute-start(s32[200,128]{1,0:T(8,128)S(1)} %get-tuple-element.45), channel_id=1, source_target_pairs={{0,24},{8,16},{16,8},{24,0},{1,25},{9,17},{17,9},{25,1},{2,26},{10... | collective-permute-start | bytes 307208 | tf_op jit(solution)/shard_map/ppermute | solution.py:741
  66.6 10.6 %collective-permute-start.11 = (s32[200,128]{1,0:T(8,128)S(1)}, s32[200,128]{1,0:T(8,128)S(1)}, u32[]{:S(2)}, u32[]{:S(2)}) collective-permute-start(s32[200,128]{1,0:T(8,128)S(1)} %get-tuple-element.37), channel_id=1, source_target_pairs={{0,8},{8,0},{16,24},{24,16},{1,9},{9,1},{17,25},{25,17},{2,10},{10... | collective-permute-start | bytes 307208 | tf_op jit(solution)/shard_map/ppermute | solution.py:741
  67.5 15.7 %collective-permute-start.12 = (s32[200,128]{1,0:T(8,128)S(1)}, s32[200,128]{1,0:T(8,128)S(1)}, u32[]{:S(2)}, u32[]{:S(2)}) collective-permute-start(s32[200,128]{1,0:T(8,128)S(1)} %get-tuple-element.38), channel_id=1, source_target_pairs={{0,16},{8,24},{16,0},{24,8},{1,17},{9,25},{17,1},{25,9},{2,18},{10... | collective-permute-start | bytes 307208 | tf_op jit(solution)/shard_map/ppermute | solution.py:741
  69.4 13.7 %collective-permute-start.13 = (s32[200,128]{1,0:T(8,128)S(1)}, s32[200,128]{1,0:T(8,128)S(1)}, u32[]{:S(2)}, u32[]{:S(2)}) collective-permute-start(s32[200,128]{1,0:T(8,128)S(1)} %get-tuple-element.39), channel_id=1, source_target_pairs={{0,24},{8,16},{16,8},{24,0},{1,25},{9,17},{17,9},{25,1},{2,26},{10... | collective-permute-start | bytes 307208 | tf_op jit(solution)/shard_map/ppermute | solution.py:741
  76.2 8.9 %collective-permute-start.19 = (s32[328,128]{1,0:T(8,128)S(1)}, s32[328,128]{1,0:T(8,128)S(1)}, u32[]{:S(2)}, u32[]{:S(2)}) collective-permute-start(s32[328,128]{1,0:T(8,128)S(1)} %get-tuple-element.47), channel_id=1, source_target_pairs={{0,1},{1,0},{2,3},{3,2},{4,5},{5,4},{6,7},{7,6},{8,9},{9,8},{10,11... | collective-permute-start | bytes 503816 | tf_op jit(solution)/shard_map/ppermute | solution.py:741
  76.3 8.9 %collective-permute-start.20 = (s32[328,128]{1,0:T(8,128)S(1)}, s32[328,128]{1,0:T(8,128)S(1)}, u32[]{:S(2)}, u32[]{:S(2)}) collective-permute-start(s32[328,128]{1,0:T(8,128)S(1)} %get-tuple-element.47), channel_id=1, source_target_pairs={{1,2},{3,4},{5,6},{2,1},{4,3},{6,5},{9,10},{11,12},{13,14},{10,9},... | collective-permute-start | bytes 503816 | tf_op jit(solution)/shard_map/ppermute | solution.py:752
  84.2 9.9 %collective-permute-start.14 = (s32[328,128]{1,0:T(8,128)S(1)}, s32[328,128]{1,0:T(8,128)S(1)}, u32[]{:S(2)}, u32[]{:S(2)}) collective-permute-start(s32[328,128]{1,0:T(8,128)S(1)} %get-tuple-element.41), channel_id=1, source_target_pairs={{0,1},{1,0},{2,3},{3,2},{4,5},{5,4},{6,7},{7,6},{8,9},{9,8},{10,11... | collective-permute-start | bytes 503816 | tf_op jit(solution)/shard_map/ppermute | solution.py:741
  84.3 9.8 %collective-permute-start.15 = (s32[328,128]{1,0:T(8,128)S(1)}, s32[328,128]{1,0:T(8,128)S(1)}, u32[]{:S(2)}, u32[]{:S(2)}) collective-permute-start(s32[328,128]{1,0:T(8,128)S(1)} %get-tuple-element.41), channel_id=1, source_target_pairs={{1,2},{3,4},{5,6},{2,1},{4,3},{6,5},{9,10},{11,12},{13,14},{10,9},... | collective-permute-start | bytes 503816 | tf_op jit(solution)/shard_map/ppermute | solution.py:752
  88.7 16.2 %collective-permute-start.24 = (s32[328,128]{1,0:T(8,128)S(1)}, s32[328,128]{1,0:T(8,128)S(1)}, u32[]{:S(2)}, u32[]{:S(2)}) collective-permute-start(s32[328,128]{1,0:T(8,128)S(1)} %pull_back.3.rest_1_), channel_id=1, source_target_pairs={{0,16},{8,24},{16,0},{24,8},{1,17},{9,25},{17,1},{25,9},{2,18},{10... | collective-permute-start | bytes 503816 | tf_op jit(solution)/shard_map/ppermute | solution.py:741
  94.1 16.9 %collective-permute-start.22 = (s32[328,128]{1,0:T(8,128)S(1)}, s32[328,128]{1,0:T(8,128)S(1)}, u32[]{:S(2)}, u32[]{:S(2)}) collective-permute-start(s32[328,128]{1,0:T(8,128)S(1)} %pull_back.3.rest_1_), channel_id=1, source_target_pairs={{0,8},{8,0},{16,24},{24,16},{1,9},{9,1},{17,25},{25,17},{2,10},{10... | collective-permute-start | bytes 503816 | tf_op jit(solution)/shard_map/ppermute | solution.py:741
  97.6 13.4 %collective-permute-start.21 = (s32[328,128]{1,0:T(8,128)S(1)}, s32[328,128]{1,0:T(8,128)}, u32[]{:S(2)}, u32[]{:S(2)}) collective-permute-start(s32[328,128]{1,0:T(8,128)S(1)} %pull_back.2.rest_0_), channel_id=1, source_target_pairs={{0,8},{8,0},{16,24},{24,16},{1,9},{9,1},{17,25},{25,17},{2,10},{10... | collective-permute-start | bytes 503816 | tf_op jit(solution)/shard_map/ppermute | solution.py:741
  99.6 8.4 %collective-permute-start.23 = (s32[328,128]{1,0:T(8,128)S(1)}, s32[328,128]{1,0:T(8,128)S(1)}, u32[]{:S(2)}, u32[]{:S(2)}) collective-permute-start(s32[328,128]{1,0:T(8,128)S(1)} %pull_back.2.rest_0_), channel_id=1, source_target_pairs={{0,16},{8,24},{16,0},{24,8},{1,17},{9,25},{17,1},{25,9},{2,18},{10... | collective-permute-start | bytes 503816 | tf_op jit(solution)/shard_map/ppermute | solution.py:741
  104.9 10.3 %collective-permute-start.26 = (s32[328,128]{1,0:T(8,128)S(1)}, s32[328,128]{1,0:T(8,128)S(1)}, u32[]{:S(2)}, u32[]{:S(2)}) collective-permute-start(s32[328,128]{1,0:T(8,128)S(1)} %collective-permute-done.24.rest_1_), channel_id=1, source_target_pairs={{0,8},{8,0},{16,24},{24,16},{1,9},{9,1},{17,25},{25,17},{2,10},{10... | collective-permute-start | bytes 503816 | tf_op jit(solution)/shard_map/ppermute | solution.py:741
  108.0 8.2 %collective-permute-start.25 = (s32[328,128]{1,0:T(8,128)S(1)}, s32[328,128]{1,0:T(8,128)S(1)}, u32[]{:S(2)}, u32[]{:S(2)}) collective-permute-start(s32[328,128]{1,0:T(8,128)S(1)} %collective-permute-done.23.rest_0_), channel_id=1, source_target_pairs={{0,8},{8,0},{16,24},{24,16},{1,9},{9,1},{17,25},{25,17},{2,10},{10... | collective-permute-start | bytes 503816 | tf_op jit(solution)/shard_map/ppermute | solution.py:741
  (17 other events, 121.5 us)

commit v9 on v7

--- a/solution.py
+++ b/solution.py
@@ -9,10 +9,10 @@
 from jax.sharding import PartitionSpec as P
 
 LANES = 128
-CHUNK = 96
+CHUNK = 192
 COPIES = 12
 STREAM_MIB = 40
-KEPT, KEPT_OF = 1, 2
+KEPT, KEPT_OF = 0, 2
 BACK_GROUPS = 2
 SUBLANES = 8
 MIB = 1024 * 1024

time: 134 us -> 133 us (level)
  Pallas kernels: 50.5 us -> 48.3 us
  waiting for transfers between devices: 24.8 us -> 26.5 us
    ppermute x29, waiting for transfers between devices: 24.8 us -> 26.5 us  [crossed(): lax.ppermute(value, axis, [(i, i ^ by) for i in range(lax.axis_size(axis))])]
    pallas_call x3 -> x2, Pallas kernels: 11.1 us -> 9.41 us  [preload(): pl.pallas_call(functools.partial(preload_kernel, first), in_specs=[pl.Blo...]
  transfers between devices with their start and end apart: 32 -> 32, of which waited for: 14 -> 14; matrix products, arithmetic and copies ran while one was open for 2% -> 2% of each run, Pallas kernels for 20% -> 19%
where the time goes in v9:
time: 133 us
  starting transfers between devices  50.3 us (38%)
  Pallas kernels  48.3 us (36%)
  waiting for transfers between devices  26.5 us (20%)
  local copies, waits for them, and re-layouts  4.05 us (3%)
  other arithmetic  2.93 us (2%)
    ppermute x29, starting transfers between devices, crossed(): lax.ppermute(value, axis, [(i, i ^ by) for i in range(lax.axis_size(axis))])  48 us
    ppermute x29, waiting for transfers between devices, crossed(): lax.ppermute(value, axis, [(i, i ^ by) for i in range(lax.axis_size(axis))])  26.5 us
    pallas_call x2, Pallas kernels, preload(): pl.pallas_call(functools.partial(preload_kernel, first), in_specs=[pl.Blo...  9.41 us
    pallas_call x4, Pallas kernels, grams(): pl.pallas_call(functools.partial(gram_kernel, places, count, rhs), in_spe...  9.14 us
    pallas_call x2, Pallas kernels, pull_back(): pl.pallas_call(pull_back_kernel, in_specs=[pl.BlockSpec(memory_space=pltp...  6.97 us
    pallas_call x1, Pallas kernels, update(): pl.pallas_call(update_kernel, grid=(weeks,), in_specs=[whole(sums.shape)]...  6.39 us
    pallas_call x1, Pallas kernels, spread_lon(): pl.pallas_call(spread_lon_kernel, in_specs=in_vmem(2), out_specs=in_vmem(...  4.72 us
    pallas_call x1, Pallas kernels, forward(): pl.pallas_call(functools.partial(forward_kernel, len(pieces)), in_specs=[...  4.51 us
  transfers between devices with their start and end apart: 32, of which 14 were waited for; matrix products, arithmetic and copies ran while one was open for 2% of the time, Pallas kernels for 19%

profile of v9, /device:TPU:0, one launch (start us, length us, event | category | flops | bytes accessed | tf_op | source)
XLA Modules:
  0.0 133.1 jit_solution(4951408781285434357)
XLA Ops:
  2.6 4.7 %spread_lon.1 = (f32[2,4,32,640]{3,2,1,0:T(8,128)S(1)}, s32[656,128]{1,0:T(8,128)S(1)}) custom-call(f32[2,4,32,640]{3,2,1,0:T(8,128)S(1)} %constant_dynamic-slice_fusion.field_ref, s32[32,640]{1,0:T(8,128)S(1)} %broadcast_in_dim.21.count_ref), custom_call_target="tpu_custom_call" | custom-call | flops 16384000 | bytes 1638400 | tf_op jit(solution)/shard_map/spread_lon/pallas_call | solution.py:196
  8.5 2.7 %collective-permute-start = (s32[1,1,384]{2,1,0:T(1,128)}, s32[1,1,384]{2,1,0:T(1,128)S(1)}, u32[]{:S(2)}, u32[]{:S(2)}) collective-permute-start(s32[1,1,384]{2,1,0:T(1,128)} %param.12), channel_id=1, source_target_pairs={{0,8},{8,0},{16,24},{24,16},{1,9},{9,1},{17,25},{25,17},{2,10},{10... | collective-permute-start | bytes 4616 | tf_op jit(solution)/shard_map/ppermute | solution.py:741
  11.2 2.6 %collective-permute-start.1 = (s32[1,1,384]{2,1,0:T(1,128)}, s32[1,1,384]{2,1,0:T(1,128)S(1)}, u32[]{:S(2)}, u32[]{:S(2)}) collective-permute-start(s32[1,1,384]{2,1,0:T(1,128)} %param.12), channel_id=1, source_target_pairs={{0,16},{8,24},{16,0},{24,8},{1,17},{9,25},{17,1},{25,9},{2,18},{10... | collective-permute-start | bytes 4616 | tf_op jit(solution)/shard_map/ppermute | solution.py:741
  15.9 3.5 %collective-permute-done.2 = s32[1,1,384]{2,1,0:T(1,128)S(1)} collective-permute-done((s32[1,1,384]{2,1,0:T(1,128)}, s32[1,1,384]{2,1,0:T(1,128)S(1)}, u32[]{:S(2)}, u32[]{:S(2)}) %collective-permute-start.2) | collective-permute-done | bytes 1568 | tf_op jit(solution)/shard_map/ppermute | solution.py:741
  22.7 3.7 %collective-permute-start.7 = (bf16[2,384,128]{2,1,0:T(8,128)(2,1)S(1)}, bf16[2,384,128]{2,1,0:T(8,128)(2,1)S(1)}, u32[]{:S(2)}, u32[]{:S(2)}) collective-permute-start(bf16[2,384,128]{2,1,0:T(8,128)(2,1)S(1)} %get-tuple-element.35), channel_id=1, source_target_pairs={{0,24},{8,16},{16,8},{24,0},{1,25},{9,17},{17,9},{25,1},{2,26},{10... | collective-permute-start | bytes 589832 | tf_op jit(solution)/shard_map/ppermute | solution.py:741
  26.5 4.7 %preload.2.rest_0_ = bf16[384,128,128]{2,1,0:T(8,128)(2,1)S(1)} custom-call(bf16[2,384,128]{2,1,0:T(8,128)(2,1)S(1)} %get-tuple-element.32.after_ref.rest_1_, bf16[384,128,128]{2,1,0:T(8,128)(2,1)} %bitcast.29), custom_call_target="tpu_custom_call" | custom-call | bytes 25165824 | tf_op jit(solution)/shard_map/preload/pallas_call | solution.py:301
  33.3 3.2 %collective-permute-done.7.rest_4_ = bf16[2,384,128]{2,1,0:T(8,128)(2,1)S(1)} collective-permute-done((bf16[2,384,128]{2,1,0:T(8,128)(2,1)S(1)}, bf16[2,384,128]{2,1,0:T(8,128)(2,1)S(1)}, u32[]{:S(2)}, u32[]{:S(2)}) %collective-permute-start.7) | collective-permute-done | bytes 196640 | tf_op jit(solution)/shard_map/ppermute | solution.py:741
  36.5 4.5 %forward.1 = f32[256,128]{1,0:T(8,128)S(1)} custom-call(s32[384]{0:T(512)S(1)} %reduce.1.row_ref, f32[384]{0:T(512)S(1)} %exponential_reduce_fusion.scale_ref, bf16[384,128,128]{2,1,0:T(8,128)(2,1)S(1)} %preload.2.rest_0_, bf16[2,384,128]{2,1,0:T(8,128)(2,1)S(1)} %get-tuple-element.32.after_ref.rest_1_, ...), custom_call_target="tpu_custom_call" | custom-call | flops 100663296 | bytes 12582912 | tf_op jit(solution)/shard_map/forward/pallas_call | solution.py:357
  41.0 4.1 %collective-permute-start.8 = (f32[256,128]{1,0:T(8,128)S(1)}, f32[256,128]{1,0:T(8,128)S(1)}, u32[]{:S(2)}, u32[]{:S(2)}) collective-permute-start(f32[256,128]{1,0:T(8,128)S(1)} %forward.1), channel_id=1, source_target_pairs={{0,1},{1,0},{2,3},{3,2},{4,5},{5,4},{6,7},{7,6},{8,9},{9,8},{10,11... | collective-permute-start | bytes 393224 | tf_op jit(solution)/shard_map/ppermute | solution.py:741
  46.1 2.7 %collective-permute-start.10 = (f32[256,128]{1,0:T(8,128)S(1)}, f32[256,128]{1,0:T(8,128)S(1)}, u32[]{:S(2)}, u32[]{:S(2)}) collective-permute-start(f32[256,128]{1,0:T(8,128)S(1)} %add.194.after_ref), channel_id=1, source_target_pairs={{0,4},{1,5},{2,6},{3,7},{4,0},{5,1},{6,2},{7,3},{8,12},{9,13},{10,... | collective-permute-start | bytes 393224 | tf_op jit(solution)/shard_map/ppermute | solution.py:741
  50.4 4.7 %preload.3.rest_0_ = bf16[384,128,128]{2,1,0:T(8,128)(2,1)S(1)} custom-call(f32[256,128]{1,0:T(8,128)S(1)} %add.194.after_ref, bf16[384,128,128]{2,1,0:T(8,128)(2,1)} %bitcast.30), custom_call_target="tpu_custom_call" | custom-call | bytes 25165824 | tf_op jit(solution)/shard_map/preload/pallas_call | solution.py:301
  56.8 3.1 %adjoint.1 = (s32[200,128]{1,0:T(8,128)S(1)}, s32[200,128]{1,0:T(8,128)S(1)}, s32[200,128]{1,0:T(8,128)S(1)}, s32[200,128]{1,0:T(8,128)S(1)}, s32[200,128]{1,0:T...) custom-call(s32[384]{0:T(512)S(1)} %reduce.1.row_ref, ...), custom_call_target="tpu_custom_call" | custom-call | flops 100663296 | bytes 12582912 | tf_op jit(solution)/shard_map/adjoint/pallas_call | solution.py:410
  59.8 3.6 %collective-permute-start.17 = (s32[200,128]{1,0:T(8,128)S(1)}, s32[200,128]{1,0:T(8,128)S(1)}, u32[]{:S(2)}, u32[]{:S(2)}) collective-permute-start(s32[200,128]{1,0:T(8,128)S(1)} %get-tuple-element.43), channel_id=1, source_target_pairs={{0,8},{8,0},{16,24},{24,16},{1,9},{9,1},{17,25},{25,17},{2,10},{10... | collective-permute-start | bytes 307208 | tf_op jit(solution)/shard_map/ppermute | solution.py:741
  63.6 2.3 %collective-permute-start.19 = (s32[200,128]{1,0:T(8,128)S(1)}, s32[200,128]{1,0:T(8,128)S(1)}, u32[]{:S(2)}, u32[]{:S(2)}) collective-permute-start(s32[200,128]{1,0:T(8,128)S(1)} %get-tuple-element.45), channel_id=1, source_target_pairs={{0,24},{8,16},{16,8},{24,0},{1,25},{9,17},{17,9},{25,1},{2,26},{10... | collective-permute-start | bytes 307208 | tf_op jit(solution)/shard_map/ppermute | solution.py:741
  68.0 2.3 %collective-permute-start.14 = (s32[200,128]{1,0:T(8,128)S(1)}, s32[200,128]{1,0:T(8,128)S(1)}, u32[]{:S(2)}, u32[]{:S(2)}) collective-permute-start(s32[200,128]{1,0:T(8,128)S(1)} %get-tuple-element.39), channel_id=1, source_target_pairs={{0,24},{8,16},{16,8},{24,0},{1,25},{9,17},{17,9},{25,1},{2,26},{10... | collective-permute-start | bytes 307208 | tf_op jit(solution)/shard_map/ppermute | solution.py:741
  70.9 3.8 %collective-permute-done.18.rest_2_ = s32[200,128]{1,0:T(8,128)S(1)} collective-permute-done((s32[200,128]{1,0:T(8,128)S(1)}, s32[200,128]{1,0:T(8,128)S(1)}, u32[]{:S(2)}, u32[]{:S(2)}) %collective-permute-start.18) | collective-permute-done | bytes 102432 | tf_op jit(solution)/shard_map/ppermute | solution.py:741
  76.7 5.5 %collective-permute-done.13.rest_2_ = s32[200,128]{1,0:T(8,128)S(1)} collective-permute-done((s32[200,128]{1,0:T(8,128)S(1)}, s32[200,128]{1,0:T(8,128)S(1)}, u32[]{:S(2)}, u32[]{:S(2)}) %collective-permute-start.13) | collective-permute-done | bytes 102432 | tf_op jit(solution)/shard_map/ppermute | solution.py:741
  84.2 3.5 %pull_back.3.rest_1_ = s32[328,128]{1,0:T(8,128)S(1)} custom-call(s32[1]{0:T(128)} %bitcast.side_ref, f32[1,4,32,640]{3,2,1,0:T(8,128)S(1)} %get-tuple-element.46.own_ref, s32[328,128]{1,0:T(8,128)S(1)} %collective-permute-done.20.pair_ref, s32[328,128]{1,0:T(8,128)S(1)} %collective-permute-done.21.cross_ref, f32[32,96]{1,0:T(8,128)S(1)} %get-tuple-element.61.weights_ref, ...), custom_call_target="tpu_custom_call" | custom-call | flops 24576000 | bytes 819200 | tf_op jit(solution)/shard_map/pull_back/pallas_call | solution.py:498
  87.7 4.3 %collective-permute-start.25 = (s32[328,128]{1,0:T(8,128)S(1)}, s32[328,128]{1,0:T(8,128)S(1)}, u32[]{:S(2)}, u32[]{:S(2)}) collective-permute-start(s32[328,128]{1,0:T(8,128)S(1)} %pull_back.3.rest_1_), channel_id=1, source_target_pairs={{0,16},{8,24},{16,0},{24,8},{1,17},{9,25},{17,1},{25,9},{2,18},{10... | collective-permute-start | bytes 503816 | tf_op jit(solution)/shard_map/ppermute | solution.py:741
  92.1 3.5 %pull_back.2.rest_0_ = s32[328,128]{1,0:T(8,128)S(1)} custom-call(s32[1]{0:T(128)} %bitcast.side_ref, f32[1,4,32,640]{3,2,1,0:T(8,128)S(1)} %get-tuple-element.40.own_ref, s32[328,128]{1,0:T(8,128)S(1)} %collective-permute-done.15.pair_ref, s32[328,128]{1,0:T(8,128)S(1)} %collective-permute-done.16.cross_ref, f32[32,96]{1,0:T(8,128)S(1)} %get-tuple-element.61.weights_ref, ...), custom_call_target="tpu_custom_call" | custom-call | flops 24576000 | bytes 819200 | tf_op jit(solution)/shard_map/pull_back/pallas_call | solution.py:498
  100.2 2.9 %grams.4 = (f32[8,4,32,640]{3,2,1,0:T(8,128)S(1)}, f32[8,256]{1,0:T(8,128)S(1)}) custom-call(s32[8]{0:T(128)S(1)} %add.175.order_ref, f32[8,256]{1,0:T(8,128)S(1)} %broadcast_in_dim.20.sums_before, f32[8,4,32,640]{3,2,1,0:T(8,128)S(1)} %copy-done.1, f32[8,4,32,640]{3,2,1,0:T(8,128)S(1)} %copy-done, s32[328,128]{1,0:T(8,128)S(1)} %pull_back.2.rest_0_, ...), custom_call_target="tpu_custom_call" | custom-call | flops 41943040 | bytes 10485760 | tf_op jit(solution)/shard_map/grams/pallas_call | solution.py:594
  106.0 3.1 %collective-permute-start.26 = (s32[328,128]{1,0:T(8,128)S(1)}, s32[328,128]{1,0:T(8,128)S(1)}, u32[]{:S(2)}, u32[]{:S(2)}) collective-permute-start(s32[328,128]{1,0:T(8,128)S(1)} %collective-permute-done.24.rest_0_), channel_id=1, source_target_pairs={{0,8},{8,0},{16,24},{24,16},{1,9},{9,1},{17,25},{25,17},{2,10},{10... | collective-permute-start | bytes 503816 | tf_op jit(solution)/shard_map/ppermute | solution.py:741
  119.0 2.5 %collective-permute-start.29 = (f32[8,256]{1,0:T(8,128)S(1)}, f32[8,256]{1,0:T(8,128)S(1)}, u32[]{:S(2)}, u32[]{:S(2)}) collective-permute-start(f32[8,256]{1,0:T(8,128)S(1)} %add.198), channel_id=1, source_target_pairs={{0,2},{1,3},{2,0},{3,1},{4,6},{5,7},{6,4},{7,5},{8,10},{9,11},{10,... | collective-permute-start | bytes 24584 | tf_op jit(solution)/shard_map/ppermute | solution.py:741
  126.7 6.4 %update.1 = (f32[8,4,32,640]{3,2,1,0:T(8,128)}, f32[8,4,32,640]{3,2,1,0:T(8,128)}, f32[8,4,32,640]{3,2,1,0:T(8,128)}) custom-call(f32[8,256]{1,0:T(8,128)S(1)} %add_add_fusion.sums_ref, f32[8,4,32,640]{3,2,1,0:T(8,128)S(1)} %copy-done.3, f32[8,4,32,640]{3,2,1,0:T(8,128)S(1)} %copy-done.2, f32[8,4,32,640]{3,2,1,0:T(8,128)S(1)} %copy-done, ...), custom_call_target="tpu_custom_call" | custom-call | flops 31457280 | bytes 18350080 | tf_op jit(solution)/shard_map/update/pallas_call | solution.py:725
  (105 shorter events, 44.3 us)
Async XLA Ops:
  7.3 12.6 %collective-permute-start.3 = (s32[656,128]{1,0:T(8,128)S(1)}, s32[656,128]{1,0:T(8,128)S(1)}, u32[]{:S(2)}, u32[]{:S(2)}) collective-permute-start(s32[656,128]{1,0:T(8,128)S(1)} %get-tuple-element.31), channel_id=1, source_target_pairs={{0,1},{1,0},{2,3},{3,2},{4,5},{5,4},{6,7},{7,6},{8,9},{9,8},{10,11... | collective-permute-start | bytes 1007624 | tf_op jit(solution)/shard_map/ppermute | solution.py:741
  7.9 12.0 %collective-permute-start.4 = (s32[656,128]{1,0:T(8,128)S(1)}, s32[656,128]{1,0:T(8,128)S(1)}, u32[]{:S(2)}, u32[]{:S(2)}) collective-permute-start(s32[656,128]{1,0:T(8,128)S(1)} %get-tuple-element.31), channel_id=1, source_target_pairs={{1,2},{3,4},{5,6},{2,1},{4,3},{6,5},{9,10},{11,12},{13,14},{10,9},... | collective-permute-start | bytes 1007624 | tf_op jit(solution)/shard_map/ppermute | solution.py:752
  8.5 7.1 %collective-permute-start = (s32[1,1,384]{2,1,0:T(1,128)}, s32[1,1,384]{2,1,0:T(1,128)S(1)}, u32[]{:S(2)}, u32[]{:S(2)}) collective-permute-start(s32[1,1,384]{2,1,0:T(1,128)} %param.12), channel_id=1, source_target_pairs={{0,8},{8,0},{16,24},{24,16},{1,9},{9,1},{17,25},{25,17},{2,10},{10... | collective-permute-start | bytes 4616 | tf_op jit(solution)/shard_map/ppermute | solution.py:741
  22.0 11.3 %collective-permute-start.5 = (bf16[2,384,128]{2,1,0:T(8,128)(2,1)S(1)}, bf16[2,384,128]{2,1,0:T(8,128)(2,1)S(1)}, u32[]{:S(2)}, u32[]{:S(2)}) collective-permute-start(bf16[2,384,128]{2,1,0:T(8,128)(2,1)S(1)} %get-tuple-element.33), channel_id=1, source_target_pairs={{0,8},{8,0},{16,24},{24,16},{1,9},{9,1},{17,25},{25,17},{2,10},{10... | collective-permute-start | bytes 589832 | tf_op jit(solution)/shard_map/ppermute | solution.py:741
  22.0 11.2 %collective-permute-start.6 = (bf16[2,384,128]{2,1,0:T(8,128)(2,1)S(1)}, bf16[2,384,128]{2,1,0:T(8,128)(2,1)S(1)}, u32[]{:S(2)}, u32[]{:S(2)}) collective-permute-start(bf16[2,384,128]{2,1,0:T(8,128)(2,1)S(1)} %get-tuple-element.34), channel_id=1, source_target_pairs={{0,16},{8,24},{16,0},{24,8},{1,17},{9,25},{17,1},{25,9},{2,18},{10... | collective-permute-start | bytes 589832 | tf_op jit(solution)/shard_map/ppermute | solution.py:741
  22.7 13.8 %collective-permute-start.7 = (bf16[2,384,128]{2,1,0:T(8,128)(2,1)S(1)}, bf16[2,384,128]{2,1,0:T(8,128)(2,1)S(1)}, u32[]{:S(2)}, u32[]{:S(2)}) collective-permute-start(bf16[2,384,128]{2,1,0:T(8,128)(2,1)S(1)} %get-tuple-element.35), channel_id=1, source_target_pairs={{0,24},{8,16},{16,8},{24,0},{1,25},{9,17},{17,9},{25,1},{2,26},{10... | collective-permute-start | bytes 589832 | tf_op jit(solution)/shard_map/ppermute | solution.py:741
  46.1 9.0 %collective-permute-start.10 = (f32[256,128]{1,0:T(8,128)S(1)}, f32[256,128]{1,0:T(8,128)S(1)}, u32[]{:S(2)}, u32[]{:S(2)}) collective-permute-start(f32[256,128]{1,0:T(8,128)S(1)} %add.194.after_ref), channel_id=1, source_target_pairs={{0,4},{1,5},{2,6},{3,7},{4,0},{5,1},{6,2},{7,3},{8,12},{9,13},{10,... | collective-permute-start | bytes 393224 | tf_op jit(solution)/shard_map/ppermute | solution.py:741
  48.8 7.3 %collective-permute-start.11 = (f32[256,128]{1,0:T(8,128)S(1)}, f32[256,128]{1,0:T(8,128)S(1)}, u32[]{:S(2)}, u32[]{:S(2)}) collective-permute-start(f32[256,128]{1,0:T(8,128)S(1)} %add.194.after_ref), channel_id=1, source_target_pairs={{0,6},{1,7},{2,4},{3,5},{4,2},{5,3},{6,0},{7,1},{8,14},{9,15},{10,... | collective-permute-start | bytes 393224 | tf_op jit(solution)/shard_map/ppermute | solution.py:741
  59.8 8.2 %collective-permute-start.17 = (s32[200,128]{1,0:T(8,128)S(1)}, s32[200,128]{1,0:T(8,128)S(1)}, u32[]{:S(2)}, u32[]{:S(2)}) collective-permute-start(s32[200,128]{1,0:T(8,128)S(1)} %get-tuple-element.43), channel_id=1, source_target_pairs={{0,8},{8,0},{16,24},{24,16},{1,9},{9,1},{17,25},{25,17},{2,10},{10... | collective-permute-start | bytes 307208 | tf_op jit(solution)/shard_map/ppermute | solution.py:741
  63.5 11.2 %collective-permute-start.18 = (s32[200,128]{1,0:T(8,128)S(1)}, s32[200,128]{1,0:T(8,128)S(1)}, u32[]{:S(2)}, u32[]{:S(2)}) collective-permute-start(s32[200,128]{1,0:T(8,128)S(1)} %get-tuple-element.44), channel_id=1, source_target_pairs={{0,16},{8,24},{16,0},{24,8},{1,17},{9,25},{17,1},{25,9},{2,18},{10... | collective-permute-start | bytes 307208 | tf_op jit(solution)/shard_map/ppermute | solution.py:741
  63.6 11.1 %collective-permute-start.19 = (s32[200,128]{1,0:T(8,128)S(1)}, s32[200,128]{1,0:T(8,128)S(1)}, u32[]{:S(2)}, u32[]{:S(2)}) collective-permute-start(s32[200,128]{1,0:T(8,128)S(1)} %get-tuple-element.45), channel_id=1, source_target_pairs={{0,24},{8,16},{16,8},{24,0},{1,25},{9,17},{17,9},{25,1},{2,26},{10... | collective-permute-start | bytes 307208 | tf_op jit(solution)/shard_map/ppermute | solution.py:741
  65.9 10.8 %collective-permute-start.12 = (s32[200,128]{1,0:T(8,128)S(1)}, s32[200,128]{1,0:T(8,128)S(1)}, u32[]{:S(2)}, u32[]{:S(2)}) collective-permute-start(s32[200,128]{1,0:T(8,128)S(1)} %get-tuple-element.37), channel_id=1, source_target_pairs={{0,8},{8,0},{16,24},{24,16},{1,9},{9,1},{17,25},{25,17},{2,10},{10... | collective-permute-start | bytes 307208 | tf_op jit(solution)/shard_map/ppermute | solution.py:741
  67.0 15.2 %collective-permute-start.13 = (s32[200,128]{1,0:T(8,128)S(1)}, s32[200,128]{1,0:T(8,128)S(1)}, u32[]{:S(2)}, u32[]{:S(2)}) collective-permute-start(s32[200,128]{1,0:T(8,128)S(1)} %get-tuple-element.38), channel_id=1, source_target_pairs={{0,16},{8,24},{16,0},{24,8},{1,17},{9,25},{17,1},{25,9},{2,18},{10... | collective-permute-start | bytes 307208 | tf_op jit(solution)/shard_map/ppermute | solution.py:741
  68.0 14.2 %collective-permute-start.14 = (s32[200,128]{1,0:T(8,128)S(1)}, s32[200,128]{1,0:T(8,128)S(1)}, u32[]{:S(2)}, u32[]{:S(2)}) collective-permute-start(s32[200,128]{1,0:T(8,128)S(1)} %get-tuple-element.39), channel_id=1, source_target_pairs={{0,24},{8,16},{16,8},{24,0},{1,25},{9,17},{17,9},{25,1},{2,26},{10... | collective-permute-start | bytes 307208 | tf_op jit(solution)/shard_map/ppermute | solution.py:741
  75.8 8.4 %collective-permute-start.20 = (s32[328,128]{1,0:T(8,128)S(1)}, s32[328,128]{1,0:T(8,128)S(1)}, u32[]{:S(2)}, u32[]{:S(2)}) collective-permute-start(s32[328,128]{1,0:T(8,128)S(1)} %get-tuple-element.47), channel_id=1, source_target_pairs={{0,1},{1,0},{2,3},{3,2},{4,5},{5,4},{6,7},{7,6},{8,9},{9,8},{10,11... | collective-permute-start | bytes 503816 | tf_op jit(solution)/shard_map/ppermute | solution.py:741
  75.9 8.4 %collective-permute-start.21 = (s32[328,128]{1,0:T(8,128)S(1)}, s32[328,128]{1,0:T(8,128)S(1)}, u32[]{:S(2)}, u32[]{:S(2)}) collective-permute-start(s32[328,128]{1,0:T(8,128)S(1)} %get-tuple-element.47), channel_id=1, source_target_pairs={{1,2},{3,4},{5,6},{2,1},{4,3},{6,5},{9,10},{11,12},{13,14},{10,9},... | collective-permute-start | bytes 503816 | tf_op jit(solution)/shard_map/ppermute | solution.py:752
  83.3 8.8 %collective-permute-start.15 = (s32[328,128]{1,0:T(8,128)S(1)}, s32[328,128]{1,0:T(8,128)S(1)}, u32[]{:S(2)}, u32[]{:S(2)}) collective-permute-start(s32[328,128]{1,0:T(8,128)S(1)} %get-tuple-element.41), channel_id=1, source_target_pairs={{0,1},{1,0},{2,3},{3,2},{4,5},{5,4},{6,7},{7,6},{8,9},{9,8},{10,11... | collective-permute-start | bytes 503816 | tf_op jit(solution)/shard_map/ppermute | solution.py:741
  83.3 8.7 %collective-permute-start.16 = (s32[328,128]{1,0:T(8,128)S(1)}, s32[328,128]{1,0:T(8,128)S(1)}, u32[]{:S(2)}, u32[]{:S(2)}) collective-permute-start(s32[328,128]{1,0:T(8,128)S(1)} %get-tuple-element.41), channel_id=1, source_target_pairs={{1,2},{3,4},{5,6},{2,1},{4,3},{6,5},{9,10},{11,12},{13,14},{10,9},... | collective-permute-start | bytes 503816 | tf_op jit(solution)/shard_map/ppermute | solution.py:752
  87.7 15.4 %collective-permute-start.25 = (s32[328,128]{1,0:T(8,128)S(1)}, s32[328,128]{1,0:T(8,128)S(1)}, u32[]{:S(2)}, u32[]{:S(2)}) collective-permute-start(s32[328,128]{1,0:T(8,128)S(1)} %pull_back.3.rest_1_), channel_id=1, source_target_pairs={{0,16},{8,24},{16,0},{24,8},{1,17},{9,25},{17,1},{25,9},{2,18},{10... | collective-permute-start | bytes 503816 | tf_op jit(solution)/shard_map/ppermute | solution.py:741
  92.1 17.1 %collective-permute-start.23 = (s32[328,128]{1,0:T(8,128)S(1)}, s32[328,128]{1,0:T(8,128)S(1)}, u32[]{:S(2)}, u32[]{:S(2)}) collective-permute-start(s32[328,128]{1,0:T(8,128)S(1)} %pull_back.3.rest_1_), channel_id=1, source_target_pairs={{0,8},{8,0},{16,24},{24,16},{1,9},{9,1},{17,25},{25,17},{2,10},{10... | collective-permute-start | bytes 503816 | tf_op jit(solution)/shard_map/ppermute | solution.py:741
  95.6 13.6 %collective-permute-start.22 = (s32[328,128]{1,0:T(8,128)S(1)}, s32[328,128]{1,0:T(8,128)}, u32[]{:S(2)}, u32[]{:S(2)}) collective-permute-start(s32[328,128]{1,0:T(8,128)S(1)} %pull_back.2.rest_0_), channel_id=1, source_target_pairs={{0,8},{8,0},{16,24},{24,16},{1,9},{9,1},{17,25},{25,17},{2,10},{10... | collective-permute-start | bytes 503816 | tf_op jit(solution)/shard_map/ppermute | solution.py:741
  97.6 8.3 %collective-permute-start.24 = (s32[328,128]{1,0:T(8,128)S(1)}, s32[328,128]{1,0:T(8,128)S(1)}, u32[]{:S(2)}, u32[]{:S(2)}) collective-permute-start(s32[328,128]{1,0:T(8,128)S(1)} %pull_back.2.rest_0_), channel_id=1, source_target_pairs={{0,16},{8,24},{16,0},{24,8},{1,17},{9,25},{17,1},{25,9},{2,18},{10... | collective-permute-start | bytes 503816 | tf_op jit(solution)/shard_map/ppermute | solution.py:741
  103.1 10.2 %collective-permute-start.27 = (s32[328,128]{1,0:T(8,128)S(1)}, s32[328,128]{1,0:T(8,128)S(1)}, u32[]{:S(2)}, u32[]{:S(2)}) collective-permute-start(s32[328,128]{1,0:T(8,128)S(1)} %collective-permute-done.25.rest_1_), channel_id=1, source_target_pairs={{0,8},{8,0},{16,24},{24,16},{1,9},{9,1},{17,25},{25,17},{2,10},{10... | collective-permute-start | bytes 503816 | tf_op jit(solution)/shard_map/ppermute | solution.py:741
  106.0 8.1 %collective-permute-start.26 = (s32[328,128]{1,0:T(8,128)S(1)}, s32[328,128]{1,0:T(8,128)S(1)}, u32[]{:S(2)}, u32[]{:S(2)}) collective-permute-start(s32[328,128]{1,0:T(8,128)S(1)} %collective-permute-done.24.rest_0_), channel_id=1, source_target_pairs={{0,8},{8,0},{16,24},{24,16},{1,9},{9,1},{17,25},{25,17},{2,10},{10... | collective-permute-start | bytes 503816 | tf_op jit(solution)/shard_map/ppermute | solution.py:741
  (15 other events, 107.9 us)
